TPU v7x, 32 devices: a whole 2x2x4 slice. The times are simulated.
32 devices in a mesh: parts: 2 (over y), layer: 4 (over x, core), blk: 4 (over z).
Axes of the slice: x: 2, y: 2, z: 4, core: 2. Of those that a mesh axis runs over, the one named last changes fastest.
Arguments:
- queries: bfloat16 [4, 256, 4096], P('layer', ('parts', 'blk')), parts along dimension 1, may hold values from -6 to 6
- store: bfloat16 [4, 8192, 4096], P('layer', ('parts', 'blk')), parts along dimension 1, may hold values from -0.09375 to 0.09375
- left_factor: float32 [4, 64, 64], P('layer')
- right_factor: float32 [4, 64, 64], P('layer')
- candidates: int32 [256, 16], P(('parts', 'layer')), parts along dimension 0, may hold values from 0 to 31, as said below
Outputs:
- scores: bfloat16 [256, 4096], P(('parts', 'layer'), 'blk'), parts along dimension 0
There are 2 independent parts, one for each index of `parts`. A program takes and returns all parts, laid end to end along the dimension named above; an argument that names none is the same for every part. Nothing has to cross between parts.
Inputs may be any that keep to these rules, and one draw needn't show every extreme that they name: `candidates`: each row lists 16 different tiles.
All inputs are finite; a program needn't handle non-finite values.
Results may differ from a plain program's by a relative error of at most 0.0049.
Values may be sent and summed in bfloat16 or wider, within the bound.
No kernel may reach another device: no remote copies, remote signals or barrier semaphores. Data moves between devices by JAX's collectives and lax.ppermute only.
A program may use at most 64 MiB of HBM per device.

v0:
```python
import jax
import jax.numpy as jnp
from jax import lax
from jax.sharding import PartitionSpec as P

TILE = 128


def from_behind(value, axis, steps):
    count = lax.axis_size(axis)
    pairs = [(source, (source + steps) % count) for source in range(count)]
    return lax.ppermute(value, axis, pairs)


def precondition(queries, left_factor, right_factor):
    layers_here, count, entries = queries.shape
    side = left_factor.shape[1]
    grid = queries.astype(jnp.float32).reshape(layers_here, count, side, side)
    halfway = jnp.einsum("lij,lqjk->lqik", left_factor, grid, precision=lax.Precision.HIGHEST)
    result = jnp.einsum("lqik,lkm->lqim", halfway, right_factor, precision=lax.Precision.HIGHEST)
    return result.reshape(layers_here, count, entries).astype(jnp.bfloat16)


def per_device(queries, store, left_factor, right_factor, candidates):
    conditioned = precondition(queries, left_factor, right_factor)
    block_rows = conditioned.shape[1]
    local_examples = store.shape[1]
    cycle_size = lax.axis_size("blk")
    cycle_index = lax.axis_index("blk")

    def block_scores(block):
        return jnp.einsum("lqk,lek->qe", block, store, preferred_element_type=jnp.float32)

    def place(partial_value, block, source):
        source = jnp.mod(source, cycle_size)
        return lax.dynamic_update_slice(
            partial_value, block_scores(block), (source * block_rows, jnp.int32(0))
        )

    empty = jnp.zeros((block_rows * cycle_size, local_examples), jnp.float32)

    def one_hop(hop_count, carry):
        partial_value, moving = carry
        moving = from_behind(moving, "blk", 1)
        return (place(partial_value, moving, cycle_index - hop_count), moving)

    partial_value = place(empty, conditioned, cycle_index)
    partial_value, unused = lax.fori_loop(1, cycle_size, one_hop, (partial_value, conditioned))
    summed = lax.psum_scatter(partial_value, "layer", scatter_dimension=0, tiled=True)
    total_layers = conditioned.shape[0] * lax.axis_size("layer")
    all_tiles = local_examples * cycle_size // TILE
    chosen = jnp.any(
        candidates[:, :, None] == jnp.arange(all_tiles, dtype=jnp.int32)[None, None, :], axis=1
    )
    tiles_here = local_examples // TILE
    mine = lax.dynamic_slice_in_dim(chosen, cycle_index * tiles_here, tiles_here, 1)
    keep = jnp.repeat(mine, TILE, axis=1)
    scaled = summed / jnp.sqrt(jnp.float32(total_layers))
    return jnp.where(keep, scaled, jnp.float32(0.0)).astype(jnp.bfloat16)


def solution(mesh):
    placed = (
        P("layer", ("parts", "blk"), None),
        P("layer", ("parts", "blk"), None),
        P("layer", None, None),
        P("layer", None, None),
        P(("parts", "layer"), None),
    )
    return jax.shard_map(
        per_device,
        mesh=mesh,
        in_specs=placed,
        out_specs=P(("parts", "layer"), "blk"),
        check_vma=False,
    )
```

profile of v0, /device:TPU:0, one launch (start us, length us, event | category | flops | bytes accessed | tf_op | source)
XLA Modules:
  0.0 94.2 jit_solution(10380623942066507208)
XLA Ops:
  6.5 1.5 %reshape.58 = bf16[32,64,64]{2,1,0:T(8,128)(2,1)S(1)} reshape(bf16[1,32,4096]{2,1,0:T(8,128)(2,1)} %param.7) | data formatting | bytes 524288 | tf_op jit(solution)/shard_map/reshape
  8.0 0.7 convolution_bitcast_fusion
  8.7 2.6 %convolution_convert_fusion = bf16[32,64,64]{2,1,0:T(8,128)(2,1)S(1)} fusion(f32[32,64,64]{1,2,0:T(8,128)S(1)} %convolution_bitcast_fusion, f32[1,64,64]{2,1,0:T(8,128)} %param.10), kind=kOutput, calls=%fused_computation.7 | convolution fusion | flops 100794368 | bytes 802816 | tf_op jit(solution)/shard_map/lqik,lkm->lqim/dot_general | solution.py:20
  11.3 0.5 convert_element_type.24
  11.7 0.5 convert_element_type.23
  12.3 6.0 %fusion.8 = f32[128,1024]{1,0:T(8,128)S(1)} fusion(f32[128,1024]{1,0:T(8,128)S(1)} %broadcast_in_dim.13, s32[]{:T(128)S(6)} %select_n.46, bf16[32,4096]{1,0:T(8,128)(2,1)S(1)} %convert_element_type.23, bf16[1,1024,4096]{2,1,0:T(8,128)(2,1)} %param.8), kind=kOutput, calls=%fused_computation.8 | convolution fusion | flops 268435456 | bytes 8781828 | tf_op jit(solution)/shard_map/lqk,lek->qe/dot_general | solution.py:32
  18.2 47.1 %while.17 = (s32[]{:T(128)}, f32[128,1024]{1,0:T(8,128)S(1)}, bf16[1,32,4096]{2,1,0:T(8,128)(2,1)S(1)}, bf16[1,1024,4096]{2,1,0:T(8,128)(2,1)}, s32[]{:T(128)}, ...) while((s32[]{:T(128)}, f32[128,1024]{1,0:T(8,128)S(1)}, ...), condition=%wide.region_2.3_spmd, body=%wide.region_1.2_spmd.sunk | while | flops 268435488 | bytes 10355008 | solution.py:48
  18.2 3.1 %collective-permute-start = (bf16[1,32,4096]{2,1,0:T(8,128)(2,1)S(1)}, bf16[1,32,4096]{2,1,0:T(8,128)(2,1)S(1)}, u32[]{:S(2)}, u32[]{:S(2)}) collective-permute-start(bf16[1,32,4096]{2,1,0:T(8,128)(2,1)S(1)} %get-tuple-element.193), channel_id=1, source_target_pairs={{0,1},{1,2},{2,3},{3,0},{4,5},{5,6},{6,7},{7,4},{8,9},{9,10},{10,1... | collective-permute-start | bytes 786440 | tf_op jit(solution)/shard_map/while/body/eval_jaxpr/ppermute | solution.py:12
  21.3 8.3 %collective-permute-done = bf16[1,32,4096]{2,1,0:T(8,128)(2,1)S(1)} collective-permute-done((bf16[1,32,4096]{2,1,0:T(8,128)(2,1)S(1)}, bf16[1,32,4096]{2,1,0:T(8,128)(2,1)S(1)}, u32[]{:S(2)}, u32[]{:S(2)}) %collective-permute-start) | collective-permute-done | bytes 262176 | tf_op jit(solution)/shard_map/while/body/eval_jaxpr/ppermute | solution.py:12
  29.7 6.0 %fusion.22 = f32[128,1024]{1,0:T(8,128)S(1)} fusion(f32[128,1024]{1,0:T(8,128)S(1)} %get-tuple-element.192, s32[]{:T(128)S(6)} %select_n.52, bf16[1,1024,4096]{2,1,0:T(8,128)(2,1)} %get-tuple-element.205, bf16[1,32,4096]{2,1,0:T(8,128)(2,1)S(1)} %collective-permute-done), kind=kOutput, calls=%fused_computation.2.clone.1 | convolution fusion | flops 268435456 | bytes 8781828 | tf_op jit(solution)/shard_map/while/body/eval_jaxpr/lqk,lek->qe/dot_general | solution.py:32
  35.6 0.0 collective-permute-start
  35.7 9.3 %collective-permute-done = bf16[1,32,4096]{2,1,0:T(8,128)(2,1)S(1)} collective-permute-done((bf16[1,32,4096]{2,1,0:T(8,128)(2,1)S(1)}, bf16[1,32,4096]{2,1,0:T(8,128)(2,1)S(1)}, u32[]{:S(2)}, u32[]{:S(2)}) %collective-permute-start) | collective-permute-done | bytes 262176 | tf_op jit(solution)/shard_map/while/body/eval_jaxpr/ppermute | solution.py:12
  45.0 6.0 %fusion.22 = f32[128,1024]{1,0:T(8,128)S(1)} fusion(f32[128,1024]{1,0:T(8,128)S(1)} %get-tuple-element.192, s32[]{:T(128)S(6)} %select_n.52, bf16[1,1024,4096]{2,1,0:T(8,128)(2,1)} %get-tuple-element.205, bf16[1,32,4096]{2,1,0:T(8,128)(2,1)S(1)} %collective-permute-done), kind=kOutput, calls=%fused_computation.2.clone.1 | convolution fusion | flops 268435456 | bytes 8781828 | tf_op jit(solution)/shard_map/while/body/eval_jaxpr/lqk,lek->qe/dot_general | solution.py:32
  50.9 0.0 collective-permute-start
  51.0 8.3 %collective-permute-done = bf16[1,32,4096]{2,1,0:T(8,128)(2,1)S(1)} collective-permute-done((bf16[1,32,4096]{2,1,0:T(8,128)(2,1)S(1)}, bf16[1,32,4096]{2,1,0:T(8,128)(2,1)S(1)}, u32[]{:S(2)}, u32[]{:S(2)}) %collective-permute-start) | collective-permute-done | bytes 262176 | tf_op jit(solution)/shard_map/while/body/eval_jaxpr/ppermute | solution.py:12
  59.3 6.0 %fusion.22 = f32[128,1024]{1,0:T(8,128)S(1)} fusion(f32[128,1024]{1,0:T(8,128)S(1)} %get-tuple-element.192, s32[]{:T(128)S(6)} %select_n.52, bf16[1,1024,4096]{2,1,0:T(8,128)(2,1)} %get-tuple-element.205, bf16[1,32,4096]{2,1,0:T(8,128)(2,1)S(1)} %collective-permute-done), kind=kOutput, calls=%fused_computation.2.clone.1 | convolution fusion | flops 268435456 | bytes 8781828 | tf_op jit(solution)/shard_map/while/body/eval_jaxpr/lqk,lek->qe/dot_general | solution.py:32
  65.3 0.8 copy-done.1
  66.1 0.0 reduce-scatter.2.cloned.1.call-update
  66.1 0.1 copy.9
  66.2 0.2 fusion.11
  66.4 0.1 constant_dynamic-slice_fusion
  66.5 19.3 %reduce-scatter.2.cloned.1.call-done = f32[32,1024]{1,0:T(8,128)} async-done(((f32[128,1024]{1,0:T(8,128)}), f32[32,1024]{1,0:T(8,128)}) %reduce-scatter.2.cloned.1.call-update) | async-done | bytes 131088 | tf_op jit(solution)/shard_map/reduce_scatter | solution.py:49
  85.7 0.1 broadcast_in_dim.12
  85.8 1.6 %select_convert_fusion = bf16[32,1024]{1,0:T(8,128)(2,1)} fusion(f32[32,1024]{1,0:T(8,128)} %reduce-scatter.2.cloned.1.call-done, pred[4,8,8,128]{3,2,1,0:T(8,128)(4,1)S(1)} %bitcast.37), kind=kLoop, calls=%fused_computation.11 | loop fusion | flops 98304 | bytes 229376 | tf_op jit(solution)/shard_map/convert_element_type | solution.py:59
  (10 shorter events, 0.1 us)
Async XLA Ops:
  6.5 1.5 %copy-start = (f32[1,64,64]{2,1,0:T(8,128)S(1)}, f32[1,64,64]{2,1,0:T(8,128)}, u32[]{:S(2)}) copy-start(f32[1,64,64]{2,1,0:T(8,128)} %param.9) | copy-start | bytes 49156
  6.5 79.2 %reduce-scatter.2.cloned.1.call-start = ((), (), s32[]{:S(2)}) async-start(), calls=%async_computation.1 | async-start | bytes 655360 | tf_op jit(solution)/shard_map/reduce_scatter | solution.py:49
  18.2 47.9 %copy-start.2 = (s32[32,16]{0,1:T(8,128)S(1)}, s32[32,16]{0,1:T(8,128)}, u32[]{:S(2)}) copy-start(s32[32,16]{0,1:T(8,128)} %param.11) | copy-start | bytes 6148
  18.2 11.4 %collective-permute-start = (bf16[1,32,4096]{2,1,0:T(8,128)(2,1)S(1)}, bf16[1,32,4096]{2,1,0:T(8,128)(2,1)S(1)}, u32[]{:S(2)}, u32[]{:S(2)}) collective-permute-start(bf16[1,32,4096]{2,1,0:T(8,128)(2,1)S(1)} %get-tuple-element.193), channel_id=1, source_target_pairs={{0,1},{1,2},{2,3},{3,0},{4,5},{5,6},{6,7},{7,4},{8,9},{9,10},{10,1... | collective-permute-start | bytes 786440 | tf_op jit(solution)/shard_map/while/body/eval_jaxpr/ppermute | solution.py:12
  35.6 9.3 %collective-permute-start = (bf16[1,32,4096]{2,1,0:T(8,128)(2,1)S(1)}, bf16[1,32,4096]{2,1,0:T(8,128)(2,1)S(1)}, u32[]{:S(2)}, u32[]{:S(2)}) collective-permute-start(bf16[1,32,4096]{2,1,0:T(8,128)(2,1)S(1)} %get-tuple-element.193), channel_id=1, source_target_pairs={{0,1},{1,2},{2,3},{3,0},{4,5},{5,6},{6,7},{7,4},{8,9},{9,10},{10,1... | collective-permute-start | bytes 786440 | tf_op jit(solution)/shard_map/while/body/eval_jaxpr/ppermute | solution.py:12
  50.9 8.4 %collective-permute-start = (bf16[1,32,4096]{2,1,0:T(8,128)(2,1)S(1)}, bf16[1,32,4096]{2,1,0:T(8,128)(2,1)S(1)}, u32[]{:S(2)}, u32[]{:S(2)}) collective-permute-start(bf16[1,32,4096]{2,1,0:T(8,128)(2,1)S(1)} %get-tuple-element.193), channel_id=1, source_target_pairs={{0,1},{1,2},{2,3},{3,0},{4,5},{5,6},{6,7},{7,4},{8,9},{9,10},{10,1... | collective-permute-start | bytes 786440 | tf_op jit(solution)/shard_map/while/body/eval_jaxpr/ppermute | solution.py:12
  65.3 0.8 copy-start.1
Sparse Core Ops, SparseCore 0:
  66.2 19.4 reduce-scatter.1
where the time goes:
time: 94.6 us; the launch traced here: 94.2 us
  waiting for transfers between devices  45.2 us (48%)
  matrix products  27.1 us (29%)
  between operations  13.5 us (14%)
  local copies, waits for them, and re-layouts  3.57 us (4%)
  starting transfers between devices  3.11 us (3%)
  other arithmetic  1.72 us (2%)
    ppermute x3, waiting for transfers between devices, from_behind(): return lax.ppermute(value, axis, pairs)  25.9 us
    dot_general x4, matrix products, block_scores(): jnp.einsum('lqk,lek->qe', block, store, preferred_element_type=jnp.float32)  23.8 us
    reduce_scatter x1, waiting for transfers between devices, per_device(): lax.psum_scatter(partial_value, 'layer', scatter_dimension=0, tiled=True)  19.3 us
    ppermute x3, starting transfers between devices, from_behind(): return lax.ppermute(value, axis, pairs)  3.11 us
    dot_general x1, matrix products, precondition(): jnp.einsum('lqik,lkm->lqim', halfway, right_factor, precision=lax.Precisi...  2.56 us
  transfers between devices with their start and end apart: 4, of which 4 were waited for; matrix products, arithmetic and copies ran while one was open for 0% of the time, Pallas kernels for 0%

commit v1 on v0

v1 whole, which is shorter than its diff:
```python
import functools

import jax
import jax.numpy as jnp
from jax import lax
from jax.experimental import pallas as pl
from jax.experimental.pallas import tpu as pltpu
from jax.sharding import PartitionSpec as P

TILE = 128
GROUP = 32
LANES = 128
ROWS = 8
PIECES = 4
VMEM = 56 * 1024 * 1024


def two_parts(value):
    high = value.astype(jnp.bfloat16)
    low = (value - high.astype(jnp.float32)).astype(jnp.bfloat16)
    return high, low


def iota(shape, axis):
    return lax.broadcasted_iota(jnp.int32, shape, axis)


def dot(left, right):
    return jnp.dot(left, right, preferred_element_type=jnp.float32)


def ones_where(condition):
    return jnp.where(condition, 1.0, 0.0).astype(jnp.bfloat16)


def spread_left(left_factor, first, count):
    side = left_factor.shape[0]
    wide = ones_where(iota((side, side * ROWS), 1) // ROWS == iota((side, side * ROWS), 0))
    tall = ones_where(iota((count * ROWS, side), 0) // ROWS + first == iota((count * ROWS, side), 1))
    shape = (count * ROWS, side * ROWS)
    same = iota(shape, 0) % ROWS == iota(shape, 1) % ROWS

    def one(part):
        columns = dot(part, wide).astype(jnp.bfloat16)
        return jnp.where(same, dot(tall, columns), 0.0).astype(jnp.bfloat16)

    return [one(part) for part in two_parts(left_factor)]


def spread_right(right_factor):
    side = right_factor.shape[0]
    tall = ones_where(iota((2 * side, side), 0) % side == iota((2 * side, side), 1))
    wide = ones_where(iota((side, 8 * side), 1) % side == iota((side, 8 * side), 0))
    shape = (2 * side, 8 * side)
    same = iota(shape, 0) // side == iota(shape, 1) // (4 * side)

    def one(part):
        rows = dot(tall, part).astype(jnp.bfloat16)
        return jnp.where(same, dot(rows, wide), 0.0).astype(jnp.bfloat16)

    return [one(part) for part in two_parts(right_factor)]


def condition_kernel(first, count, queries, left_factor, right_factor, *outs):
    side = left_factor.shape[0]
    pairs = side // 2
    per_out = count // len(outs)
    lefts = spread_left(left_factor[...], first, count)
    rights = spread_right(right_factor[...])
    low_half = iota((1, 1, LANES), 2) < side
    for block in range(queries.shape[0] // GROUP):
        rows = pl.ds(block * GROUP, GROUP)
        stacked = jnp.concatenate(
            [queries[rows, pl.ds(pair * LANES, LANES)] for pair in range(pairs)], axis=0
        )
        mixed = dot(stacked, rights[0]) + dot(stacked, rights[1])
        mixed = mixed.reshape(pairs, GROUP // ROWS, ROWS, 8 * side)

        def lanes(group, parity, half):
            start = parity * 4 * side + half * LANES
            return mixed[:, group, :, start : start + LANES]

        def half_of(half):
            both = [
                jnp.where(low_half, lanes(2 * half, parity, half), lanes(2 * half + 1, parity, half))
                for parity in range(2)
            ]
            return jnp.stack(both, axis=1).reshape(side * ROWS, LANES)

        high, low = two_parts(jnp.concatenate([half_of(0), half_of(1)], axis=1))
        result = dot(lefts[0], high) + dot(lefts[0], low) + dot(lefts[1], high)
        result = result.reshape(count // 2, 2, ROWS, 2 * LANES)
        groups = []
        for half in range(2):
            even = result[:, 0, :, half * LANES : (half + 1) * LANES]
            odd = result[:, 1, :, half * LANES : (half + 1) * LANES]
            groups.append(jnp.where(low_half, even, pltpu.roll(odd, side, 2)))
            groups.append(jnp.where(low_half, pltpu.roll(even, side, 2), odd))
        done = jnp.concatenate(groups, axis=1).astype(jnp.bfloat16)
        for pair in range(count // 2):
            out = outs[2 * pair // per_out]
            out[rows, pl.ds((pair % (per_out // 2)) * LANES, LANES)] = done[pair]


def condition(queries, left_factor, right_factor, first, count, pieces):
    block_rows = queries.shape[0]
    side = left_factor.shape[0]
    width = count * side // pieces
    return pl.pallas_call(
        functools.partial(condition_kernel, first, count),
        out_shape=[jax.ShapeDtypeStruct((block_rows, width), jnp.bfloat16)] * pieces,
        compiler_params=pltpu.CompilerParams(vmem_limit_bytes=VMEM),
        cost_estimate=pl.CostEstimate(
            flops=2 * block_rows * count * side * side * 8, bytes_accessed=queries.size * 2, transcendentals=0
        ),
        name="condition",
    )(queries, left_factor, right_factor)


def score_dot(blocks, store):
    queries = jnp.concatenate([block[...] for block in blocks], axis=0)
    return lax.dot_general(
        queries, store[...], (((1,), (1,)), ((), ())), preferred_element_type=jnp.float32
    )


def score_kernel(has_sum, blocks_count, *refs):
    blocks, rest = refs[:blocks_count], refs[blocks_count:]
    value = score_dot(blocks, rest[0])
    if has_sum:
        value = value + rest[1][...]
    rest[-1][...] = value


def last_score_kernel(blocks_count, block_rows, own_rows, *refs):
    blocks, rest = refs[:blocks_count], refs[blocks_count:]
    store, so_far, outs, total = rest[0], rest[1], rest[2:-1], rest[-1]
    total[...] = score_dot(blocks, store) + so_far[...]
    cycle_index = lax.axis_index("blk")
    layer_index = lax.axis_index("layer")
    piece = min(own_rows, block_rows)
    for shift, out in enumerate(outs):
        owner = lax.rem(layer_index + shift, len(outs))
        for start in range(0, own_rows, piece):
            row = owner * own_rows + start
            slot = lax.rem(cycle_index - row // block_rows + blocks_count, blocks_count)
            place = pl.multiple_of(slot * block_rows + lax.rem(row, block_rows), piece)
            out[pl.ds(start, piece), :] = total[pl.ds(place, piece), :].astype(out.dtype)


def score(blocks, store, so_far, piece, last, layers):
    block_rows, width = blocks[0].shape
    count = block_rows * len(blocks)
    examples = store.shape[0]
    tile = 256
    whole = [pl.BlockSpec((block_rows, width), lambda e: (0, 0))] * len(blocks)
    columns = pl.BlockSpec((count, tile), lambda e: (0, e))
    operands = [*blocks, store] + ([] if so_far is None else [so_far])
    in_specs = whole + [pl.BlockSpec((tile, width), lambda e: (e, piece))]
    in_specs += [] if so_far is None else [columns]
    cost = pl.CostEstimate(
        flops=2 * count * width * examples, bytes_accessed=examples * width * 2, transcendentals=0
    )
    params = pltpu.CompilerParams(vmem_limit_bytes=VMEM)
    if not last:
        return pl.pallas_call(
            functools.partial(score_kernel, so_far is not None, len(blocks)),
            grid=(examples // tile,),
            in_specs=in_specs,
            out_specs=columns,
            out_shape=jax.ShapeDtypeStruct((count, examples), jnp.float32),
            compiler_params=params,
            cost_estimate=cost,
            name="score",
        )(*operands)
    own_rows = count // layers
    return pl.pallas_call(
        functools.partial(last_score_kernel, len(blocks), block_rows, own_rows),
        grid=(examples // tile,),
        in_specs=in_specs,
        out_specs=[pl.BlockSpec((own_rows, tile), lambda e: (0, e))] * layers,
        out_shape=[
            jax.ShapeDtypeStruct((own_rows, examples), jnp.float32 if shift == 0 else jnp.bfloat16)
            for shift in range(layers)
        ],
        scratch_shapes=[pltpu.VMEM((count, tile), jnp.float32)],
        compiler_params=params,
        cost_estimate=cost,
        name="last_score",
    )(*operands)


def finish_kernel(layers, candidates, *refs):
    parts, out = refs[:-1], refs[-1]
    total = parts[0][...]
    for part in parts[1:]:
        total = total + part[...].astype(jnp.float32)
    scaled = total / jnp.sqrt(jnp.float32(layers))
    tiles_here = out.shape[1] // TILE
    first = lax.axis_index("blk") * tiles_here
    listed = candidates[...]
    for tile in range(tiles_here):
        hit = jnp.max(jnp.where(listed == first + tile, 1.0, 0.0), axis=1, keepdims=True)
        columns = slice(tile * TILE, (tile + 1) * TILE)
        out[:, columns] = jnp.where(hit > 0.0, scaled[:, columns], 0.0).astype(out.dtype)


def finish(parts, candidates, layers):
    return pl.pallas_call(
        functools.partial(finish_kernel, layers),
        out_shape=jax.ShapeDtypeStruct(parts[0].shape, jnp.bfloat16),
        compiler_params=pltpu.CompilerParams(vmem_limit_bytes=VMEM),
        name="finish",
    )(candidates, *parts)


def shifted(value, axis, steps):
    count = lax.axis_size(axis)
    return lax.ppermute(value, axis, [(source, (source + steps) % count) for source in range(count)])


def per_device(queries, store, left_factor, right_factor, candidates):
    queries, store = queries[0], store[0]
    left_factor, right_factor = left_factor[0], right_factor[0]
    side = left_factor.shape[0]
    cycle = lax.axis_size("blk")
    layers = lax.axis_size("layer")
    count = side // PIECES
    own = condition(queries, left_factor, right_factor, 0, count, 1)
    own += condition(queries, left_factor, right_factor, count, side - count, PIECES - 1)
    held = [[piece] for piece in own]
    for _ in range(cycle - 1):
        for blocks in held:
            blocks.append(shifted(blocks[-1], "blk", 1))
    so_far = None
    for piece, blocks in enumerate(held):
        so_far = score(blocks, store, so_far, piece, piece == PIECES - 1, layers)
    parts = [so_far[0]]
    for shift in range(1, layers):
        parts.append(shifted(so_far[shift], "layer", shift))
    return finish(parts, candidates, layers)


def solution(mesh):
    placed = (
        P("layer", ("parts", "blk"), None),
        P("layer", ("parts", "blk"), None),
        P("layer", None, None),
        P("layer", None, None),
        P(("parts", "layer"), None),
    )
    return jax.shard_map(
        per_device,
        mesh=mesh,
        in_specs=placed,
        out_specs=P(("parts", "layer"), "blk"),
        check_vma=False,
    )
```

time: 94.6 us -> 56 us (0.59)
  waiting for transfers between devices: 45.2 us -> 13.6 us
  matrix products: 27.1 us -> 0 us
  Pallas kernels: 0 us -> 26 us
  between operations: 13.5 us -> 0.11 us
  starting transfers between devices: 3.11 us -> 11.8 us
  other arithmetic: 1.72 us -> 0 us
    dot_general x6 -> x0, matrix products: 27.1 us -> none  [the longest x4 23.8 us: block_scores(): jnp.einsum('lqk,lek->qe', block, store, preferred_element_type=jnp.float32)]
    pallas_call x0 -> x7, Pallas kernels: none -> 26 us  [the longest x3 12.4 us: score(): pl.pallas_call(functools.partial(score_kernel, so_far is not None, len(bl...]
    reduce_scatter x1 -> x0, waiting for transfers between devices: 19.3 us -> none  [per_device(): lax.psum_scatter(partial_value, 'layer', scatter_dimension=0, tiled=True)]
    ppermute x3 -> x15, waiting for transfers between devices: 25.9 us -> 13.6 us  [shifted(): lax.ppermute(value, axis, [(source, (source + steps) % count) for source...]
    ppermute x3 -> x15, starting transfers between devices: 3.11 us -> 11.8 us  [shifted(): lax.ppermute(value, axis, [(source, (source + steps) % count) for source...]
    unnamed x7 -> x33, local copies, waits for them, and re-layouts: 0.89 us -> 3.82 us
    convert_element_type x1 -> x0, other arithmetic: 1.56 us -> none  [per_device(): return jnp.where(keep, scaled, jnp.float32(0.0)).astype(jnp.bfloat16)]
    reshape x1 -> x0, local copies, waits for them, and re-layouts: 1.48 us -> none
  transfers between devices with their start and end apart: 4 -> 15, of which waited for: 4 -> 11; matrix products, arithmetic and copies ran while one was open for 0% -> 1% of each run, Pallas kernels for 0% -> 30%
where the time goes in v1:
time: 56 us; the launch traced here: 55.4 us
  Pallas kernels  26 us (46%)
  waiting for transfers between devices  13.6 us (24%)
  starting transfers between devices  11.8 us (21%)
  local copies, waits for them, and re-layouts  3.82 us (7%)
    ppermute x15, waiting for transfers between devices, shifted(): lax.ppermute(value, axis, [(source, (source + steps) % count) for source...  13.6 us
    pallas_call x3, Pallas kernels, score(): pl.pallas_call(functools.partial(score_kernel, so_far is not None, len(bl...  12.4 us
    ppermute x15, starting transfers between devices, shifted(): lax.ppermute(value, axis, [(source, (source + steps) % count) for source...  11.8 us
    pallas_call x2, Pallas kernels, condition(): pl.pallas_call(functools.partial(condition_kernel, first, count), out_sha...  7.74 us
    pallas_call x1, Pallas kernels, score(): pl.pallas_call(functools.partial(last_score_kernel, len(blocks), block_ro...  4.16 us
    unnamed x33, local copies, waits for them, and re-layouts  3.82 us
    pallas_call x1, Pallas kernels, finish(): pl.pallas_call(functools.partial(finish_kernel, layers), out_shape=jax.Sh...  1.72 us
  transfers between devices with their start and end apart: 15, of which 11 were waited for; matrix products, arithmetic and copies ran while one was open for 1% of the time, Pallas kernels for 30%

profile of v1, /device:TPU:0, one launch (start us, length us, event | category | flops | bytes accessed | tf_op | source)
XLA Modules:
  0.0 55.4 jit_solution(10705693449729446234)
XLA Ops:
  0.0 3.6 %condition.3.refs_0_ = bf16[32,1024]{1,0:T(8,128)(2,1)} custom-call(bf16[32,4096]{1,0:T(8,128)(2,1)} %bitcast.8, f32[64,64]{1,0:T(8,128)} %bitcast.10, f32[64,64]{1,0:T(8,128)} %bitcast.12), custom_call_target="tpu_custom_call" | custom-call | flops 33554432 | bytes 262144 | tf_op jit(solution)/shard_map/condition/pallas_call | solution.py:109
  3.6 3.0 %collective-permute-start.9 = (bf16[32,1024]{1,0:T(8,128)(2,1)}, bf16[32,1024]{1,0:T(8,128)(2,1)S(1)}, u32[]{:S(2)}, u32[]{:S(2)}) collective-permute-start(bf16[32,1024]{1,0:T(8,128)(2,1)} %condition.3.refs_0_), channel_id=1, source_target_pairs={{0,1},{1,2},{2,3},{3,0},{4,5},{5,6},{6,7},{7,4},{8,9},{9,10},{10,1... | collective-permute-start | bytes 196616 | tf_op jit(solution)/shard_map/ppermute | solution.py:219
  6.6 4.2 %condition.2 = (bf16[32,1024]{1,0:T(8,128)(2,1)}, bf16[32,1024]{1,0:T(8,128)(2,1)}, bf16[32,1024]{1,0:T(8,128)(2,1)}) custom-call(bf16[32,4096]{1,0:T(8,128)(2,1)} %bitcast.9, f32[64,64]{1,0:T(8,128)} %bitcast.11, f32[64,64]{1,0:T(8,128)} %bitcast.13), custom_call_target="tpu_custom_call" | custom-call | flops 100663296 | bytes 262144 | tf_op jit(solution)/shard_map/condition/pallas_call | solution.py:109
  10.8 1.6 %collective-permute-start.6 = (bf16[32,1024]{1,0:T(8,128)(2,1)}, bf16[32,1024]{1,0:T(8,128)(2,1)S(1)}, u32[]{:S(2)}, u32[]{:S(2)}) collective-permute-start(bf16[32,1024]{1,0:T(8,128)(2,1)} %get-tuple-element.14.refs_0_), channel_id=1, source_target_pairs={{0,1},{1,2},{2,3},{3,0},{4,5},{5,6},{6,7},{7,4},{8,9},{9,10},{10,1... | collective-permute-start | bytes 196616 | tf_op jit(solution)/shard_map/ppermute | solution.py:219
  12.3 1.6 %collective-permute-start.3 = (bf16[32,1024]{1,0:T(8,128)(2,1)}, bf16[32,1024]{1,0:T(8,128)(2,1)S(1)}, u32[]{:S(2)}, u32[]{:S(2)}) collective-permute-start(bf16[32,1024]{1,0:T(8,128)(2,1)} %get-tuple-element.13.refs_0_), channel_id=1, source_target_pairs={{0,1},{1,2},{2,3},{3,0},{4,5},{5,6},{6,7},{7,4},{8,9},{9,10},{10,1... | collective-permute-start | bytes 196616 | tf_op jit(solution)/shard_map/ppermute | solution.py:219
  14.0 1.7 %collective-permute-start.10 = (bf16[32,1024]{1,0:T(8,128)(2,1)S(1)}, bf16[32,1024]{1,0:T(8,128)(2,1)S(1)}, u32[]{:S(2)}, u32[]{:S(2)}) collective-permute-start(bf16[32,1024]{1,0:T(8,128)(2,1)S(1)} %collective-permute-done.9.refs_1_), channel_id=1, source_target_pairs={{0,1},{1,2},{2,3},{3,0},{4,5},{5,6},{6,7},{7,4},{8,9},{9,10},{10,1... | collective-permute-start | bytes 196616 | tf_op jit(solution)/shard_map/ppermute | solution.py:219
  15.7 2.0 %collective-permute-done.6.refs_1_ = bf16[32,1024]{1,0:T(8,128)(2,1)S(1)} collective-permute-done((bf16[32,1024]{1,0:T(8,128)(2,1)}, bf16[32,1024]{1,0:T(8,128)(2,1)S(1)}, u32[]{:S(2)}, u32[]{:S(2)}) %collective-permute-start.6) | collective-permute-done | bytes 65568 | tf_op jit(solution)/shard_map/ppermute | solution.py:219
  17.7 1.6 %collective-permute-done.3.refs_1_ = bf16[32,1024]{1,0:T(8,128)(2,1)S(1)} collective-permute-done((bf16[32,1024]{1,0:T(8,128)(2,1)}, bf16[32,1024]{1,0:T(8,128)(2,1)S(1)}, u32[]{:S(2)}, u32[]{:S(2)}) %collective-permute-start.3) | collective-permute-done | bytes 65568 | tf_op jit(solution)/shard_map/ppermute | solution.py:219
  19.3 1.6 %collective-permute-done.refs_1_ = bf16[32,1024]{1,0:T(8,128)(2,1)S(1)} collective-permute-done((bf16[32,1024]{1,0:T(8,128)(2,1)}, bf16[32,1024]{1,0:T(8,128)(2,1)S(1)}, u32[]{:S(2)}, u32[]{:S(2)}) %collective-permute-start) | collective-permute-done | bytes 65568 | tf_op jit(solution)/shard_map/ppermute | solution.py:219
  21.0 0.9 %collective-permute-done.10.refs_2_ = bf16[32,1024]{1,0:T(8,128)(2,1)S(1)} collective-permute-done((bf16[32,1024]{1,0:T(8,128)(2,1)S(1)}, bf16[32,1024]{1,0:T(8,128)(2,1)S(1)}, u32[]{:S(2)}, u32[]{:S(2)}) %collective-permute-start.10) | collective-permute-done | bytes 65568 | tf_op jit(solution)/shard_map/ppermute | solution.py:219
  21.8 0.8 %collective-permute-start.11 = (bf16[32,1024]{1,0:T(8,128)(2,1)S(1)}, bf16[32,1024]{1,0:T(8,128)(2,1)S(1)}, u32[]{:S(2)}, u32[]{:S(2)}) collective-permute-start(bf16[32,1024]{1,0:T(8,128)(2,1)S(1)} %collective-permute-done.10.refs_2_), channel_id=1, source_target_pairs={{0,1},{1,2},{2,3},{3,0},{4,5},{5,6},{6,7},{7,4},{8,9},{9,10},{10,1... | collective-permute-start | bytes 196616 | tf_op jit(solution)/shard_map/ppermute | solution.py:219
  22.7 1.6 %collective-permute-done.7.refs_2_ = bf16[32,1024]{1,0:T(8,128)(2,1)S(1)} collective-permute-done((bf16[32,1024]{1,0:T(8,128)(2,1)S(1)}, bf16[32,1024]{1,0:T(8,128)(2,1)S(1)}, u32[]{:S(2)}, u32[]{:S(2)}) %collective-permute-start.7) | collective-permute-done | bytes 65568 | tf_op jit(solution)/shard_map/ppermute | solution.py:219
  24.3 1.6 %collective-permute-done.4.refs_2_ = bf16[32,1024]{1,0:T(8,128)(2,1)S(1)} collective-permute-done((bf16[32,1024]{1,0:T(8,128)(2,1)S(1)}, bf16[32,1024]{1,0:T(8,128)(2,1)S(1)}, u32[]{:S(2)}, u32[]{:S(2)}) %collective-permute-start.4) | collective-permute-done | bytes 65568 | tf_op jit(solution)/shard_map/ppermute | solution.py:219
  25.9 1.8 %collective-permute-done.1.refs_2_ = bf16[32,1024]{1,0:T(8,128)(2,1)S(1)} collective-permute-done((bf16[32,1024]{1,0:T(8,128)(2,1)S(1)}, bf16[32,1024]{1,0:T(8,128)(2,1)S(1)}, u32[]{:S(2)}, u32[]{:S(2)}) %collective-permute-start.1) | collective-permute-done | bytes 65568 | tf_op jit(solution)/shard_map/ppermute | solution.py:219
  27.7 1.0 %collective-permute-done.11.refs_3_ = bf16[32,1024]{1,0:T(8,128)(2,1)S(1)} collective-permute-done((bf16[32,1024]{1,0:T(8,128)(2,1)S(1)}, bf16[32,1024]{1,0:T(8,128)(2,1)S(1)}, u32[]{:S(2)}, u32[]{:S(2)}) %collective-permute-start.11) | collective-permute-done | bytes 65568 | tf_op jit(solution)/shard_map/ppermute | solution.py:219
  29.3 4.1 %score.3.refs_5_ = f32[128,1024]{1,0:T(8,128)} custom-call(bf16[32,1024]{1,0:T(8,128)(2,1)} %condition.3.refs_0_, bf16[32,1024]{1,0:T(8,128)(2,1)} %copy-done.2, bf16[32,1024]{1,0:T(8,128)(2,1)} %copy-done.7, bf16[32,1024]{1,0:T(8,128)(2,1)} %copy-done.11, bf16[1024,4096]{1,0:T(8,128)(2,1)} %bitcast.4), custom_call_target="tpu_custom_call" | custom-call | flops 268435456 | bytes 2097152 | tf_op jit(solution)/shard_map/score/pallas_call | solution.py:166
  34.0 4.2 %score.4.refs_5_ = f32[128,1024]{1,0:T(8,128)} custom-call(bf16[32,1024]{1,0:T(8,128)(2,1)} %get-tuple-element.14.refs_0_, bf16[32,1024]{1,0:T(8,128)(2,1)} %copy-done.3, bf16[32,1024]{1,0:T(8,128)(2,1)} %copy-done.6, bf16[32,1024]{1,0:T(8,128)(2,1)} %copy-done.10, bf16[1024,4096]{1,0:T(8,128)(2,1)} %bitcast.5, f32[128,1024]{1,0:T(8,128)} %score.3.refs_5_), custom_call_target="tpu_custom_call" | custom-call | flops 268435456 | bytes 2097152 | tf_op jit(solution)/shard_map/score/pallas_call | solution.py:166
  38.9 4.2 %score.5.refs_5_ = f32[128,1024]{1,0:T(8,128)} custom-call(bf16[32,1024]{1,0:T(8,128)(2,1)} %get-tuple-element.13.refs_0_, bf16[32,1024]{1,0:T(8,128)(2,1)} %copy-done.1, bf16[32,1024]{1,0:T(8,128)(2,1)} %copy-done.5, bf16[32,1024]{1,0:T(8,128)(2,1)} %copy-done.9, bf16[1024,4096]{1,0:T(8,128)(2,1)} %bitcast.6, f32[128,1024]{1,0:T(8,128)} %score.4.refs_5_), custom_call_target="tpu_custom_call" | custom-call | flops 268435456 | bytes 2097152 | tf_op jit(solution)/shard_map/score/pallas_call | solution.py:166
  43.7 4.2 %last_score.1 = (f32[32,1024]{1,0:T(8,128)}, bf16[32,1024]{1,0:T(8,128)(2,1)}, bf16[32,1024]{1,0:T(8,128)(2,1)}, bf16[32,1024]{1,0:T(8,128)(2,1)}) custom-call(bf16[32,1024]{1,0:T(8,128)(2,1)} %get-tuple-element.12.refs_0_, bf16[32,1024]{1,0:T(8,128)(2,1)} %copy-done, bf16[32,1024]{1,0:T(8,128)(2,1)} %copy-done.4, bf16[32,1024]{1,0:T(8,128)(2,1)} %copy-done.8, ...), custom_call_target="tpu_custom_call" | custom-call | flops 268435456 | bytes 2097152 | tf_op jit(solution)/shard_map/last_score/pallas_call | solution.py:177
  47.9 1.5 %collective-permute-start.13 = (bf16[32,1024]{1,0:T(8,128)(2,1)}, bf16[32,1024]{1,0:T(8,128)(2,1)S(1)}, u32[]{:S(2)}, u32[]{:S(2)}) collective-permute-start(bf16[32,1024]{1,0:T(8,128)(2,1)} %get-tuple-element.17), channel_id=1, source_target_pairs={{0,8},{4,12},{8,0},{12,4},{1,9},{5,13},{9,1},{13,5},{2,10},{6,14},... | collective-permute-start | bytes 196616 | tf_op jit(solution)/shard_map/ppermute | solution.py:219
  49.4 1.4 %collective-permute-start.14 = (bf16[32,1024]{1,0:T(8,128)(2,1)}, bf16[32,1024]{1,0:T(8,128)(2,1)S(1)}, u32[]{:S(2)}, u32[]{:S(2)}) collective-permute-start(bf16[32,1024]{1,0:T(8,128)(2,1)} %get-tuple-element.18), channel_id=1, source_target_pairs={{0,12},{4,0},{8,4},{12,8},{1,13},{5,1},{9,5},{13,9},{2,14},{6,2},{... | collective-permute-start | bytes 196616 | tf_op jit(solution)/shard_map/ppermute | solution.py:219
  50.8 0.7 %copy.6.candidates = s32[32,16]{1,0:T(8,128)} copy(s32[32,16]{0,1:T(8,128)S(1)} %copy-done.15) | data formatting | bytes 4096 | tf_op args[4]
  51.9 0.9 %collective-permute-done.13.refs_2_ = bf16[32,1024]{1,0:T(8,128)(2,1)S(1)} collective-permute-done((bf16[32,1024]{1,0:T(8,128)(2,1)}, bf16[32,1024]{1,0:T(8,128)(2,1)S(1)}, u32[]{:S(2)}, u32[]{:S(2)}) %collective-permute-start.13) | collective-permute-done | bytes 65568 | tf_op jit(solution)/shard_map/ppermute | solution.py:219
  53.7 1.7 %finish.1 = bf16[32,1024]{1,0:T(8,128)(2,1)} custom-call(s32[32,16]{1,0:T(8,128)} %copy.6.candidates, f32[32,1024]{1,0:T(8,128)} %get-tuple-element.15.refs_0_, bf16[32,1024]{1,0:T(8,128)(2,1)} %copy-done.12, bf16[32,1024]{1,0:T(8,128)(2,1)} %copy-done.13, bf16[32,1024]{1,0:T(8,128)(2,1)} %copy-done.14), custom_call_target="tpu_custom_call" | custom-call | tf_op jit(solution)/shard_map/finish/pallas_call | solution.py:209
  (46 shorter events, 3.9 us)
Async XLA Ops:
  3.6 10.4 %collective-permute-start.9 = (bf16[32,1024]{1,0:T(8,128)(2,1)}, bf16[32,1024]{1,0:T(8,128)(2,1)S(1)}, u32[]{:S(2)}, u32[]{:S(2)}) collective-permute-start(bf16[32,1024]{1,0:T(8,128)(2,1)} %condition.3.refs_0_), channel_id=1, source_target_pairs={{0,1},{1,2},{2,3},{3,0},{4,5},{5,6},{6,7},{7,4},{8,9},{9,10},{10,1... | collective-permute-start | bytes 196616 | tf_op jit(solution)/shard_map/ppermute | solution.py:219
  10.8 6.9 %collective-permute-start.6 = (bf16[32,1024]{1,0:T(8,128)(2,1)}, bf16[32,1024]{1,0:T(8,128)(2,1)S(1)}, u32[]{:S(2)}, u32[]{:S(2)}) collective-permute-start(bf16[32,1024]{1,0:T(8,128)(2,1)} %get-tuple-element.14.refs_0_), channel_id=1, source_target_pairs={{0,1},{1,2},{2,3},{3,0},{4,5},{5,6},{6,7},{7,4},{8,9},{9,10},{10,1... | collective-permute-start | bytes 196616 | tf_op jit(solution)/shard_map/ppermute | solution.py:219
  12.3 7.0 %collective-permute-start.3 = (bf16[32,1024]{1,0:T(8,128)(2,1)}, bf16[32,1024]{1,0:T(8,128)(2,1)S(1)}, u32[]{:S(2)}, u32[]{:S(2)}) collective-permute-start(bf16[32,1024]{1,0:T(8,128)(2,1)} %get-tuple-element.13.refs_0_), channel_id=1, source_target_pairs={{0,1},{1,2},{2,3},{3,0},{4,5},{5,6},{6,7},{7,4},{8,9},{9,10},{10,1... | collective-permute-start | bytes 196616 | tf_op jit(solution)/shard_map/ppermute | solution.py:219
  13.9 7.0 %collective-permute-start = (bf16[32,1024]{1,0:T(8,128)(2,1)}, bf16[32,1024]{1,0:T(8,128)(2,1)S(1)}, u32[]{:S(2)}, u32[]{:S(2)}) collective-permute-start(bf16[32,1024]{1,0:T(8,128)(2,1)} %get-tuple-element.12.refs_0_), channel_id=1, source_target_pairs={{0,1},{1,2},{2,3},{3,0},{4,5},{5,6},{6,7},{7,4},{8,9},{9,10},{10,1... | collective-permute-start | bytes 196616 | tf_op jit(solution)/shard_map/ppermute | solution.py:219
  14.0 14.7 %copy-start.2 = (bf16[32,1024]{1,0:T(8,128)(2,1)}, bf16[32,1024]{1,0:T(8,128)(2,1)S(1)}, u32[]{:S(2)}) copy-start(bf16[32,1024]{1,0:T(8,128)(2,1)S(1)} %collective-permute-done.9.refs_1_) | copy-start | bytes 196612
  14.0 7.9 %collective-permute-start.10 = (bf16[32,1024]{1,0:T(8,128)(2,1)S(1)}, bf16[32,1024]{1,0:T(8,128)(2,1)S(1)}, u32[]{:S(2)}, u32[]{:S(2)}) collective-permute-start(bf16[32,1024]{1,0:T(8,128)(2,1)S(1)} %collective-permute-done.9.refs_1_), channel_id=1, source_target_pairs={{0,1},{1,2},{2,3},{3,0},{4,5},{5,6},{6,7},{7,4},{8,9},{9,10},{10,1... | collective-permute-start | bytes 196616 | tf_op jit(solution)/shard_map/ppermute | solution.py:219
  17.7 15.7 %copy-start.3 = (bf16[32,1024]{1,0:T(8,128)(2,1)}, bf16[32,1024]{1,0:T(8,128)(2,1)S(1)}, u32[]{:S(2)}) copy-start(bf16[32,1024]{1,0:T(8,128)(2,1)S(1)} %collective-permute-done.6.refs_1_) | copy-start | bytes 196612
  17.7 6.6 %collective-permute-start.7 = (bf16[32,1024]{1,0:T(8,128)(2,1)S(1)}, bf16[32,1024]{1,0:T(8,128)(2,1)S(1)}, u32[]{:S(2)}, u32[]{:S(2)}) collective-permute-start(bf16[32,1024]{1,0:T(8,128)(2,1)S(1)} %collective-permute-done.6.refs_1_), channel_id=1, source_target_pairs={{0,1},{1,2},{2,3},{3,0},{4,5},{5,6},{6,7},{7,4},{8,9},{9,10},{10,1... | collective-permute-start | bytes 196616 | tf_op jit(solution)/shard_map/ppermute | solution.py:219
  19.3 18.9 %copy-start.1 = (bf16[32,1024]{1,0:T(8,128)(2,1)}, bf16[32,1024]{1,0:T(8,128)(2,1)S(1)}, u32[]{:S(2)}) copy-start(bf16[32,1024]{1,0:T(8,128)(2,1)S(1)} %collective-permute-done.3.refs_1_) | copy-start | bytes 196612
  19.3 6.6 %collective-permute-start.4 = (bf16[32,1024]{1,0:T(8,128)(2,1)S(1)}, bf16[32,1024]{1,0:T(8,128)(2,1)S(1)}, u32[]{:S(2)}, u32[]{:S(2)}) collective-permute-start(bf16[32,1024]{1,0:T(8,128)(2,1)S(1)} %collective-permute-done.3.refs_1_), channel_id=1, source_target_pairs={{0,1},{1,2},{2,3},{3,0},{4,5},{5,6},{6,7},{7,4},{8,9},{9,10},{10,1... | collective-permute-start | bytes 196616 | tf_op jit(solution)/shard_map/ppermute | solution.py:219
  21.0 17.3 %copy-start = (bf16[32,1024]{1,0:T(8,128)(2,1)}, bf16[32,1024]{1,0:T(8,128)(2,1)S(1)}, u32[]{:S(2)}) copy-start(bf16[32,1024]{1,0:T(8,128)(2,1)S(1)} %collective-permute-done.refs_1_) | copy-start | bytes 196612
  21.0 6.7 %collective-permute-start.1 = (bf16[32,1024]{1,0:T(8,128)(2,1)S(1)}, bf16[32,1024]{1,0:T(8,128)(2,1)S(1)}, u32[]{:S(2)}, u32[]{:S(2)}) collective-permute-start(bf16[32,1024]{1,0:T(8,128)(2,1)S(1)} %collective-permute-done.refs_1_), channel_id=1, source_target_pairs={{0,1},{1,2},{2,3},{3,0},{4,5},{5,6},{6,7},{7,4},{8,9},{9,10},{10,1... | collective-permute-start | bytes 196616 | tf_op jit(solution)/shard_map/ppermute | solution.py:219
  21.8 6.9 %copy-start.7 = (bf16[32,1024]{1,0:T(8,128)(2,1)}, bf16[32,1024]{1,0:T(8,128)(2,1)S(1)}, u32[]{:S(2)}) copy-start(bf16[32,1024]{1,0:T(8,128)(2,1)S(1)} %collective-permute-done.10.refs_2_) | copy-start | bytes 196612
  21.8 6.8 %collective-permute-start.11 = (bf16[32,1024]{1,0:T(8,128)(2,1)S(1)}, bf16[32,1024]{1,0:T(8,128)(2,1)S(1)}, u32[]{:S(2)}, u32[]{:S(2)}) collective-permute-start(bf16[32,1024]{1,0:T(8,128)(2,1)S(1)} %collective-permute-done.10.refs_2_), channel_id=1, source_target_pairs={{0,1},{1,2},{2,3},{3,0},{4,5},{5,6},{6,7},{7,4},{8,9},{9,10},{10,1... | collective-permute-start | bytes 196616 | tf_op jit(solution)/shard_map/ppermute | solution.py:219
  24.3 9.1 %copy-start.6 = (bf16[32,1024]{1,0:T(8,128)(2,1)}, bf16[32,1024]{1,0:T(8,128)(2,1)S(1)}, u32[]{:S(2)}) copy-start(bf16[32,1024]{1,0:T(8,128)(2,1)S(1)} %collective-permute-done.7.refs_2_) | copy-start | bytes 196612
  24.3 9.1 %collective-permute-start.8 = (bf16[32,1024]{1,0:T(8,128)(2,1)S(1)}, bf16[32,1024]{1,0:T(8,128)(2,1)S(1)}, u32[]{:S(2)}, u32[]{:S(2)}) collective-permute-start(bf16[32,1024]{1,0:T(8,128)(2,1)S(1)} %collective-permute-done.7.refs_2_), channel_id=1, source_target_pairs={{0,1},{1,2},{2,3},{3,0},{4,5},{5,6},{6,7},{7,4},{8,9},{9,10},{10,1... | collective-permute-start | bytes 196616 | tf_op jit(solution)/shard_map/ppermute | solution.py:219
  25.9 12.3 %copy-start.5 = (bf16[32,1024]{1,0:T(8,128)(2,1)}, bf16[32,1024]{1,0:T(8,128)(2,1)S(1)}, u32[]{:S(2)}) copy-start(bf16[32,1024]{1,0:T(8,128)(2,1)S(1)} %collective-permute-done.4.refs_2_) | copy-start | bytes 196612
  25.9 12.3 %collective-permute-start.5 = (bf16[32,1024]{1,0:T(8,128)(2,1)S(1)}, bf16[32,1024]{1,0:T(8,128)(2,1)S(1)}, u32[]{:S(2)}, u32[]{:S(2)}) collective-permute-start(bf16[32,1024]{1,0:T(8,128)(2,1)S(1)} %collective-permute-done.4.refs_2_), channel_id=1, source_target_pairs={{0,1},{1,2},{2,3},{3,0},{4,5},{5,6},{6,7},{7,4},{8,9},{9,10},{10,1... | collective-permute-start | bytes 196616 | tf_op jit(solution)/shard_map/ppermute | solution.py:219
  27.7 10.5 %copy-start.4 = (bf16[32,1024]{1,0:T(8,128)(2,1)}, bf16[32,1024]{1,0:T(8,128)(2,1)S(1)}, u32[]{:S(2)}) copy-start(bf16[32,1024]{1,0:T(8,128)(2,1)S(1)} %collective-permute-done.1.refs_2_) | copy-start | bytes 196612
  27.7 15.4 %collective-permute-start.2 = (bf16[32,1024]{1,0:T(8,128)(2,1)S(1)}, bf16[32,1024]{1,0:T(8,128)(2,1)S(1)}, u32[]{:S(2)}, u32[]{:S(2)}) collective-permute-start(bf16[32,1024]{1,0:T(8,128)(2,1)S(1)} %collective-permute-done.1.refs_2_), channel_id=1, source_target_pairs={{0,1},{1,2},{2,3},{3,0},{4,5},{5,6},{6,7},{7,4},{8,9},{9,10},{10,1... | collective-permute-start | bytes 196616 | tf_op jit(solution)/shard_map/ppermute | solution.py:219
  38.2 12.6 %copy-start.15 = (s32[32,16]{0,1:T(8,128)S(1)}, s32[32,16]{0,1:T(8,128)}, u32[]{:S(2)}) copy-start(s32[32,16]{0,1:T(8,128)} %param.9) | copy-start | bytes 6148
  47.8 4.0 %collective-permute-start.12 = (bf16[32,1024]{1,0:T(8,128)(2,1)}, bf16[32,1024]{1,0:T(8,128)(2,1)S(1)}, u32[]{:S(2)}, u32[]{:S(2)}) collective-permute-start(bf16[32,1024]{1,0:T(8,128)(2,1)} %get-tuple-element.16), channel_id=1, source_target_pairs={{0,4},{4,8},{8,12},{12,0},{1,5},{5,9},{9,13},{13,1},{2,6},{6,10},{... | collective-permute-start | bytes 196616 | tf_op jit(solution)/shard_map/ppermute | solution.py:219
  47.9 4.9 %collective-permute-start.13 = (bf16[32,1024]{1,0:T(8,128)(2,1)}, bf16[32,1024]{1,0:T(8,128)(2,1)S(1)}, u32[]{:S(2)}, u32[]{:S(2)}) collective-permute-start(bf16[32,1024]{1,0:T(8,128)(2,1)} %get-tuple-element.17), channel_id=1, source_target_pairs={{0,8},{4,12},{8,0},{12,4},{1,9},{5,13},{9,1},{13,5},{2,10},{6,14},... | collective-permute-start | bytes 196616 | tf_op jit(solution)/shard_map/ppermute | solution.py:219
  49.4 3.6 %collective-permute-start.14 = (bf16[32,1024]{1,0:T(8,128)(2,1)}, bf16[32,1024]{1,0:T(8,128)(2,1)S(1)}, u32[]{:S(2)}, u32[]{:S(2)}) collective-permute-start(bf16[32,1024]{1,0:T(8,128)(2,1)} %get-tuple-element.18), channel_id=1, source_target_pairs={{0,12},{4,0},{8,4},{12,8},{1,13},{5,1},{9,5},{13,9},{2,14},{6,2},{... | collective-permute-start | bytes 196616 | tf_op jit(solution)/shard_map/ppermute | solution.py:219
  (7 other events, 4.9 us)

commit v2 on v0

v2 whole, which is shorter than its diff:
```python
import functools

import jax
import jax.numpy as jnp
from jax import lax
from jax.experimental import pallas as pl
from jax.experimental.pallas import tpu as pltpu
from jax.sharding import PartitionSpec as P

TILE = 128
GROUP = 32
LANES = 128
ROWS = 8
VMEM = 24 * 1024 * 1024


def two_parts(value):
    high = value.astype(jnp.bfloat16)
    low = (value - high.astype(jnp.float32)).astype(jnp.bfloat16)
    return high, low


def iota(shape, axis):
    return lax.broadcasted_iota(jnp.int32, shape, axis)


def dot(left, right):
    return jnp.dot(left, right, preferred_element_type=jnp.float32)


def ones_where(condition):
    return jnp.where(condition, 1.0, 0.0).astype(jnp.bfloat16)


def spread_left(left_factor):
    side = left_factor.shape[0]
    wide = ones_where(iota((side, side * ROWS), 1) // ROWS == iota((side, side * ROWS), 0))
    columns = dot(jnp.concatenate(two_parts(left_factor), axis=0), wide).reshape(2, side, 1, side * ROWS)
    same = iota((1, ROWS, side * ROWS), 1) == iota((1, ROWS, side * ROWS), 2) % ROWS
    parts = [jnp.where(same, columns[part], 0.0).reshape(side * ROWS, side * ROWS) for part in range(2)]
    return jnp.concatenate([part.astype(jnp.bfloat16) for part in parts], axis=1)


def spread_right(right_factor):
    side = right_factor.shape[0]
    wide = ones_where(iota((side, 4 * side), 1) % side == iota((side, 4 * side), 0))
    same = iota((4 * side, 4 * side), 0) // side == iota((4 * side, 4 * side), 1) // side
    high, low = [
        jnp.where(same, jnp.concatenate([dot(part, wide)] * 4, axis=0), 0.0).astype(jnp.bfloat16)
        for part in two_parts(right_factor)
    ]
    return jnp.concatenate([high, low, high], axis=0)


def condition_kernel(queries, left_factor, right_factor, whole, *halves):
    side = left_factor.shape[0]
    pairs = side // 2
    left = spread_left(left_factor[...])
    right = spread_right(right_factor[...])
    low_half = iota((1, 1, LANES), 2) < side
    per_half = pairs // len(halves)
    for block in range(queries.shape[0] // GROUP):
        rows = pl.ds(block * GROUP, GROUP)
        straight = jnp.stack(
            [queries[rows, pl.ds(pair * LANES, LANES)].astype(jnp.float32) for pair in range(pairs)]
        )
        swapped = pltpu.roll(straight, side, 2).reshape(pairs, GROUP // ROWS, ROWS, LANES)
        straight = straight.reshape(pairs, GROUP // ROWS, ROWS, LANES)
        columns = []
        for group in (0, 2):
            even = jnp.where(low_half, straight[:, group], swapped[:, group + 1])
            odd = jnp.where(low_half, swapped[:, group], straight[:, group + 1])
            columns.append(jnp.stack([even, odd], axis=1).reshape(side * ROWS, LANES))
        grid = jnp.concatenate(columns, axis=1).astype(jnp.bfloat16)
        halfway = dot(left, jnp.concatenate([grid, grid], axis=0))
        high, low = two_parts(halfway)
        result = dot(jnp.concatenate([high, high, low], axis=1), right)
        result = result.reshape(pairs, 2, ROWS, 2 * LANES)
        groups = []
        for half in range(2):
            even = result[:, 0, :, half * LANES : (half + 1) * LANES]
            odd = result[:, 1, :, half * LANES : (half + 1) * LANES]
            groups.append(jnp.where(low_half, even, pltpu.roll(odd, side, 2)))
            groups.append(jnp.where(low_half, pltpu.roll(even, side, 2), odd))
        done = jnp.concatenate(groups, axis=1).astype(jnp.bfloat16)
        for pair in range(pairs):
            whole[rows, pl.ds(pair * LANES, LANES)] = done[pair]
            halves[pair // per_half][rows, pl.ds(pair % per_half * LANES, LANES)] = done[pair]


def in_vmem(count):
    return [pl.BlockSpec(memory_space=pltpu.VMEM)] * count


def condition(queries, left_factor, right_factor):
    block_rows, entries = queries.shape
    shapes = [entries, entries // 2, entries // 2]
    return pl.pallas_call(
        condition_kernel,
        in_specs=in_vmem(3),
        out_specs=in_vmem(3),
        out_shape=[jax.ShapeDtypeStruct((block_rows, width), jnp.bfloat16) for width in shapes],
        compiler_params=pltpu.CompilerParams(vmem_limit_bytes=VMEM),
        cost_estimate=pl.CostEstimate(
            flops=block_rows * entries * 4096, bytes_accessed=queries.size * 4, transcendentals=0
        ),
        name="condition",
    )(queries, left_factor, right_factor)


def score_block(blocks, store, first, write):
    rows = [jnp.concatenate([piece[...] for piece in pieces], axis=1) for pieces in blocks]
    queries = jnp.concatenate(rows, axis=0)
    turned = queries.T
    width = queries.shape[1]
    tile = 256

    def one(step, carry):
        place = pl.ds(pl.multiple_of(step * tile, tile), tile)
        value = dot(store[place, pl.ds(first, width)], turned)
        write(place, value.T)
        return carry

    lax.fori_loop(0, store.shape[0] // tile, one, 0)


def score_kernel(layout, first, *refs):
    refs = list(refs)
    blocks = [[refs.pop(0) for _ in range(pieces)] for pieces in layout]
    store, out = refs

    def write(place, value):
        out[:, place] = value

    score_block(blocks, store, first, write)


def score(blocks, store, first):
    count = sum(pieces[0].shape[0] for pieces in blocks)
    width = sum(piece.shape[1] for piece in blocks[0])
    operands = [piece for pieces in blocks for piece in pieces]
    examples = store.shape[0]
    return pl.pallas_call(
        functools.partial(score_kernel, [len(pieces) for pieces in blocks], first),
        in_specs=in_vmem(len(operands) + 1),
        out_specs=in_vmem(1)[0],
        out_shape=jax.ShapeDtypeStruct((count, examples), jnp.float32),
        compiler_params=pltpu.CompilerParams(vmem_limit_bytes=VMEM),
        cost_estimate=pl.CostEstimate(
            flops=2 * count * width * examples, bytes_accessed=examples * width * 2, transcendentals=0
        ),
        name="score",
    )(*operands, store)


def last_score_kernel(first, slot_of, last_piece, store, early, late, out, total):
    early_rows = early.shape[0]
    block_rows = last_piece.shape[0]
    total[pl.ds(0, early_rows), :] = early[...]

    def write(place, value):
        total[pl.ds(early_rows, block_rows), place] = late[:, place] + value

    score_block([[last_piece]], store, first, write)
    index = lax.axis_index("blk")
    owners, own_rows = out.shape[:2]
    piece = min(own_rows, block_rows)
    for owner in range(owners):
        for start in range(0, own_rows, piece):
            block, row = divmod(owner * own_rows + start, block_rows)
            place = pl.multiple_of(slot_of(index, block) * block_rows + row, piece)
            out[owner, pl.ds(start, piece), :] = total[pl.ds(place, piece), :].astype(out.dtype)


def last_score(last_piece, store, first, early, late, slot_of, layers):
    block_rows, width = last_piece.shape
    examples = store.shape[0]
    count = early.shape[0] + block_rows
    return pl.pallas_call(
        functools.partial(last_score_kernel, first, slot_of),
        in_specs=in_vmem(4),
        out_specs=in_vmem(1)[0],
        out_shape=jax.ShapeDtypeStruct((layers, count // layers, examples), jnp.bfloat16),
        scratch_shapes=[pltpu.VMEM((count, examples), jnp.float32)],
        compiler_params=pltpu.CompilerParams(vmem_limit_bytes=VMEM),
        cost_estimate=pl.CostEstimate(
            flops=2 * block_rows * width * examples, bytes_accessed=examples * width * 2, transcendentals=0
        ),
        name="last_score",
    )(last_piece, store, early, late)


def finish_kernel(layers, candidates, parts, out):
    total = parts[0].astype(jnp.float32)
    for layer in range(1, layers):
        total = total + parts[layer].astype(jnp.float32)
    scaled = total / jnp.sqrt(jnp.float32(layers))
    tiles_here = out.shape[1] // TILE
    first = lax.axis_index("blk") * tiles_here
    listed = candidates[...]
    for tile in range(tiles_here):
        hit = jnp.max(jnp.where(listed == first + tile, 1.0, 0.0), axis=1, keepdims=True)
        columns = slice(tile * TILE, (tile + 1) * TILE)
        out[:, columns] = jnp.where(hit > 0.0, scaled[:, columns], 0.0).astype(out.dtype)


def finish(parts, candidates):
    layers, own_rows, examples = parts.shape
    return pl.pallas_call(
        functools.partial(finish_kernel, layers),
        in_specs=in_vmem(2),
        out_specs=in_vmem(1)[0],
        out_shape=jax.ShapeDtypeStruct((own_rows, examples), jnp.bfloat16),
        compiler_params=pltpu.CompilerParams(vmem_limit_bytes=VMEM),
        name="finish",
    )(candidates, parts)


def permuted(value, target_of):
    count = lax.axis_size("blk")
    return lax.ppermute(value, "blk", [(source, target_of(source) % count) for source in range(count)])


def gather_line(own):
    whole, halves = own[0], own[1:]
    far = [permuted(half, lambda source: source ^ 2) for half in halves]
    near = permuted(whole, lambda source: source ^ 1)
    last = [permuted(half, lambda source: source ^ 1) for half in far]
    return [[whole], [near], far], last, lax.bitwise_xor


def gather_ring(own):
    count = lax.axis_size("blk")
    held, moving = [[own[0]]], own[1:]
    for _ in range(count - 1):
        moving = [permuted(half, lambda source: source + 1) for half in moving]
        held.append(moving)
    return held[:-1], held[-1], lambda index, block: lax.rem(index - block + count, count)


def per_device(queries, store, left_factor, right_factor, candidates):
    queries, store = queries[0], store[0]
    layers = lax.axis_size("layer")
    own = condition(queries, left_factor[0], right_factor[0])
    gather = gather_line if lax.axis_size("blk") == 4 else gather_ring
    early, last, slot_of = gather(own)
    half = last[0].shape[1]
    early_scores = score(early, store, 0)
    late_scores = score([[last[0]]], store, 0)
    partial = last_score(last[1], store, half, early_scores, late_scores, slot_of, layers)
    return finish(lax.all_to_all(partial, "layer", 0, 0), candidates)


def solution(mesh):
    placed = (
        P("layer", ("parts", "blk"), None),
        P("layer", ("parts", "blk"), None),
        P("layer", None, None),
        P("layer", None, None),
        P(("parts", "layer"), None),
    )
    return jax.shard_map(
        per_device,
        mesh=mesh,
        in_specs=placed,
        out_specs=P(("parts", "layer"), "blk"),
        check_vma=False,
    )
```

time: 94.6 us -> 47.3 us (0.50)
  matrix products: 27.1 us -> 0 us
  waiting for transfers between devices: 45.2 us -> 18.1 us
  between operations: 13.5 us -> 0.05 us
  Pallas kernels: 0 us -> 9.46 us
  starting transfers between devices: 3.11 us -> 11.8 us
  local copies, waits for them, and re-layouts: 3.57 us -> 7.49 us
  other arithmetic: 1.72 us -> 0 us
    dot_general x6 -> x0, matrix products: 27.1 us -> none  [the longest x4 23.8 us: block_scores(): jnp.einsum('lqk,lek->qe', block, store, preferred_element_type=jnp.float32)]
    reduce_scatter x1 -> x0, waiting for transfers between devices: 19.3 us -> none  [per_device(): lax.psum_scatter(partial_value, 'layer', scatter_dimension=0, tiled=True)]
    ppermute x3 -> x5, waiting for transfers between devices: 25.9 us -> 12.2 us  [permuted(): lax.ppermute(value, 'blk', [(source, target_of(source) % count) for sourc...]
    pallas_call x0 -> x5, Pallas kernels: none -> 9.46 us  [the longest x2 4.89 us: score(): pl.pallas_call(functools.partial(score_kernel, [len(pieces) for pieces in...]
    unnamed x7 -> x13, local copies, waits for them, and re-layouts: 0.89 us -> 7.49 us
    all_to_all x0 -> x1, waiting for transfers between devices: none -> 5.92 us  [per_device(): return finish(lax.all_to_all(partial, 'layer', 0, 0), candidates)]
    ppermute x3 -> x5, starting transfers between devices: 3.11 us -> 8.37 us  [permuted(): lax.ppermute(value, 'blk', [(source, target_of(source) % count) for sourc...]
    all_to_all x0 -> x1, starting transfers between devices: none -> 3.4 us  [per_device(): return finish(lax.all_to_all(partial, 'layer', 0, 0), candidates)]
  transfers between devices with their start and end apart: 4 -> 6, of which waited for: 4 -> 4; matrix products, arithmetic and copies ran while one was open for 0% -> 0% of each run, Pallas kernels for 0% -> 10%
where the time goes in v2:
time: 47.3 us; the launch traced here: 46.9 us
  waiting for transfers between devices  18.1 us (38%)
  starting transfers between devices  11.8 us (25%)
  Pallas kernels  9.46 us (20%)
  local copies, waits for them, and re-layouts  7.49 us (16%)
    ppermute x5, waiting for transfers between devices, permuted(): lax.ppermute(value, 'blk', [(source, target_of(source) % count) for sourc...  12.2 us
    ppermute x5, starting transfers between devices, permuted(): lax.ppermute(value, 'blk', [(source, target_of(source) % count) for sourc...  8.37 us
    unnamed x13, local copies, waits for them, and re-layouts  7.49 us
    all_to_all x1, waiting for transfers between devices, per_device(): return finish(lax.all_to_all(partial, 'layer', 0, 0), candidates)  5.92 us
    pallas_call x2, Pallas kernels, score(): pl.pallas_call(functools.partial(score_kernel, [len(pieces) for pieces in...  4.89 us
    all_to_all x1, starting transfers between devices, per_device(): return finish(lax.all_to_all(partial, 'layer', 0, 0), candidates)  3.4 us
    pallas_call x1, Pallas kernels, last_score(): pl.pallas_call(functools.partial(last_score_kernel, first, slot_of), in_s...  2.57 us
    pallas_call x1, Pallas kernels, condition(): pl.pallas_call(condition_kernel, in_specs=in_vmem(3), out_specs=in_vmem(3...  1.25 us
  transfers between devices with their start and end apart: 6, of which 4 were waited for; matrix products, arithmetic and copies ran while one was open for 0% of the time, Pallas kernels for 10%

profile of v2, /device:TPU:0, one launch (start us, length us, event | category | flops | bytes accessed | tf_op | source)
XLA Modules:
  0.0 46.9 jit_solution(13976008506675656838)
XLA Ops:
  0.0 0.9 %copy-done.2 = bf16[1,32,4096]{2,1,0:T(8,128)(2,1)S(1)} copy-done((bf16[1,32,4096]{2,1,0:T(8,128)(2,1)S(1)}, bf16[1,32,4096]{2,1,0:T(8,128)(2,1)}, u32[]{:S(2)}) %copy-start.2) | copy-done | bytes 262168
  1.0 0.8 %copy-done.3 = f32[1,64,64]{2,1,0:T(8,128)S(1)} copy-done((f32[1,64,64]{2,1,0:T(8,128)S(1)}, f32[1,64,64]{2,1,0:T(8,128)}, u32[]{:S(2)}) %copy-start.3) | copy-done | bytes 16408
  1.7 0.8 %copy-done.4 = f32[1,64,64]{2,1,0:T(8,128)S(1)} copy-done((f32[1,64,64]{2,1,0:T(8,128)S(1)}, f32[1,64,64]{2,1,0:T(8,128)}, u32[]{:S(2)}) %copy-start.4) | copy-done | bytes 16408
  2.5 1.3 %condition.1 = (bf16[32,4096]{1,0:T(8,128)(2,1)S(1)}, bf16[32,2048]{1,0:T(8,128)(2,1)S(1)}, bf16[32,2048]{1,0:T(8,128)(2,1)S(1)}) custom-call(bf16[32,4096]{1,0:T(8,128)(2,1)S(1)} %bitcast.7, f32[64,64]{1,0:T(8,128)S(1)} %bitcast.8, f32[64,64]{1,0:T(8,128)S(1)} %bitcast.9), custom_call_target="tpu_custom_call" | custom-call | flops 536870912 | bytes 524288 | tf_op jit(solution)/shard_map/condition/pallas_call | solution.py:98
  3.7 4.1 %collective-permute-start.3 = (bf16[32,2048]{1,0:T(8,128)(2,1)S(1)}, bf16[32,2048]{1,0:T(8,128)(2,1)S(1)}, u32[]{:S(2)}, u32[]{:S(2)}) collective-permute-start(bf16[32,2048]{1,0:T(8,128)(2,1)S(1)} %get-tuple-element.10), channel_id=1, source_target_pairs={{0,2},{1,3},{2,0},{3,1},{4,6},{5,7},{6,4},{7,5},{8,10},{9,11},{10,... | collective-permute-start | bytes 393224 | tf_op jit(solution)/shard_map/ppermute | solution.py:221
  7.8 1.6 %collective-permute-start.2 = (bf16[32,4096]{1,0:T(8,128)(2,1)S(1)}, bf16[32,4096]{1,0:T(8,128)(2,1)S(1)}, u32[]{:S(2)}, u32[]{:S(2)}) collective-permute-start(bf16[32,4096]{1,0:T(8,128)(2,1)S(1)} %get-tuple-element.9.refs_0_), channel_id=1, source_target_pairs={{0,1},{1,0},{2,3},{3,2},{4,5},{5,4},{6,7},{7,6},{8,9},{9,8},{10,11... | collective-permute-start | bytes 786440 | tf_op jit(solution)/shard_map/ppermute | solution.py:221
  9.4 0.3 collective-permute-start
  9.7 5.3 %collective-permute-done.3.refs_2_ = bf16[32,2048]{1,0:T(8,128)(2,1)S(1)} collective-permute-done((bf16[32,2048]{1,0:T(8,128)(2,1)S(1)}, bf16[32,2048]{1,0:T(8,128)(2,1)S(1)}, u32[]{:S(2)}, u32[]{:S(2)}) %collective-permute-start.3) | collective-permute-done | bytes 131104 | tf_op jit(solution)/shard_map/ppermute | solution.py:221
  15.1 0.0 collective-permute-start.4
  15.1 5.1 %collective-permute-done.refs_3_ = bf16[32,2048]{1,0:T(8,128)(2,1)S(1)} collective-permute-done((bf16[32,2048]{1,0:T(8,128)(2,1)S(1)}, bf16[32,2048]{1,0:T(8,128)(2,1)S(1)}, u32[]{:S(2)}, u32[]{:S(2)}) %collective-permute-start) | collective-permute-done | bytes 131104 | tf_op jit(solution)/shard_map/ppermute | solution.py:221
  20.2 2.4 %collective-permute-start.1 = (bf16[32,2048]{1,0:T(8,128)(2,1)S(1)}, bf16[32,2048]{1,0:T(8,128)(2,1)S(1)}, u32[]{:S(2)}, u32[]{:S(2)}) collective-permute-start(bf16[32,2048]{1,0:T(8,128)(2,1)S(1)} %collective-permute-done.refs_3_), channel_id=1, source_target_pairs={{0,1},{1,0},{2,3},{3,2},{4,5},{5,4},{6,7},{7,6},{8,9},{9,8},{10,11... | collective-permute-start | bytes 393224 | tf_op jit(solution)/shard_map/ppermute | solution.py:221
  22.5 1.7 %collective-permute-done.4.refs_0_ = bf16[32,2048]{1,0:T(8,128)(2,1)S(1)} collective-permute-done((bf16[32,2048]{1,0:T(8,128)(2,1)S(1)}, bf16[32,2048]{1,0:T(8,128)(2,1)S(1)}, u32[]{:S(2)}, u32[]{:S(2)}) %collective-permute-start.4) | collective-permute-done | bytes 131104 | tf_op jit(solution)/shard_map/ppermute | solution.py:221
  24.3 3.4 %copy-done = bf16[1,1024,4096]{2,1,0:T(8,128)(2,1)S(1)} copy-done((bf16[1,1024,4096]{2,1,0:T(8,128)(2,1)S(1)}, bf16[1,1024,4096]{2,1,0:T(8,128)(2,1)}, u32[]{:S(2)}) %copy-start) | copy-done | bytes 8388632
  27.6 1.8 %score.3.late = f32[32,1024]{1,0:T(8,128)S(1)} custom-call(bf16[32,2048]{1,0:T(8,128)(2,1)S(1)} %collective-permute-done.4.refs_0_, bf16[1024,4096]{1,0:T(8,128)(2,1)S(1)} %bitcast.4), custom_call_target="tpu_custom_call" | custom-call | flops 134217728 | bytes 4194304 | tf_op jit(solution)/shard_map/score/pallas_call | solution.py:143
  29.5 0.0 collective-permute-done.2.refs_1_
  29.5 1.6 %copy-done.1 = bf16[1,1024,4096]{2,1,0:T(8,128)(2,1)S(1)} copy-done((bf16[1,1024,4096]{2,1,0:T(8,128)(2,1)S(1)}, bf16[1,1024,4096]{2,1,0:T(8,128)(2,1)}, u32[]{:S(2)}) %copy-start.1) | copy-done | bytes 8388632
  31.0 3.1 %score.2.early = f32[96,1024]{1,0:T(8,128)S(1)} custom-call(bf16[32,4096]{1,0:T(8,128)(2,1)S(1)} %get-tuple-element.9.refs_0_, bf16[32,4096]{1,0:T(8,128)(2,1)S(1)} %collective-permute-done.2.refs_1_, bf16[32,2048]{1,0:T(8,128)(2,1)S(1)} %collective-permute-done.3.refs_2_, bf16[32,2048]{1,0:T(8,128)(2,1)S(1)} %collective-permute-done.refs_3_, ...), custom_call_target="tpu_custom_call" | custom-call | flops 805306368 | bytes 8388608 | tf_op jit(solution)/shard_map/score/pallas_call | solution.py:143
  34.1 0.0 collective-permute-done.1.last_piece
  34.1 2.6 %last_score.1 = bf16[4,32,1024]{2,1,0:T(8,128)(2,1)} custom-call(bf16[32,2048]{1,0:T(8,128)(2,1)S(1)} %collective-permute-done.1.last_piece, bf16[1024,4096]{1,0:T(8,128)(2,1)S(1)} %bitcast.6, f32[96,1024]{1,0:T(8,128)S(1)} %score.2.early, f32[32,1024]{1,0:T(8,128)S(1)} %score.3.late), custom_call_target="tpu_custom_call" | custom-call | flops 134217728 | bytes 4194304 | tf_op jit(solution)/shard_map/last_score/pallas_call | solution.py:179
  36.7 3.4 %all-to-all-start = ((bf16[4,32,1024]{2,1,0:T(8,128)(2,1)}), bf16[4,32,1024]{2,1,0:T(8,128)(2,1)S(1)}, u32[]{:S(2)}, u32[]{:S(2)}) async-start(bf16[4,32,1024]{2,1,0:T(8,128)(2,1)} %last_score.1), calls=%async_computation | async-start | bytes 524288 | tf_op jit(solution)/shard_map/all_to_all | solution.py:251
  40.1 0.0 copy-done.5
  40.1 0.1 copy.6.candidates
  40.2 5.9 %all-to-all-done.parts = bf16[4,32,1024]{2,1,0:T(8,128)(2,1)S(1)} async-done(((bf16[4,32,1024]{2,1,0:T(8,128)(2,1)}), bf16[4,32,1024]{2,1,0:T(8,128)(2,1)S(1)}, u32[]{:S(2)}, u32[]{:S(2)}) %all-to-all-start) | async-done | bytes 262176 | tf_op jit(solution)/shard_map/all_to_all | solution.py:251
  46.1 0.7 %finish.1 = bf16[32,1024]{1,0:T(8,128)(2,1)} custom-call(s32[32,16]{1,0:T(8,128)S(1)} %copy.6.candidates, bf16[4,32,1024]{2,1,0:T(8,128)(2,1)S(1)} %all-to-all-done.parts), custom_call_target="tpu_custom_call" | custom-call | tf_op jit(solution)/shard_map/finish/pallas_call | solution.py:209
  (6 shorter events, 0.0 us)
Async XLA Ops:
  0.0 0.9 %copy-start.2 = (bf16[1,32,4096]{2,1,0:T(8,128)(2,1)S(1)}, bf16[1,32,4096]{2,1,0:T(8,128)(2,1)}, u32[]{:S(2)}) copy-start(bf16[1,32,4096]{2,1,0:T(8,128)(2,1)} %param.5) | copy-start | bytes 786436
  1.0 0.8 %copy-start.3 = (f32[1,64,64]{2,1,0:T(8,128)S(1)}, f32[1,64,64]{2,1,0:T(8,128)}, u32[]{:S(2)}) copy-start(f32[1,64,64]{2,1,0:T(8,128)} %param.7) | copy-start | bytes 49156
  1.7 0.8 %copy-start.4 = (f32[1,64,64]{2,1,0:T(8,128)S(1)}, f32[1,64,64]{2,1,0:T(8,128)}, u32[]{:S(2)}) copy-start(f32[1,64,64]{2,1,0:T(8,128)} %param.8) | copy-start | bytes 49156
  3.7 11.3 %collective-permute-start.3 = (bf16[32,2048]{1,0:T(8,128)(2,1)S(1)}, bf16[32,2048]{1,0:T(8,128)(2,1)S(1)}, u32[]{:S(2)}, u32[]{:S(2)}) collective-permute-start(bf16[32,2048]{1,0:T(8,128)(2,1)S(1)} %get-tuple-element.10), channel_id=1, source_target_pairs={{0,2},{1,3},{2,0},{3,1},{4,6},{5,7},{6,4},{7,5},{8,10},{9,11},{10,... | collective-permute-start | bytes 393224 | tf_op jit(solution)/shard_map/ppermute | solution.py:221
  7.8 21.6 %collective-permute-start.2 = (bf16[32,4096]{1,0:T(8,128)(2,1)S(1)}, bf16[32,4096]{1,0:T(8,128)(2,1)S(1)}, u32[]{:S(2)}, u32[]{:S(2)}) collective-permute-start(bf16[32,4096]{1,0:T(8,128)(2,1)S(1)} %get-tuple-element.9.refs_0_), channel_id=1, source_target_pairs={{0,1},{1,0},{2,3},{3,2},{4,5},{5,4},{6,7},{7,6},{8,9},{9,8},{10,11... | collective-permute-start | bytes 786440 | tf_op jit(solution)/shard_map/ppermute | solution.py:221
  9.4 10.8 %collective-permute-start = (bf16[32,2048]{1,0:T(8,128)(2,1)S(1)}, bf16[32,2048]{1,0:T(8,128)(2,1)S(1)}, u32[]{:S(2)}, u32[]{:S(2)}) collective-permute-start(bf16[32,2048]{1,0:T(8,128)(2,1)S(1)} %get-tuple-element.8), channel_id=1, source_target_pairs={{0,2},{1,3},{2,0},{3,1},{4,6},{5,7},{6,4},{7,5},{8,10},{9,11},{10,... | collective-permute-start | bytes 393224 | tf_op jit(solution)/shard_map/ppermute | solution.py:221
  15.1 9.2 %collective-permute-start.4 = (bf16[32,2048]{1,0:T(8,128)(2,1)S(1)}, bf16[32,2048]{1,0:T(8,128)(2,1)S(1)}, u32[]{:S(2)}, u32[]{:S(2)}) collective-permute-start(bf16[32,2048]{1,0:T(8,128)(2,1)S(1)} %collective-permute-done.3.refs_2_), channel_id=1, source_target_pairs={{0,1},{1,0},{2,3},{3,2},{4,5},{5,4},{6,7},{7,6},{8,9},{9,8},{10,11... | collective-permute-start | bytes 393224 | tf_op jit(solution)/shard_map/ppermute | solution.py:221
  20.2 13.9 %collective-permute-start.1 = (bf16[32,2048]{1,0:T(8,128)(2,1)S(1)}, bf16[32,2048]{1,0:T(8,128)(2,1)S(1)}, u32[]{:S(2)}, u32[]{:S(2)}) collective-permute-start(bf16[32,2048]{1,0:T(8,128)(2,1)S(1)} %collective-permute-done.refs_3_), channel_id=1, source_target_pairs={{0,1},{1,0},{2,3},{3,2},{4,5},{5,4},{6,7},{7,6},{8,9},{9,8},{10,11... | collective-permute-start | bytes 393224 | tf_op jit(solution)/shard_map/ppermute | solution.py:221
  24.3 3.4 %copy-start = (bf16[1,1024,4096]{2,1,0:T(8,128)(2,1)S(1)}, bf16[1,1024,4096]{2,1,0:T(8,128)(2,1)}, u32[]{:S(2)}) copy-start(bf16[1,1024,4096]{2,1,0:T(8,128)(2,1)} %param.6) | copy-start | bytes 25165828
  27.6 3.4 %copy-start.1 = (bf16[1,1024,4096]{2,1,0:T(8,128)(2,1)S(1)}, bf16[1,1024,4096]{2,1,0:T(8,128)(2,1)}, u32[]{:S(2)}) copy-start(bf16[1,1024,4096]{2,1,0:T(8,128)(2,1)} %param.6) | copy-start | bytes 25165828
  29.5 10.7 %copy-start.5 = (s32[32,16]{0,1:T(8,128)S(1)}, s32[32,16]{0,1:T(8,128)}, u32[]{:S(2)}) copy-start(s32[32,16]{0,1:T(8,128)} %param.9) | copy-start | bytes 6148
  36.7 9.4 %all-to-all-start = ((bf16[4,32,1024]{2,1,0:T(8,128)(2,1)}), bf16[4,32,1024]{2,1,0:T(8,128)(2,1)S(1)}, u32[]{:S(2)}, u32[]{:S(2)}) async-start(bf16[4,32,1024]{2,1,0:T(8,128)(2,1)} %last_score.1), calls=%async_computation | async-start | bytes 524288 | tf_op jit(solution)/shard_map/all_to_all | solution.py:251

commit v3 on v2

v3 whole, which is shorter than its diff:
```python
import functools

import jax
import jax.numpy as jnp
from jax import lax
from jax.experimental import pallas as pl
from jax.experimental.pallas import tpu as pltpu
from jax.sharding import PartitionSpec as P

TILE = 128
GROUP = 32
LANES = 128
ROWS = 8
VMEM = 24 * 1024 * 1024


def two_parts(value):
    high = value.astype(jnp.bfloat16)
    low = (value - high.astype(jnp.float32)).astype(jnp.bfloat16)
    return high, low


def iota(shape, axis):
    return lax.broadcasted_iota(jnp.int32, shape, axis)


def dot(left, right):
    return jnp.dot(left, right, preferred_element_type=jnp.float32)


def ones_where(condition):
    return jnp.where(condition, 1.0, 0.0).astype(jnp.bfloat16)


def spread_left(left_factor):
    side = left_factor.shape[0]
    wide = ones_where(iota((side, side * ROWS), 1) // ROWS == iota((side, side * ROWS), 0))
    columns = dot(jnp.concatenate(two_parts(left_factor), axis=0), wide).reshape(2, side, 1, side * ROWS)
    same = iota((1, ROWS, side * ROWS), 1) == iota((1, ROWS, side * ROWS), 2) % ROWS
    parts = [jnp.where(same, columns[part], 0.0).reshape(side * ROWS, side * ROWS) for part in range(2)]
    return jnp.concatenate([part.astype(jnp.bfloat16) for part in parts], axis=1)


def spread_right(right_factor):
    side = right_factor.shape[0]
    wide = ones_where(iota((side, 4 * side), 1) % side == iota((side, 4 * side), 0))
    same = iota((4 * side, 4 * side), 0) // side == iota((4 * side, 4 * side), 1) // side
    high, low = [
        jnp.where(same, jnp.concatenate([dot(part, wide)] * 4, axis=0), 0.0).astype(jnp.bfloat16)
        for part in two_parts(right_factor)
    ]
    return jnp.concatenate([high, low, high], axis=0)


def condition_kernel(queries_in, left_in, right_in, whole, low, high, queries, left_factor, right_factor, arrived):
    halves = (low, high)
    copies = [
        pltpu.make_async_copy(source.at[0], target, arrived.at[place])
        for place, (source, target) in enumerate(
            [(left_in, left_factor), (right_in, right_factor), (queries_in, queries)]
        )
    ]
    for copy in copies:
        copy.start()
    side = left_factor.shape[0]
    pairs = side // 2
    copies[0].wait()
    copies[1].wait()
    left = spread_left(left_factor[...])
    right = spread_right(right_factor[...])
    low_half = iota((1, 1, LANES), 2) < side
    per_half = pairs // len(halves)
    copies[2].wait()
    for block in range(queries.shape[0] // GROUP):
        rows = pl.ds(block * GROUP, GROUP)
        straight = jnp.stack(
            [queries[rows, pl.ds(pair * LANES, LANES)].astype(jnp.float32) for pair in range(pairs)]
        )
        swapped = pltpu.roll(straight, side, 2).reshape(pairs, GROUP // ROWS, ROWS, LANES)
        straight = straight.reshape(pairs, GROUP // ROWS, ROWS, LANES)
        columns = []
        for group in (0, 2):
            even = jnp.where(low_half, straight[:, group], swapped[:, group + 1])
            odd = jnp.where(low_half, swapped[:, group], straight[:, group + 1])
            columns.append(jnp.stack([even, odd], axis=1).reshape(side * ROWS, LANES))
        grid = jnp.concatenate(columns, axis=1).astype(jnp.bfloat16)
        halfway = dot(left, jnp.concatenate([grid, grid], axis=0))
        high, low = two_parts(halfway)
        result = dot(jnp.concatenate([high, high, low], axis=1), right)
        result = result.reshape(pairs, 2, ROWS, 2 * LANES)
        groups = []
        for half in range(2):
            even = result[:, 0, :, half * LANES : (half + 1) * LANES]
            odd = result[:, 1, :, half * LANES : (half + 1) * LANES]
            groups.append(jnp.where(low_half, even, pltpu.roll(odd, side, 2)))
            groups.append(jnp.where(low_half, pltpu.roll(even, side, 2), odd))
        done = jnp.concatenate(groups, axis=1).astype(jnp.bfloat16)
        for pair in range(pairs):
            whole[rows, pl.ds(pair * LANES, LANES)] = done[pair]
            halves[pair // per_half][rows, pl.ds(pair % per_half * LANES, LANES)] = done[pair]


def in_vmem(count):
    return [pl.BlockSpec(memory_space=pltpu.VMEM)] * count


def condition(queries, left_factor, right_factor):
    unused, block_rows, entries = queries.shape
    side = left_factor.shape[1]
    shapes = [entries, entries // 2, entries // 2]
    return pl.pallas_call(
        condition_kernel,
        in_specs=[pl.BlockSpec(memory_space=pltpu.HBM)] * 3,
        out_specs=in_vmem(3),
        out_shape=[jax.ShapeDtypeStruct((block_rows, width), jnp.bfloat16) for width in shapes],
        scratch_shapes=[
            pltpu.VMEM((block_rows, entries), jnp.bfloat16),
            pltpu.VMEM((side, side), jnp.float32),
            pltpu.VMEM((side, side), jnp.float32),
            pltpu.SemaphoreType.DMA((3,)),
        ],
        compiler_params=pltpu.CompilerParams(vmem_limit_bytes=VMEM),
        cost_estimate=pl.CostEstimate(
            flops=block_rows * entries * 4096, bytes_accessed=queries.size * 4, transcendentals=0
        ),
        name="condition",
    )(*[pltpu.with_memory_space_constraint(value, pltpu.HBM) for value in (queries, left_factor, right_factor)])


STEP = 256


def score_block(blocks, store, first, write, arrived=None):
    rows = [jnp.concatenate([piece[...] for piece in pieces], axis=1) for pieces in blocks]
    queries = jnp.concatenate(rows, axis=0)
    turned = queries.T
    width = queries.shape[1]

    def one(step, carry):
        place = pl.ds(pl.multiple_of(step * STEP, STEP), STEP)
        if arrived is not None:
            arrived(step)
        value = dot(store[0, place, pl.ds(first, width)], turned)
        write(place, value.T)
        return carry

    lax.fori_loop(0, store.shape[1] // STEP, one, 0)


def score_kernel(layout, first, *refs):
    refs = list(refs)
    blocks = [[refs.pop(0) for _ in range(pieces)] for pieces in layout]
    store, out = refs

    def write(place, value):
        out[:, place] = value

    score_block(blocks, store, first, write)


def call_score(kernel, blocks, store, others, name, store_space=pltpu.VMEM, **shapes):
    operands = [piece for pieces in blocks for piece in pieces]
    count = sum(pieces[0].shape[0] for pieces in blocks)
    width = sum(piece.shape[1] for piece in blocks[0])
    examples = store.shape[1]
    return pl.pallas_call(
        kernel,
        in_specs=in_vmem(len(operands)) + [pl.BlockSpec(memory_space=store_space)] + in_vmem(len(others)),
        out_specs=jax.tree.map(lambda unused: in_vmem(1)[0], shapes["out_shape"]),
        compiler_params=pltpu.CompilerParams(vmem_limit_bytes=VMEM),
        cost_estimate=pl.CostEstimate(
            flops=2 * count * width * examples, bytes_accessed=examples * width * 2, transcendentals=0
        ),
        name=name,
        **shapes,
    )(*operands, store, *others)


def score(blocks, store, first):
    count = sum(pieces[0].shape[0] for pieces in blocks)
    layout = [len(pieces) for pieces in blocks]
    shape = jax.ShapeDtypeStruct((count, store.shape[1]), jnp.float32)
    kernel = functools.partial(score_kernel, layout, first)
    return call_score(kernel, blocks, store, [], "score", out_shape=shape)


def pair_kernel(layout, first, has_sum, layers, *refs):
    refs = list(refs)
    blocks = [[refs.pop(0) for _ in range(pieces)] for pieces in layout]
    store = refs.pop(0)
    so_far = refs.pop(0) if has_sum else None
    arrived = None
    if not has_sum:
        far_store = store
        store, semaphores = refs[-2:]
        refs = refs[:-2]

        def copy_of(step):
            place = pl.ds(pl.multiple_of(step * STEP, STEP), STEP)
            return pltpu.make_async_copy(far_store.at[0, place], store.at[0, place], semaphores.at[step])

        for step in range(store.shape[1] // STEP):
            copy_of(step).start()

        def arrived(step):
            copy_of(step).wait()

    outs, total = refs[:-1], refs[-1]

    def write(place, value):
        total[:, place] = value if so_far is None else value + so_far[:, place]

    score_block(blocks, store, first, write, arrived)
    rows = outs[0].shape[0]
    index, layer = lax.axis_index("blk"), lax.axis_index("layer")
    for shift, out in enumerate(outs):
        owner = lax.rem(layer + shift, layers)
        slot = lax.bitwise_and(lax.bitwise_xor(index, owner), 1)
        out[...] = total[pl.ds(pl.multiple_of(slot * rows, rows), rows), :].astype(out.dtype)


def score_pair(blocks, store, first, so_far, layers):
    rows = blocks[0][0].shape[0]
    examples = store.shape[1]
    kernel = functools.partial(pair_kernel, [len(pieces) for pieces in blocks], first, so_far is not None, layers)
    scratch = [pltpu.VMEM((2 * rows, examples), jnp.float32)]
    if so_far is None:
        scratch += [pltpu.VMEM(store.shape, store.dtype), pltpu.SemaphoreType.DMA((examples // STEP,))]
        store = pltpu.with_memory_space_constraint(store, pltpu.HBM)
    return call_score(
        kernel,
        blocks,
        store,
        [] if so_far is None else [so_far],
        "score_pair",
        pltpu.HBM if so_far is None else pltpu.VMEM,
        out_shape=[
            jax.ShapeDtypeStruct((rows, examples), jnp.float32 if shift == 0 else jnp.bfloat16)
            for shift in range(layers)
        ],
        scratch_shapes=scratch,
    )


def write_rows(total, layers, listed, out):
    scaled = total / jnp.sqrt(jnp.float32(layers))
    tiles_here = out.shape[1] // TILE
    first = lax.axis_index("blk") * tiles_here
    for tile in range(tiles_here):
        hit = jnp.max(jnp.where(listed == first + tile, 1.0, 0.0), axis=1, keepdims=True)
        columns = slice(tile * TILE, (tile + 1) * TILE)
        out[:, columns] = jnp.where(hit > 0.0, scaled[:, columns], 0.0).astype(out.dtype)


def finish_kernel(layers, candidates, *refs):
    sets, out = refs[:-1], refs[-1]
    sets = [sets[start : start + layers] for start in range(0, len(sets), layers)]
    index, layer = lax.axis_index("blk"), lax.axis_index("layer")
    which = lax.bitwise_xor(index, layer) // 2
    for place, parts in enumerate(sets):

        @pl.when((which == place) | (len(sets) == 1))
        def _():
            total = parts[0][...].astype(jnp.float32)
            for part in parts[1:]:
                total = total + part[...].astype(jnp.float32)
            write_rows(total, layers, candidates[...], out)


def finish(sets, candidates, layers):
    parts = [part for one_set in sets for part in one_set]
    return pl.pallas_call(
        functools.partial(finish_kernel, layers),
        in_specs=in_vmem(1 + len(parts)),
        out_specs=in_vmem(1)[0],
        out_shape=jax.ShapeDtypeStruct(parts[0].shape, jnp.bfloat16),
        compiler_params=pltpu.CompilerParams(vmem_limit_bytes=VMEM),
        name="finish",
    )(candidates, *parts)


def permuted(value, target_of):
    count = lax.axis_size("blk")
    return lax.ppermute(value, "blk", [(source, target_of(source) % count) for source in range(count)])


def to_owners(parts, slots):
    layers, count = lax.axis_size("layer"), lax.axis_size("blk")
    out = [parts[0]]
    for shift in range(1, layers):
        pairs = [
            (((index ^ slot) - shift) % layers * count + index, (index ^ slot) * count + index)
            for index in range(count)
            for slot in slots
        ]
        out.append(lax.ppermute(parts[shift], ("layer", "blk"), pairs))
    return out


def on_line(own, store, candidates, layers):
    whole, halves = own[0], own[1:]
    half = halves[0].shape[1]
    far_low = permuted(halves[0], lambda source: source ^ 2)
    near = permuted(whole, lambda source: source ^ 1)
    far_high = permuted(halves[1], lambda source: source ^ 2)
    last_low = permuted(far_low, lambda source: source ^ 1)
    near, far_low = lax.optimization_barrier((near, far_low))
    early = score_pair([[whole], [near]], store, 0, None, layers)
    far_high, early = lax.optimization_barrier((far_high, early))
    last_high = permuted(far_high, lambda source: source ^ 1)
    early = to_owners(early, (0, 1))
    low_scores = score([[far_low], [last_low]], store, 0)
    late = to_owners(score_pair([[far_high], [last_high]], store, half, low_scores, layers), (2, 3))
    return finish([early, late], candidates, layers)


def on_ring(own, store, candidates, layers):
    count = lax.axis_size("blk")
    rows = own[0].shape[0]
    slots, moving = [score([[own[0]]], store, 0)], own[0]
    for _ in range(count - 1):
        moving = permuted(moving, lambda source: source + 1)
        slots.append(score([[moving]], store, 0))
    turns = lax.rem(lax.axis_index("blk") - jnp.arange(count) + count, count)
    total = jnp.stack(slots)[turns].reshape(layers, count * rows // layers, store.shape[1])
    parts = lax.all_to_all(total.astype(jnp.bfloat16), "layer", 0, 0)
    return finish([[parts[layer] for layer in range(layers)]], candidates, layers)


def per_device(queries, store, left_factor, right_factor, candidates):
    layers, count = lax.axis_size("layer"), lax.axis_size("blk")
    own = condition(queries, left_factor, right_factor)
    way = on_line if layers == 4 and count == 4 else on_ring
    return way(own, store, candidates, layers)


def solution(mesh):
    placed = (
        P("layer", ("parts", "blk"), None),
        P("layer", ("parts", "blk"), None),
        P("layer", None, None),
        P("layer", None, None),
        P(("parts", "layer"), None),
    )
    return jax.shard_map(
        per_device,
        mesh=mesh,
        in_specs=placed,
        out_specs=P(("parts", "layer"), "blk"),
        check_vma=False,
    )
```

time: 47.3 us -> 44.5 us (0.941)
  the two profiles are of different devices: /device:TPU:0 before, /device:TPU:20 now
where the time goes in v3:
time: 44.5 us; the launch traced here: 44.2 us
  starting transfers between devices  19.5 us (44%)
  waiting for transfers between devices  12.9 us (29%)
  Pallas kernels  11.6 us (26%)
    ppermute x6, starting transfers between devices, to_owners(): out.append(lax.ppermute(parts[shift], ('layer', 'blk'), pairs))  12.2 us
    pallas_call x3, Pallas kernels, call_score(): pl.pallas_call(kernel, in_specs=in_vmem(len(operands)) + [pl.BlockSpec(me...  8.5 us
    ppermute x5, waiting for transfers between devices, permuted(): lax.ppermute(value, 'blk', [(source, target_of(source) % count) for sourc...  8.18 us
    ppermute x5, starting transfers between devices, permuted(): lax.ppermute(value, 'blk', [(source, target_of(source) % count) for sourc...  7.27 us
    ppermute x6, waiting for transfers between devices, to_owners(): out.append(lax.ppermute(parts[shift], ('layer', 'blk'), pairs))  4.77 us
    pallas_call x1, Pallas kernels, condition(): pl.pallas_call(condition_kernel, in_specs=[pl.BlockSpec(memory_space=pltp...  2.32 us
  transfers between devices with their start and end apart: 11, of which 4 were waited for; matrix products, arithmetic and copies ran while one was open for 0% of the time, Pallas kernels for 19%

profile of v3, /device:TPU:20, one launch (start us, length us, event | category | flops | bytes accessed | tf_op | source)
XLA Modules:
  0.0 44.2 jit_solution(16707254743679123117)
XLA Ops:
  0.0 2.3 %condition.1 = (bf16[32,4096]{1,0:T(8,128)(2,1)S(1)}, bf16[32,2048]{1,0:T(8,128)(2,1)S(1)}, bf16[32,2048]{1,0:T(8,128)(2,1)S(1)}) custom-call(bf16[1,32,4096]{2,1,0:T(8,128)(2,1)} %queries_in.1, f32[1,64,64]{2,1,0:T(8,128)} %left_in.1, f32[1,64,64]{2,1,0:T(8,128)} %right_in.1), custom_call_target="tpu_custom_call" | custom-call | flops 536870912 | bytes 524288 | tf_op jit(solution)/shard_map/condition/pallas_call | solution.py:111
  2.3 1.6 %collective-permute-start.1 = (bf16[32,4096]{1,0:T(8,128)(2,1)S(1)}, bf16[32,4096]{1,0:T(8,128)(2,1)S(1)}, u32[]{:S(2)}, u32[]{:S(2)}) collective-permute-start(bf16[32,4096]{1,0:T(8,128)(2,1)S(1)} %get-tuple-element.24.refs_0_), channel_id=1, source_target_pairs={{0,1},{1,0},{2,3},{3,2},{4,5},{5,4},{6,7},{7,6},{8,9},{9,8},{10,11... | collective-permute-start | bytes 786440 | tf_op jit(solution)/shard_map/ppermute | solution.py:284
  4.0 0.3 collective-permute-start.2
  4.3 2.6 %collective-permute-start = (bf16[32,2048]{1,0:T(8,128)(2,1)S(1)}, bf16[32,2048]{1,0:T(8,128)(2,1)S(1)}, u32[]{:S(2)}, u32[]{:S(2)}) collective-permute-start(bf16[32,2048]{1,0:T(8,128)(2,1)S(1)} %get-tuple-element.23), channel_id=1, source_target_pairs={{0,2},{1,3},{2,0},{3,1},{4,6},{5,7},{6,4},{7,5},{8,10},{9,11},{10,... | collective-permute-start | bytes 393224 | tf_op jit(solution)/shard_map/ppermute | solution.py:284
  6.9 7.5 %collective-permute-done.2.refs_0_ = bf16[32,2048]{1,0:T(8,128)(2,1)S(1)} collective-permute-done((bf16[32,2048]{1,0:T(8,128)(2,1)S(1)}, bf16[32,2048]{1,0:T(8,128)(2,1)S(1)}, u32[]{:S(2)}, u32[]{:S(2)}) %collective-permute-start.2) | collective-permute-done | bytes 131104 | tf_op jit(solution)/shard_map/ppermute | solution.py:284
  14.4 0.0 collective-permute-start.7
  14.4 0.7 %collective-permute-done.1.refs_1_ = bf16[32,4096]{1,0:T(8,128)(2,1)S(1)} collective-permute-done((bf16[32,4096]{1,0:T(8,128)(2,1)S(1)}, bf16[32,4096]{1,0:T(8,128)(2,1)S(1)}, u32[]{:S(2)}, u32[]{:S(2)}) %collective-permute-start.1) | collective-permute-done | bytes 262176 | tf_op jit(solution)/shard_map/ppermute | solution.py:284
  15.1 4.6 %score_pair.2 = (f32[32,1024]{1,0:T(8,128)S(1)}, bf16[32,1024]{1,0:T(8,128)(2,1)S(1)}, bf16[32,1024]{1,0:T(8,128)(2,1)S(1)}, bf16[32,1024]{1,0:T(8,128)(2,1)S(1)}) custom-call(bf16[32,4096]{1,0:T(8,128)(2,1)S(1)} %get-tuple-element.24.refs_0_, bf16[32,4096]{1,0:T(8,128)(2,1)S(1)} %collective-permute-done.1.refs_1_, bf16[1,1024,4096]{2,1,0:T(8,128)(2,1)} %refs_2_.5), custom_call_target="tpu_custom_call" | custom-call | flops 536870912 | bytes 8388608 | tf_op jit(solution)/shard_map/score_pair/pallas_call | solution.py:166
  19.7 0.0 collective-permute-done.refs_0_
  19.7 0.0 copy-start.1
  19.7 2.7 %collective-permute-start.6 = (bf16[32,2048]{1,0:T(8,128)(2,1)S(1)}, bf16[32,2048]{1,0:T(8,128)(2,1)S(1)}, u32[]{:S(2)}, u32[]{:S(2)}) collective-permute-start(bf16[32,2048]{1,0:T(8,128)(2,1)S(1)} %collective-permute-done.refs_0_), channel_id=1, source_target_pairs={{0,1},{1,0},{2,3},{3,2},{4,5},{5,4},{6,7},{7,6},{8,9},{9,8},{10,11... | collective-permute-start | bytes 393224 | tf_op jit(solution)/shard_map/ppermute | solution.py:284
  22.4 0.7 %collective-permute-start.3 = (bf16[32,1024]{1,0:T(8,128)(2,1)S(1)}, bf16[32,1024]{1,0:T(8,128)(2,1)S(1)}, u32[]{:S(2)}, u32[]{:S(2)}) collective-permute-start(bf16[32,1024]{1,0:T(8,128)(2,1)S(1)} %get-tuple-element.32), channel_id=1, source_target_pairs={{12,0},{0,4},{1,5},{13,1},{6,10},{10,14},{11,15},{7,11},{28,16},{1... | collective-permute-start | bytes 196616 | tf_op jit(solution)/shard_map/ppermute | solution.py:296
  23.1 4.7 %collective-permute-start.4 = (bf16[32,1024]{1,0:T(8,128)(2,1)S(1)}, bf16[32,1024]{1,0:T(8,128)(2,1)S(1)}, u32[]{:S(2)}, u32[]{:S(2)}) collective-permute-start(bf16[32,1024]{1,0:T(8,128)(2,1)S(1)} %get-tuple-element.33), channel_id=1, source_target_pairs={{8,0},{12,4},{13,5},{9,1},{2,10},{6,14},{7,15},{3,11},{24,16},{28,... | collective-permute-start | bytes 196616 | tf_op jit(solution)/shard_map/ppermute | solution.py:296
  27.8 1.3 %collective-permute-start.5 = (bf16[32,1024]{1,0:T(8,128)(2,1)S(1)}, bf16[32,1024]{1,0:T(8,128)(2,1)S(1)}, u32[]{:S(2)}, u32[]{:S(2)}) collective-permute-start(bf16[32,1024]{1,0:T(8,128)(2,1)S(1)} %get-tuple-element.34), channel_id=1, source_target_pairs={{4,0},{8,4},{9,5},{5,1},{14,10},{2,14},{3,15},{15,11},{20,16},{24,... | collective-permute-start | bytes 196616 | tf_op jit(solution)/shard_map/ppermute | solution.py:296
  29.1 0.0 collective-permute-done.7.refs_1_
  29.1 1.9 %score.1.refs_3_ = f32[64,1024]{1,0:T(8,128)S(1)} custom-call(bf16[32,2048]{1,0:T(8,128)(2,1)S(1)} %collective-permute-done.2.refs_0_, bf16[32,2048]{1,0:T(8,128)(2,1)S(1)} %collective-permute-done.7.refs_1_, bf16[1,1024,4096]{2,1,0:T(8,128)(2,1)S(1)} %copy-done), custom_call_target="tpu_custom_call" | custom-call | flops 268435456 | bytes 4194304 | tf_op jit(solution)/shard_map/score/pallas_call | solution.py:166
  31.0 1.9 %score_pair.3 = (f32[32,1024]{1,0:T(8,128)S(1)}, bf16[32,1024]{1,0:T(8,128)(2,1)S(1)}, bf16[32,1024]{1,0:T(8,128)(2,1)S(1)}, bf16[32,1024]{1,0:T(8,128)(2,1)S(1)}) custom-call(bf16[32,2048]{1,0:T(8,128)(2,1)S(1)} %collective-permute-done.refs_0_, bf16[32,2048]{1,0:T(8,128)(2,1)S(1)} %collective-permute-done.6.refs_1_, bf16[1,1024,4096]{2,1,0:T(8,128)(2,1)S(1)} %copy-done, ...), custom_call_target="tpu_custom_call" | custom-call | flops 268435456 | bytes 4194304 | tf_op jit(solution)/shard_map/score_pair/pallas_call | solution.py:166
  33.0 1.3 %collective-permute-start.10 = (bf16[32,1024]{1,0:T(8,128)(2,1)S(1)}, bf16[32,1024]{1,0:T(8,128)(2,1)S(1)}, u32[]{:S(2)}, u32[]{:S(2)}) collective-permute-start(bf16[32,1024]{1,0:T(8,128)(2,1)S(1)} %get-tuple-element.40), channel_id=1, source_target_pairs={{12,8},{0,12},{1,13},{13,9},{6,2},{10,6},{11,7},{7,3},{28,24},{16,... | collective-permute-start | bytes 196616 | tf_op jit(solution)/shard_map/ppermute | solution.py:296
  34.3 3.0 %collective-permute-start.8 = (bf16[32,1024]{1,0:T(8,128)(2,1)S(1)}, bf16[32,1024]{1,0:T(8,128)(2,1)S(1)}, u32[]{:S(2)}, u32[]{:S(2)}) collective-permute-start(bf16[32,1024]{1,0:T(8,128)(2,1)S(1)} %get-tuple-element.38), channel_id=1, source_target_pairs={{4,8},{8,12},{9,13},{5,9},{14,2},{2,6},{3,7},{15,3},{20,24},{24,28... | collective-permute-start | bytes 196616 | tf_op jit(solution)/shard_map/ppermute | solution.py:296
  37.3 1.3 %collective-permute-start.9 = (bf16[32,1024]{1,0:T(8,128)(2,1)S(1)}, bf16[32,1024]{1,0:T(8,128)(2,1)S(1)}, u32[]{:S(2)}, u32[]{:S(2)}) collective-permute-start(bf16[32,1024]{1,0:T(8,128)(2,1)S(1)} %get-tuple-element.39), channel_id=1, source_target_pairs={{0,8},{4,12},{5,13},{1,9},{10,2},{14,6},{15,7},{11,3},{16,24},{20,... | collective-permute-start | bytes 196616 | tf_op jit(solution)/shard_map/ppermute | solution.py:296
  38.6 0.1 copy.6.candidates
  38.7 1.1 %collective-permute-done.8.refs_5_ = bf16[32,1024]{1,0:T(8,128)(2,1)S(1)} collective-permute-done((bf16[32,1024]{1,0:T(8,128)(2,1)S(1)}, bf16[32,1024]{1,0:T(8,128)(2,1)S(1)}, u32[]{:S(2)}, u32[]{:S(2)}) %collective-permute-start.8) | collective-permute-done | bytes 65568 | tf_op jit(solution)/shard_map/ppermute | solution.py:296
  39.8 3.6 %collective-permute-done.9.refs_6_ = bf16[32,1024]{1,0:T(8,128)(2,1)S(1)} collective-permute-done((bf16[32,1024]{1,0:T(8,128)(2,1)S(1)}, bf16[32,1024]{1,0:T(8,128)(2,1)S(1)}, u32[]{:S(2)}, u32[]{:S(2)}) %collective-permute-start.9) | collective-permute-done | bytes 65568 | tf_op jit(solution)/shard_map/ppermute | solution.py:296
  43.5 0.7 %finish.1 = bf16[32,1024]{1,0:T(8,128)(2,1)} custom-call(s32[32,16]{1,0:T(8,128)S(1)} %copy.6.candidates, f32[32,1024]{1,0:T(8,128)S(1)} %get-tuple-element.31.refs_0_, bf16[32,1024]{1,0:T(8,128)(2,1)S(1)} %collective-permute-done.3.refs_1_, bf16[32,1024]{1,0:T(8,128)(2,1)S(1)} %collective-permute-done.4.refs_2_, ...), custom_call_target="tpu_custom_call" | custom-call | tf_op jit(solution)/shard_map/finish/pallas_call | solution.py:272
  (8 shorter events, 0.0 us)
Async XLA Ops:
  0.0 29.1 %copy-start = (bf16[1,1024,4096]{2,1,0:T(8,128)(2,1)S(1)}, bf16[1,1024,4096]{2,1,0:T(8,128)(2,1)}, u32[]{:S(2)}) copy-start(bf16[1,1024,4096]{2,1,0:T(8,128)(2,1)} %refs_2_.5) | copy-start | bytes 25165828
  2.3 12.7 %collective-permute-start.1 = (bf16[32,4096]{1,0:T(8,128)(2,1)S(1)}, bf16[32,4096]{1,0:T(8,128)(2,1)S(1)}, u32[]{:S(2)}, u32[]{:S(2)}) collective-permute-start(bf16[32,4096]{1,0:T(8,128)(2,1)S(1)} %get-tuple-element.24.refs_0_), channel_id=1, source_target_pairs={{0,1},{1,0},{2,3},{3,2},{4,5},{5,4},{6,7},{7,6},{8,9},{9,8},{10,11... | collective-permute-start | bytes 786440 | tf_op jit(solution)/shard_map/ppermute | solution.py:284
  4.0 10.4 %collective-permute-start.2 = (bf16[32,2048]{1,0:T(8,128)(2,1)S(1)}, bf16[32,2048]{1,0:T(8,128)(2,1)S(1)}, u32[]{:S(2)}, u32[]{:S(2)}) collective-permute-start(bf16[32,2048]{1,0:T(8,128)(2,1)S(1)} %get-tuple-element.25), channel_id=1, source_target_pairs={{0,2},{1,3},{2,0},{3,1},{4,6},{5,7},{6,4},{7,5},{8,10},{9,11},{10,... | collective-permute-start | bytes 393224 | tf_op jit(solution)/shard_map/ppermute | solution.py:284
  4.3 15.4 %collective-permute-start = (bf16[32,2048]{1,0:T(8,128)(2,1)S(1)}, bf16[32,2048]{1,0:T(8,128)(2,1)S(1)}, u32[]{:S(2)}, u32[]{:S(2)}) collective-permute-start(bf16[32,2048]{1,0:T(8,128)(2,1)S(1)} %get-tuple-element.23), channel_id=1, source_target_pairs={{0,2},{1,3},{2,0},{3,1},{4,6},{5,7},{6,4},{7,5},{8,10},{9,11},{10,... | collective-permute-start | bytes 393224 | tf_op jit(solution)/shard_map/ppermute | solution.py:284
  14.4 14.7 %collective-permute-start.7 = (bf16[32,2048]{1,0:T(8,128)(2,1)S(1)}, bf16[32,2048]{1,0:T(8,128)(2,1)S(1)}, u32[]{:S(2)}, u32[]{:S(2)}) collective-permute-start(bf16[32,2048]{1,0:T(8,128)(2,1)S(1)} %collective-permute-done.2.refs_0_), channel_id=1, source_target_pairs={{0,1},{1,0},{2,3},{3,2},{4,5},{5,4},{6,7},{7,6},{8,9},{9,8},{10,11... | collective-permute-start | bytes 393224 | tf_op jit(solution)/shard_map/ppermute | solution.py:284
  19.7 18.9 %copy-start.1 = (s32[32,16]{0,1:T(8,128)S(1)}, s32[32,16]{0,1:T(8,128)}, u32[]{:S(2)}) copy-start(s32[32,16]{0,1:T(8,128)} %param.9) | copy-start | bytes 6148
  19.7 11.2 %collective-permute-start.6 = (bf16[32,2048]{1,0:T(8,128)(2,1)S(1)}, bf16[32,2048]{1,0:T(8,128)(2,1)S(1)}, u32[]{:S(2)}, u32[]{:S(2)}) collective-permute-start(bf16[32,2048]{1,0:T(8,128)(2,1)S(1)} %collective-permute-done.refs_0_), channel_id=1, source_target_pairs={{0,1},{1,0},{2,3},{3,2},{4,5},{5,4},{6,7},{7,6},{8,9},{9,8},{10,11... | collective-permute-start | bytes 393224 | tf_op jit(solution)/shard_map/ppermute | solution.py:284
  22.4 14.9 %collective-permute-start.3 = (bf16[32,1024]{1,0:T(8,128)(2,1)S(1)}, bf16[32,1024]{1,0:T(8,128)(2,1)S(1)}, u32[]{:S(2)}, u32[]{:S(2)}) collective-permute-start(bf16[32,1024]{1,0:T(8,128)(2,1)S(1)} %get-tuple-element.32), channel_id=1, source_target_pairs={{12,0},{0,4},{1,5},{13,1},{6,10},{10,14},{11,15},{7,11},{28,16},{1... | collective-permute-start | bytes 196616 | tf_op jit(solution)/shard_map/ppermute | solution.py:296
  23.1 15.6 %collective-permute-start.4 = (bf16[32,1024]{1,0:T(8,128)(2,1)S(1)}, bf16[32,1024]{1,0:T(8,128)(2,1)S(1)}, u32[]{:S(2)}, u32[]{:S(2)}) collective-permute-start(bf16[32,1024]{1,0:T(8,128)(2,1)S(1)} %get-tuple-element.33), channel_id=1, source_target_pairs={{8,0},{12,4},{13,5},{9,1},{2,10},{6,14},{7,15},{3,11},{24,16},{28,... | collective-permute-start | bytes 196616 | tf_op jit(solution)/shard_map/ppermute | solution.py:296
  27.8 10.9 %collective-permute-start.5 = (bf16[32,1024]{1,0:T(8,128)(2,1)S(1)}, bf16[32,1024]{1,0:T(8,128)(2,1)S(1)}, u32[]{:S(2)}, u32[]{:S(2)}) collective-permute-start(bf16[32,1024]{1,0:T(8,128)(2,1)S(1)} %get-tuple-element.34), channel_id=1, source_target_pairs={{4,0},{8,4},{9,5},{5,1},{14,10},{2,14},{3,15},{15,11},{20,16},{24,... | collective-permute-start | bytes 196616 | tf_op jit(solution)/shard_map/ppermute | solution.py:296
  33.0 5.7 %collective-permute-start.10 = (bf16[32,1024]{1,0:T(8,128)(2,1)S(1)}, bf16[32,1024]{1,0:T(8,128)(2,1)S(1)}, u32[]{:S(2)}, u32[]{:S(2)}) collective-permute-start(bf16[32,1024]{1,0:T(8,128)(2,1)S(1)} %get-tuple-element.40), channel_id=1, source_target_pairs={{12,8},{0,12},{1,13},{13,9},{6,2},{10,6},{11,7},{7,3},{28,24},{16,... | collective-permute-start | bytes 196616 | tf_op jit(solution)/shard_map/ppermute | solution.py:296
  34.3 5.6 %collective-permute-start.8 = (bf16[32,1024]{1,0:T(8,128)(2,1)S(1)}, bf16[32,1024]{1,0:T(8,128)(2,1)S(1)}, u32[]{:S(2)}, u32[]{:S(2)}) collective-permute-start(bf16[32,1024]{1,0:T(8,128)(2,1)S(1)} %get-tuple-element.38), channel_id=1, source_target_pairs={{4,8},{8,12},{9,13},{5,9},{14,2},{2,6},{3,7},{15,3},{20,24},{24,28... | collective-permute-start | bytes 196616 | tf_op jit(solution)/shard_map/ppermute | solution.py:296
  37.3 6.2 %collective-permute-start.9 = (bf16[32,1024]{1,0:T(8,128)(2,1)S(1)}, bf16[32,1024]{1,0:T(8,128)(2,1)S(1)}, u32[]{:S(2)}, u32[]{:S(2)}) collective-permute-start(bf16[32,1024]{1,0:T(8,128)(2,1)S(1)} %get-tuple-element.39), channel_id=1, source_target_pairs={{0,8},{4,12},{5,13},{1,9},{10,2},{14,6},{15,7},{11,3},{16,24},{20,... | collective-permute-start | bytes 196616 | tf_op jit(solution)/shard_map/ppermute | solution.py:296

commit v4 on v3

v4 whole, which is shorter than its diff:
```python
import functools

import jax
import jax.numpy as jnp
from jax import lax
from jax.experimental import pallas as pl
from jax.experimental.pallas import tpu as pltpu
from jax.sharding import PartitionSpec as P

TILE = 128
GROUP = 32
LANES = 128
ROWS = 8
VMEM = 24 * 1024 * 1024


def two_parts(value):
    high = value.astype(jnp.bfloat16)
    low = (value - high.astype(jnp.float32)).astype(jnp.bfloat16)
    return high, low


def iota(shape, axis):
    return lax.broadcasted_iota(jnp.int32, shape, axis)


def dot(left, right):
    return jnp.dot(left, right, preferred_element_type=jnp.float32)


def ones_where(condition):
    return jnp.where(condition, 1.0, 0.0).astype(jnp.bfloat16)


def spread_left(left_factor):
    side = left_factor.shape[0]
    wide = ones_where(iota((side, side * ROWS), 1) // ROWS == iota((side, side * ROWS), 0))
    columns = dot(jnp.concatenate(two_parts(left_factor), axis=0), wide).reshape(2, side, 1, side * ROWS)
    same = iota((1, ROWS, side * ROWS), 1) == iota((1, ROWS, side * ROWS), 2) % ROWS
    parts = [jnp.where(same, columns[part], 0.0).reshape(side * ROWS, side * ROWS) for part in range(2)]
    return jnp.concatenate([part.astype(jnp.bfloat16) for part in parts], axis=1)


def spread_right(right_factor):
    side = right_factor.shape[0]
    wide = ones_where(iota((side, 4 * side), 1) % side == iota((side, 4 * side), 0))
    same = iota((4 * side, 4 * side), 0) // side == iota((4 * side, 4 * side), 1) // side
    high, low = [
        jnp.where(same, jnp.concatenate([dot(part, wide)] * 4, axis=0), 0.0).astype(jnp.bfloat16)
        for part in two_parts(right_factor)
    ]
    return jnp.concatenate([high, low, high], axis=0)


def condition_kernel(queries_in, left_in, right_in, low, high, queries, left_factor, right_factor, arrived):
    halves = (low, high)
    copies = [
        pltpu.make_async_copy(source.at[0], target, arrived.at[place])
        for place, (source, target) in enumerate(
            [(left_in, left_factor), (right_in, right_factor), (queries_in, queries)]
        )
    ]
    for copy in copies:
        copy.start()
    side = left_factor.shape[0]
    pairs = side // 2
    copies[0].wait()
    copies[1].wait()
    left = spread_left(left_factor[...])
    right = spread_right(right_factor[...])
    low_half = iota((1, 1, LANES), 2) < side
    per_half = pairs // len(halves)
    copies[2].wait()
    for block in range(queries.shape[0] // GROUP):
        rows = pl.ds(block * GROUP, GROUP)
        straight = jnp.stack(
            [queries[rows, pl.ds(pair * LANES, LANES)].astype(jnp.float32) for pair in range(pairs)]
        )
        swapped = pltpu.roll(straight, side, 2).reshape(pairs, GROUP // ROWS, ROWS, LANES)
        straight = straight.reshape(pairs, GROUP // ROWS, ROWS, LANES)
        columns = []
        for group in (0, 2):
            even = jnp.where(low_half, straight[:, group], swapped[:, group + 1])
            odd = jnp.where(low_half, swapped[:, group], straight[:, group + 1])
            columns.append(jnp.stack([even, odd], axis=1).reshape(side * ROWS, LANES))
        grid = jnp.concatenate(columns, axis=1).astype(jnp.bfloat16)
        halfway = dot(left, jnp.concatenate([grid, grid], axis=0))
        high, low = two_parts(halfway)
        result = dot(jnp.concatenate([high, high, low], axis=1), right)
        result = result.reshape(pairs, 2, ROWS, 2 * LANES)
        groups = []
        for half in range(2):
            even = result[:, 0, :, half * LANES : (half + 1) * LANES]
            odd = result[:, 1, :, half * LANES : (half + 1) * LANES]
            groups.append(jnp.where(low_half, even, pltpu.roll(odd, side, 2)))
            groups.append(jnp.where(low_half, pltpu.roll(even, side, 2), odd))
        done = jnp.concatenate(groups, axis=1).astype(jnp.bfloat16)
        for pair in range(pairs):
            halves[pair // per_half][rows, pl.ds(pair % per_half * LANES, LANES)] = done[pair]


def in_vmem(count):
    return [pl.BlockSpec(memory_space=pltpu.VMEM)] * count


def condition(queries, left_factor, right_factor):
    unused, block_rows, entries = queries.shape
    side = left_factor.shape[1]
    return pl.pallas_call(
        condition_kernel,
        in_specs=[pl.BlockSpec(memory_space=pltpu.HBM)] * 3,
        out_specs=in_vmem(2),
        out_shape=[jax.ShapeDtypeStruct((block_rows, entries // 2), jnp.bfloat16)] * 2,
        scratch_shapes=[
            pltpu.VMEM((block_rows, entries), jnp.bfloat16),
            pltpu.VMEM((side, side), jnp.float32),
            pltpu.VMEM((side, side), jnp.float32),
            pltpu.SemaphoreType.DMA((3,)),
        ],
        compiler_params=pltpu.CompilerParams(vmem_limit_bytes=VMEM),
        cost_estimate=pl.CostEstimate(
            flops=block_rows * entries * 4096, bytes_accessed=queries.size * 4, transcendentals=0
        ),
        name="condition",
    )(*[pltpu.with_memory_space_constraint(value, pltpu.HBM) for value in (queries, left_factor, right_factor)])


STEP = 256


def score_block(queries, store, first, write, arrived=None):
    turned = queries.T
    width = queries.shape[1]

    def one(step, carry):
        place = pl.ds(pl.multiple_of(step * STEP, STEP), STEP)
        if arrived is not None:
            arrived(step)
        value = dot(store[0, place, pl.ds(first, width)], turned)
        write(place, value.T)
        return carry

    lax.fori_loop(0, store.shape[1] // STEP, one, 0)


def own_kernel(queries, far_store, out, store, semaphores):
    def copy_of(step):
        place = pl.ds(pl.multiple_of(step * STEP, STEP), STEP)
        return pltpu.make_async_copy(far_store.at[0, place], store.at[0, place], semaphores.at[step])

    for step in range(store.shape[1] // STEP):
        copy_of(step).start()

    def write(place, value):
        out[:, place] = value

    score_block(queries[...], store, 0, write, lambda step: copy_of(step).wait())


def score_cost(count, width, examples):
    return pl.CostEstimate(
        flops=2 * count * width * examples, bytes_accessed=examples * width * 2, transcendentals=0
    )


def score_own(queries, store):
    rows, entries = queries.shape
    examples = store.shape[1]
    return pl.pallas_call(
        own_kernel,
        in_specs=in_vmem(1) + [pl.BlockSpec(memory_space=pltpu.HBM)],
        out_specs=in_vmem(1)[0],
        out_shape=jax.ShapeDtypeStruct((rows, examples), jnp.float32),
        scratch_shapes=[pltpu.VMEM(store.shape, store.dtype), pltpu.SemaphoreType.DMA((examples // STEP,))],
        compiler_params=pltpu.CompilerParams(vmem_limit_bytes=VMEM),
        cost_estimate=score_cost(rows, entries, examples),
        name="score_own",
    )(queries, pltpu.with_memory_space_constraint(store, pltpu.HBM))


def three_blocks(near, far, last, first):
    return jnp.concatenate([near[:, pl.ds(first, far.shape[1])], far[...], last[...]], axis=0)


def low_kernel(near, far, last, store, out):
    def write(place, value):
        out[:, place] = value

    score_block(three_blocks(near, far, last, 0), store, 0, write)


def score_low(near, far, last, store):
    rows, width = far.shape
    examples = store.shape[1]
    return pl.pallas_call(
        low_kernel,
        in_specs=in_vmem(4),
        out_specs=in_vmem(1)[0],
        out_shape=jax.ShapeDtypeStruct((3 * rows, examples), jnp.float32),
        compiler_params=pltpu.CompilerParams(vmem_limit_bytes=VMEM),
        cost_estimate=score_cost(3 * rows, width, examples),
        name="score_low",
    )(near, far, last, store)


def high_kernel(first, near, far, last, store, own, low, *refs):
    outs, total = refs[:-1], refs[-1]
    rows = own.shape[0]
    total[pl.ds(0, rows), :] = own[...]

    def write(place, value):
        total[pl.ds(rows, 3 * rows), place] = value + low[:, place]

    score_block(three_blocks(near, far, last, first), store, first, write)
    home = lax.bitwise_xor(lax.axis_index("blk"), lax.axis_index("layer"))
    for mask, out in enumerate(outs):
        slot = lax.bitwise_xor(home, mask)
        out[...] = total[pl.ds(pl.multiple_of(slot * rows, rows), rows), :].astype(out.dtype)


def score_high(near, far, last, store, own, low):
    rows, width = far.shape
    examples = store.shape[1]
    return pl.pallas_call(
        functools.partial(high_kernel, near.shape[1] - width),
        in_specs=in_vmem(6),
        out_specs=in_vmem(4),
        out_shape=[
            jax.ShapeDtypeStruct((rows, examples), jnp.bfloat16 if mask else jnp.float32) for mask in range(4)
        ],
        scratch_shapes=[pltpu.VMEM((4 * rows, examples), jnp.float32)],
        compiler_params=pltpu.CompilerParams(vmem_limit_bytes=VMEM),
        cost_estimate=score_cost(3 * rows, width, examples),
        name="score_high",
    )(near, far, last, store, own, low)


def write_rows(total, layers, listed, out):
    scaled = total / jnp.sqrt(jnp.float32(layers))
    tiles_here = out.shape[1] // TILE
    first = lax.axis_index("blk") * tiles_here
    for tile in range(tiles_here):
        hit = jnp.max(jnp.where(listed == first + tile, 1.0, 0.0), axis=1, keepdims=True)
        columns = slice(tile * TILE, (tile + 1) * TILE)
        out[:, columns] = jnp.where(hit > 0.0, scaled[:, columns], 0.0).astype(out.dtype)


def finish_kernel(layers, candidates, *refs):
    parts, out = refs[:-1], refs[-1]
    total = parts[0][...].astype(jnp.float32)
    for part in parts[1:]:
        total = total + part[...].astype(jnp.float32)
    write_rows(total, layers, candidates[...], out)


def finish(parts, candidates, layers):
    return pl.pallas_call(
        functools.partial(finish_kernel, layers),
        in_specs=in_vmem(1 + len(parts)),
        out_specs=in_vmem(1)[0],
        out_shape=jax.ShapeDtypeStruct(parts[0].shape, jnp.bfloat16),
        compiler_params=pltpu.CompilerParams(vmem_limit_bytes=VMEM),
        name="finish",
    )(candidates, *parts)


def permuted(value, axis, target_of):
    count = lax.axis_size(axis)
    return lax.ppermute(value, axis, [(source, target_of(source) % count) for source in range(count)])


def swapped(value, axis, mask):
    return permuted(value, axis, lambda source: source ^ mask)


def on_line(own, store, candidates, layers):
    far = [swapped(half, "blk", 2) for half in own]
    whole = jnp.concatenate(own, axis=1)
    near = swapped(whole, "blk", 1)
    own_scores = score_own(whole, store)
    far[0], own_scores = lax.optimization_barrier((far[0], own_scores))
    last = [swapped(half, "blk", 1) for half in far]
    low_scores = score_low(near, far[0], last[0], store)
    parts = score_high(near, far[1], last[1], store, own_scores, low_scores)
    received = {mask: swapped(parts[mask], "layer", mask) for mask in (3, 2, 1)}
    return finish([parts[0]] + [received[mask] for mask in (1, 2, 3)], candidates, layers)


def on_ring(own, store, candidates, layers):
    count = lax.axis_size("blk")
    moving = jnp.concatenate(own, axis=1)
    rows = moving.shape[0]
    slots = [score_own(moving, store)]
    for _ in range(count - 1):
        moving = permuted(moving, "blk", lambda source: source + 1)
        slots.append(score_own(moving, store))
    turns = lax.rem(lax.axis_index("blk") - jnp.arange(count) + count, count)
    total = jnp.stack(slots)[turns].reshape(layers, count * rows // layers, store.shape[1])
    parts = lax.all_to_all(total.astype(jnp.bfloat16), "layer", 0, 0)
    return finish([parts[layer] for layer in range(layers)], candidates, layers)


def per_device(queries, store, left_factor, right_factor, candidates):
    layers, count = lax.axis_size("layer"), lax.axis_size("blk")
    own = condition(queries, left_factor, right_factor)
    way = on_line if layers == 4 and count == 4 else on_ring
    return way(own, store, candidates, layers)


def solution(mesh):
    placed = (
        P("layer", ("parts", "blk"), None),
        P("layer", ("parts", "blk"), None),
        P("layer", None, None),
        P("layer", None, None),
        P(("parts", "layer"), None),
    )
    return jax.shard_map(
        per_device,
        mesh=mesh,
        in_specs=placed,
        out_specs=P(("parts", "layer"), "blk"),
        check_vma=False,
    )
```

time: 44.5 us -> 33.6 us (0.76)
  the two profiles are of different devices: /device:TPU:20 before, /device:TPU:0 now
where the time goes in v4:
time: 33.6 us; the launch traced here: 33.5 us
  Pallas kernels  11.6 us (35%)
  waiting for transfers between devices  11.3 us (34%)
  starting transfers between devices  10.4 us (31%)
    ppermute x8, waiting for transfers between devices, permuted(): lax.ppermute(value, axis, [(source, target_of(source) % count) for source...  11.3 us
    ppermute x8, starting transfers between devices, permuted(): lax.ppermute(value, axis, [(source, target_of(source) % count) for source...  10.4 us
    pallas_call x1, Pallas kernels, score_own(): pl.pallas_call(own_kernel, in_specs=in_vmem(1) + [pl.BlockSpec(memory_spa...  4.53 us
    pallas_call x1, Pallas kernels, condition(): pl.pallas_call(condition_kernel, in_specs=[pl.BlockSpec(memory_space=pltp...  2.32 us
    pallas_call x1, Pallas kernels, score_high(): pl.pallas_call(functools.partial(high_kernel, near.shape[1] - width), in_...  2.02 us
    pallas_call x1, Pallas kernels, score_low(): pl.pallas_call(low_kernel, in_specs=in_vmem(4), out_specs=in_vmem(1)[0],...  1.97 us
    pallas_call x1, Pallas kernels, finish(): pl.pallas_call(functools.partial(finish_kernel, layers), in_specs=in_vmem...  0.74 us
  transfers between devices with their start and end apart: 8, of which 5 were waited for; matrix products, arithmetic and copies ran while one was open for 0% of the time, Pallas kernels for 19%

profile of v4, /device:TPU:0, one launch (start us, length us, event | category | flops | bytes accessed | tf_op | source)
XLA Modules:
  0.0 33.5 jit_solution(11356284215493086307)
XLA Ops:
  0.0 2.3 %condition.1 = (bf16[32,2048]{1,0:T(8,128)(2,1)S(1)}, bf16[32,2048]{1,0:T(8,128)(2,1)S(1)}) custom-call(bf16[1,32,4096]{2,1,0:T(8,128)(2,1)} %queries_in.1, f32[1,64,64]{2,1,0:T(8,128)} %left_in.1, f32[1,64,64]{2,1,0:T(8,128)} %right_in.1), custom_call_target="tpu_custom_call" | custom-call | flops 536870912 | bytes 524288 | tf_op jit(solution)/shard_map/condition/pallas_call | solution.py:109
  2.3 4.1 %collective-permute-start.3 = (bf16[32,2048]{1,0:T(8,128)(2,1)S(1)}, bf16[32,2048]{1,0:T(8,128)(2,1)S(1)}, u32[]{:S(2)}, u32[]{:S(2)}) collective-permute-start(bf16[32,2048]{1,0:T(8,128)(2,1)S(1)} %get-tuple-element.13), channel_id=1, source_target_pairs={{0,2},{1,3},{2,0},{3,1},{4,6},{5,7},{6,4},{7,5},{8,10},{9,11},{10,... | collective-permute-start | bytes 393224 | tf_op jit(solution)/shard_map/ppermute | solution.py:269
  6.5 1.6 %collective-permute-start = (bf16[32,4096]{1,0:T(8,128)(2,1)S(1)}, bf16[32,4096]{1,0:T(8,128)(2,1)S(1)}, u32[]{:S(2)}, u32[]{:S(2)}) collective-permute-start(bf16[32,4096]{1,0:T(8,128)(2,1)S(1)} %constant_dynamic-update-slice_fusion.queries), channel_id=1, source_target_pairs={{0,1},{1,0},{2,3},{3,2},{4,5},{5,4},{6,7},{7,6},{8,9},{9,8},{10,11... | collective-permute-start | bytes 786440 | tf_op jit(solution)/shard_map/ppermute | solution.py:269
  8.1 0.3 %collective-permute-start.1 = (bf16[32,2048]{1,0:T(8,128)(2,1)S(1)}, bf16[32,2048]{1,0:T(8,128)(2,1)S(1)}, u32[]{:S(2)}, u32[]{:S(2)}) collective-permute-start(bf16[32,2048]{1,0:T(8,128)(2,1)S(1)} %get-tuple-element.14), channel_id=1, source_target_pairs={{0,2},{1,3},{2,0},{3,1},{4,6},{5,7},{6,4},{7,5},{8,10},{9,11},{10,... | collective-permute-start | bytes 393224 | tf_op jit(solution)/shard_map/ppermute | solution.py:269
  8.4 4.5 %score_own.1.own = f32[32,1024]{1,0:T(8,128)S(1)} custom-call(bf16[32,4096]{1,0:T(8,128)(2,1)S(1)} %constant_dynamic-update-slice_fusion.queries, bf16[1,1024,4096]{2,1,0:T(8,128)(2,1)} %store.3), custom_call_target="tpu_custom_call" | custom-call | flops 268435456 | bytes 8388608 | tf_op jit(solution)/shard_map/score_own/pallas_call | solution.py:169
  13.0 0.0 copy-start.1
  13.0 0.7 %collective-permute-done.3.far = bf16[32,2048]{1,0:T(8,128)(2,1)S(1)} collective-permute-done((bf16[32,2048]{1,0:T(8,128)(2,1)S(1)}, bf16[32,2048]{1,0:T(8,128)(2,1)S(1)}, u32[]{:S(2)}, u32[]{:S(2)}) %collective-permute-start.3) | collective-permute-done | bytes 131104 | tf_op jit(solution)/shard_map/ppermute | solution.py:269
  13.7 0.0 collective-permute-start.4
  13.7 5.1 %collective-permute-done.1.far = bf16[32,2048]{1,0:T(8,128)(2,1)S(1)} collective-permute-done((bf16[32,2048]{1,0:T(8,128)(2,1)S(1)}, bf16[32,2048]{1,0:T(8,128)(2,1)S(1)}, u32[]{:S(2)}, u32[]{:S(2)}) %collective-permute-start.1) | collective-permute-done | bytes 131104 | tf_op jit(solution)/shard_map/ppermute | solution.py:269
  18.8 2.4 %collective-permute-start.2 = (bf16[32,2048]{1,0:T(8,128)(2,1)S(1)}, bf16[32,2048]{1,0:T(8,128)(2,1)S(1)}, u32[]{:S(2)}, u32[]{:S(2)}) collective-permute-start(bf16[32,2048]{1,0:T(8,128)(2,1)S(1)} %collective-permute-done.1.far), channel_id=1, source_target_pairs={{0,1},{1,0},{2,3},{3,2},{4,5},{5,4},{6,7},{7,6},{8,9},{9,8},{10,11... | collective-permute-start | bytes 393224 | tf_op jit(solution)/shard_map/ppermute | solution.py:269
  21.1 1.8 %collective-permute-done.4.last = bf16[32,2048]{1,0:T(8,128)(2,1)S(1)} collective-permute-done((bf16[32,2048]{1,0:T(8,128)(2,1)S(1)}, bf16[32,2048]{1,0:T(8,128)(2,1)S(1)}, u32[]{:S(2)}, u32[]{:S(2)}) %collective-permute-start.4) | collective-permute-done | bytes 131104 | tf_op jit(solution)/shard_map/ppermute | solution.py:269
  23.0 0.0 collective-permute-done.near
  23.0 0.0 copy-done
  23.0 2.0 %score_low.1.low = f32[96,1024]{1,0:T(8,128)S(1)} custom-call(bf16[32,4096]{1,0:T(8,128)(2,1)S(1)} %collective-permute-done.near, bf16[32,2048]{1,0:T(8,128)(2,1)S(1)} %collective-permute-done.3.far, bf16[32,2048]{1,0:T(8,128)(2,1)S(1)} %collective-permute-done.4.last, bf16[1,1024,4096]{2,1,0:T(8,128)(2,1)S(1)} %copy-done), custom_call_target="tpu_custom_call" | custom-call | flops 402653184 | bytes 4194304 | tf_op jit(solution)/shard_map/score_low/pallas_call | solution.py:195
  24.9 0.0 collective-permute-done.2.last
  25.0 2.0 %score_high.1 = (f32[32,1024]{1,0:T(8,128)S(1)}, bf16[32,1024]{1,0:T(8,128)(2,1)S(1)}, bf16[32,1024]{1,0:T(8,128)(2,1)S(1)}, bf16[32,1024]{1,0:T(8,128)(2,1)S(1)}) custom-call(bf16[32,4096]{1,0:T(8,128)(2,1)S(1)} %collective-permute-done.near, bf16[32,2048]{1,0:T(8,128)(2,1)S(1)} %collective-permute-done.1.far, ...), custom_call_target="tpu_custom_call" | custom-call | flops 402653184 | bytes 4194304 | tf_op jit(solution)/shard_map/score_high/pallas_call | solution.py:224
  27.0 0.1 collective-permute-start.5
  27.1 1.6 %collective-permute-start.6 = (bf16[32,1024]{1,0:T(8,128)(2,1)S(1)}, bf16[32,1024]{1,0:T(8,128)(2,1)S(1)}, u32[]{:S(2)}, u32[]{:S(2)}) collective-permute-start(bf16[32,1024]{1,0:T(8,128)(2,1)S(1)} %get-tuple-element.19), channel_id=1, source_target_pairs={{0,8},{4,12},{8,0},{12,4},{1,9},{5,13},{9,1},{13,5},{2,10},{6,14},... | collective-permute-start | bytes 196616 | tf_op jit(solution)/shard_map/ppermute | solution.py:269
  28.7 0.2 collective-permute-start.7
  28.9 0.1 copy.6.candidates
  29.0 0.0 collective-permute-done.5.refs_1_
  29.0 2.6 %collective-permute-done.6.refs_2_ = bf16[32,1024]{1,0:T(8,128)(2,1)S(1)} collective-permute-done((bf16[32,1024]{1,0:T(8,128)(2,1)S(1)}, bf16[32,1024]{1,0:T(8,128)(2,1)S(1)}, u32[]{:S(2)}, u32[]{:S(2)}) %collective-permute-start.6) | collective-permute-done | bytes 65568 | tf_op jit(solution)/shard_map/ppermute | solution.py:269
  31.6 1.2 %collective-permute-done.7.refs_3_ = bf16[32,1024]{1,0:T(8,128)(2,1)S(1)} collective-permute-done((bf16[32,1024]{1,0:T(8,128)(2,1)S(1)}, bf16[32,1024]{1,0:T(8,128)(2,1)S(1)}, u32[]{:S(2)}, u32[]{:S(2)}) %collective-permute-start.7) | collective-permute-done | bytes 65568 | tf_op jit(solution)/shard_map/ppermute | solution.py:269
  32.7 0.7 %finish.1 = bf16[32,1024]{1,0:T(8,128)(2,1)} custom-call(s32[32,16]{1,0:T(8,128)S(1)} %copy.6.candidates, f32[32,1024]{1,0:T(8,128)S(1)} %get-tuple-element.17.refs_0_, bf16[32,1024]{1,0:T(8,128)(2,1)S(1)} %collective-permute-done.5.refs_1_, bf16[32,1024]{1,0:T(8,128)(2,1)S(1)} %collective-permute-done.6.refs_2_, ...), custom_call_target="tpu_custom_call" | custom-call | tf_op jit(solution)/shard_map/finish/pallas_call | solution.py:257
  (4 shorter events, 0.0 us)
Async XLA Ops:
  0.0 23.0 %copy-start = (bf16[1,1024,4096]{2,1,0:T(8,128)(2,1)S(1)}, bf16[1,1024,4096]{2,1,0:T(8,128)(2,1)}, u32[]{:S(2)}) copy-start(bf16[1,1024,4096]{2,1,0:T(8,128)(2,1)} %store.3) | copy-start | bytes 25165828
  2.3 11.3 %collective-permute-start.3 = (bf16[32,2048]{1,0:T(8,128)(2,1)S(1)}, bf16[32,2048]{1,0:T(8,128)(2,1)S(1)}, u32[]{:S(2)}, u32[]{:S(2)}) collective-permute-start(bf16[32,2048]{1,0:T(8,128)(2,1)S(1)} %get-tuple-element.13), channel_id=1, source_target_pairs={{0,2},{1,3},{2,0},{3,1},{4,6},{5,7},{6,4},{7,5},{8,10},{9,11},{10,... | collective-permute-start | bytes 393224 | tf_op jit(solution)/shard_map/ppermute | solution.py:269
  6.5 16.5 %collective-permute-start = (bf16[32,4096]{1,0:T(8,128)(2,1)S(1)}, bf16[32,4096]{1,0:T(8,128)(2,1)S(1)}, u32[]{:S(2)}, u32[]{:S(2)}) collective-permute-start(bf16[32,4096]{1,0:T(8,128)(2,1)S(1)} %constant_dynamic-update-slice_fusion.queries), channel_id=1, source_target_pairs={{0,1},{1,0},{2,3},{3,2},{4,5},{5,4},{6,7},{7,6},{8,9},{9,8},{10,11... | collective-permute-start | bytes 786440 | tf_op jit(solution)/shard_map/ppermute | solution.py:269
  8.1 10.7 %collective-permute-start.1 = (bf16[32,2048]{1,0:T(8,128)(2,1)S(1)}, bf16[32,2048]{1,0:T(8,128)(2,1)S(1)}, u32[]{:S(2)}, u32[]{:S(2)}) collective-permute-start(bf16[32,2048]{1,0:T(8,128)(2,1)S(1)} %get-tuple-element.14), channel_id=1, source_target_pairs={{0,2},{1,3},{2,0},{3,1},{4,6},{5,7},{6,4},{7,5},{8,10},{9,11},{10,... | collective-permute-start | bytes 393224 | tf_op jit(solution)/shard_map/ppermute | solution.py:269
  13.0 15.9 %copy-start.1 = (s32[32,16]{0,1:T(8,128)S(1)}, s32[32,16]{0,1:T(8,128)}, u32[]{:S(2)}) copy-start(s32[32,16]{0,1:T(8,128)} %param.9) | copy-start | bytes 6148
  13.7 9.3 %collective-permute-start.4 = (bf16[32,2048]{1,0:T(8,128)(2,1)S(1)}, bf16[32,2048]{1,0:T(8,128)(2,1)S(1)}, u32[]{:S(2)}, u32[]{:S(2)}) collective-permute-start(bf16[32,2048]{1,0:T(8,128)(2,1)S(1)} %collective-permute-done.3.far), channel_id=1, source_target_pairs={{0,1},{1,0},{2,3},{3,2},{4,5},{5,4},{6,7},{7,6},{8,9},{9,8},{10,11... | collective-permute-start | bytes 393224 | tf_op jit(solution)/shard_map/ppermute | solution.py:269
  18.8 6.2 %collective-permute-start.2 = (bf16[32,2048]{1,0:T(8,128)(2,1)S(1)}, bf16[32,2048]{1,0:T(8,128)(2,1)S(1)}, u32[]{:S(2)}, u32[]{:S(2)}) collective-permute-start(bf16[32,2048]{1,0:T(8,128)(2,1)S(1)} %collective-permute-done.1.far), channel_id=1, source_target_pairs={{0,1},{1,0},{2,3},{3,2},{4,5},{5,4},{6,7},{7,6},{8,9},{9,8},{10,11... | collective-permute-start | bytes 393224 | tf_op jit(solution)/shard_map/ppermute | solution.py:269
  27.0 2.0 %collective-permute-start.5 = (bf16[32,1024]{1,0:T(8,128)(2,1)S(1)}, bf16[32,1024]{1,0:T(8,128)(2,1)S(1)}, u32[]{:S(2)}, u32[]{:S(2)}) collective-permute-start(bf16[32,1024]{1,0:T(8,128)(2,1)S(1)} %get-tuple-element.18), channel_id=1, source_target_pairs={{0,4},{4,0},{8,12},{12,8},{1,5},{5,1},{9,13},{13,9},{2,6},{6,2},{1... | collective-permute-start | bytes 196616 | tf_op jit(solution)/shard_map/ppermute | solution.py:269
  27.1 4.5 %collective-permute-start.6 = (bf16[32,1024]{1,0:T(8,128)(2,1)S(1)}, bf16[32,1024]{1,0:T(8,128)(2,1)S(1)}, u32[]{:S(2)}, u32[]{:S(2)}) collective-permute-start(bf16[32,1024]{1,0:T(8,128)(2,1)S(1)} %get-tuple-element.19), channel_id=1, source_target_pairs={{0,8},{4,12},{8,0},{12,4},{1,9},{5,13},{9,1},{13,5},{2,10},{6,14},... | collective-permute-start | bytes 196616 | tf_op jit(solution)/shard_map/ppermute | solution.py:269
  28.7 4.0 %collective-permute-start.7 = (bf16[32,1024]{1,0:T(8,128)(2,1)S(1)}, bf16[32,1024]{1,0:T(8,128)(2,1)S(1)}, u32[]{:S(2)}, u32[]{:S(2)}) collective-permute-start(bf16[32,1024]{1,0:T(8,128)(2,1)S(1)} %get-tuple-element.20), channel_id=1, source_target_pairs={{0,12},{4,8},{8,4},{12,0},{1,13},{5,9},{9,5},{13,1},{2,14},{6,10},... | collective-permute-start | bytes 196616 | tf_op jit(solution)/shard_map/ppermute | solution.py:269

commit v5 on v4

--- a/solution.py
+++ b/solution.py
@@ -52,14 +52,16 @@
     return jnp.concatenate([high, low, high], axis=0)
 
 
-def condition_kernel(queries_in, left_in, right_in, low, high, queries, left_factor, right_factor, arrived):
-    halves = (low, high)
-    copies = [
-        pltpu.make_async_copy(source.at[0], target, arrived.at[place])
-        for place, (source, target) in enumerate(
-            [(left_in, left_factor), (right_in, right_factor), (queries_in, queries)]
-        )
-    ]
+def condition_kernel(rows_each, count, unused, *refs):
+    sources, (left_in, right_in), refs = refs[: len(rows_each)], refs[len(rows_each) :][:2], refs[len(rows_each) + 2 + unused :]
+    outs, (queries, left_factor, right_factor, arrived) = refs[:count], refs[count:]
+    copies = [pltpu.make_async_copy(left_in.at[0], left_factor, arrived.at[0])]
+    copies += [pltpu.make_async_copy(right_in.at[0], right_factor, arrived.at[1])]
+    start = 0
+    for place, (source, rows) in enumerate(zip(sources, rows_each)):
+        target = queries.at[pl.ds(start, rows)]
+        copies.append(pltpu.make_async_copy(source.at[0], target, arrived.at[2 + place]))
+        start += rows
     for copy in copies:
         copy.start()
     side = left_factor.shape[0]
@@ -69,8 +71,8 @@
     left = spread_left(left_factor[...])
     right = spread_right(right_factor[...])
     low_half = iota((1, 1, LANES), 2) < side
-    per_half = pairs // len(halves)
-    copies[2].wait()
+    for copy in copies[2:]:
+        copy.wait()
     for block in range(queries.shape[0] // GROUP):
         rows = pl.ds(block * GROUP, GROUP)
         straight = jnp.stack(
@@ -96,33 +98,40 @@
             groups.append(jnp.where(low_half, pltpu.roll(even, side, 2), odd))
         done = jnp.concatenate(groups, axis=1).astype(jnp.bfloat16)
         for pair in range(pairs):
-            halves[pair // per_half][rows, pl.ds(pair % per_half * LANES, LANES)] = done[pair]
+            outs[0][rows, pl.ds(pair * LANES, LANES)] = done[pair]
+        for out in outs[1:]:
+            kept = out.shape[0]
+            for pair in range(pairs):
+                out[:, pl.ds(pair * LANES, LANES)] = done[pair, GROUP - kept :]
 
 
 def in_vmem(count):
     return [pl.BlockSpec(memory_space=pltpu.VMEM)] * count
 
 
-def condition(queries, left_factor, right_factor):
-    unused, block_rows, entries = queries.shape
+def condition(sources, left_factor, right_factor, pieces, others=()):
+    rows_each = [source.shape[1] for source in sources]
+    block_rows, entries = sum(rows_each), sources[0].shape[2]
     side = left_factor.shape[1]
-    return pl.pallas_call(
-        condition_kernel,
-        in_specs=[pl.BlockSpec(memory_space=pltpu.HBM)] * 3,
-        out_specs=in_vmem(2),
-        out_shape=[jax.ShapeDtypeStruct((block_rows, entries // 2), jnp.bfloat16)] * 2,
+    shapes = [(block_rows, entries)] + ([(pieces, entries)] if pieces else [])
+    operands = (*sources, left_factor, right_factor, *others)
+    return pl.pallas_call(
+        functools.partial(condition_kernel, rows_each, len(shapes), len(others)),
+        in_specs=[pl.BlockSpec(memory_space=pl.ANY)] * len(operands),
+        out_specs=in_vmem(len(shapes)),
+        out_shape=[jax.ShapeDtypeStruct(shape, jnp.bfloat16) for shape in shapes],
         scratch_shapes=[
             pltpu.VMEM((block_rows, entries), jnp.bfloat16),
             pltpu.VMEM((side, side), jnp.float32),
             pltpu.VMEM((side, side), jnp.float32),
-            pltpu.SemaphoreType.DMA((3,)),
+            pltpu.SemaphoreType.DMA((len(operands),)),
         ],
         compiler_params=pltpu.CompilerParams(vmem_limit_bytes=VMEM),
         cost_estimate=pl.CostEstimate(
-            flops=block_rows * entries * 4096, bytes_accessed=queries.size * 4, transcendentals=0
+            flops=block_rows * entries * 4096, bytes_accessed=block_rows * entries * 4, transcendentals=0
         ),
         name="condition",
-    )(*[pltpu.with_memory_space_constraint(value, pltpu.HBM) for value in (queries, left_factor, right_factor)])
+    )(*operands)
 
 
 STEP = 256
@@ -178,82 +187,100 @@
     )(queries, pltpu.with_memory_space_constraint(store, pltpu.HBM))
 
 
-def three_blocks(near, far, last, first):
-    return jnp.concatenate([near[:, pl.ds(first, far.shape[1])], far[...], last[...]], axis=0)
-
-
-def low_kernel(near, far, last, store, out):
+def all_blocks(own, near, mixed, far, last, first):
+    rows, width = last.shape
+    entries = pl.ds(first, width)
+    slots = [own[:, entries], near[:, entries]]
+    slots += [mixed[pl.ds(0, rows), entries], far[:, entries], mixed[pl.ds(rows, rows), entries], last[...]]
+    return jnp.concatenate(slots, axis=0)
+
+
+def low_kernel(own, near, mixed, far, last, store, out):
     def write(place, value):
         out[:, place] = value
 
-    score_block(three_blocks(near, far, last, 0), store, 0, write)
-
-
-def score_low(near, far, last, store):
-    rows, width = far.shape
-    examples = store.shape[1]
-    return pl.pallas_call(
-        low_kernel,
-        in_specs=in_vmem(4),
-        out_specs=in_vmem(1)[0],
-        out_shape=jax.ShapeDtypeStruct((3 * rows, examples), jnp.float32),
-        compiler_params=pltpu.CompilerParams(vmem_limit_bytes=VMEM),
-        cost_estimate=score_cost(3 * rows, width, examples),
-        name="score_low",
-    )(near, far, last, store)
-
-
-def high_kernel(first, near, far, last, store, own, low, *refs):
+    score_block(all_blocks(own, near, mixed, far, last, 0), store, 0, write)
+
+
+def high_kernel(first, own, near, mixed, far, last, store, low, *refs):
     outs, total = refs[:-1], refs[-1]
     rows = own.shape[0]
-    total[pl.ds(0, rows), :] = own[...]
 
     def write(place, value):
-        total[pl.ds(rows, 3 * rows), place] = value + low[:, place]
-
-    score_block(three_blocks(near, far, last, first), store, first, write)
+        total[:, place] = value + low[:, place]
+
+    score_block(all_blocks(own, near, mixed, far, last, first), store, first, write)
     home = lax.bitwise_xor(lax.axis_index("blk"), lax.axis_index("layer"))
     for mask, out in enumerate(outs):
         slot = lax.bitwise_xor(home, mask)
         out[...] = total[pl.ds(pl.multiple_of(slot * rows, rows), rows), :].astype(out.dtype)
 
 
-def score_high(near, far, last, store, own, low):
-    rows, width = far.shape
+def score_low(own, near, mixed, far, last, store):
+    count, width = 4 * own.shape[0], last.shape[1]
     examples = store.shape[1]
     return pl.pallas_call(
-        functools.partial(high_kernel, near.shape[1] - width),
+        low_kernel,
         in_specs=in_vmem(6),
+        out_specs=in_vmem(1)[0],
+        out_shape=jax.ShapeDtypeStruct((count, examples), jnp.float32),
+        compiler_params=pltpu.CompilerParams(vmem_limit_bytes=VMEM),
+        cost_estimate=score_cost(count, width, examples),
+        name="score_low",
+    )(own, near, mixed, far, last, store)
+
+
+def score_high(own, near, mixed, far, last, store, low):
+    rows, entries = own.shape
+    width = last.shape[1]
+    examples = store.shape[1]
+    return pl.pallas_call(
+        functools.partial(high_kernel, entries - width),
+        in_specs=in_vmem(7),
         out_specs=in_vmem(4),
         out_shape=[
             jax.ShapeDtypeStruct((rows, examples), jnp.bfloat16 if mask else jnp.float32) for mask in range(4)
         ],
         scratch_shapes=[pltpu.VMEM((4 * rows, examples), jnp.float32)],
         compiler_params=pltpu.CompilerParams(vmem_limit_bytes=VMEM),
-        cost_estimate=score_cost(3 * rows, width, examples),
+        cost_estimate=score_cost(4 * rows, width, examples),
         name="score_high",
-    )(near, far, last, store, own, low)
-
-
-def write_rows(total, layers, listed, out):
-    scaled = total / jnp.sqrt(jnp.float32(layers))
-    tiles_here = out.shape[1] // TILE
+    )(own, near, mixed, far, last, store, low)
+
+
+def keep_kernel(tiles_here, candidates, out):
+    listed = candidates[...]
     first = lax.axis_index("blk") * tiles_here
+    kept = jnp.zeros(out.shape, jnp.float32)
     for tile in range(tiles_here):
         hit = jnp.max(jnp.where(listed == first + tile, 1.0, 0.0), axis=1, keepdims=True)
+        kept = jnp.where(iota(out.shape, 1) == tile, hit, kept)
+    out[...] = kept
+
+
+def kept_tiles(candidates, examples):
+    return pl.pallas_call(
+        functools.partial(keep_kernel, examples // TILE),
+        in_specs=in_vmem(1),
+        out_specs=in_vmem(1)[0],
+        out_shape=jax.ShapeDtypeStruct((candidates.shape[0], LANES), jnp.float32),
+        compiler_params=pltpu.CompilerParams(vmem_limit_bytes=VMEM),
+        name="kept_tiles",
+    )(candidates)
+
+
+def finish_kernel(layers, kept, *refs):
+    parts, out = refs[:-1], refs[-1]
+    for tile in range(out.shape[1] // TILE):
         columns = slice(tile * TILE, (tile + 1) * TILE)
-        out[:, columns] = jnp.where(hit > 0.0, scaled[:, columns], 0.0).astype(out.dtype)
-
-
-def finish_kernel(layers, candidates, *refs):
-    parts, out = refs[:-1], refs[-1]
-    total = parts[0][...].astype(jnp.float32)
-    for part in parts[1:]:
-        total = total + part[...].astype(jnp.float32)
-    write_rows(total, layers, candidates[...], out)
-
-
-def finish(parts, candidates, layers):
+        total = parts[0][:, columns].astype(jnp.float32)
+        for part in parts[1:]:
+            total = total + part[:, columns].astype(jnp.float32)
+        scaled = total / jnp.sqrt(jnp.float32(layers))
+        out[:, columns] = jnp.where(kept[:, tile : tile + 1] > 0.0, scaled, 0.0).astype(out.dtype)
+
+
+def finish(parts, kept, layers):
     return pl.pallas_call(
         functools.partial(finish_kernel, layers),
         in_specs=in_vmem(1 + len(parts)),
@@ -261,7 +288,7 @@
         out_shape=jax.ShapeDtypeStruct(parts[0].shape, jnp.bfloat16),
         compiler_params=pltpu.CompilerParams(vmem_limit_bytes=VMEM),
         name="finish",
-    )(candidates, *parts)
+    )(kept, *parts)
 
 
 def permuted(value, axis, target_of):
@@ -273,22 +300,31 @@
     return permuted(value, axis, lambda source: source ^ mask)
 
 
-def on_line(own, store, candidates, layers):
-    far = [swapped(half, "blk", 2) for half in own]
-    whole = jnp.concatenate(own, axis=1)
-    near = swapped(whole, "blk", 1)
-    own_scores = score_own(whole, store)
-    far[0], own_scores = lax.optimization_barrier((far[0], own_scores))
-    last = [swapped(half, "blk", 1) for half in far]
-    low_scores = score_low(near, far[0], last[0], store)
-    parts = score_high(near, far[1], last[1], store, own_scores, low_scores)
+def on_line(queries, store, factors, candidates, layers):
+    rows = queries.shape[1] // 2
+    raw_far = swapped(queries[:, :rows], "blk", 2)
+    raw_near = swapped(queries, "blk", 1)
+    stays = [pltpu.with_memory_space_constraint(value, pltpu.HBM) for value in (queries, store)]
+    own, leaving = condition(stays[:1], *factors, rows, stays[1:])
+    far = swapped(leaving, "blk", 2)
+    candidates, own = lax.optimization_barrier((candidates, own))
+    kept = kept_tiles(candidates, store.shape[1])
+    raw_near, kept = lax.optimization_barrier((raw_near, kept))
+    (near,) = condition([raw_near], *factors, 0)
+    raw_far, near = lax.optimization_barrier((raw_far, near))
+    raw_last = swapped(raw_far, "blk", 1)
+    half = far.shape[1] // 2
+    last = [swapped(far[:, start : start + half], "blk", 1) for start in (0, half)]
+    (mixed,) = condition([raw_far, raw_last], *factors, 0)
+    low_scores = score_low(own, near, mixed, far, last[0], store)
+    parts = score_high(own, near, mixed, far, last[1], store, low_scores)
     received = {mask: swapped(parts[mask], "layer", mask) for mask in (3, 2, 1)}
-    return finish([parts[0]] + [received[mask] for mask in (1, 2, 3)], candidates, layers)
-
-
-def on_ring(own, store, candidates, layers):
+    return finish([parts[0]] + [received[mask] for mask in (1, 2, 3)], kept, layers)
+
+
+def on_ring(queries, store, factors, candidates, layers):
     count = lax.axis_size("blk")
-    moving = jnp.concatenate(own, axis=1)
+    (moving,) = condition([queries], *factors, 0)
     rows = moving.shape[0]
     slots = [score_own(moving, store)]
     for _ in range(count - 1):
@@ -297,14 +333,15 @@
     turns = lax.rem(lax.axis_index("blk") - jnp.arange(count) + count, count)
     total = jnp.stack(slots)[turns].reshape(layers, count * rows // layers, store.shape[1])
     parts = lax.all_to_all(total.astype(jnp.bfloat16), "layer", 0, 0)
-    return finish([parts[layer] for layer in range(layers)], candidates, layers)
+    kept = kept_tiles(candidates, store.shape[1])
+    return finish([parts[layer] for layer in range(layers)], kept, layers)
 
 
 def per_device(queries, store, left_factor, right_factor, candidates):
     layers, count = lax.axis_size("layer"), lax.axis_size("blk")
-    own = condition(queries, left_factor, right_factor)
+    factors = [pltpu.with_memory_space_constraint(factor, pltpu.HBM) for factor in (left_factor, right_factor)]
     way = on_line if layers == 4 and count == 4 else on_ring
-    return way(own, store, candidates, layers)
+    return way(queries, store, factors, candidates, layers)
 
 
 def solution(mesh):

time: 33.6 us -> 38.3 us (1.14)
  local copies, waits for them, and re-layouts: 0.1 us -> 4.41 us
  starting transfers between devices: 10.4 us -> 11.3 us
  waiting for transfers between devices: 11.3 us -> 10.7 us
    unnamed x6 -> x4, local copies, waits for them, and re-layouts: 0.09 us -> 3.39 us
    slice x0 -> x2, local copies, waits for them, and re-layouts: none -> 0.96 us  [the longest x1 0.95 us: on_line(): raw_far = swapped(queries[:, :rows], 'blk', 2)]
    ppermute x8 -> x9, starting transfers between devices: 10.4 us -> 11.3 us  [permuted(): lax.ppermute(value, axis, [(source, target_of(source) % count) for source...]
    ppermute x8 -> x9, waiting for transfers between devices: 11.3 us -> 10.7 us  [permuted(): lax.ppermute(value, axis, [(source, target_of(source) % count) for source...]
    pallas_call x4 -> x6, Pallas kernels: 10.8 us -> 10.8 us  [the longest x3 6.55 us: condition(): pl.pallas_call(functools.partial(condition_kernel, rows_each, len(shapes)...]
  transfers between devices with their start and end apart: 8 -> 9, of which waited for: 5 -> 4; matrix products, arithmetic and copies ran while one was open for 0% -> 3% of each run, Pallas kernels for 19% -> 23%
where the time goes in v5:
time: 38.3 us; the launch traced here: 38 us
  Pallas kernels  11.5 us (30%)
  starting transfers between devices  11.3 us (30%)
  waiting for transfers between devices  10.7 us (28%)
  local copies, waits for them, and re-layouts  4.41 us (12%)
    ppermute x9, starting transfers between devices, permuted(): lax.ppermute(value, axis, [(source, target_of(source) % count) for source...  11.3 us
    ppermute x9, waiting for transfers between devices, permuted(): lax.ppermute(value, axis, [(source, target_of(source) % count) for source...  10.7 us
    pallas_call x3, Pallas kernels, condition(): pl.pallas_call(functools.partial(condition_kernel, rows_each, len(shapes)...  6.55 us
    unnamed x4, local copies, waits for them, and re-layouts  3.39 us
    pallas_call x1, Pallas kernels, score_high(): pl.pallas_call(functools.partial(high_kernel, entries - width), in_specs=...  2.1 us
    pallas_call x1, Pallas kernels, score_low(): pl.pallas_call(low_kernel, in_specs=in_vmem(6), out_specs=in_vmem(1)[0],...  2.06 us
    slice x1, local copies, waits for them, and re-layouts, on_line(): raw_far = swapped(queries[:, :rows], 'blk', 2)  0.95 us
  transfers between devices with their start and end apart: 9, of which 4 were waited for; matrix products, arithmetic and copies ran while one was open for 3% of the time, Pallas kernels for 23%

profile of v5, /device:TPU:0, one launch (start us, length us, event | category | flops | bytes accessed | tf_op | source)
XLA Modules:
  0.0 38.0 jit_solution(15969101732874364755)
XLA Ops:
  0.0 3.0 %collective-permute-start = (bf16[1,32,4096]{2,1,0:T(8,128)(2,1)}, bf16[1,32,4096]{2,1,0:T(8,128)(2,1)S(1)}, u32[]{:S(2)}, u32[]{:S(2)}) collective-permute-start(bf16[1,32,4096]{2,1,0:T(8,128)(2,1)} %refs_0_.1), channel_id=1, source_target_pairs={{0,1},{1,0},{2,3},{3,2},{4,5},{5,4},{6,7},{7,6},{8,9},{9,8},{10,11... | collective-permute-start | bytes 786440 | tf_op jit(solution)/shard_map/ppermute | solution.py:296
  3.0 0.9 %slice.9 = bf16[1,16,4096]{2,1,0:T(8,128)(2,1)S(1)} slice(bf16[1,32,4096]{2,1,0:T(8,128)(2,1)} %refs_0_.1), slice={[0:1], [0:16], [0:4096]} | slice | bytes 262144 | tf_op jit(solution)/shard_map/slice | solution.py:305
  4.0 2.7 %collective-permute-start.1 = (bf16[1,16,4096]{2,1,0:T(8,128)(2,1)S(1)}, bf16[1,16,4096]{2,1,0:T(8,128)(2,1)S(1)}, u32[]{:S(2)}, u32[]{:S(2)}) collective-permute-start(bf16[1,16,4096]{2,1,0:T(8,128)(2,1)S(1)} %slice.9), channel_id=1, source_target_pairs={{0,2},{1,3},{2,0},{3,1},{4,6},{5,7},{6,4},{7,5},{8,10},{9,11},{10,... | collective-permute-start | bytes 393224 | tf_op jit(solution)/shard_map/ppermute | solution.py:296
  6.6 2.2 %condition.3 = (bf16[32,4096]{1,0:T(8,128)(2,1)S(1)}, bf16[16,4096]{1,0:T(8,128)(2,1)S(1)}) custom-call(bf16[1,32,4096]{2,1,0:T(8,128)(2,1)} %refs_0_.1, f32[1,64,64]{2,1,0:T(8,128)} %refs_2_.5, f32[1,64,64]{2,1,0:T(8,128)} %refs_3_.3, bf16[1,1024,4096]{2,1,0:T(8,128)(2,1)} %store.3), custom_call_target="tpu_custom_call" | custom-call | flops 536870912 | bytes 524288 | tf_op jit(solution)/shard_map/condition/pallas_call | solution.py:118
  8.8 0.4 %collective-permute-start.3 = (bf16[16,4096]{1,0:T(8,128)(2,1)S(1)}, bf16[16,4096]{1,0:T(8,128)(2,1)S(1)}, u32[]{:S(2)}, u32[]{:S(2)}) collective-permute-start(bf16[16,4096]{1,0:T(8,128)(2,1)S(1)} %get-tuple-element.24), channel_id=1, source_target_pairs={{0,2},{1,3},{2,0},{3,1},{4,6},{5,7},{6,4},{7,5},{8,10},{9,11},{10,... | collective-permute-start | bytes 393224 | tf_op jit(solution)/shard_map/ppermute | solution.py:296
  9.2 0.1 copy.6.candidates
  9.3 0.1 kept_tiles.1.kept
  9.4 3.5 %collective-permute-done.refs_0_ = bf16[1,32,4096]{2,1,0:T(8,128)(2,1)S(1)} collective-permute-done((bf16[1,32,4096]{2,1,0:T(8,128)(2,1)}, bf16[1,32,4096]{2,1,0:T(8,128)(2,1)S(1)}, u32[]{:S(2)}, u32[]{:S(2)}) %collective-permute-start) | collective-permute-done | bytes 262176 | tf_op jit(solution)/shard_map/ppermute | solution.py:296
  13.0 2.2 %condition.4.near = bf16[32,4096]{1,0:T(8,128)(2,1)S(1)} custom-call(bf16[1,32,4096]{2,1,0:T(8,128)(2,1)S(1)} %collective-permute-done.refs_0_, f32[1,64,64]{2,1,0:T(8,128)} %refs_2_.5, f32[1,64,64]{2,1,0:T(8,128)} %refs_3_.3), custom_call_target="tpu_custom_call" | custom-call | flops 536870912 | bytes 524288 | tf_op jit(solution)/shard_map/condition/pallas_call | solution.py:118
  15.2 1.2 %collective-permute-start.2 = (bf16[1,16,4096]{2,1,0:T(8,128)(2,1)S(1)}, bf16[1,16,4096]{2,1,0:T(8,128)(2,1)S(1)}, u32[]{:S(2)}, u32[]{:S(2)}) collective-permute-start(bf16[1,16,4096]{2,1,0:T(8,128)(2,1)S(1)} %collective-permute-done.1.refs_0_), channel_id=1, source_target_pairs={{0,1},{1,0},{2,3},{3,2},{4,5},{5,4},{6,7},{7,6},{8,9},{9,8},{10,11... | collective-permute-start | bytes 393224 | tf_op jit(solution)/shard_map/ppermute | solution.py:296
  16.4 3.3 %collective-permute-done.3.far = bf16[16,4096]{1,0:T(8,128)(2,1)S(1)} collective-permute-done((bf16[16,4096]{1,0:T(8,128)(2,1)S(1)}, bf16[16,4096]{1,0:T(8,128)(2,1)S(1)}, u32[]{:S(2)}, u32[]{:S(2)}) %collective-permute-start.3) | collective-permute-done | bytes 131104 | tf_op jit(solution)/shard_map/ppermute | solution.py:296
  19.7 0.1 collective-permute-start.5
  19.7 2.0 %collective-permute-start.4 = (bf16[16,2048]{1,0:T(8,128)(2,1)S(1)}, bf16[16,2048]{1,0:T(8,128)(2,1)S(1)}, u32[]{:S(2)}, u32[]{:S(2)}) collective-permute-start(bf16[16,2048]{1,0:T(8,128)(2,1)S(1)} %get-tuple-element.30), channel_id=1, source_target_pairs={{0,1},{1,0},{2,3},{3,2},{4,5},{5,4},{6,7},{7,6},{8,9},{9,8},{10,11... | collective-permute-start | bytes 196616 | tf_op jit(solution)/shard_map/ppermute | solution.py:296
  21.8 2.2 %condition.5.mixed = bf16[32,4096]{1,0:T(8,128)(2,1)S(1)} custom-call(bf16[1,16,4096]{2,1,0:T(8,128)(2,1)S(1)} %collective-permute-done.1.refs_0_, bf16[1,16,4096]{2,1,0:T(8,128)(2,1)S(1)} %collective-permute-done.2.refs_1_, f32[1,64,64]{2,1,0:T(8,128)} %refs_2_.5, f32[1,64,64]{2,1,0:T(8,128)} %refs_3_.3), custom_call_target="tpu_custom_call" | custom-call | flops 536870912 | bytes 524288 | tf_op jit(solution)/shard_map/condition/pallas_call | solution.py:118
  24.0 0.0 collective-permute-done.5.last
  24.0 3.4 %copy-done = bf16[1,1024,4096]{2,1,0:T(8,128)(2,1)S(1)} copy-done((bf16[1,1024,4096]{2,1,0:T(8,128)(2,1)S(1)}, bf16[1,1024,4096]{2,1,0:T(8,128)(2,1)}, u32[]{:S(2)}) %copy-start) | copy-done | bytes 8388632
  27.4 2.1 %score_low.1.low = f32[128,1024]{1,0:T(8,128)S(1)} custom-call(bf16[32,4096]{1,0:T(8,128)(2,1)S(1)} %get-tuple-element.20.own, bf16[32,4096]{1,0:T(8,128)(2,1)S(1)} %condition.4.near, bf16[32,4096]{1,0:T(8,128)(2,1)S(1)} %condition.5.mixed, bf16[16,4096]{1,0:T(8,128)(2,1)S(1)} %collective-permute-done.3.far, ...), custom_call_target="tpu_custom_call" | custom-call | flops 536870912 | bytes 4194304 | tf_op jit(solution)/shard_map/score_low/pallas_call | solution.py:222
  29.5 2.1 %score_high.1 = (f32[32,1024]{1,0:T(8,128)S(1)}, bf16[32,1024]{1,0:T(8,128)(2,1)S(1)}, bf16[32,1024]{1,0:T(8,128)(2,1)S(1)}, bf16[32,1024]{1,0:T(8,128)(2,1)S(1)}) custom-call(bf16[32,4096]{1,0:T(8,128)(2,1)S(1)} %get-tuple-element.20.own, bf16[32,4096]{1,0:T(8,128)(2,1)S(1)} %condition.4.near, bf16[32,4096]{1,0:T(8,128)(2,1)S(1)} %condition.5.mixed, ...), custom_call_target="tpu_custom_call" | custom-call | flops 536870912 | bytes 4194304 | tf_op jit(solution)/shard_map/score_high/pallas_call | solution.py:237
  31.6 0.1 collective-permute-start.6
  31.6 1.6 %collective-permute-start.7 = (bf16[32,1024]{1,0:T(8,128)(2,1)S(1)}, bf16[32,1024]{1,0:T(8,128)(2,1)S(1)}, u32[]{:S(2)}, u32[]{:S(2)}) collective-permute-start(bf16[32,1024]{1,0:T(8,128)(2,1)S(1)} %get-tuple-element.27), channel_id=1, source_target_pairs={{0,8},{4,12},{8,0},{12,4},{1,9},{5,13},{9,1},{13,5},{2,10},{6,14},... | collective-permute-start | bytes 196616 | tf_op jit(solution)/shard_map/ppermute | solution.py:296
  33.2 0.3 collective-permute-start.8
  33.5 2.6 %collective-permute-done.7.refs_2_ = bf16[32,1024]{1,0:T(8,128)(2,1)S(1)} collective-permute-done((bf16[32,1024]{1,0:T(8,128)(2,1)S(1)}, bf16[32,1024]{1,0:T(8,128)(2,1)S(1)}, u32[]{:S(2)}, u32[]{:S(2)}) %collective-permute-start.7) | collective-permute-done | bytes 65568 | tf_op jit(solution)/shard_map/ppermute | solution.py:296
  36.2 1.1 %collective-permute-done.8.refs_3_ = bf16[32,1024]{1,0:T(8,128)(2,1)S(1)} collective-permute-done((bf16[32,1024]{1,0:T(8,128)(2,1)S(1)}, bf16[32,1024]{1,0:T(8,128)(2,1)S(1)}, u32[]{:S(2)}, u32[]{:S(2)}) %collective-permute-start.8) | collective-permute-done | bytes 65568 | tf_op jit(solution)/shard_map/ppermute | solution.py:296
  37.3 0.7 %finish.1 = bf16[32,1024]{1,0:T(8,128)(2,1)} custom-call(f32[32,128]{1,0:T(8,128)S(1)} %kept_tiles.1.kept, f32[32,1024]{1,0:T(8,128)S(1)} %get-tuple-element.25.refs_0_, bf16[32,1024]{1,0:T(8,128)(2,1)S(1)} %collective-permute-done.6.refs_1_, bf16[32,1024]{1,0:T(8,128)(2,1)S(1)} %collective-permute-done.7.refs_2_, ...), custom_call_target="tpu_custom_call" | custom-call | tf_op jit(solution)/shard_map/finish/pallas_call | solution.py:284
  (8 shorter events, 0.0 us)
Async XLA Ops:
  0.0 9.2 %copy-start.1 = (s32[32,16]{0,1:T(8,128)S(1)}, s32[32,16]{0,1:T(8,128)}, u32[]{:S(2)}) copy-start(s32[32,16]{0,1:T(8,128)} %param.9) | copy-start | bytes 6148
  0.0 13.0 %collective-permute-start = (bf16[1,32,4096]{2,1,0:T(8,128)(2,1)}, bf16[1,32,4096]{2,1,0:T(8,128)(2,1)S(1)}, u32[]{:S(2)}, u32[]{:S(2)}) collective-permute-start(bf16[1,32,4096]{2,1,0:T(8,128)(2,1)} %refs_0_.1), channel_id=1, source_target_pairs={{0,1},{1,0},{2,3},{3,2},{4,5},{5,4},{6,7},{7,6},{8,9},{9,8},{10,11... | collective-permute-start | bytes 786440 | tf_op jit(solution)/shard_map/ppermute | solution.py:296
  4.0 11.2 %collective-permute-start.1 = (bf16[1,16,4096]{2,1,0:T(8,128)(2,1)S(1)}, bf16[1,16,4096]{2,1,0:T(8,128)(2,1)S(1)}, u32[]{:S(2)}, u32[]{:S(2)}) collective-permute-start(bf16[1,16,4096]{2,1,0:T(8,128)(2,1)S(1)} %slice.9), channel_id=1, source_target_pairs={{0,2},{1,3},{2,0},{3,1},{4,6},{5,7},{6,4},{7,5},{8,10},{9,11},{10,... | collective-permute-start | bytes 393224 | tf_op jit(solution)/shard_map/ppermute | solution.py:296
  8.8 10.8 %collective-permute-start.3 = (bf16[16,4096]{1,0:T(8,128)(2,1)S(1)}, bf16[16,4096]{1,0:T(8,128)(2,1)S(1)}, u32[]{:S(2)}, u32[]{:S(2)}) collective-permute-start(bf16[16,4096]{1,0:T(8,128)(2,1)S(1)} %get-tuple-element.24), channel_id=1, source_target_pairs={{0,2},{1,3},{2,0},{3,1},{4,6},{5,7},{6,4},{7,5},{8,10},{9,11},{10,... | collective-permute-start | bytes 393224 | tf_op jit(solution)/shard_map/ppermute | solution.py:296
  15.2 6.6 %collective-permute-start.2 = (bf16[1,16,4096]{2,1,0:T(8,128)(2,1)S(1)}, bf16[1,16,4096]{2,1,0:T(8,128)(2,1)S(1)}, u32[]{:S(2)}, u32[]{:S(2)}) collective-permute-start(bf16[1,16,4096]{2,1,0:T(8,128)(2,1)S(1)} %collective-permute-done.1.refs_0_), channel_id=1, source_target_pairs={{0,1},{1,0},{2,3},{3,2},{4,5},{5,4},{6,7},{7,6},{8,9},{9,8},{10,11... | collective-permute-start | bytes 393224 | tf_op jit(solution)/shard_map/ppermute | solution.py:296
  19.7 4.3 %collective-permute-start.5 = (bf16[16,2048]{1,0:T(8,128)(2,1)S(1)}, bf16[16,2048]{1,0:T(8,128)(2,1)S(1)}, u32[]{:S(2)}, u32[]{:S(2)}) collective-permute-start(bf16[16,2048]{1,0:T(8,128)(2,1)S(1)} %get-tuple-element.29), channel_id=1, source_target_pairs={{0,1},{1,0},{2,3},{3,2},{4,5},{5,4},{6,7},{7,6},{8,9},{9,8},{10,11... | collective-permute-start | bytes 196616 | tf_op jit(solution)/shard_map/ppermute | solution.py:296
  19.7 9.7 %collective-permute-start.4 = (bf16[16,2048]{1,0:T(8,128)(2,1)S(1)}, bf16[16,2048]{1,0:T(8,128)(2,1)S(1)}, u32[]{:S(2)}, u32[]{:S(2)}) collective-permute-start(bf16[16,2048]{1,0:T(8,128)(2,1)S(1)} %get-tuple-element.30), channel_id=1, source_target_pairs={{0,1},{1,0},{2,3},{3,2},{4,5},{5,4},{6,7},{7,6},{8,9},{9,8},{10,11... | collective-permute-start | bytes 196616 | tf_op jit(solution)/shard_map/ppermute | solution.py:296
  24.0 3.4 %copy-start = (bf16[1,1024,4096]{2,1,0:T(8,128)(2,1)S(1)}, bf16[1,1024,4096]{2,1,0:T(8,128)(2,1)}, u32[]{:S(2)}) copy-start(bf16[1,1024,4096]{2,1,0:T(8,128)(2,1)} %store.3) | copy-start | bytes 25165828
  31.6 1.9 %collective-permute-start.6 = (bf16[32,1024]{1,0:T(8,128)(2,1)S(1)}, bf16[32,1024]{1,0:T(8,128)(2,1)S(1)}, u32[]{:S(2)}, u32[]{:S(2)}) collective-permute-start(bf16[32,1024]{1,0:T(8,128)(2,1)S(1)} %get-tuple-element.26), channel_id=1, source_target_pairs={{0,4},{4,0},{8,12},{12,8},{1,5},{5,1},{9,13},{13,9},{2,6},{6,2},{1... | collective-permute-start | bytes 196616 | tf_op jit(solution)/shard_map/ppermute | solution.py:296
  31.6 4.5 %collective-permute-start.7 = (bf16[32,1024]{1,0:T(8,128)(2,1)S(1)}, bf16[32,1024]{1,0:T(8,128)(2,1)S(1)}, u32[]{:S(2)}, u32[]{:S(2)}) collective-permute-start(bf16[32,1024]{1,0:T(8,128)(2,1)S(1)} %get-tuple-element.27), channel_id=1, source_target_pairs={{0,8},{4,12},{8,0},{12,4},{1,9},{5,13},{9,1},{13,5},{2,10},{6,14},... | collective-permute-start | bytes 196616 | tf_op jit(solution)/shard_map/ppermute | solution.py:296
  33.2 4.0 %collective-permute-start.8 = (bf16[32,1024]{1,0:T(8,128)(2,1)S(1)}, bf16[32,1024]{1,0:T(8,128)(2,1)S(1)}, u32[]{:S(2)}, u32[]{:S(2)}) collective-permute-start(bf16[32,1024]{1,0:T(8,128)(2,1)S(1)} %get-tuple-element.28), channel_id=1, source_target_pairs={{0,12},{4,8},{8,4},{12,0},{1,13},{5,9},{9,5},{13,1},{2,14},{6,10},... | collective-permute-start | bytes 196616 | tf_op jit(solution)/shard_map/ppermute | solution.py:296

commit v6 on v4

--- a/solution.py
+++ b/solution.py
@@ -128,14 +128,12 @@
 STEP = 256
 
 
-def score_block(queries, store, first, write, arrived=None):
+def score_block(queries, store, first, write):
     turned = queries.T
     width = queries.shape[1]
 
     def one(step, carry):
         place = pl.ds(pl.multiple_of(step * STEP, STEP), STEP)
-        if arrived is not None:
-            arrived(step)
         value = dot(store[0, place, pl.ds(first, width)], turned)
         write(place, value.T)
         return carry
@@ -143,18 +141,28 @@
     lax.fori_loop(0, store.shape[1] // STEP, one, 0)
 
 
-def own_kernel(queries, far_store, out, store, semaphores):
-    def copy_of(step):
-        place = pl.ds(pl.multiple_of(step * STEP, STEP), STEP)
-        return pltpu.make_async_copy(far_store.at[0, place], store.at[0, place], semaphores.at[step])
-
+def fetch_kernel(far_store, store, semaphores):
+    copies = []
     for step in range(store.shape[1] // STEP):
-        copy_of(step).start()
-
-    def write(place, value):
-        out[:, place] = value
-
-    score_block(queries[...], store, 0, write, lambda step: copy_of(step).wait())
+        place = pl.ds(step * STEP, STEP)
+        copies.append(pltpu.make_async_copy(far_store.at[0, place], store.at[0, place], semaphores.at[step]))
+    for copy in copies:
+        copy.start()
+    for copy in copies:
+        copy.wait()
+
+
+def fetch(store):
+    return pl.pallas_call(
+        fetch_kernel,
+        in_specs=[pl.BlockSpec(memory_space=pltpu.HBM)],
+        out_specs=in_vmem(1)[0],
+        out_shape=jax.ShapeDtypeStruct(store.shape, store.dtype),
+        scratch_shapes=[pltpu.SemaphoreType.DMA((store.shape[1] // STEP,))],
+        compiler_params=pltpu.CompilerParams(vmem_limit_bytes=VMEM),
+        cost_estimate=pl.CostEstimate(flops=0, bytes_accessed=2 * store.size * 2, transcendentals=0),
+        name="fetch",
+    )(pltpu.with_memory_space_constraint(store, pltpu.HBM))
 
 
 def score_cost(count, width, examples):
@@ -163,97 +171,99 @@
     )
 
 
-def score_own(queries, store):
-    rows, entries = queries.shape
-    examples = store.shape[1]
-    return pl.pallas_call(
-        own_kernel,
-        in_specs=in_vmem(1) + [pl.BlockSpec(memory_space=pltpu.HBM)],
-        out_specs=in_vmem(1)[0],
-        out_shape=jax.ShapeDtypeStruct((rows, examples), jnp.float32),
-        scratch_shapes=[pltpu.VMEM(store.shape, store.dtype), pltpu.SemaphoreType.DMA((examples // STEP,))],
-        compiler_params=pltpu.CompilerParams(vmem_limit_bytes=VMEM),
-        cost_estimate=score_cost(rows, entries, examples),
-        name="score_own",
-    )(queries, pltpu.with_memory_space_constraint(store, pltpu.HBM))
-
-
-def three_blocks(near, far, last, first):
-    return jnp.concatenate([near[:, pl.ds(first, far.shape[1])], far[...], last[...]], axis=0)
-
-
-def low_kernel(near, far, last, store, out):
+def stacked(blocks):
+    return jnp.concatenate([block[...] for block in blocks], axis=0)
+
+
+def low_kernel(*refs):
+    blocks, (store, out) = refs[:-2], refs[-2:]
+
     def write(place, value):
         out[:, place] = value
 
-    score_block(three_blocks(near, far, last, 0), store, 0, write)
-
-
-def score_low(near, far, last, store):
-    rows, width = far.shape
+    score_block(stacked(blocks), store, 0, write)
+
+
+def score_low(blocks, store):
+    count, width = sum(block.shape[0] for block in blocks), blocks[0].shape[1]
     examples = store.shape[1]
     return pl.pallas_call(
         low_kernel,
-        in_specs=in_vmem(4),
+        in_specs=in_vmem(len(blocks) + 1),
         out_specs=in_vmem(1)[0],
-        out_shape=jax.ShapeDtypeStruct((3 * rows, examples), jnp.float32),
-        compiler_params=pltpu.CompilerParams(vmem_limit_bytes=VMEM),
-        cost_estimate=score_cost(3 * rows, width, examples),
+        out_shape=jax.ShapeDtypeStruct((count, examples), jnp.float32),
+        compiler_params=pltpu.CompilerParams(vmem_limit_bytes=VMEM),
+        cost_estimate=score_cost(count, width, examples),
         name="score_low",
-    )(near, far, last, store)
-
-
-def high_kernel(first, near, far, last, store, own, low, *refs):
-    outs, total = refs[:-1], refs[-1]
-    rows = own.shape[0]
-    total[pl.ds(0, rows), :] = own[...]
+    )(*blocks, store)
+
+
+def high_kernel(first, count, *refs):
+    blocks, (store, low), outs, total = refs[:count], refs[count : count + 2], refs[count + 2 : -1], refs[-1]
 
     def write(place, value):
-        total[pl.ds(rows, 3 * rows), place] = value + low[:, place]
-
-    score_block(three_blocks(near, far, last, first), store, first, write)
+        total[:, place] = value + low[:, place]
+
+    score_block(stacked(blocks), store, first, write)
+    rows = blocks[0].shape[0]
     home = lax.bitwise_xor(lax.axis_index("blk"), lax.axis_index("layer"))
     for mask, out in enumerate(outs):
         slot = lax.bitwise_xor(home, mask)
         out[...] = total[pl.ds(pl.multiple_of(slot * rows, rows), rows), :].astype(out.dtype)
 
 
-def score_high(near, far, last, store, own, low):
-    rows, width = far.shape
+def score_high(blocks, store, low):
+    rows, width = blocks[0].shape
+    count = len(blocks)
     examples = store.shape[1]
     return pl.pallas_call(
-        functools.partial(high_kernel, near.shape[1] - width),
-        in_specs=in_vmem(6),
-        out_specs=in_vmem(4),
+        functools.partial(high_kernel, store.shape[2] - width, count),
+        in_specs=in_vmem(count + 2),
+        out_specs=in_vmem(count),
         out_shape=[
-            jax.ShapeDtypeStruct((rows, examples), jnp.bfloat16 if mask else jnp.float32) for mask in range(4)
+            jax.ShapeDtypeStruct((rows, examples), jnp.bfloat16 if mask else jnp.float32)
+            for mask in range(count)
         ],
-        scratch_shapes=[pltpu.VMEM((4 * rows, examples), jnp.float32)],
-        compiler_params=pltpu.CompilerParams(vmem_limit_bytes=VMEM),
-        cost_estimate=score_cost(3 * rows, width, examples),
+        scratch_shapes=[pltpu.VMEM((count * rows, examples), jnp.float32)],
+        compiler_params=pltpu.CompilerParams(vmem_limit_bytes=VMEM),
+        cost_estimate=score_cost(count * rows, width, examples),
         name="score_high",
-    )(near, far, last, store, own, low)
-
-
-def write_rows(total, layers, listed, out):
-    scaled = total / jnp.sqrt(jnp.float32(layers))
-    tiles_here = out.shape[1] // TILE
+    )(*blocks, store, low)
+
+
+def keep_kernel(tiles_here, candidates, out):
+    listed = candidates[...]
     first = lax.axis_index("blk") * tiles_here
+    kept = jnp.zeros(out.shape, jnp.float32)
     for tile in range(tiles_here):
         hit = jnp.max(jnp.where(listed == first + tile, 1.0, 0.0), axis=1, keepdims=True)
+        kept = jnp.where(iota(out.shape, 1) == tile, hit, kept)
+    out[...] = kept
+
+
+def kept_tiles(candidates, examples):
+    return pl.pallas_call(
+        functools.partial(keep_kernel, examples // TILE),
+        in_specs=in_vmem(1),
+        out_specs=in_vmem(1)[0],
+        out_shape=jax.ShapeDtypeStruct((candidates.shape[0], LANES), jnp.float32),
+        compiler_params=pltpu.CompilerParams(vmem_limit_bytes=VMEM),
+        name="kept_tiles",
+    )(candidates)
+
+
+def finish_kernel(layers, kept, *refs):
+    parts, out = refs[:-1], refs[-1]
+    for tile in range(out.shape[1] // TILE):
         columns = slice(tile * TILE, (tile + 1) * TILE)
-        out[:, columns] = jnp.where(hit > 0.0, scaled[:, columns], 0.0).astype(out.dtype)
-
-
-def finish_kernel(layers, candidates, *refs):
-    parts, out = refs[:-1], refs[-1]
-    total = parts[0][...].astype(jnp.float32)
-    for part in parts[1:]:
-        total = total + part[...].astype(jnp.float32)
-    write_rows(total, layers, candidates[...], out)
-
-
-def finish(parts, candidates, layers):
+        total = parts[0][:, columns].astype(jnp.float32)
+        for part in parts[1:]:
+            total = total + part[:, columns].astype(jnp.float32)
+        scaled = total / jnp.sqrt(jnp.float32(layers))
+        out[:, columns] = jnp.where(kept[:, tile : tile + 1] > 0.0, scaled, 0.0).astype(out.dtype)
+
+
+def finish(parts, kept, layers):
     return pl.pallas_call(
         functools.partial(finish_kernel, layers),
         in_specs=in_vmem(1 + len(parts)),
@@ -261,7 +271,7 @@
         out_shape=jax.ShapeDtypeStruct(parts[0].shape, jnp.bfloat16),
         compiler_params=pltpu.CompilerParams(vmem_limit_bytes=VMEM),
         name="finish",
-    )(candidates, *parts)
+    )(kept, *parts)
 
 
 def permuted(value, axis, target_of):
@@ -275,34 +285,34 @@
 
 def on_line(own, store, candidates, layers):
     far = [swapped(half, "blk", 2) for half in own]
-    whole = jnp.concatenate(own, axis=1)
-    near = swapped(whole, "blk", 1)
-    own_scores = score_own(whole, store)
-    far[0], own_scores = lax.optimization_barrier((far[0], own_scores))
+    near = [swapped(half, "blk", 1) for half in own]
+    candidates, store, own[1] = lax.optimization_barrier((candidates, store, own[1]))
+    kept, store = kept_tiles(candidates, store.shape[1]), fetch(store)
+    far[0], kept, store = lax.optimization_barrier((far[0], kept, store))
     last = [swapped(half, "blk", 1) for half in far]
-    low_scores = score_low(near, far[0], last[0], store)
-    parts = score_high(near, far[1], last[1], store, own_scores, low_scores)
+    low, high = zip(own, near, far, last)
+    parts = score_high(high, store, score_low(low, store))
     received = {mask: swapped(parts[mask], "layer", mask) for mask in (3, 2, 1)}
-    return finish([parts[0]] + [received[mask] for mask in (1, 2, 3)], candidates, layers)
+    return finish([parts[0]] + [received[mask] for mask in (1, 2, 3)], kept, layers)
 
 
 def on_ring(own, store, candidates, layers):
     count = lax.axis_size("blk")
     moving = jnp.concatenate(own, axis=1)
     rows = moving.shape[0]
-    slots = [score_own(moving, store)]
+    slots = [score_low([moving], store)]
     for _ in range(count - 1):
         moving = permuted(moving, "blk", lambda source: source + 1)
-        slots.append(score_own(moving, store))
+        slots.append(score_low([moving], store))
     turns = lax.rem(lax.axis_index("blk") - jnp.arange(count) + count, count)
     total = jnp.stack(slots)[turns].reshape(layers, count * rows // layers, store.shape[1])
     parts = lax.all_to_all(total.astype(jnp.bfloat16), "layer", 0, 0)
-    return finish([parts[layer] for layer in range(layers)], candidates, layers)
+    return finish([parts[layer] for layer in range(layers)], kept_tiles(candidates, store.shape[1]), layers)
 
 
 def per_device(queries, store, left_factor, right_factor, candidates):
     layers, count = lax.axis_size("layer"), lax.axis_size("blk")
-    own = condition(queries, left_factor, right_factor)
+    own = list(condition(queries, left_factor, right_factor))
     way = on_line if layers == 4 and count == 4 else on_ring
     return way(own, store, candidates, layers)
 

time: 33.6 us -> 37.2 us (1.11)
  local copies, waits for them, and re-layouts: 0.1 us -> 6.68 us
  waiting for transfers between devices: 11.3 us -> 8.87 us
  Pallas kernels: 11.6 us -> 10.7 us
    unnamed x6, local copies, waits for them, and re-layouts: 0.09 us -> 6.6 us
    ppermute x8 -> x9, waiting for transfers between devices: 11.3 us -> 8.87 us  [permuted(): lax.ppermute(value, axis, [(source, target_of(source) % count) for source...]
    pallas_call x3 -> x4, Pallas kernels: 8.51 us -> 7.75 us  [the longest x1 3.5 us: fetch(): pl.pallas_call(fetch_kernel, in_specs=[pl.BlockSpec(memory_space=pltpu.HB...]
    ppermute x8 -> x9, starting transfers between devices: 10.4 us -> 10.7 us  [permuted(): lax.ppermute(value, axis, [(source, target_of(source) % count) for source...]
  transfers between devices with their start and end apart: 8 -> 9, of which waited for: 5 -> 5; matrix products, arithmetic and copies ran while one was open for 0% -> 0% of each run, Pallas kernels for 19% -> 15%
where the time goes in v6:
time: 37.2 us; the launch traced here: 37 us
  Pallas kernels  10.7 us (29%)
  starting transfers between devices  10.7 us (29%)
  waiting for transfers between devices  8.87 us (24%)
  local copies, waits for them, and re-layouts  6.68 us (18%)
    ppermute x9, starting transfers between devices, permuted(): lax.ppermute(value, axis, [(source, target_of(source) % count) for source...  10.7 us
    ppermute x9, waiting for transfers between devices, permuted(): lax.ppermute(value, axis, [(source, target_of(source) % count) for source...  8.87 us
    unnamed x6, local copies, waits for them, and re-layouts  6.6 us
    pallas_call x1, Pallas kernels, fetch(): pl.pallas_call(fetch_kernel, in_specs=[pl.BlockSpec(memory_space=pltpu.HB...  3.5 us
    pallas_call x1, Pallas kernels, condition(): pl.pallas_call(condition_kernel, in_specs=[pl.BlockSpec(memory_space=pltp...  2.18 us
    pallas_call x1, Pallas kernels, score_high(): pl.pallas_call(functools.partial(high_kernel, store.shape[2] - width, cou...  2.09 us
    pallas_call x1, Pallas kernels, score_low(): pl.pallas_call(low_kernel, in_specs=in_vmem(len(blocks) + 1), out_specs=i...  2.05 us
  transfers between devices with their start and end apart: 9, of which 5 were waited for; matrix products, arithmetic and copies ran while one was open for 0% of the time, Pallas kernels for 15%

profile of v6, /device:TPU:0, one launch (start us, length us, event | category | flops | bytes accessed | tf_op | source)
XLA Modules:
  0.0 37.0 jit_solution(10861858759042698979)
XLA Ops:
  0.0 2.2 %condition.1 = (bf16[32,2048]{1,0:T(8,128)(2,1)S(1)}, bf16[32,2048]{1,0:T(8,128)(2,1)S(1)}) custom-call(bf16[1,32,4096]{2,1,0:T(8,128)(2,1)} %queries_in.1, f32[1,64,64]{2,1,0:T(8,128)} %left_in.1, f32[1,64,64]{2,1,0:T(8,128)} %right_in.1), custom_call_target="tpu_custom_call" | custom-call | flops 536870912 | bytes 524288 | tf_op jit(solution)/shard_map/condition/pallas_call | solution.py:109
  2.2 4.1 %collective-permute-start = (bf16[32,2048]{1,0:T(8,128)(2,1)S(1)}, bf16[32,2048]{1,0:T(8,128)(2,1)S(1)}, u32[]{:S(2)}, u32[]{:S(2)}) collective-permute-start(bf16[32,2048]{1,0:T(8,128)(2,1)S(1)} %get-tuple-element.17.refs_0_), channel_id=1, source_target_pairs={{0,2},{1,3},{2,0},{3,1},{4,6},{5,7},{6,4},{7,5},{8,10},{9,11},{10,... | collective-permute-start | bytes 393224 | tf_op jit(solution)/shard_map/ppermute | solution.py:279
  6.3 0.1 collective-permute-start.2
  6.4 1.8 %collective-permute-start.4 = (bf16[32,2048]{1,0:T(8,128)(2,1)S(1)}, bf16[32,2048]{1,0:T(8,128)(2,1)S(1)}, u32[]{:S(2)}, u32[]{:S(2)}) collective-permute-start(bf16[32,2048]{1,0:T(8,128)(2,1)S(1)} %get-tuple-element.17.refs_0_), channel_id=1, source_target_pairs={{0,1},{1,0},{2,3},{3,2},{4,5},{5,4},{6,7},{7,6},{8,9},{9,8},{10,11... | collective-permute-start | bytes 393224 | tf_op jit(solution)/shard_map/ppermute | solution.py:279
  8.2 3.5 %fetch.1.refs_4_ = bf16[1,1024,4096]{2,1,0:T(8,128)(2,1)S(1)} custom-call(bf16[1,1024,4096]{2,1,0:T(8,128)(2,1)} %far_store), custom_call_target="tpu_custom_call" | custom-call | bytes 16777216 | tf_op jit(solution)/shard_map/fetch/pallas_call | solution.py:156
  11.7 3.2 %copy-done = bf16[1,1024,4096]{2,1,0:T(8,128)(2,1)} copy-done((bf16[1,1024,4096]{2,1,0:T(8,128)(2,1)}, bf16[1,1024,4096]{2,1,0:T(8,128)(2,1)S(1)}, u32[]{:S(2)}) %copy-start) | copy-done | bytes 8388632
  14.9 0.1 copy.6.candidates
  15.0 0.1 kept_tiles.1.kept
  15.1 1.1 %collective-permute-done.refs_2_ = bf16[32,2048]{1,0:T(8,128)(2,1)S(1)} collective-permute-done((bf16[32,2048]{1,0:T(8,128)(2,1)S(1)}, bf16[32,2048]{1,0:T(8,128)(2,1)S(1)}, u32[]{:S(2)}, u32[]{:S(2)}) %collective-permute-start) | collective-permute-done | bytes 131104 | tf_op jit(solution)/shard_map/ppermute | solution.py:279
  16.2 0.0 collective-permute-start.5
  16.2 2.0 %collective-permute-start.1 = (bf16[32,2048]{1,0:T(8,128)(2,1)S(1)}, bf16[32,2048]{1,0:T(8,128)(2,1)S(1)}, u32[]{:S(2)}, u32[]{:S(2)}) collective-permute-start(bf16[32,2048]{1,0:T(8,128)(2,1)S(1)} %get-tuple-element.22.refs_0_), channel_id=1, source_target_pairs={{0,1},{1,0},{2,3},{3,2},{4,5},{5,4},{6,7},{7,6},{8,9},{9,8},{10,11... | collective-permute-start | bytes 393224 | tf_op jit(solution)/shard_map/ppermute | solution.py:279
  18.3 0.1 collective-permute-done.2.refs_2_
  18.3 0.6 %collective-permute-start.3 = (bf16[32,2048]{1,0:T(8,128)(2,1)S(1)}, bf16[32,2048]{1,0:T(8,128)(2,1)S(1)}, u32[]{:S(2)}, u32[]{:S(2)}) collective-permute-start(bf16[32,2048]{1,0:T(8,128)(2,1)S(1)} %collective-permute-done.2.refs_2_), channel_id=1, source_target_pairs={{0,1},{1,0},{2,3},{3,2},{4,5},{5,4},{6,7},{7,6},{8,9},{9,8},{10,11... | collective-permute-start | bytes 393224 | tf_op jit(solution)/shard_map/ppermute | solution.py:279
  18.9 3.7 %collective-permute-done.5.refs_3_ = bf16[32,2048]{1,0:T(8,128)(2,1)S(1)} collective-permute-done((bf16[32,2048]{1,0:T(8,128)(2,1)S(1)}, bf16[32,2048]{1,0:T(8,128)(2,1)S(1)}, u32[]{:S(2)}, u32[]{:S(2)}) %collective-permute-start.5) | collective-permute-done | bytes 131104 | tf_op jit(solution)/shard_map/ppermute | solution.py:279
  22.7 3.4 %copy-done.1 = bf16[1,1024,4096]{2,1,0:T(8,128)(2,1)S(1)} copy-done((bf16[1,1024,4096]{2,1,0:T(8,128)(2,1)S(1)}, bf16[1,1024,4096]{2,1,0:T(8,128)(2,1)}, u32[]{:S(2)}) %copy-start.1) | copy-done | bytes 8388632
  26.1 2.1 %score_low.1.refs_5_ = f32[128,1024]{1,0:T(8,128)S(1)} custom-call(bf16[32,2048]{1,0:T(8,128)(2,1)S(1)} %get-tuple-element.17.refs_0_, bf16[32,2048]{1,0:T(8,128)(2,1)S(1)} %collective-permute-done.4.refs_1_, bf16[32,2048]{1,0:T(8,128)(2,1)S(1)} %collective-permute-done.refs_2_, bf16[32,2048]{1,0:T(8,128)(2,1)S(1)} %collective-permute-done.5.refs_3_, ...), custom_call_target="tpu_custom_call" | custom-call | flops 536870912 | bytes 4194304 | tf_op jit(solution)/shard_map/score_low/pallas_call | solution.py:190
  28.1 0.0 collective-permute-done.3.refs_3_
  28.1 2.1 %score_high.1 = (f32[32,1024]{1,0:T(8,128)S(1)}, bf16[32,1024]{1,0:T(8,128)(2,1)S(1)}, bf16[32,1024]{1,0:T(8,128)(2,1)S(1)}, bf16[32,1024]{1,0:T(8,128)(2,1)S(1)}) custom-call(bf16[32,2048]{1,0:T(8,128)(2,1)S(1)} %get-tuple-element.22.refs_0_, bf16[32,2048]{1,0:T(8,128)(2,1)S(1)} %collective-permute-done.1.refs_1_, ...), custom_call_target="tpu_custom_call" | custom-call | flops 536870912 | bytes 4194304 | tf_op jit(solution)/shard_map/score_high/pallas_call | solution.py:219
  30.2 0.1 collective-permute-start.6
  30.3 1.9 %collective-permute-start.7 = (bf16[32,1024]{1,0:T(8,128)(2,1)S(1)}, bf16[32,1024]{1,0:T(8,128)(2,1)S(1)}, u32[]{:S(2)}, u32[]{:S(2)}) collective-permute-start(bf16[32,1024]{1,0:T(8,128)(2,1)S(1)} %get-tuple-element.27), channel_id=1, source_target_pairs={{0,8},{4,12},{8,0},{12,4},{1,9},{5,13},{9,1},{13,5},{2,10},{6,14},... | collective-permute-start | bytes 196616 | tf_op jit(solution)/shard_map/ppermute | solution.py:279
  32.2 0.1 collective-permute-start.8
  32.3 2.6 %collective-permute-done.7.refs_2_ = bf16[32,1024]{1,0:T(8,128)(2,1)S(1)} collective-permute-done((bf16[32,1024]{1,0:T(8,128)(2,1)S(1)}, bf16[32,1024]{1,0:T(8,128)(2,1)S(1)}, u32[]{:S(2)}, u32[]{:S(2)}) %collective-permute-start.7) | collective-permute-done | bytes 65568 | tf_op jit(solution)/shard_map/ppermute | solution.py:279
  34.9 1.4 %collective-permute-done.8.refs_3_ = bf16[32,1024]{1,0:T(8,128)(2,1)S(1)} collective-permute-done((bf16[32,1024]{1,0:T(8,128)(2,1)S(1)}, bf16[32,1024]{1,0:T(8,128)(2,1)S(1)}, u32[]{:S(2)}, u32[]{:S(2)}) %collective-permute-start.8) | collective-permute-done | bytes 65568 | tf_op jit(solution)/shard_map/ppermute | solution.py:279
  36.3 0.7 %finish.1 = bf16[32,1024]{1,0:T(8,128)(2,1)} custom-call(f32[32,128]{1,0:T(8,128)S(1)} %kept_tiles.1.kept, f32[32,1024]{1,0:T(8,128)S(1)} %get-tuple-element.25.refs_0_, bf16[32,1024]{1,0:T(8,128)(2,1)S(1)} %collective-permute-done.6.refs_1_, bf16[32,1024]{1,0:T(8,128)(2,1)S(1)} %collective-permute-done.7.refs_2_, ...), custom_call_target="tpu_custom_call" | custom-call | tf_op jit(solution)/shard_map/finish/pallas_call | solution.py:267
  (7 shorter events, 0.0 us)
Async XLA Ops:
  2.2 14.0 %collective-permute-start = (bf16[32,2048]{1,0:T(8,128)(2,1)S(1)}, bf16[32,2048]{1,0:T(8,128)(2,1)S(1)}, u32[]{:S(2)}, u32[]{:S(2)}) collective-permute-start(bf16[32,2048]{1,0:T(8,128)(2,1)S(1)} %get-tuple-element.17.refs_0_), channel_id=1, source_target_pairs={{0,2},{1,3},{2,0},{3,1},{4,6},{5,7},{6,4},{7,5},{8,10},{9,11},{10,... | collective-permute-start | bytes 393224 | tf_op jit(solution)/shard_map/ppermute | solution.py:279
  6.3 8.7 %copy-start.2 = (s32[32,16]{0,1:T(8,128)S(1)}, s32[32,16]{0,1:T(8,128)}, u32[]{:S(2)}) copy-start(s32[32,16]{0,1:T(8,128)} %param.9) | copy-start | bytes 6148
  6.3 12.0 %collective-permute-start.2 = (bf16[32,2048]{1,0:T(8,128)(2,1)S(1)}, bf16[32,2048]{1,0:T(8,128)(2,1)S(1)}, u32[]{:S(2)}, u32[]{:S(2)}) collective-permute-start(bf16[32,2048]{1,0:T(8,128)(2,1)S(1)} %get-tuple-element.22.refs_0_), channel_id=1, source_target_pairs={{0,2},{1,3},{2,0},{3,1},{4,6},{5,7},{6,4},{7,5},{8,10},{9,11},{10,... | collective-permute-start | bytes 393224 | tf_op jit(solution)/shard_map/ppermute | solution.py:279
  6.4 12.6 %collective-permute-start.4 = (bf16[32,2048]{1,0:T(8,128)(2,1)S(1)}, bf16[32,2048]{1,0:T(8,128)(2,1)S(1)}, u32[]{:S(2)}, u32[]{:S(2)}) collective-permute-start(bf16[32,2048]{1,0:T(8,128)(2,1)S(1)} %get-tuple-element.17.refs_0_), channel_id=1, source_target_pairs={{0,1},{1,0},{2,3},{3,2},{4,5},{5,4},{6,7},{7,6},{8,9},{9,8},{10,11... | collective-permute-start | bytes 393224 | tf_op jit(solution)/shard_map/ppermute | solution.py:279
  11.7 3.2 %copy-start = (bf16[1,1024,4096]{2,1,0:T(8,128)(2,1)}, bf16[1,1024,4096]{2,1,0:T(8,128)(2,1)S(1)}, u32[]{:S(2)}) copy-start(bf16[1,1024,4096]{2,1,0:T(8,128)(2,1)S(1)} %fetch.1.refs_4_) | copy-start | bytes 25165828
  16.2 6.4 %collective-permute-start.5 = (bf16[32,2048]{1,0:T(8,128)(2,1)S(1)}, bf16[32,2048]{1,0:T(8,128)(2,1)S(1)}, u32[]{:S(2)}, u32[]{:S(2)}) collective-permute-start(bf16[32,2048]{1,0:T(8,128)(2,1)S(1)} %collective-permute-done.refs_2_), channel_id=1, source_target_pairs={{0,1},{1,0},{2,3},{3,2},{4,5},{5,4},{6,7},{7,6},{8,9},{9,8},{10,11... | collective-permute-start | bytes 393224 | tf_op jit(solution)/shard_map/ppermute | solution.py:279
  16.2 11.9 %collective-permute-start.1 = (bf16[32,2048]{1,0:T(8,128)(2,1)S(1)}, bf16[32,2048]{1,0:T(8,128)(2,1)S(1)}, u32[]{:S(2)}, u32[]{:S(2)}) collective-permute-start(bf16[32,2048]{1,0:T(8,128)(2,1)S(1)} %get-tuple-element.22.refs_0_), channel_id=1, source_target_pairs={{0,1},{1,0},{2,3},{3,2},{4,5},{5,4},{6,7},{7,6},{8,9},{9,8},{10,11... | collective-permute-start | bytes 393224 | tf_op jit(solution)/shard_map/ppermute | solution.py:279
  18.3 9.8 %collective-permute-start.3 = (bf16[32,2048]{1,0:T(8,128)(2,1)S(1)}, bf16[32,2048]{1,0:T(8,128)(2,1)S(1)}, u32[]{:S(2)}, u32[]{:S(2)}) collective-permute-start(bf16[32,2048]{1,0:T(8,128)(2,1)S(1)} %collective-permute-done.2.refs_2_), channel_id=1, source_target_pairs={{0,1},{1,0},{2,3},{3,2},{4,5},{5,4},{6,7},{7,6},{8,9},{9,8},{10,11... | collective-permute-start | bytes 393224 | tf_op jit(solution)/shard_map/ppermute | solution.py:279
  22.7 3.4 %copy-start.1 = (bf16[1,1024,4096]{2,1,0:T(8,128)(2,1)S(1)}, bf16[1,1024,4096]{2,1,0:T(8,128)(2,1)}, u32[]{:S(2)}) copy-start(bf16[1,1024,4096]{2,1,0:T(8,128)(2,1)} %copy-done) | copy-start | bytes 25165828
  30.2 2.1 %collective-permute-start.6 = (bf16[32,1024]{1,0:T(8,128)(2,1)S(1)}, bf16[32,1024]{1,0:T(8,128)(2,1)S(1)}, u32[]{:S(2)}, u32[]{:S(2)}) collective-permute-start(bf16[32,1024]{1,0:T(8,128)(2,1)S(1)} %get-tuple-element.26), channel_id=1, source_target_pairs={{0,4},{4,0},{8,12},{12,8},{1,5},{5,1},{9,13},{13,9},{2,6},{6,2},{1... | collective-permute-start | bytes 196616 | tf_op jit(solution)/shard_map/ppermute | solution.py:279
  30.3 4.6 %collective-permute-start.7 = (bf16[32,1024]{1,0:T(8,128)(2,1)S(1)}, bf16[32,1024]{1,0:T(8,128)(2,1)S(1)}, u32[]{:S(2)}, u32[]{:S(2)}) collective-permute-start(bf16[32,1024]{1,0:T(8,128)(2,1)S(1)} %get-tuple-element.27), channel_id=1, source_target_pairs={{0,8},{4,12},{8,0},{12,4},{1,9},{5,13},{9,1},{13,5},{2,10},{6,14},... | collective-permute-start | bytes 196616 | tf_op jit(solution)/shard_map/ppermute | solution.py:279
  32.2 4.0 %collective-permute-start.8 = (bf16[32,1024]{1,0:T(8,128)(2,1)S(1)}, bf16[32,1024]{1,0:T(8,128)(2,1)S(1)}, u32[]{:S(2)}, u32[]{:S(2)}) collective-permute-start(bf16[32,1024]{1,0:T(8,128)(2,1)S(1)} %get-tuple-element.28), channel_id=1, source_target_pairs={{0,12},{4,8},{8,4},{12,0},{1,13},{5,9},{9,5},{13,1},{2,14},{6,10},... | collective-permute-start | bytes 196616 | tf_op jit(solution)/shard_map/ppermute | solution.py:279

commit v7 on v6

--- a/solution.py
+++ b/solution.py
@@ -128,41 +128,46 @@
 STEP = 256
 
 
-def score_block(queries, store, first, write):
+def score_block(queries, store, write):
     turned = queries.T
-    width = queries.shape[1]
 
     def one(step, carry):
         place = pl.ds(pl.multiple_of(step * STEP, STEP), STEP)
-        value = dot(store[0, place, pl.ds(first, width)], turned)
-        write(place, value.T)
+        write(place, dot(store[place, :], turned).T)
         return carry
 
-    lax.fori_loop(0, store.shape[1] // STEP, one, 0)
+    lax.fori_loop(0, store.shape[0] // STEP, one, 0)
+
+
+def copies_of(far_store, first, store, semaphores):
+    copies = []
+    for step in range(store.shape[0] // STEP):
+        place = pl.ds(step * STEP, STEP)
+        source = far_store.at[0, place, pl.ds(first, store.shape[1])]
+        copies.append(pltpu.make_async_copy(source, store.at[place], semaphores.at[step]))
+    return copies
 
 
 def fetch_kernel(far_store, store, semaphores):
-    copies = []
-    for step in range(store.shape[1] // STEP):
-        place = pl.ds(step * STEP, STEP)
-        copies.append(pltpu.make_async_copy(far_store.at[0, place], store.at[0, place], semaphores.at[step]))
+    copies = copies_of(far_store, 0, store, semaphores)
     for copy in copies:
         copy.start()
     for copy in copies:
         copy.wait()
 
 
-def fetch(store):
+def fetch_low(store, width):
+    examples = store.shape[1]
     return pl.pallas_call(
         fetch_kernel,
         in_specs=[pl.BlockSpec(memory_space=pltpu.HBM)],
         out_specs=in_vmem(1)[0],
-        out_shape=jax.ShapeDtypeStruct(store.shape, store.dtype),
-        scratch_shapes=[pltpu.SemaphoreType.DMA((store.shape[1] // STEP,))],
-        compiler_params=pltpu.CompilerParams(vmem_limit_bytes=VMEM),
-        cost_estimate=pl.CostEstimate(flops=0, bytes_accessed=2 * store.size * 2, transcendentals=0),
-        name="fetch",
-    )(pltpu.with_memory_space_constraint(store, pltpu.HBM))
+        out_shape=jax.ShapeDtypeStruct((examples, width), store.dtype),
+        scratch_shapes=[pltpu.SemaphoreType.DMA((examples // STEP,))],
+        compiler_params=pltpu.CompilerParams(vmem_limit_bytes=VMEM),
+        cost_estimate=pl.CostEstimate(flops=0, bytes_accessed=4 * examples * width, transcendentals=0),
+        name="fetch_low",
+    )(store)
 
 
 def score_cost(count, width, examples):
@@ -175,36 +180,46 @@
     return jnp.concatenate([block[...] for block in blocks], axis=0)
 
 
-def low_kernel(*refs):
-    blocks, (store, out) = refs[:-2], refs[-2:]
+def low_kernel(count, *refs):
+    blocks, (low_store, far_store, out, high_store, semaphores) = refs[:count], refs[count:]
+    copies = copies_of(far_store, low_store.shape[1], high_store, semaphores)
+    for copy in copies:
+        copy.start()
 
     def write(place, value):
         out[:, place] = value
 
-    score_block(stacked(blocks), store, 0, write)
-
-
-def score_low(blocks, store):
-    count, width = sum(block.shape[0] for block in blocks), blocks[0].shape[1]
-    examples = store.shape[1]
-    return pl.pallas_call(
-        low_kernel,
-        in_specs=in_vmem(len(blocks) + 1),
-        out_specs=in_vmem(1)[0],
-        out_shape=jax.ShapeDtypeStruct((count, examples), jnp.float32),
+    score_block(stacked(blocks), low_store, write)
+    for copy in copies:
+        copy.wait()
+
+
+def score_low(blocks, low_store, far_store):
+    count = sum(block.shape[0] for block in blocks)
+    examples, width = low_store.shape
+    rest = far_store.shape[2] - width
+    return pl.pallas_call(
+        functools.partial(low_kernel, len(blocks)),
+        in_specs=in_vmem(len(blocks) + 1) + [pl.BlockSpec(memory_space=pltpu.HBM)],
+        out_specs=in_vmem(2),
+        out_shape=[
+            jax.ShapeDtypeStruct((count, examples), jnp.float32),
+            jax.ShapeDtypeStruct((examples, rest), far_store.dtype),
+        ],
+        scratch_shapes=[pltpu.SemaphoreType.DMA((examples // STEP,))],
         compiler_params=pltpu.CompilerParams(vmem_limit_bytes=VMEM),
         cost_estimate=score_cost(count, width, examples),
         name="score_low",
-    )(*blocks, store)
-
-
-def high_kernel(first, count, *refs):
+    )(*blocks, low_store, far_store)
+
+
+def high_kernel(count, *refs):
     blocks, (store, low), outs, total = refs[:count], refs[count : count + 2], refs[count + 2 : -1], refs[-1]
 
     def write(place, value):
         total[:, place] = value + low[:, place]
 
-    score_block(stacked(blocks), store, first, write)
+    score_block(stacked(blocks), store, write)
     rows = blocks[0].shape[0]
     home = lax.bitwise_xor(lax.axis_index("blk"), lax.axis_index("layer"))
     for mask, out in enumerate(outs):
@@ -215,9 +230,9 @@
 def score_high(blocks, store, low):
     rows, width = blocks[0].shape
     count = len(blocks)
-    examples = store.shape[1]
-    return pl.pallas_call(
-        functools.partial(high_kernel, store.shape[2] - width, count),
+    examples = store.shape[0]
+    return pl.pallas_call(
+        functools.partial(high_kernel, count),
         in_specs=in_vmem(count + 2),
         out_specs=in_vmem(count),
         out_shape=[
@@ -286,12 +301,15 @@
 def on_line(own, store, candidates, layers):
     far = [swapped(half, "blk", 2) for half in own]
     near = [swapped(half, "blk", 1) for half in own]
-    candidates, store, own[1] = lax.optimization_barrier((candidates, store, own[1]))
-    kept, store = kept_tiles(candidates, store.shape[1]), fetch(store)
-    far[0], kept, store = lax.optimization_barrier((far[0], kept, store))
+    candidates, own[1] = lax.optimization_barrier((candidates, own[1]))
+    kept = kept_tiles(candidates, store.shape[1])
+    far[0], kept = lax.optimization_barrier((far[0], kept))
     last = [swapped(half, "blk", 1) for half in far]
+    store = pltpu.with_memory_space_constraint(store, pltpu.HBM)
+    near[0], far[1], store = lax.optimization_barrier((near[0], far[1], store))
     low, high = zip(own, near, far, last)
-    parts = score_high(high, store, score_low(low, store))
+    low_scores, high_store = score_low(low, fetch_low(store, own[0].shape[1]), store)
+    parts = score_high(high, high_store, low_scores)
     received = {mask: swapped(parts[mask], "layer", mask) for mask in (3, 2, 1)}
     return finish([parts[0]] + [received[mask] for mask in (1, 2, 3)], kept, layers)
 
@@ -300,10 +318,14 @@
     count = lax.axis_size("blk")
     moving = jnp.concatenate(own, axis=1)
     rows = moving.shape[0]
-    slots = [score_low([moving], store)]
+
+    def scores():
+        return lax.dot_general(moving, store[0], (((1,), (1,)), ((), ())), preferred_element_type=jnp.float32)
+
+    slots = [scores()]
     for _ in range(count - 1):
         moving = permuted(moving, "blk", lambda source: source + 1)
-        slots.append(score_low([moving], store))
+        slots.append(scores())
     turns = lax.rem(lax.axis_index("blk") - jnp.arange(count) + count, count)
     total = jnp.stack(slots)[turns].reshape(layers, count * rows // layers, store.shape[1])
     parts = lax.all_to_all(total.astype(jnp.bfloat16), "layer", 0, 0)

time: 37.2 us -> 35.4 us (0.952)
  local copies, waits for them, and re-layouts: 6.68 us -> 0.77 us
  waiting for transfers between devices: 8.87 us -> 14.3 us
  Pallas kernels: 10.7 us -> 9.54 us
    unnamed x6 -> x0, local copies, waits for them, and re-layouts: 6.6 us -> none
    ppermute x9, waiting for transfers between devices: 8.87 us -> 14.3 us  [permuted(): lax.ppermute(value, axis, [(source, target_of(source) % count) for source...]
    pallas_call x3, Pallas kernels: 7.65 us -> 6.51 us  [the longest x1 2.21 us: score_low(): pl.pallas_call(functools.partial(low_kernel, len(blocks)), in_specs=in_vm...]
    optimization_barrier x1, local copies, waits for them, and re-layouts: 0.07 us -> 0.77 us  [on_line(): candidates, own[1] = lax.optimization_barrier((candidates, own[1]))]
  transfers between devices with their start and end apart: 9 -> 9, of which waited for: 5 -> 7; matrix products, arithmetic and copies ran while one was open for 0% -> 2% of each run, Pallas kernels for 15% -> 13%
where the time goes in v7:
time: 35.4 us; the launch traced here: 35.2 us
  waiting for transfers between devices  14.3 us (40%)
  starting transfers between devices  10.6 us (30%)
  Pallas kernels  9.54 us (27%)
  local copies, waits for them, and re-layouts  0.77 us (2%)
    ppermute x9, waiting for transfers between devices, permuted(): lax.ppermute(value, axis, [(source, target_of(source) % count) for source...  14.3 us
    ppermute x9, starting transfers between devices, permuted(): lax.ppermute(value, axis, [(source, target_of(source) % count) for source...  10.6 us
    pallas_call x1, Pallas kernels, score_low(): pl.pallas_call(functools.partial(low_kernel, len(blocks)), in_specs=in_vm...  2.21 us
    pallas_call x1, Pallas kernels, fetch_low(): pl.pallas_call(fetch_kernel, in_specs=[pl.BlockSpec(memory_space=pltpu.HB...  2.21 us
    pallas_call x1, Pallas kernels, condition(): pl.pallas_call(condition_kernel, in_specs=[pl.BlockSpec(memory_space=pltp...  2.18 us
    pallas_call x1, Pallas kernels, score_high(): pl.pallas_call(functools.partial(high_kernel, count), in_specs=in_vmem(co...  2.1 us
    optimization_barrier x1, local copies, waits for them, and re-layouts, on_line(): candidates, own[1] = lax.optimization_barrier((candidates, own[1]))  0.77 us
    pallas_call x1, Pallas kernels, finish(): pl.pallas_call(functools.partial(finish_kernel, layers), in_specs=in_vmem...  0.74 us
  transfers between devices with their start and end apart: 9, of which 7 were waited for; matrix products, arithmetic and copies ran while one was open for 2% of the time, Pallas kernels for 13%

profile of v7, /device:TPU:0, one launch (start us, length us, event | category | flops | bytes accessed | tf_op | source)
XLA Modules:
  0.0 35.2 jit_solution(544151069820338643)
XLA Ops:
  0.0 2.2 %condition.1 = (bf16[32,2048]{1,0:T(8,128)(2,1)S(1)}, bf16[32,2048]{1,0:T(8,128)(2,1)S(1)}) custom-call(bf16[1,32,4096]{2,1,0:T(8,128)(2,1)} %queries_in.1, f32[1,64,64]{2,1,0:T(8,128)} %left_in.1, f32[1,64,64]{2,1,0:T(8,128)} %right_in.1), custom_call_target="tpu_custom_call" | custom-call | flops 536870912 | bytes 524288 | tf_op jit(solution)/shard_map/condition/pallas_call | solution.py:109
  2.2 4.1 %collective-permute-start = (bf16[32,2048]{1,0:T(8,128)(2,1)S(1)}, bf16[32,2048]{1,0:T(8,128)(2,1)S(1)}, u32[]{:S(2)}, u32[]{:S(2)}) collective-permute-start(bf16[32,2048]{1,0:T(8,128)(2,1)S(1)} %get-tuple-element.20.refs_0_), channel_id=1, source_target_pairs={{0,2},{1,3},{2,0},{3,1},{4,6},{5,7},{6,4},{7,5},{8,10},{9,11},{10,... | collective-permute-start | bytes 393224 | tf_op jit(solution)/shard_map/ppermute | solution.py:294
  6.3 0.1 collective-permute-start.3
  6.4 1.8 %collective-permute-start.2 = (bf16[32,2048]{1,0:T(8,128)(2,1)S(1)}, bf16[32,2048]{1,0:T(8,128)(2,1)S(1)}, u32[]{:S(2)}, u32[]{:S(2)}) collective-permute-start(bf16[32,2048]{1,0:T(8,128)(2,1)S(1)} %get-tuple-element.20.refs_0_), channel_id=1, source_target_pairs={{0,1},{1,0},{2,3},{3,2},{4,5},{5,4},{6,7},{7,6},{8,9},{9,8},{10,11... | collective-permute-start | bytes 393224 | tf_op jit(solution)/shard_map/ppermute | solution.py:294
  8.2 0.8 %copy.6.candidates = s32[32,16]{1,0:T(8,128)S(1)} copy(s32[32,16]{0,1:T(8,128)} %param.9) | data formatting | bytes 4096 | tf_op jit(solution)/shard_map/optimization_barrier | solution.py:304
  9.0 0.1 kept_tiles.1.kept
  9.1 7.1 %collective-permute-done.refs_2_ = bf16[32,2048]{1,0:T(8,128)(2,1)S(1)} collective-permute-done((bf16[32,2048]{1,0:T(8,128)(2,1)S(1)}, bf16[32,2048]{1,0:T(8,128)(2,1)S(1)}, u32[]{:S(2)}, u32[]{:S(2)}) %collective-permute-start) | collective-permute-done | bytes 131104 | tf_op jit(solution)/shard_map/ppermute | solution.py:294
  16.2 2.0 %collective-permute-start.1 = (bf16[32,2048]{1,0:T(8,128)(2,1)S(1)}, bf16[32,2048]{1,0:T(8,128)(2,1)S(1)}, u32[]{:S(2)}, u32[]{:S(2)}) collective-permute-start(bf16[32,2048]{1,0:T(8,128)(2,1)S(1)} %get-tuple-element.24.refs_0_), channel_id=1, source_target_pairs={{0,1},{1,0},{2,3},{3,2},{4,5},{5,4},{6,7},{7,6},{8,9},{9,8},{10,11... | collective-permute-start | bytes 393224 | tf_op jit(solution)/shard_map/ppermute | solution.py:294
  18.3 0.1 collective-permute-done.3.refs_2_
  18.3 0.6 %collective-permute-start.4 = (bf16[32,2048]{1,0:T(8,128)(2,1)S(1)}, bf16[32,2048]{1,0:T(8,128)(2,1)S(1)}, u32[]{:S(2)}, u32[]{:S(2)}) collective-permute-start(bf16[32,2048]{1,0:T(8,128)(2,1)S(1)} %collective-permute-done.3.refs_2_), channel_id=1, source_target_pairs={{0,1},{1,0},{2,3},{3,2},{4,5},{5,4},{6,7},{7,6},{8,9},{9,8},{10,11... | collective-permute-start | bytes 393224 | tf_op jit(solution)/shard_map/ppermute | solution.py:294
  18.9 0.0 collective-permute-done.2.refs_1_
  18.9 2.2 %fetch_low.1.refs_4_ = bf16[1024,2048]{1,0:T(8,128)(2,1)S(1)} custom-call(bf16[1,1024,4096]{2,1,0:T(8,128)(2,1)} %refs_5_), custom_call_target="tpu_custom_call" | custom-call | bytes 8388608 | tf_op jit(solution)/shard_map/fetch_low/pallas_call | solution.py:161
  21.2 1.5 %collective-permute-done.5.refs_3_ = bf16[32,2048]{1,0:T(8,128)(2,1)S(1)} collective-permute-done((bf16[32,2048]{1,0:T(8,128)(2,1)S(1)}, bf16[32,2048]{1,0:T(8,128)(2,1)S(1)}, u32[]{:S(2)}, u32[]{:S(2)}) %collective-permute-start.5) | collective-permute-done | bytes 131104 | tf_op jit(solution)/shard_map/ppermute | solution.py:294
  22.7 2.2 %score_low.1 = (f32[128,1024]{1,0:T(8,128)S(1)}, bf16[1024,2048]{1,0:T(8,128)(2,1)S(1)}) custom-call(bf16[32,2048]{1,0:T(8,128)(2,1)S(1)} %get-tuple-element.20.refs_0_, bf16[32,2048]{1,0:T(8,128)(2,1)S(1)} %collective-permute-done.2.refs_1_, bf16[32,2048]{1,0:T(8,128)(2,1)S(1)} %collective-permute-done.refs_2_, ...), custom_call_target="tpu_custom_call" | custom-call | flops 536870912 | bytes 4194304 | tf_op jit(solution)/shard_map/score_low/pallas_call | solution.py:201
  24.9 0.4 collective-permute-done.1.refs_1_
  25.2 1.4 %collective-permute-done.4.refs_3_ = bf16[32,2048]{1,0:T(8,128)(2,1)S(1)} collective-permute-done((bf16[32,2048]{1,0:T(8,128)(2,1)S(1)}, bf16[32,2048]{1,0:T(8,128)(2,1)S(1)}, u32[]{:S(2)}, u32[]{:S(2)}) %collective-permute-start.4) | collective-permute-done | bytes 131104 | tf_op jit(solution)/shard_map/ppermute | solution.py:294
  26.6 2.1 %score_high.1 = (f32[32,1024]{1,0:T(8,128)S(1)}, bf16[32,1024]{1,0:T(8,128)(2,1)S(1)}, bf16[32,1024]{1,0:T(8,128)(2,1)S(1)}, bf16[32,1024]{1,0:T(8,128)(2,1)S(1)}) custom-call(bf16[32,2048]{1,0:T(8,128)(2,1)S(1)} %get-tuple-element.24.refs_0_, bf16[32,2048]{1,0:T(8,128)(2,1)S(1)} %collective-permute-done.1.refs_1_, ...), custom_call_target="tpu_custom_call" | custom-call | flops 536870912 | bytes 4194304 | tf_op jit(solution)/shard_map/score_high/pallas_call | solution.py:234
  28.7 0.1 collective-permute-start.6
  28.8 1.6 %collective-permute-start.7 = (bf16[32,1024]{1,0:T(8,128)(2,1)S(1)}, bf16[32,1024]{1,0:T(8,128)(2,1)S(1)}, u32[]{:S(2)}, u32[]{:S(2)}) collective-permute-start(bf16[32,1024]{1,0:T(8,128)(2,1)S(1)} %get-tuple-element.33), channel_id=1, source_target_pairs={{0,8},{4,12},{8,0},{12,4},{1,9},{5,13},{9,1},{13,5},{2,10},{6,14},... | collective-permute-start | bytes 196616 | tf_op jit(solution)/shard_map/ppermute | solution.py:294
  30.4 0.3 collective-permute-start.8
  30.7 0.0 collective-permute-done.6.refs_1_
  30.7 2.6 %collective-permute-done.7.refs_2_ = bf16[32,1024]{1,0:T(8,128)(2,1)S(1)} collective-permute-done((bf16[32,1024]{1,0:T(8,128)(2,1)S(1)}, bf16[32,1024]{1,0:T(8,128)(2,1)S(1)}, u32[]{:S(2)}, u32[]{:S(2)}) %collective-permute-start.7) | collective-permute-done | bytes 65568 | tf_op jit(solution)/shard_map/ppermute | solution.py:294
  33.3 1.1 %collective-permute-done.8.refs_3_ = bf16[32,1024]{1,0:T(8,128)(2,1)S(1)} collective-permute-done((bf16[32,1024]{1,0:T(8,128)(2,1)S(1)}, bf16[32,1024]{1,0:T(8,128)(2,1)S(1)}, u32[]{:S(2)}, u32[]{:S(2)}) %collective-permute-start.8) | collective-permute-done | bytes 65568 | tf_op jit(solution)/shard_map/ppermute | solution.py:294
  34.5 0.7 %finish.1 = bf16[32,1024]{1,0:T(8,128)(2,1)} custom-call(f32[32,128]{1,0:T(8,128)S(1)} %kept_tiles.1.kept, f32[32,1024]{1,0:T(8,128)S(1)} %get-tuple-element.31.refs_0_, bf16[32,1024]{1,0:T(8,128)(2,1)S(1)} %collective-permute-done.6.refs_1_, bf16[32,1024]{1,0:T(8,128)(2,1)S(1)} %collective-permute-done.7.refs_2_, ...), custom_call_target="tpu_custom_call" | custom-call | tf_op jit(solution)/shard_map/finish/pallas_call | solution.py:282
  (1 shorter events, 0.0 us)
Async XLA Ops:
  2.2 14.0 %collective-permute-start = (bf16[32,2048]{1,0:T(8,128)(2,1)S(1)}, bf16[32,2048]{1,0:T(8,128)(2,1)S(1)}, u32[]{:S(2)}, u32[]{:S(2)}) collective-permute-start(bf16[32,2048]{1,0:T(8,128)(2,1)S(1)} %get-tuple-element.20.refs_0_), channel_id=1, source_target_pairs={{0,2},{1,3},{2,0},{3,1},{4,6},{5,7},{6,4},{7,5},{8,10},{9,11},{10,... | collective-permute-start | bytes 393224 | tf_op jit(solution)/shard_map/ppermute | solution.py:294
  6.3 12.0 %collective-permute-start.3 = (bf16[32,2048]{1,0:T(8,128)(2,1)S(1)}, bf16[32,2048]{1,0:T(8,128)(2,1)S(1)}, u32[]{:S(2)}, u32[]{:S(2)}) collective-permute-start(bf16[32,2048]{1,0:T(8,128)(2,1)S(1)} %get-tuple-element.24.refs_0_), channel_id=1, source_target_pairs={{0,2},{1,3},{2,0},{3,1},{4,6},{5,7},{6,4},{7,5},{8,10},{9,11},{10,... | collective-permute-start | bytes 393224 | tf_op jit(solution)/shard_map/ppermute | solution.py:294
  6.4 12.6 %collective-permute-start.2 = (bf16[32,2048]{1,0:T(8,128)(2,1)S(1)}, bf16[32,2048]{1,0:T(8,128)(2,1)S(1)}, u32[]{:S(2)}, u32[]{:S(2)}) collective-permute-start(bf16[32,2048]{1,0:T(8,128)(2,1)S(1)} %get-tuple-element.20.refs_0_), channel_id=1, source_target_pairs={{0,1},{1,0},{2,3},{3,2},{4,5},{5,4},{6,7},{7,6},{8,9},{9,8},{10,11... | collective-permute-start | bytes 393224 | tf_op jit(solution)/shard_map/ppermute | solution.py:294
  16.2 6.4 %collective-permute-start.5 = (bf16[32,2048]{1,0:T(8,128)(2,1)S(1)}, bf16[32,2048]{1,0:T(8,128)(2,1)S(1)}, u32[]{:S(2)}, u32[]{:S(2)}) collective-permute-start(bf16[32,2048]{1,0:T(8,128)(2,1)S(1)} %collective-permute-done.refs_2_), channel_id=1, source_target_pairs={{0,1},{1,0},{2,3},{3,2},{4,5},{5,4},{6,7},{7,6},{8,9},{9,8},{10,11... | collective-permute-start | bytes 393224 | tf_op jit(solution)/shard_map/ppermute | solution.py:294
  16.2 9.0 %collective-permute-start.1 = (bf16[32,2048]{1,0:T(8,128)(2,1)S(1)}, bf16[32,2048]{1,0:T(8,128)(2,1)S(1)}, u32[]{:S(2)}, u32[]{:S(2)}) collective-permute-start(bf16[32,2048]{1,0:T(8,128)(2,1)S(1)} %get-tuple-element.24.refs_0_), channel_id=1, source_target_pairs={{0,1},{1,0},{2,3},{3,2},{4,5},{5,4},{6,7},{7,6},{8,9},{9,8},{10,11... | collective-permute-start | bytes 393224 | tf_op jit(solution)/shard_map/ppermute | solution.py:294
  18.3 8.3 %collective-permute-start.4 = (bf16[32,2048]{1,0:T(8,128)(2,1)S(1)}, bf16[32,2048]{1,0:T(8,128)(2,1)S(1)}, u32[]{:S(2)}, u32[]{:S(2)}) collective-permute-start(bf16[32,2048]{1,0:T(8,128)(2,1)S(1)} %collective-permute-done.3.refs_2_), channel_id=1, source_target_pairs={{0,1},{1,0},{2,3},{3,2},{4,5},{5,4},{6,7},{7,6},{8,9},{9,8},{10,11... | collective-permute-start | bytes 393224 | tf_op jit(solution)/shard_map/ppermute | solution.py:294
  28.7 1.9 %collective-permute-start.6 = (bf16[32,1024]{1,0:T(8,128)(2,1)S(1)}, bf16[32,1024]{1,0:T(8,128)(2,1)S(1)}, u32[]{:S(2)}, u32[]{:S(2)}) collective-permute-start(bf16[32,1024]{1,0:T(8,128)(2,1)S(1)} %get-tuple-element.32), channel_id=1, source_target_pairs={{0,4},{4,0},{8,12},{12,8},{1,5},{5,1},{9,13},{13,9},{2,6},{6,2},{1... | collective-permute-start | bytes 196616 | tf_op jit(solution)/shard_map/ppermute | solution.py:294
  28.8 4.5 %collective-permute-start.7 = (bf16[32,1024]{1,0:T(8,128)(2,1)S(1)}, bf16[32,1024]{1,0:T(8,128)(2,1)S(1)}, u32[]{:S(2)}, u32[]{:S(2)}) collective-permute-start(bf16[32,1024]{1,0:T(8,128)(2,1)S(1)} %get-tuple-element.33), channel_id=1, source_target_pairs={{0,8},{4,12},{8,0},{12,4},{1,9},{5,13},{9,1},{13,5},{2,10},{6,14},... | collective-permute-start | bytes 196616 | tf_op jit(solution)/shard_map/ppermute | solution.py:294
  30.4 4.0 %collective-permute-start.8 = (bf16[32,1024]{1,0:T(8,128)(2,1)S(1)}, bf16[32,1024]{1,0:T(8,128)(2,1)S(1)}, u32[]{:S(2)}, u32[]{:S(2)}) collective-permute-start(bf16[32,1024]{1,0:T(8,128)(2,1)S(1)} %get-tuple-element.34), channel_id=1, source_target_pairs={{0,12},{4,8},{8,4},{12,0},{1,13},{5,9},{9,5},{13,1},{2,14},{6,10},... | collective-permute-start | bytes 196616 | tf_op jit(solution)/shard_map/ppermute | solution.py:294

commit v8 on v4

--- a/solution.py
+++ b/solution.py
@@ -128,19 +128,19 @@
 STEP = 256
 
 
-def score_block(queries, store, first, write, arrived=None):
+def score_block(queries, store, first, write, arrived=None, step_rows=STEP):
     turned = queries.T
     width = queries.shape[1]
 
     def one(step, carry):
-        place = pl.ds(pl.multiple_of(step * STEP, STEP), STEP)
+        place = pl.ds(pl.multiple_of(step * step_rows, step_rows), step_rows)
         if arrived is not None:
             arrived(step)
         value = dot(store[0, place, pl.ds(first, width)], turned)
         write(place, value.T)
         return carry
 
-    lax.fori_loop(0, store.shape[1] // STEP, one, 0)
+    lax.fori_loop(0, store.shape[1] // step_rows, one, 0)
 
 
 def own_kernel(queries, far_store, out, store, semaphores):
@@ -186,7 +186,7 @@
     def write(place, value):
         out[:, place] = value
 
-    score_block(three_blocks(near, far, last, 0), store, 0, write)
+    score_block(three_blocks(near, far, last, 0), store, 0, write, step_rows=store.shape[1])
 
 
 def score_low(near, far, last, store):
@@ -211,7 +211,7 @@
     def write(place, value):
         total[pl.ds(rows, 3 * rows), place] = value + low[:, place]
 
-    score_block(three_blocks(near, far, last, first), store, first, write)
+    score_block(three_blocks(near, far, last, first), store, first, write, step_rows=store.shape[1])
     home = lax.bitwise_xor(lax.axis_index("blk"), lax.axis_index("layer"))
     for mask, out in enumerate(outs):
         slot = lax.bitwise_xor(home, mask)

time: 33.6 us -> 32.3 us (0.961)
  Pallas kernels: 11.6 us -> 10.2 us
    pallas_call x1, Pallas kernels: 2.02 us -> 1.34 us  [score_high(): pl.pallas_call(functools.partial(high_kernel, near.shape[1] - width), in_...]
    pallas_call x1, Pallas kernels: 1.97 us -> 1.3 us  [score_low(): pl.pallas_call(low_kernel, in_specs=in_vmem(4), out_specs=in_vmem(1)[0],...]
  transfers between devices with their start and end apart: 8 -> 8, of which waited for: 5 -> 6; matrix products, arithmetic and copies ran while one was open for 0% -> 0% of each run, Pallas kernels for 19% -> 18%
where the time goes in v8:
time: 32.3 us; the launch traced here: 32.2 us
  waiting for transfers between devices  11.4 us (35%)
  starting transfers between devices  10.4 us (32%)
  Pallas kernels  10.2 us (32%)
    ppermute x8, waiting for transfers between devices, permuted(): lax.ppermute(value, axis, [(source, target_of(source) % count) for source...  11.4 us
    ppermute x8, starting transfers between devices, permuted(): lax.ppermute(value, axis, [(source, target_of(source) % count) for source...  10.4 us
    pallas_call x1, Pallas kernels, score_own(): pl.pallas_call(own_kernel, in_specs=in_vmem(1) + [pl.BlockSpec(memory_spa...  4.53 us
    pallas_call x1, Pallas kernels, condition(): pl.pallas_call(condition_kernel, in_specs=[pl.BlockSpec(memory_space=pltp...  2.32 us
    pallas_call x1, Pallas kernels, score_high(): pl.pallas_call(functools.partial(high_kernel, near.shape[1] - width), in_...  1.34 us
    pallas_call x1, Pallas kernels, score_low(): pl.pallas_call(low_kernel, in_specs=in_vmem(4), out_specs=in_vmem(1)[0],...  1.3 us
    pallas_call x1, Pallas kernels, finish(): pl.pallas_call(functools.partial(finish_kernel, layers), in_specs=in_vmem...  0.74 us
  transfers between devices with their start and end apart: 8, of which 6 were waited for; matrix products, arithmetic and copies ran while one was open for 0% of the time, Pallas kernels for 18%

profile of v8, /device:TPU:0, one launch (start us, length us, event | category | flops | bytes accessed | tf_op | source)
XLA Modules:
  0.0 32.2 jit_solution(15438900971861764061)
XLA Ops:
  0.0 2.3 %condition.1 = (bf16[32,2048]{1,0:T(8,128)(2,1)S(1)}, bf16[32,2048]{1,0:T(8,128)(2,1)S(1)}) custom-call(bf16[1,32,4096]{2,1,0:T(8,128)(2,1)} %queries_in.1, f32[1,64,64]{2,1,0:T(8,128)} %left_in.1, f32[1,64,64]{2,1,0:T(8,128)} %right_in.1), custom_call_target="tpu_custom_call" | custom-call | flops 536870912 | bytes 524288 | tf_op jit(solution)/shard_map/condition/pallas_call | solution.py:109
  2.3 4.1 %collective-permute-start.3 = (bf16[32,2048]{1,0:T(8,128)(2,1)S(1)}, bf16[32,2048]{1,0:T(8,128)(2,1)S(1)}, u32[]{:S(2)}, u32[]{:S(2)}) collective-permute-start(bf16[32,2048]{1,0:T(8,128)(2,1)S(1)} %get-tuple-element.13), channel_id=1, source_target_pairs={{0,2},{1,3},{2,0},{3,1},{4,6},{5,7},{6,4},{7,5},{8,10},{9,11},{10,... | collective-permute-start | bytes 393224 | tf_op jit(solution)/shard_map/ppermute | solution.py:269
  6.5 1.6 %collective-permute-start = (bf16[32,4096]{1,0:T(8,128)(2,1)S(1)}, bf16[32,4096]{1,0:T(8,128)(2,1)S(1)}, u32[]{:S(2)}, u32[]{:S(2)}) collective-permute-start(bf16[32,4096]{1,0:T(8,128)(2,1)S(1)} %constant_dynamic-update-slice_fusion.queries), channel_id=1, source_target_pairs={{0,1},{1,0},{2,3},{3,2},{4,5},{5,4},{6,7},{7,6},{8,9},{9,8},{10,11... | collective-permute-start | bytes 786440 | tf_op jit(solution)/shard_map/ppermute | solution.py:269
  8.1 0.3 %collective-permute-start.1 = (bf16[32,2048]{1,0:T(8,128)(2,1)S(1)}, bf16[32,2048]{1,0:T(8,128)(2,1)S(1)}, u32[]{:S(2)}, u32[]{:S(2)}) collective-permute-start(bf16[32,2048]{1,0:T(8,128)(2,1)S(1)} %get-tuple-element.14), channel_id=1, source_target_pairs={{0,2},{1,3},{2,0},{3,1},{4,6},{5,7},{6,4},{7,5},{8,10},{9,11},{10,... | collective-permute-start | bytes 393224 | tf_op jit(solution)/shard_map/ppermute | solution.py:269
  8.4 4.5 %score_own.1.own = f32[32,1024]{1,0:T(8,128)S(1)} custom-call(bf16[32,4096]{1,0:T(8,128)(2,1)S(1)} %constant_dynamic-update-slice_fusion.queries, bf16[1,1024,4096]{2,1,0:T(8,128)(2,1)} %store.3), custom_call_target="tpu_custom_call" | custom-call | flops 268435456 | bytes 8388608 | tf_op jit(solution)/shard_map/score_own/pallas_call | solution.py:169
  13.0 0.0 copy-start.1
  13.0 0.7 %collective-permute-done.3.far = bf16[32,2048]{1,0:T(8,128)(2,1)S(1)} collective-permute-done((bf16[32,2048]{1,0:T(8,128)(2,1)S(1)}, bf16[32,2048]{1,0:T(8,128)(2,1)S(1)}, u32[]{:S(2)}, u32[]{:S(2)}) %collective-permute-start.3) | collective-permute-done | bytes 131104 | tf_op jit(solution)/shard_map/ppermute | solution.py:269
  13.7 0.0 collective-permute-start.4
  13.7 5.1 %collective-permute-done.1.far = bf16[32,2048]{1,0:T(8,128)(2,1)S(1)} collective-permute-done((bf16[32,2048]{1,0:T(8,128)(2,1)S(1)}, bf16[32,2048]{1,0:T(8,128)(2,1)S(1)}, u32[]{:S(2)}, u32[]{:S(2)}) %collective-permute-start.1) | collective-permute-done | bytes 131104 | tf_op jit(solution)/shard_map/ppermute | solution.py:269
  18.8 2.4 %collective-permute-start.2 = (bf16[32,2048]{1,0:T(8,128)(2,1)S(1)}, bf16[32,2048]{1,0:T(8,128)(2,1)S(1)}, u32[]{:S(2)}, u32[]{:S(2)}) collective-permute-start(bf16[32,2048]{1,0:T(8,128)(2,1)S(1)} %collective-permute-done.1.far), channel_id=1, source_target_pairs={{0,1},{1,0},{2,3},{3,2},{4,5},{5,4},{6,7},{7,6},{8,9},{9,8},{10,11... | collective-permute-start | bytes 393224 | tf_op jit(solution)/shard_map/ppermute | solution.py:269
  21.1 1.8 %collective-permute-done.4.last = bf16[32,2048]{1,0:T(8,128)(2,1)S(1)} collective-permute-done((bf16[32,2048]{1,0:T(8,128)(2,1)S(1)}, bf16[32,2048]{1,0:T(8,128)(2,1)S(1)}, u32[]{:S(2)}, u32[]{:S(2)}) %collective-permute-start.4) | collective-permute-done | bytes 131104 | tf_op jit(solution)/shard_map/ppermute | solution.py:269
  23.0 0.0 collective-permute-done.near
  23.0 1.3 %score_low.1.low = f32[96,1024]{1,0:T(8,128)S(1)} custom-call(bf16[32,4096]{1,0:T(8,128)(2,1)S(1)} %collective-permute-done.near, bf16[32,2048]{1,0:T(8,128)(2,1)S(1)} %collective-permute-done.3.far, bf16[32,2048]{1,0:T(8,128)(2,1)S(1)} %collective-permute-done.4.last, bf16[1,1024,4096]{2,1,0:T(8,128)(2,1)S(1)} %copy-done), custom_call_target="tpu_custom_call" | custom-call | flops 402653184 | bytes 4194304 | tf_op jit(solution)/shard_map/score_low/pallas_call | solution.py:195
  24.3 0.1 collective-permute-done.2.last
  24.4 1.3 %score_high.1 = (f32[32,1024]{1,0:T(8,128)S(1)}, bf16[32,1024]{1,0:T(8,128)(2,1)S(1)}, bf16[32,1024]{1,0:T(8,128)(2,1)S(1)}, bf16[32,1024]{1,0:T(8,128)(2,1)S(1)}) custom-call(bf16[32,4096]{1,0:T(8,128)(2,1)S(1)} %collective-permute-done.near, bf16[32,2048]{1,0:T(8,128)(2,1)S(1)} %collective-permute-done.1.far, ...), custom_call_target="tpu_custom_call" | custom-call | flops 402653184 | bytes 4194304 | tf_op jit(solution)/shard_map/score_high/pallas_call | solution.py:224
  25.7 0.1 collective-permute-start.5
  25.8 1.6 %collective-permute-start.6 = (bf16[32,1024]{1,0:T(8,128)(2,1)S(1)}, bf16[32,1024]{1,0:T(8,128)(2,1)S(1)}, u32[]{:S(2)}, u32[]{:S(2)}) collective-permute-start(bf16[32,1024]{1,0:T(8,128)(2,1)S(1)} %get-tuple-element.19), channel_id=1, source_target_pairs={{0,8},{4,12},{8,0},{12,4},{1,9},{5,13},{9,1},{13,5},{2,10},{6,14},... | collective-permute-start | bytes 196616 | tf_op jit(solution)/shard_map/ppermute | solution.py:269
  27.4 0.3 collective-permute-start.7
  27.7 0.0 copy-done.1
  27.7 0.1 copy.6.candidates
  27.7 0.0 collective-permute-done.5.refs_1_
  27.7 2.6 %collective-permute-done.6.refs_2_ = bf16[32,1024]{1,0:T(8,128)(2,1)S(1)} collective-permute-done((bf16[32,1024]{1,0:T(8,128)(2,1)S(1)}, bf16[32,1024]{1,0:T(8,128)(2,1)S(1)}, u32[]{:S(2)}, u32[]{:S(2)}) %collective-permute-start.6) | collective-permute-done | bytes 65568 | tf_op jit(solution)/shard_map/ppermute | solution.py:269
  30.3 1.1 %collective-permute-done.7.refs_3_ = bf16[32,1024]{1,0:T(8,128)(2,1)S(1)} collective-permute-done((bf16[32,1024]{1,0:T(8,128)(2,1)S(1)}, bf16[32,1024]{1,0:T(8,128)(2,1)S(1)}, u32[]{:S(2)}, u32[]{:S(2)}) %collective-permute-start.7) | collective-permute-done | bytes 65568 | tf_op jit(solution)/shard_map/ppermute | solution.py:269
  31.4 0.7 %finish.1 = bf16[32,1024]{1,0:T(8,128)(2,1)} custom-call(s32[32,16]{1,0:T(8,128)S(1)} %copy.6.candidates, f32[32,1024]{1,0:T(8,128)S(1)} %get-tuple-element.17.refs_0_, bf16[32,1024]{1,0:T(8,128)(2,1)S(1)} %collective-permute-done.5.refs_1_, bf16[32,1024]{1,0:T(8,128)(2,1)S(1)} %collective-permute-done.6.refs_2_, ...), custom_call_target="tpu_custom_call" | custom-call | tf_op jit(solution)/shard_map/finish/pallas_call | solution.py:257
  (4 shorter events, 0.0 us)
Async XLA Ops:
  0.0 23.0 %copy-start = (bf16[1,1024,4096]{2,1,0:T(8,128)(2,1)S(1)}, bf16[1,1024,4096]{2,1,0:T(8,128)(2,1)}, u32[]{:S(2)}) copy-start(bf16[1,1024,4096]{2,1,0:T(8,128)(2,1)} %store.3) | copy-start | bytes 25165828
  2.3 11.3 %collective-permute-start.3 = (bf16[32,2048]{1,0:T(8,128)(2,1)S(1)}, bf16[32,2048]{1,0:T(8,128)(2,1)S(1)}, u32[]{:S(2)}, u32[]{:S(2)}) collective-permute-start(bf16[32,2048]{1,0:T(8,128)(2,1)S(1)} %get-tuple-element.13), channel_id=1, source_target_pairs={{0,2},{1,3},{2,0},{3,1},{4,6},{5,7},{6,4},{7,5},{8,10},{9,11},{10,... | collective-permute-start | bytes 393224 | tf_op jit(solution)/shard_map/ppermute | solution.py:269
  6.5 16.5 %collective-permute-start = (bf16[32,4096]{1,0:T(8,128)(2,1)S(1)}, bf16[32,4096]{1,0:T(8,128)(2,1)S(1)}, u32[]{:S(2)}, u32[]{:S(2)}) collective-permute-start(bf16[32,4096]{1,0:T(8,128)(2,1)S(1)} %constant_dynamic-update-slice_fusion.queries), channel_id=1, source_target_pairs={{0,1},{1,0},{2,3},{3,2},{4,5},{5,4},{6,7},{7,6},{8,9},{9,8},{10,11... | collective-permute-start | bytes 786440 | tf_op jit(solution)/shard_map/ppermute | solution.py:269
  8.1 10.7 %collective-permute-start.1 = (bf16[32,2048]{1,0:T(8,128)(2,1)S(1)}, bf16[32,2048]{1,0:T(8,128)(2,1)S(1)}, u32[]{:S(2)}, u32[]{:S(2)}) collective-permute-start(bf16[32,2048]{1,0:T(8,128)(2,1)S(1)} %get-tuple-element.14), channel_id=1, source_target_pairs={{0,2},{1,3},{2,0},{3,1},{4,6},{5,7},{6,4},{7,5},{8,10},{9,11},{10,... | collective-permute-start | bytes 393224 | tf_op jit(solution)/shard_map/ppermute | solution.py:269
  13.0 14.7 %copy-start.1 = (s32[32,16]{0,1:T(8,128)S(1)}, s32[32,16]{0,1:T(8,128)}, u32[]{:S(2)}) copy-start(s32[32,16]{0,1:T(8,128)} %param.9) | copy-start | bytes 6148
  13.7 9.3 %collective-permute-start.4 = (bf16[32,2048]{1,0:T(8,128)(2,1)S(1)}, bf16[32,2048]{1,0:T(8,128)(2,1)S(1)}, u32[]{:S(2)}, u32[]{:S(2)}) collective-permute-start(bf16[32,2048]{1,0:T(8,128)(2,1)S(1)} %collective-permute-done.3.far), channel_id=1, source_target_pairs={{0,1},{1,0},{2,3},{3,2},{4,5},{5,4},{6,7},{7,6},{8,9},{9,8},{10,11... | collective-permute-start | bytes 393224 | tf_op jit(solution)/shard_map/ppermute | solution.py:269
  18.8 5.6 %collective-permute-start.2 = (bf16[32,2048]{1,0:T(8,128)(2,1)S(1)}, bf16[32,2048]{1,0:T(8,128)(2,1)S(1)}, u32[]{:S(2)}, u32[]{:S(2)}) collective-permute-start(bf16[32,2048]{1,0:T(8,128)(2,1)S(1)} %collective-permute-done.1.far), channel_id=1, source_target_pairs={{0,1},{1,0},{2,3},{3,2},{4,5},{5,4},{6,7},{7,6},{8,9},{9,8},{10,11... | collective-permute-start | bytes 393224 | tf_op jit(solution)/shard_map/ppermute | solution.py:269
  25.7 2.0 %collective-permute-start.5 = (bf16[32,1024]{1,0:T(8,128)(2,1)S(1)}, bf16[32,1024]{1,0:T(8,128)(2,1)S(1)}, u32[]{:S(2)}, u32[]{:S(2)}) collective-permute-start(bf16[32,1024]{1,0:T(8,128)(2,1)S(1)} %get-tuple-element.18), channel_id=1, source_target_pairs={{0,4},{4,0},{8,12},{12,8},{1,5},{5,1},{9,13},{13,9},{2,6},{6,2},{1... | collective-permute-start | bytes 196616 | tf_op jit(solution)/shard_map/ppermute | solution.py:269
  25.8 4.5 %collective-permute-start.6 = (bf16[32,1024]{1,0:T(8,128)(2,1)S(1)}, bf16[32,1024]{1,0:T(8,128)(2,1)S(1)}, u32[]{:S(2)}, u32[]{:S(2)}) collective-permute-start(bf16[32,1024]{1,0:T(8,128)(2,1)S(1)} %get-tuple-element.19), channel_id=1, source_target_pairs={{0,8},{4,12},{8,0},{12,4},{1,9},{5,13},{9,1},{13,5},{2,10},{6,14},... | collective-permute-start | bytes 196616 | tf_op jit(solution)/shard_map/ppermute | solution.py:269
  27.4 4.0 %collective-permute-start.7 = (bf16[32,1024]{1,0:T(8,128)(2,1)S(1)}, bf16[32,1024]{1,0:T(8,128)(2,1)S(1)}, u32[]{:S(2)}, u32[]{:S(2)}) collective-permute-start(bf16[32,1024]{1,0:T(8,128)(2,1)S(1)} %get-tuple-element.20), channel_id=1, source_target_pairs={{0,12},{4,8},{8,4},{12,0},{1,13},{5,9},{9,5},{13,1},{2,14},{6,10},... | collective-permute-start | bytes 196616 | tf_op jit(solution)/shard_map/ppermute | solution.py:269

commit v9 on v8

--- a/solution.py
+++ b/solution.py
@@ -126,6 +126,7 @@
 
 
 STEP = 256
+MASKS = (0, 3, 2, 1)
 
 
 def score_block(queries, store, first, write, arrived=None, step_rows=STEP):
@@ -213,7 +214,7 @@
 
     score_block(three_blocks(near, far, last, first), store, first, write, step_rows=store.shape[1])
     home = lax.bitwise_xor(lax.axis_index("blk"), lax.axis_index("layer"))
-    for mask, out in enumerate(outs):
+    for mask, out in zip(MASKS, outs):
         slot = lax.bitwise_xor(home, mask)
         out[...] = total[pl.ds(pl.multiple_of(slot * rows, rows), rows), :].astype(out.dtype)
 
@@ -226,7 +227,7 @@
         in_specs=in_vmem(6),
         out_specs=in_vmem(4),
         out_shape=[
-            jax.ShapeDtypeStruct((rows, examples), jnp.bfloat16 if mask else jnp.float32) for mask in range(4)
+            jax.ShapeDtypeStruct((rows, examples), jnp.bfloat16 if mask else jnp.float32) for mask in MASKS
         ],
         scratch_shapes=[pltpu.VMEM((4 * rows, examples), jnp.float32)],
         compiler_params=pltpu.CompilerParams(vmem_limit_bytes=VMEM),
@@ -282,8 +283,8 @@
     last = [swapped(half, "blk", 1) for half in far]
     low_scores = score_low(near, far[0], last[0], store)
     parts = score_high(near, far[1], last[1], store, own_scores, low_scores)
-    received = {mask: swapped(parts[mask], "layer", mask) for mask in (3, 2, 1)}
-    return finish([parts[0]] + [received[mask] for mask in (1, 2, 3)], candidates, layers)
+    received = [swapped(part, "layer", mask) for mask, part in zip(MASKS[1:], parts[1:])]
+    return finish([parts[0]] + received, candidates, layers)
 
 
 def on_ring(own, store, candidates, layers):

time: 32.3 us -> 32.5 us (level)
  no operation moved by 1% of the time
where the time goes in v9:
time: 32.5 us; the launch traced here: 32.3 us
  waiting for transfers between devices  11.6 us (36%)
  starting transfers between devices  10.4 us (32%)
  Pallas kernels  10.2 us (31%)
    ppermute x8, waiting for transfers between devices, permuted(): lax.ppermute(value, axis, [(source, target_of(source) % count) for source...  11.6 us
    ppermute x8, starting transfers between devices, permuted(): lax.ppermute(value, axis, [(source, target_of(source) % count) for source...  10.4 us
    pallas_call x1, Pallas kernels, score_own(): pl.pallas_call(own_kernel, in_specs=in_vmem(1) + [pl.BlockSpec(memory_spa...  4.53 us
    pallas_call x1, Pallas kernels, condition(): pl.pallas_call(condition_kernel, in_specs=[pl.BlockSpec(memory_space=pltp...  2.32 us
    pallas_call x1, Pallas kernels, score_high(): pl.pallas_call(functools.partial(high_kernel, near.shape[1] - width), in_...  1.34 us
    pallas_call x1, Pallas kernels, score_low(): pl.pallas_call(low_kernel, in_specs=in_vmem(4), out_specs=in_vmem(1)[0],...  1.3 us
    pallas_call x1, Pallas kernels, finish(): pl.pallas_call(functools.partial(finish_kernel, layers), in_specs=in_vmem...  0.74 us
  transfers between devices with their start and end apart: 8, of which 6 were waited for; matrix products, arithmetic and copies ran while one was open for 0% of the time, Pallas kernels for 18%

profile of v9, /device:TPU:0, one launch (start us, length us, event | category | flops | bytes accessed | tf_op | source)
XLA Modules:
  0.0 32.3 jit_solution(14570953219476680552)
XLA Ops:
  0.0 2.3 %condition.1 = (bf16[32,2048]{1,0:T(8,128)(2,1)S(1)}, bf16[32,2048]{1,0:T(8,128)(2,1)S(1)}) custom-call(bf16[1,32,4096]{2,1,0:T(8,128)(2,1)} %queries_in.1, f32[1,64,64]{2,1,0:T(8,128)} %left_in.1, f32[1,64,64]{2,1,0:T(8,128)} %right_in.1), custom_call_target="tpu_custom_call" | custom-call | flops 536870912 | bytes 524288 | tf_op jit(solution)/shard_map/condition/pallas_call | solution.py:109
  2.3 4.1 %collective-permute-start.3 = (bf16[32,2048]{1,0:T(8,128)(2,1)S(1)}, bf16[32,2048]{1,0:T(8,128)(2,1)S(1)}, u32[]{:S(2)}, u32[]{:S(2)}) collective-permute-start(bf16[32,2048]{1,0:T(8,128)(2,1)S(1)} %get-tuple-element.13), channel_id=1, source_target_pairs={{0,2},{1,3},{2,0},{3,1},{4,6},{5,7},{6,4},{7,5},{8,10},{9,11},{10,... | collective-permute-start | bytes 393224 | tf_op jit(solution)/shard_map/ppermute | solution.py:270
  6.5 1.6 %collective-permute-start = (bf16[32,4096]{1,0:T(8,128)(2,1)S(1)}, bf16[32,4096]{1,0:T(8,128)(2,1)S(1)}, u32[]{:S(2)}, u32[]{:S(2)}) collective-permute-start(bf16[32,4096]{1,0:T(8,128)(2,1)S(1)} %constant_dynamic-update-slice_fusion.queries), channel_id=1, source_target_pairs={{0,1},{1,0},{2,3},{3,2},{4,5},{5,4},{6,7},{7,6},{8,9},{9,8},{10,11... | collective-permute-start | bytes 786440 | tf_op jit(solution)/shard_map/ppermute | solution.py:270
  8.1 0.3 %collective-permute-start.1 = (bf16[32,2048]{1,0:T(8,128)(2,1)S(1)}, bf16[32,2048]{1,0:T(8,128)(2,1)S(1)}, u32[]{:S(2)}, u32[]{:S(2)}) collective-permute-start(bf16[32,2048]{1,0:T(8,128)(2,1)S(1)} %get-tuple-element.14), channel_id=1, source_target_pairs={{0,2},{1,3},{2,0},{3,1},{4,6},{5,7},{6,4},{7,5},{8,10},{9,11},{10,... | collective-permute-start | bytes 393224 | tf_op jit(solution)/shard_map/ppermute | solution.py:270
  8.4 4.5 %score_own.1.own = f32[32,1024]{1,0:T(8,128)S(1)} custom-call(bf16[32,4096]{1,0:T(8,128)(2,1)S(1)} %constant_dynamic-update-slice_fusion.queries, bf16[1,1024,4096]{2,1,0:T(8,128)(2,1)} %store.3), custom_call_target="tpu_custom_call" | custom-call | flops 268435456 | bytes 8388608 | tf_op jit(solution)/shard_map/score_own/pallas_call | solution.py:170
  13.0 0.0 copy-start.1
  13.0 0.7 %collective-permute-done.3.far = bf16[32,2048]{1,0:T(8,128)(2,1)S(1)} collective-permute-done((bf16[32,2048]{1,0:T(8,128)(2,1)S(1)}, bf16[32,2048]{1,0:T(8,128)(2,1)S(1)}, u32[]{:S(2)}, u32[]{:S(2)}) %collective-permute-start.3) | collective-permute-done | bytes 131104 | tf_op jit(solution)/shard_map/ppermute | solution.py:270
  13.7 0.0 collective-permute-start.4
  13.7 5.1 %collective-permute-done.1.far = bf16[32,2048]{1,0:T(8,128)(2,1)S(1)} collective-permute-done((bf16[32,2048]{1,0:T(8,128)(2,1)S(1)}, bf16[32,2048]{1,0:T(8,128)(2,1)S(1)}, u32[]{:S(2)}, u32[]{:S(2)}) %collective-permute-start.1) | collective-permute-done | bytes 131104 | tf_op jit(solution)/shard_map/ppermute | solution.py:270
  18.8 2.4 %collective-permute-start.2 = (bf16[32,2048]{1,0:T(8,128)(2,1)S(1)}, bf16[32,2048]{1,0:T(8,128)(2,1)S(1)}, u32[]{:S(2)}, u32[]{:S(2)}) collective-permute-start(bf16[32,2048]{1,0:T(8,128)(2,1)S(1)} %collective-permute-done.1.far), channel_id=1, source_target_pairs={{0,1},{1,0},{2,3},{3,2},{4,5},{5,4},{6,7},{7,6},{8,9},{9,8},{10,11... | collective-permute-start | bytes 393224 | tf_op jit(solution)/shard_map/ppermute | solution.py:270
  21.1 1.8 %collective-permute-done.4.last = bf16[32,2048]{1,0:T(8,128)(2,1)S(1)} collective-permute-done((bf16[32,2048]{1,0:T(8,128)(2,1)S(1)}, bf16[32,2048]{1,0:T(8,128)(2,1)S(1)}, u32[]{:S(2)}, u32[]{:S(2)}) %collective-permute-start.4) | collective-permute-done | bytes 131104 | tf_op jit(solution)/shard_map/ppermute | solution.py:270
  23.0 0.0 collective-permute-done.near
  23.0 0.0 copy-done
  23.0 1.3 %score_low.1.low = f32[96,1024]{1,0:T(8,128)S(1)} custom-call(bf16[32,4096]{1,0:T(8,128)(2,1)S(1)} %collective-permute-done.near, bf16[32,2048]{1,0:T(8,128)(2,1)S(1)} %collective-permute-done.3.far, bf16[32,2048]{1,0:T(8,128)(2,1)S(1)} %collective-permute-done.4.last, bf16[1,1024,4096]{2,1,0:T(8,128)(2,1)S(1)} %copy-done), custom_call_target="tpu_custom_call" | custom-call | flops 402653184 | bytes 4194304 | tf_op jit(solution)/shard_map/score_low/pallas_call | solution.py:196
  24.3 0.1 collective-permute-done.2.last
  24.4 1.3 %score_high.1 = (f32[32,1024]{1,0:T(8,128)S(1)}, bf16[32,1024]{1,0:T(8,128)(2,1)S(1)}, bf16[32,1024]{1,0:T(8,128)(2,1)S(1)}, bf16[32,1024]{1,0:T(8,128)(2,1)S(1)}) custom-call(bf16[32,4096]{1,0:T(8,128)(2,1)S(1)} %collective-permute-done.near, bf16[32,2048]{1,0:T(8,128)(2,1)S(1)} %collective-permute-done.1.far, ...), custom_call_target="tpu_custom_call" | custom-call | flops 402653184 | bytes 4194304 | tf_op jit(solution)/shard_map/score_high/pallas_call | solution.py:225
  25.7 0.1 collective-permute-start.5
  25.8 1.6 %collective-permute-start.6 = (bf16[32,1024]{1,0:T(8,128)(2,1)S(1)}, bf16[32,1024]{1,0:T(8,128)(2,1)S(1)}, u32[]{:S(2)}, u32[]{:S(2)}) collective-permute-start(bf16[32,1024]{1,0:T(8,128)(2,1)S(1)} %get-tuple-element.19), channel_id=1, source_target_pairs={{0,8},{4,12},{8,0},{12,4},{1,9},{5,13},{9,1},{13,5},{2,10},{6,14},... | collective-permute-start | bytes 196616 | tf_op jit(solution)/shard_map/ppermute | solution.py:270
  27.4 0.2 collective-permute-start.7
  27.6 0.1 copy.6.candidates
  27.7 2.4 %collective-permute-done.5.refs_1_ = bf16[32,1024]{1,0:T(8,128)(2,1)S(1)} collective-permute-done((bf16[32,1024]{1,0:T(8,128)(2,1)S(1)}, bf16[32,1024]{1,0:T(8,128)(2,1)S(1)}, u32[]{:S(2)}, u32[]{:S(2)}) %collective-permute-start.5) | collective-permute-done | bytes 65568 | tf_op jit(solution)/shard_map/ppermute | solution.py:270
  30.1 1.5 %collective-permute-done.6.refs_2_ = bf16[32,1024]{1,0:T(8,128)(2,1)S(1)} collective-permute-done((bf16[32,1024]{1,0:T(8,128)(2,1)S(1)}, bf16[32,1024]{1,0:T(8,128)(2,1)S(1)}, u32[]{:S(2)}, u32[]{:S(2)}) %collective-permute-start.6) | collective-permute-done | bytes 65568 | tf_op jit(solution)/shard_map/ppermute | solution.py:270
  31.6 0.0 collective-permute-done.7.refs_3_
  31.6 0.7 %finish.1 = bf16[32,1024]{1,0:T(8,128)(2,1)} custom-call(s32[32,16]{1,0:T(8,128)S(1)} %copy.6.candidates, f32[32,1024]{1,0:T(8,128)S(1)} %get-tuple-element.17.refs_0_, bf16[32,1024]{1,0:T(8,128)(2,1)S(1)} %collective-permute-done.5.refs_1_, bf16[32,1024]{1,0:T(8,128)(2,1)S(1)} %collective-permute-done.6.refs_2_, ...), custom_call_target="tpu_custom_call" | custom-call | tf_op jit(solution)/shard_map/finish/pallas_call | solution.py:258
  (4 shorter events, 0.0 us)
Async XLA Ops:
  0.0 23.0 %copy-start = (bf16[1,1024,4096]{2,1,0:T(8,128)(2,1)S(1)}, bf16[1,1024,4096]{2,1,0:T(8,128)(2,1)}, u32[]{:S(2)}) copy-start(bf16[1,1024,4096]{2,1,0:T(8,128)(2,1)} %store.3) | copy-start | bytes 25165828
  2.3 11.3 %collective-permute-start.3 = (bf16[32,2048]{1,0:T(8,128)(2,1)S(1)}, bf16[32,2048]{1,0:T(8,128)(2,1)S(1)}, u32[]{:S(2)}, u32[]{:S(2)}) collective-permute-start(bf16[32,2048]{1,0:T(8,128)(2,1)S(1)} %get-tuple-element.13), channel_id=1, source_target_pairs={{0,2},{1,3},{2,0},{3,1},{4,6},{5,7},{6,4},{7,5},{8,10},{9,11},{10,... | collective-permute-start | bytes 393224 | tf_op jit(solution)/shard_map/ppermute | solution.py:270
  6.5 16.5 %collective-permute-start = (bf16[32,4096]{1,0:T(8,128)(2,1)S(1)}, bf16[32,4096]{1,0:T(8,128)(2,1)S(1)}, u32[]{:S(2)}, u32[]{:S(2)}) collective-permute-start(bf16[32,4096]{1,0:T(8,128)(2,1)S(1)} %constant_dynamic-update-slice_fusion.queries), channel_id=1, source_target_pairs={{0,1},{1,0},{2,3},{3,2},{4,5},{5,4},{6,7},{7,6},{8,9},{9,8},{10,11... | collective-permute-start | bytes 786440 | tf_op jit(solution)/shard_map/ppermute | solution.py:270
  8.1 10.7 %collective-permute-start.1 = (bf16[32,2048]{1,0:T(8,128)(2,1)S(1)}, bf16[32,2048]{1,0:T(8,128)(2,1)S(1)}, u32[]{:S(2)}, u32[]{:S(2)}) collective-permute-start(bf16[32,2048]{1,0:T(8,128)(2,1)S(1)} %get-tuple-element.14), channel_id=1, source_target_pairs={{0,2},{1,3},{2,0},{3,1},{4,6},{5,7},{6,4},{7,5},{8,10},{9,11},{10,... | collective-permute-start | bytes 393224 | tf_op jit(solution)/shard_map/ppermute | solution.py:270
  13.0 14.7 %copy-start.1 = (s32[32,16]{0,1:T(8,128)S(1)}, s32[32,16]{0,1:T(8,128)}, u32[]{:S(2)}) copy-start(s32[32,16]{0,1:T(8,128)} %param.9) | copy-start | bytes 6148
  13.7 9.3 %collective-permute-start.4 = (bf16[32,2048]{1,0:T(8,128)(2,1)S(1)}, bf16[32,2048]{1,0:T(8,128)(2,1)S(1)}, u32[]{:S(2)}, u32[]{:S(2)}) collective-permute-start(bf16[32,2048]{1,0:T(8,128)(2,1)S(1)} %collective-permute-done.3.far), channel_id=1, source_target_pairs={{0,1},{1,0},{2,3},{3,2},{4,5},{5,4},{6,7},{7,6},{8,9},{9,8},{10,11... | collective-permute-start | bytes 393224 | tf_op jit(solution)/shard_map/ppermute | solution.py:270
  18.8 5.6 %collective-permute-start.2 = (bf16[32,2048]{1,0:T(8,128)(2,1)S(1)}, bf16[32,2048]{1,0:T(8,128)(2,1)S(1)}, u32[]{:S(2)}, u32[]{:S(2)}) collective-permute-start(bf16[32,2048]{1,0:T(8,128)(2,1)S(1)} %collective-permute-done.1.far), channel_id=1, source_target_pairs={{0,1},{1,0},{2,3},{3,2},{4,5},{5,4},{6,7},{7,6},{8,9},{9,8},{10,11... | collective-permute-start | bytes 393224 | tf_op jit(solution)/shard_map/ppermute | solution.py:270
  25.7 4.4 %collective-permute-start.5 = (bf16[32,1024]{1,0:T(8,128)(2,1)S(1)}, bf16[32,1024]{1,0:T(8,128)(2,1)S(1)}, u32[]{:S(2)}, u32[]{:S(2)}) collective-permute-start(bf16[32,1024]{1,0:T(8,128)(2,1)S(1)} %get-tuple-element.18), channel_id=1, source_target_pairs={{0,12},{4,8},{8,4},{12,0},{1,13},{5,9},{9,5},{13,1},{2,14},{6,10},... | collective-permute-start | bytes 196616 | tf_op jit(solution)/shard_map/ppermute | solution.py:270
  25.8 5.8 %collective-permute-start.6 = (bf16[32,1024]{1,0:T(8,128)(2,1)S(1)}, bf16[32,1024]{1,0:T(8,128)(2,1)S(1)}, u32[]{:S(2)}, u32[]{:S(2)}) collective-permute-start(bf16[32,1024]{1,0:T(8,128)(2,1)S(1)} %get-tuple-element.19), channel_id=1, source_target_pairs={{0,8},{4,12},{8,0},{12,4},{1,9},{5,13},{9,1},{13,5},{2,10},{6,14},... | collective-permute-start | bytes 196616 | tf_op jit(solution)/shard_map/ppermute | solution.py:270
  27.4 4.2 %collective-permute-start.7 = (bf16[32,1024]{1,0:T(8,128)(2,1)S(1)}, bf16[32,1024]{1,0:T(8,128)(2,1)S(1)}, u32[]{:S(2)}, u32[]{:S(2)}) collective-permute-start(bf16[32,1024]{1,0:T(8,128)(2,1)S(1)} %get-tuple-element.20), channel_id=1, source_target_pairs={{0,4},{4,0},{8,12},{12,8},{1,5},{5,1},{9,13},{13,9},{2,6},{6,2},{1... | collective-permute-start | bytes 196616 | tf_op jit(solution)/shard_map/ppermute | solution.py:270

commit v10 on v8

--- a/solution.py
+++ b/solution.py
@@ -32,12 +32,13 @@
     return jnp.where(condition, 1.0, 0.0).astype(jnp.bfloat16)
 
 
-def spread_left(left_factor):
+def spread_left(left_factor, first, count):
     side = left_factor.shape[0]
     wide = ones_where(iota((side, side * ROWS), 1) // ROWS == iota((side, side * ROWS), 0))
-    columns = dot(jnp.concatenate(two_parts(left_factor), axis=0), wide).reshape(2, side, 1, side * ROWS)
+    parts = [part[first : first + count] for part in two_parts(left_factor)]
+    columns = dot(jnp.concatenate(parts, axis=0), wide).reshape(2, count, 1, side * ROWS)
     same = iota((1, ROWS, side * ROWS), 1) == iota((1, ROWS, side * ROWS), 2) % ROWS
-    parts = [jnp.where(same, columns[part], 0.0).reshape(side * ROWS, side * ROWS) for part in range(2)]
+    parts = [jnp.where(same, columns[part], 0.0).reshape(count * ROWS, side * ROWS) for part in range(2)]
     return jnp.concatenate([part.astype(jnp.bfloat16) for part in parts], axis=1)
 
 
@@ -52,8 +53,7 @@
     return jnp.concatenate([high, low, high], axis=0)
 
 
-def condition_kernel(queries_in, left_in, right_in, low, high, queries, left_factor, right_factor, arrived):
-    halves = (low, high)
+def condition_kernel(first, count, queries_in, left_in, right_in, out, queries, left_factor, right_factor, arrived):
     copies = [
         pltpu.make_async_copy(source.at[0], target, arrived.at[place])
         for place, (source, target) in enumerate(
@@ -66,10 +66,9 @@
     pairs = side // 2
     copies[0].wait()
     copies[1].wait()
-    left = spread_left(left_factor[...])
+    left = spread_left(left_factor[...], first, count)
     right = spread_right(right_factor[...])
     low_half = iota((1, 1, LANES), 2) < side
-    per_half = pairs // len(halves)
     copies[2].wait()
     for block in range(queries.shape[0] // GROUP):
         rows = pl.ds(block * GROUP, GROUP)
@@ -87,7 +86,7 @@
         halfway = dot(left, jnp.concatenate([grid, grid], axis=0))
         high, low = two_parts(halfway)
         result = dot(jnp.concatenate([high, high, low], axis=1), right)
-        result = result.reshape(pairs, 2, ROWS, 2 * LANES)
+        result = result.reshape(count // 2, 2, ROWS, 2 * LANES)
         groups = []
         for half in range(2):
             even = result[:, 0, :, half * LANES : (half + 1) * LANES]
@@ -95,22 +94,23 @@
             groups.append(jnp.where(low_half, even, pltpu.roll(odd, side, 2)))
             groups.append(jnp.where(low_half, pltpu.roll(even, side, 2), odd))
         done = jnp.concatenate(groups, axis=1).astype(jnp.bfloat16)
-        for pair in range(pairs):
-            halves[pair // per_half][rows, pl.ds(pair % per_half * LANES, LANES)] = done[pair]
+        for pair in range(count // 2):
+            out[rows, pl.ds(pair * LANES, LANES)] = done[pair]
 
 
 def in_vmem(count):
     return [pl.BlockSpec(memory_space=pltpu.VMEM)] * count
 
 
-def condition(queries, left_factor, right_factor):
+def condition(queries, left_factor, right_factor, half):
     unused, block_rows, entries = queries.shape
     side = left_factor.shape[1]
-    return pl.pallas_call(
-        condition_kernel,
+    operands = [pltpu.with_memory_space_constraint(value, pltpu.HBM) for value in (queries, left_factor, right_factor)]
+    return pl.pallas_call(
+        functools.partial(condition_kernel, half * side // 2, side // 2),
         in_specs=[pl.BlockSpec(memory_space=pltpu.HBM)] * 3,
-        out_specs=in_vmem(2),
-        out_shape=[jax.ShapeDtypeStruct((block_rows, entries // 2), jnp.bfloat16)] * 2,
+        out_specs=in_vmem(1)[0],
+        out_shape=jax.ShapeDtypeStruct((block_rows, entries // 2), jnp.bfloat16),
         scratch_shapes=[
             pltpu.VMEM((block_rows, entries), jnp.bfloat16),
             pltpu.VMEM((side, side), jnp.float32),
@@ -122,7 +122,7 @@
             flops=block_rows * entries * 4096, bytes_accessed=queries.size * 4, transcendentals=0
         ),
         name="condition",
-    )(*[pltpu.with_memory_space_constraint(value, pltpu.HBM) for value in (queries, left_factor, right_factor)])
+    )(*operands)
 
 
 STEP = 256
@@ -143,7 +143,7 @@
     lax.fori_loop(0, store.shape[1] // step_rows, one, 0)
 
 
-def own_kernel(queries, far_store, out, store, semaphores):
+def own_kernel(low, high, far_store, out, store, semaphores):
     def copy_of(step):
         place = pl.ds(pl.multiple_of(step * STEP, STEP), STEP)
         return pltpu.make_async_copy(far_store.at[0, place], store.at[0, place], semaphores.at[step])
@@ -154,7 +154,8 @@
     def write(place, value):
         out[:, place] = value
 
-    score_block(queries[...], store, 0, write, lambda step: copy_of(step).wait())
+    queries = jnp.concatenate([low[...], high[...]], axis=1)
+    score_block(queries, store, 0, write, lambda step: copy_of(step).wait())
 
 
 def score_cost(count, width, examples):
@@ -163,30 +164,30 @@
     )
 
 
-def score_own(queries, store):
-    rows, entries = queries.shape
+def score_own(halves, store):
+    rows, entries = halves[0].shape[0], store.shape[2]
     examples = store.shape[1]
     return pl.pallas_call(
         own_kernel,
-        in_specs=in_vmem(1) + [pl.BlockSpec(memory_space=pltpu.HBM)],
+        in_specs=in_vmem(2) + [pl.BlockSpec(memory_space=pltpu.HBM)],
         out_specs=in_vmem(1)[0],
         out_shape=jax.ShapeDtypeStruct((rows, examples), jnp.float32),
         scratch_shapes=[pltpu.VMEM(store.shape, store.dtype), pltpu.SemaphoreType.DMA((examples // STEP,))],
         compiler_params=pltpu.CompilerParams(vmem_limit_bytes=VMEM),
         cost_estimate=score_cost(rows, entries, examples),
         name="score_own",
-    )(queries, pltpu.with_memory_space_constraint(store, pltpu.HBM))
-
-
-def three_blocks(near, far, last, first):
-    return jnp.concatenate([near[:, pl.ds(first, far.shape[1])], far[...], last[...]], axis=0)
+    )(*halves, pltpu.with_memory_space_constraint(store, pltpu.HBM))
+
+
+def stacked(*blocks):
+    return jnp.concatenate([block[...] for block in blocks], axis=0)
 
 
 def low_kernel(near, far, last, store, out):
     def write(place, value):
         out[:, place] = value
 
-    score_block(three_blocks(near, far, last, 0), store, 0, write, step_rows=store.shape[1])
+    score_block(stacked(near, far, last), store, 0, write, step_rows=store.shape[1])
 
 
 def score_low(near, far, last, store):
@@ -211,7 +212,7 @@
     def write(place, value):
         total[pl.ds(rows, 3 * rows), place] = value + low[:, place]
 
-    score_block(three_blocks(near, far, last, first), store, first, write, step_rows=store.shape[1])
+    score_block(stacked(near, far, last), store, first, write, step_rows=store.shape[1])
     home = lax.bitwise_xor(lax.axis_index("blk"), lax.axis_index("layer"))
     for mask, out in enumerate(outs):
         slot = lax.bitwise_xor(home, mask)
@@ -222,7 +223,7 @@
     rows, width = far.shape
     examples = store.shape[1]
     return pl.pallas_call(
-        functools.partial(high_kernel, near.shape[1] - width),
+        functools.partial(high_kernel, store.shape[2] - width),
         in_specs=in_vmem(6),
         out_specs=in_vmem(4),
         out_shape=[
@@ -275,25 +276,24 @@
 
 def on_line(own, store, candidates, layers):
     far = [swapped(half, "blk", 2) for half in own]
-    whole = jnp.concatenate(own, axis=1)
-    near = swapped(whole, "blk", 1)
-    own_scores = score_own(whole, store)
-    far[0], own_scores = lax.optimization_barrier((far[0], own_scores))
+    near = [swapped(half, "blk", 1) for half in own]
+    own_scores = score_own(own, store)
+    far[0], near[0], own_scores = lax.optimization_barrier((far[0], near[0], own_scores))
+    far[1], near[1] = lax.optimization_barrier((far[1], near[1]))
     last = [swapped(half, "blk", 1) for half in far]
-    low_scores = score_low(near, far[0], last[0], store)
-    parts = score_high(near, far[1], last[1], store, own_scores, low_scores)
-    received = {mask: swapped(parts[mask], "layer", mask) for mask in (3, 2, 1)}
-    return finish([parts[0]] + [received[mask] for mask in (1, 2, 3)], candidates, layers)
+    low_scores = score_low(near[0], far[0], last[0], store)
+    parts = score_high(near[1], far[1], last[1], store, own_scores, low_scores)
+    received = [swapped(parts[mask], "layer", mask) for mask in (1, 2, 3)]
+    return finish([parts[0]] + received, candidates, layers)
 
 
 def on_ring(own, store, candidates, layers):
     count = lax.axis_size("blk")
-    moving = jnp.concatenate(own, axis=1)
-    rows = moving.shape[0]
-    slots = [score_own(moving, store)]
+    rows = own[0].shape[0]
+    slots = [score_own(own, store)]
     for _ in range(count - 1):
-        moving = permuted(moving, "blk", lambda source: source + 1)
-        slots.append(score_own(moving, store))
+        own = [permuted(half, "blk", lambda source: source + 1) for half in own]
+        slots.append(score_own(own, store))
     turns = lax.rem(lax.axis_index("blk") - jnp.arange(count) + count, count)
     total = jnp.stack(slots)[turns].reshape(layers, count * rows // layers, store.shape[1])
     parts = lax.all_to_all(total.astype(jnp.bfloat16), "layer", 0, 0)
@@ -302,7 +302,7 @@
 
 def per_device(queries, store, left_factor, right_factor, candidates):
     layers, count = lax.axis_size("layer"), lax.axis_size("blk")
-    own = condition(queries, left_factor, right_factor)
+    own = [condition(queries, left_factor, right_factor, half) for half in range(2)]
     way = on_line if layers == 4 and count == 4 else on_ring
     return way(own, store, candidates, layers)
 

time: 32.3 us -> 31.9 us (0.988)
  waiting for transfers between devices: 11.4 us -> 7.62 us
  starting transfers between devices: 10.4 us -> 12.3 us
  Pallas kernels: 10.2 us -> 11.7 us
    ppermute x8 -> x9, waiting for transfers between devices: 11.4 us -> 7.62 us  [permuted(): lax.ppermute(value, axis, [(source, target_of(source) % count) for source...]
    ppermute x8 -> x9, starting transfers between devices: 10.4 us -> 12.3 us  [permuted(): lax.ppermute(value, axis, [(source, target_of(source) % count) for source...]
    pallas_call x3 -> x4, Pallas kernels: 8.19 us -> 9.61 us  [the longest x1 4.52 us: score_own(): pl.pallas_call(own_kernel, in_specs=in_vmem(2) + [pl.BlockSpec(memory_spa...]
  transfers between devices with their start and end apart: 8 -> 9, of which waited for: 6 -> 6; matrix products, arithmetic and copies ran while one was open for 0% -> 0% of each run, Pallas kernels for 18% -> 24%
where the time goes in v10:
time: 31.9 us; the launch traced here: 31.7 us
  starting transfers between devices  12.3 us (39%)
  Pallas kernels  11.7 us (37%)
  waiting for transfers between devices  7.62 us (24%)
    ppermute x9, starting transfers between devices, permuted(): lax.ppermute(value, axis, [(source, target_of(source) % count) for source...  12.3 us
    ppermute x9, waiting for transfers between devices, permuted(): lax.ppermute(value, axis, [(source, target_of(source) % count) for source...  7.62 us
    pallas_call x1, Pallas kernels, score_own(): pl.pallas_call(own_kernel, in_specs=in_vmem(2) + [pl.BlockSpec(memory_spa...  4.52 us
    pallas_call x2, Pallas kernels, condition(): pl.pallas_call(functools.partial(condition_kernel, half * side // 2, side...  3.76 us
    pallas_call x1, Pallas kernels, score_high(): pl.pallas_call(functools.partial(high_kernel, store.shape[2] - width), in...  1.34 us
    pallas_call x1, Pallas kernels, score_low(): pl.pallas_call(low_kernel, in_specs=in_vmem(4), out_specs=in_vmem(1)[0],...  1.29 us
    pallas_call x1, Pallas kernels, finish(): pl.pallas_call(functools.partial(finish_kernel, layers), in_specs=in_vmem...  0.74 us
  transfers between devices with their start and end apart: 9, of which 6 were waited for; matrix products, arithmetic and copies ran while one was open for 0% of the time, Pallas kernels for 24%

profile of v10, /device:TPU:0, one launch (start us, length us, event | category | flops | bytes accessed | tf_op | source)
XLA Modules:
  0.0 31.7 jit_solution(13718785802809476756)
XLA Ops:
  0.0 2.0 %condition.3.low = bf16[32,2048]{1,0:T(8,128)(2,1)S(1)} custom-call(bf16[1,32,4096]{2,1,0:T(8,128)(2,1)} %queries_in.3, f32[1,64,64]{2,1,0:T(8,128)} %left_in.3, f32[1,64,64]{2,1,0:T(8,128)} %right_in.3), custom_call_target="tpu_custom_call" | custom-call | flops 536870912 | bytes 524288 | tf_op jit(solution)/shard_map/condition/pallas_call | solution.py:109
  2.0 4.1 %collective-permute-start.3 = (bf16[32,2048]{1,0:T(8,128)(2,1)S(1)}, bf16[32,2048]{1,0:T(8,128)(2,1)S(1)}, u32[]{:S(2)}, u32[]{:S(2)}) collective-permute-start(bf16[32,2048]{1,0:T(8,128)(2,1)S(1)} %condition.3.low), channel_id=1, source_target_pairs={{0,2},{1,3},{2,0},{3,1},{4,6},{5,7},{6,4},{7,5},{8,10},{9,11},{10,... | collective-permute-start | bytes 393224 | tf_op jit(solution)/shard_map/ppermute | solution.py:270
  6.1 1.6 %collective-permute-start.4 = (bf16[32,2048]{1,0:T(8,128)(2,1)S(1)}, bf16[32,2048]{1,0:T(8,128)(2,1)S(1)}, u32[]{:S(2)}, u32[]{:S(2)}) collective-permute-start(bf16[32,2048]{1,0:T(8,128)(2,1)S(1)} %condition.3.low), channel_id=1, source_target_pairs={{0,1},{1,0},{2,3},{3,2},{4,5},{5,4},{6,7},{7,6},{8,9},{9,8},{10,11... | collective-permute-start | bytes 393224 | tf_op jit(solution)/shard_map/ppermute | solution.py:270
  7.6 1.8 %condition.2.high = bf16[32,2048]{1,0:T(8,128)(2,1)S(1)} custom-call(bf16[1,32,4096]{2,1,0:T(8,128)(2,1)} %queries_in.3, f32[1,64,64]{2,1,0:T(8,128)} %left_in.3, f32[1,64,64]{2,1,0:T(8,128)} %right_in.3), custom_call_target="tpu_custom_call" | custom-call | flops 536870912 | bytes 524288 | tf_op jit(solution)/shard_map/condition/pallas_call | solution.py:109
  9.5 0.4 %collective-permute-start = (bf16[32,2048]{1,0:T(8,128)(2,1)S(1)}, bf16[32,2048]{1,0:T(8,128)(2,1)S(1)}, u32[]{:S(2)}, u32[]{:S(2)}) collective-permute-start(bf16[32,2048]{1,0:T(8,128)(2,1)S(1)} %condition.2.high), channel_id=1, source_target_pairs={{0,2},{1,3},{2,0},{3,1},{4,6},{5,7},{6,4},{7,5},{8,10},{9,11},{10,... | collective-permute-start | bytes 393224 | tf_op jit(solution)/shard_map/ppermute | solution.py:270
  9.9 0.2 collective-permute-start.1
  10.1 4.5 %score_own.1.own = f32[32,1024]{1,0:T(8,128)S(1)} custom-call(bf16[32,2048]{1,0:T(8,128)(2,1)S(1)} %condition.3.low, bf16[32,2048]{1,0:T(8,128)(2,1)S(1)} %condition.2.high, bf16[1,1024,4096]{2,1,0:T(8,128)(2,1)} %store.3), custom_call_target="tpu_custom_call" | custom-call | flops 268435456 | bytes 8388608 | tf_op jit(solution)/shard_map/score_own/pallas_call | solution.py:170
  14.6 0.0 copy-start.1
  14.6 0.0 collective-permute-done.3.far
  14.6 1.9 %collective-permute-start.5 = (bf16[32,2048]{1,0:T(8,128)(2,1)S(1)}, bf16[32,2048]{1,0:T(8,128)(2,1)S(1)}, u32[]{:S(2)}, u32[]{:S(2)}) collective-permute-start(bf16[32,2048]{1,0:T(8,128)(2,1)S(1)} %collective-permute-done.3.far), channel_id=1, source_target_pairs={{0,1},{1,0},{2,3},{3,2},{4,5},{5,4},{6,7},{7,6},{8,9},{9,8},{10,11... | collective-permute-start | bytes 393224 | tf_op jit(solution)/shard_map/ppermute | solution.py:270
  16.5 1.6 %collective-permute-done.far = bf16[32,2048]{1,0:T(8,128)(2,1)S(1)} collective-permute-done((bf16[32,2048]{1,0:T(8,128)(2,1)S(1)}, bf16[32,2048]{1,0:T(8,128)(2,1)S(1)}, u32[]{:S(2)}, u32[]{:S(2)}) %collective-permute-start) | collective-permute-done | bytes 131104 | tf_op jit(solution)/shard_map/ppermute | solution.py:270
  18.1 0.6 %collective-permute-done.1.near = bf16[32,2048]{1,0:T(8,128)(2,1)S(1)} collective-permute-done((bf16[32,2048]{1,0:T(8,128)(2,1)S(1)}, bf16[32,2048]{1,0:T(8,128)(2,1)S(1)}, u32[]{:S(2)}, u32[]{:S(2)}) %collective-permute-start.1) | collective-permute-done | bytes 131104 | tf_op jit(solution)/shard_map/ppermute | solution.py:270
  18.7 2.2 %collective-permute-start.2 = (bf16[32,2048]{1,0:T(8,128)(2,1)S(1)}, bf16[32,2048]{1,0:T(8,128)(2,1)S(1)}, u32[]{:S(2)}, u32[]{:S(2)}) collective-permute-start(bf16[32,2048]{1,0:T(8,128)(2,1)S(1)} %collective-permute-done.far), channel_id=1, source_target_pairs={{0,1},{1,0},{2,3},{3,2},{4,5},{5,4},{6,7},{7,6},{8,9},{9,8},{10,11... | collective-permute-start | bytes 393224 | tf_op jit(solution)/shard_map/ppermute | solution.py:270
  20.9 0.6 %collective-permute-done.5.last = bf16[32,2048]{1,0:T(8,128)(2,1)S(1)} collective-permute-done((bf16[32,2048]{1,0:T(8,128)(2,1)S(1)}, bf16[32,2048]{1,0:T(8,128)(2,1)S(1)}, u32[]{:S(2)}, u32[]{:S(2)}) %collective-permute-start.5) | collective-permute-done | bytes 131104 | tf_op jit(solution)/shard_map/ppermute | solution.py:270
  21.5 1.3 %score_low.1.low = f32[96,1024]{1,0:T(8,128)S(1)} custom-call(bf16[32,2048]{1,0:T(8,128)(2,1)S(1)} %collective-permute-done.4.near, bf16[32,2048]{1,0:T(8,128)(2,1)S(1)} %collective-permute-done.3.far, bf16[32,2048]{1,0:T(8,128)(2,1)S(1)} %collective-permute-done.5.last, bf16[1,1024,4096]{2,1,0:T(8,128)(2,1)S(1)} %copy-done), custom_call_target="tpu_custom_call" | custom-call | flops 402653184 | bytes 4194304 | tf_op jit(solution)/shard_map/score_low/pallas_call | solution.py:196
  22.8 1.1 %collective-permute-done.2.last = bf16[32,2048]{1,0:T(8,128)(2,1)S(1)} collective-permute-done((bf16[32,2048]{1,0:T(8,128)(2,1)S(1)}, bf16[32,2048]{1,0:T(8,128)(2,1)S(1)}, u32[]{:S(2)}, u32[]{:S(2)}) %collective-permute-start.2) | collective-permute-done | bytes 131104 | tf_op jit(solution)/shard_map/ppermute | solution.py:270
  23.9 1.3 %score_high.1 = (f32[32,1024]{1,0:T(8,128)S(1)}, bf16[32,1024]{1,0:T(8,128)(2,1)S(1)}, bf16[32,1024]{1,0:T(8,128)(2,1)S(1)}, bf16[32,1024]{1,0:T(8,128)(2,1)S(1)}) custom-call(bf16[32,2048]{1,0:T(8,128)(2,1)S(1)} %collective-permute-done.1.near, bf16[32,2048]{1,0:T(8,128)(2,1)S(1)} %collective-permute-done.far, ...), custom_call_target="tpu_custom_call" | custom-call | flops 402653184 | bytes 4194304 | tf_op jit(solution)/shard_map/score_high/pallas_call | solution.py:225
  25.3 0.1 collective-permute-start.6
  25.3 1.6 %collective-permute-start.7 = (bf16[32,1024]{1,0:T(8,128)(2,1)S(1)}, bf16[32,1024]{1,0:T(8,128)(2,1)S(1)}, u32[]{:S(2)}, u32[]{:S(2)}) collective-permute-start(bf16[32,1024]{1,0:T(8,128)(2,1)S(1)} %get-tuple-element.21), channel_id=1, source_target_pairs={{0,8},{4,12},{8,0},{12,4},{1,9},{5,13},{9,1},{13,5},{2,10},{6,14},... | collective-permute-start | bytes 196616 | tf_op jit(solution)/shard_map/ppermute | solution.py:270
  26.9 0.3 collective-permute-start.8
  27.2 0.1 copy.6.candidates
  27.3 2.6 %collective-permute-done.7.refs_2_ = bf16[32,1024]{1,0:T(8,128)(2,1)S(1)} collective-permute-done((bf16[32,1024]{1,0:T(8,128)(2,1)S(1)}, bf16[32,1024]{1,0:T(8,128)(2,1)S(1)}, u32[]{:S(2)}, u32[]{:S(2)}) %collective-permute-start.7) | collective-permute-done | bytes 65568 | tf_op jit(solution)/shard_map/ppermute | solution.py:270
  29.8 1.1 %collective-permute-done.8.refs_3_ = bf16[32,1024]{1,0:T(8,128)(2,1)S(1)} collective-permute-done((bf16[32,1024]{1,0:T(8,128)(2,1)S(1)}, bf16[32,1024]{1,0:T(8,128)(2,1)S(1)}, u32[]{:S(2)}, u32[]{:S(2)}) %collective-permute-start.8) | collective-permute-done | bytes 65568 | tf_op jit(solution)/shard_map/ppermute | solution.py:270
  31.0 0.7 %finish.1 = bf16[32,1024]{1,0:T(8,128)(2,1)} custom-call(s32[32,16]{1,0:T(8,128)S(1)} %copy.6.candidates, f32[32,1024]{1,0:T(8,128)S(1)} %get-tuple-element.19.refs_0_, bf16[32,1024]{1,0:T(8,128)(2,1)S(1)} %collective-permute-done.6.refs_1_, bf16[32,1024]{1,0:T(8,128)(2,1)S(1)} %collective-permute-done.7.refs_2_, ...), custom_call_target="tpu_custom_call" | custom-call | tf_op jit(solution)/shard_map/finish/pallas_call | solution.py:258
  (5 shorter events, 0.0 us)
Async XLA Ops:
  0.0 21.5 %copy-start = (bf16[1,1024,4096]{2,1,0:T(8,128)(2,1)S(1)}, bf16[1,1024,4096]{2,1,0:T(8,128)(2,1)}, u32[]{:S(2)}) copy-start(bf16[1,1024,4096]{2,1,0:T(8,128)(2,1)} %store.3) | copy-start | bytes 25165828
  2.0 12.6 %collective-permute-start.3 = (bf16[32,2048]{1,0:T(8,128)(2,1)S(1)}, bf16[32,2048]{1,0:T(8,128)(2,1)S(1)}, u32[]{:S(2)}, u32[]{:S(2)}) collective-permute-start(bf16[32,2048]{1,0:T(8,128)(2,1)S(1)} %condition.3.low), channel_id=1, source_target_pairs={{0,2},{1,3},{2,0},{3,1},{4,6},{5,7},{6,4},{7,5},{8,10},{9,11},{10,... | collective-permute-start | bytes 393224 | tf_op jit(solution)/shard_map/ppermute | solution.py:270
  6.1 8.5 %collective-permute-start.4 = (bf16[32,2048]{1,0:T(8,128)(2,1)S(1)}, bf16[32,2048]{1,0:T(8,128)(2,1)S(1)}, u32[]{:S(2)}, u32[]{:S(2)}) collective-permute-start(bf16[32,2048]{1,0:T(8,128)(2,1)S(1)} %condition.3.low), channel_id=1, source_target_pairs={{0,1},{1,0},{2,3},{3,2},{4,5},{5,4},{6,7},{7,6},{8,9},{9,8},{10,11... | collective-permute-start | bytes 393224 | tf_op jit(solution)/shard_map/ppermute | solution.py:270
  9.5 8.6 %collective-permute-start = (bf16[32,2048]{1,0:T(8,128)(2,1)S(1)}, bf16[32,2048]{1,0:T(8,128)(2,1)S(1)}, u32[]{:S(2)}, u32[]{:S(2)}) collective-permute-start(bf16[32,2048]{1,0:T(8,128)(2,1)S(1)} %condition.2.high), channel_id=1, source_target_pairs={{0,2},{1,3},{2,0},{3,1},{4,6},{5,7},{6,4},{7,5},{8,10},{9,11},{10,... | collective-permute-start | bytes 393224 | tf_op jit(solution)/shard_map/ppermute | solution.py:270
  9.9 8.8 %collective-permute-start.1 = (bf16[32,2048]{1,0:T(8,128)(2,1)S(1)}, bf16[32,2048]{1,0:T(8,128)(2,1)S(1)}, u32[]{:S(2)}, u32[]{:S(2)}) collective-permute-start(bf16[32,2048]{1,0:T(8,128)(2,1)S(1)} %condition.2.high), channel_id=1, source_target_pairs={{0,1},{1,0},{2,3},{3,2},{4,5},{5,4},{6,7},{7,6},{8,9},{9,8},{10,11... | collective-permute-start | bytes 393224 | tf_op jit(solution)/shard_map/ppermute | solution.py:270
  14.6 12.6 %copy-start.1 = (s32[32,16]{0,1:T(8,128)S(1)}, s32[32,16]{0,1:T(8,128)}, u32[]{:S(2)}) copy-start(s32[32,16]{0,1:T(8,128)} %param.9) | copy-start | bytes 6148
  14.6 6.9 %collective-permute-start.5 = (bf16[32,2048]{1,0:T(8,128)(2,1)S(1)}, bf16[32,2048]{1,0:T(8,128)(2,1)S(1)}, u32[]{:S(2)}, u32[]{:S(2)}) collective-permute-start(bf16[32,2048]{1,0:T(8,128)(2,1)S(1)} %collective-permute-done.3.far), channel_id=1, source_target_pairs={{0,1},{1,0},{2,3},{3,2},{4,5},{5,4},{6,7},{7,6},{8,9},{9,8},{10,11... | collective-permute-start | bytes 393224 | tf_op jit(solution)/shard_map/ppermute | solution.py:270
  18.7 5.2 %collective-permute-start.2 = (bf16[32,2048]{1,0:T(8,128)(2,1)S(1)}, bf16[32,2048]{1,0:T(8,128)(2,1)S(1)}, u32[]{:S(2)}, u32[]{:S(2)}) collective-permute-start(bf16[32,2048]{1,0:T(8,128)(2,1)S(1)} %collective-permute-done.far), channel_id=1, source_target_pairs={{0,1},{1,0},{2,3},{3,2},{4,5},{5,4},{6,7},{7,6},{8,9},{9,8},{10,11... | collective-permute-start | bytes 393224 | tf_op jit(solution)/shard_map/ppermute | solution.py:270
  25.3 2.0 %collective-permute-start.6 = (bf16[32,1024]{1,0:T(8,128)(2,1)S(1)}, bf16[32,1024]{1,0:T(8,128)(2,1)S(1)}, u32[]{:S(2)}, u32[]{:S(2)}) collective-permute-start(bf16[32,1024]{1,0:T(8,128)(2,1)S(1)} %get-tuple-element.20), channel_id=1, source_target_pairs={{0,4},{4,0},{8,12},{12,8},{1,5},{5,1},{9,13},{13,9},{2,6},{6,2},{1... | collective-permute-start | bytes 196616 | tf_op jit(solution)/shard_map/ppermute | solution.py:270
  25.3 4.5 %collective-permute-start.7 = (bf16[32,1024]{1,0:T(8,128)(2,1)S(1)}, bf16[32,1024]{1,0:T(8,128)(2,1)S(1)}, u32[]{:S(2)}, u32[]{:S(2)}) collective-permute-start(bf16[32,1024]{1,0:T(8,128)(2,1)S(1)} %get-tuple-element.21), channel_id=1, source_target_pairs={{0,8},{4,12},{8,0},{12,4},{1,9},{5,13},{9,1},{13,5},{2,10},{6,14},... | collective-permute-start | bytes 196616 | tf_op jit(solution)/shard_map/ppermute | solution.py:270
  26.9 4.0 %collective-permute-start.8 = (bf16[32,1024]{1,0:T(8,128)(2,1)S(1)}, bf16[32,1024]{1,0:T(8,128)(2,1)S(1)}, u32[]{:S(2)}, u32[]{:S(2)}) collective-permute-start(bf16[32,1024]{1,0:T(8,128)(2,1)S(1)} %get-tuple-element.22), channel_id=1, source_target_pairs={{0,12},{4,8},{8,4},{12,0},{1,13},{5,9},{9,5},{13,1},{2,14},{6,10},... | collective-permute-start | bytes 196616 | tf_op jit(solution)/shard_map/ppermute | solution.py:270

commit v11 on v10

--- a/solution.py
+++ b/solution.py
@@ -183,10 +183,11 @@
     return jnp.concatenate([block[...] for block in blocks], axis=0)
 
 
-def low_kernel(near, far, last, store, out):
+def low_kernel(near_first, near_second, far, last, store, out):
     def write(place, value):
         out[:, place] = value
 
+    near = (near_first[...].astype(jnp.float32) + near_second[...].astype(jnp.float32)).astype(jnp.bfloat16)
     score_block(stacked(near, far, last), store, 0, write, step_rows=store.shape[1])
 
 
@@ -195,13 +196,13 @@
     examples = store.shape[1]
     return pl.pallas_call(
         low_kernel,
-        in_specs=in_vmem(4),
+        in_specs=in_vmem(5),
         out_specs=in_vmem(1)[0],
         out_shape=jax.ShapeDtypeStruct((3 * rows, examples), jnp.float32),
         compiler_params=pltpu.CompilerParams(vmem_limit_bytes=VMEM),
         cost_estimate=score_cost(3 * rows, width, examples),
         name="score_low",
-    )(near, far, last, store)
+    )(*near, far, last, store)
 
 
 def high_kernel(first, near, far, last, store, own, low, *refs):
@@ -276,13 +277,16 @@
 
 def on_line(own, store, candidates, layers):
     far = [swapped(half, "blk", 2) for half in own]
-    near = [swapped(half, "blk", 1) for half in own]
+    near_first, near_second = [lax.ppermute(own[0], "blk", pairs) for pairs in ([(0, 1), (1, 0)], [(2, 3), (3, 2)])]
+    near_high = swapped(own[1], "blk", 1)
     own_scores = score_own(own, store)
-    far[0], near[0], own_scores = lax.optimization_barrier((far[0], near[0], own_scores))
-    far[1], near[1] = lax.optimization_barrier((far[1], near[1]))
+    near_first, far[0], near_second, own_scores = lax.optimization_barrier(
+        (near_first, far[0], near_second, own_scores)
+    )
+    near_high, far[1] = lax.optimization_barrier((near_high, far[1]))
     last = [swapped(half, "blk", 1) for half in far]
-    low_scores = score_low(near[0], far[0], last[0], store)
-    parts = score_high(near[1], far[1], last[1], store, own_scores, low_scores)
+    low_scores = score_low([near_first, near_second], far[0], last[0], store)
+    parts = score_high(near_high, far[1], last[1], store, own_scores, low_scores)
     received = [swapped(parts[mask], "layer", mask) for mask in (1, 2, 3)]
     return finish([parts[0]] + received, candidates, layers)
 

time: 31.9 us -> 35.1 us (1.10)
  starting transfers between devices: 12.3 us -> 16.7 us
  waiting for transfers between devices: 7.62 us -> 6.36 us
    ppermute x0 -> x2, starting transfers between devices: none -> 5.73 us  [on_line(): lax.ppermute(own[0], 'blk', pairs)]
    ppermute x9 -> x8, starting transfers between devices: 12.3 us -> 10.9 us  [permuted(): lax.ppermute(value, axis, [(source, target_of(source) % count) for source...]
    ppermute x9 -> x8, waiting for transfers between devices: 7.62 us -> 6.35 us  [permuted(): lax.ppermute(value, axis, [(source, target_of(source) % count) for source...]
  transfers between devices with their start and end apart: 9 -> 10, of which waited for: 6 -> 4; matrix products, arithmetic and copies ran while one was open for 0% -> 0% of each run, Pallas kernels for 24% -> 22%
where the time goes in v11:
time: 35.1 us; the launch traced here: 34.9 us
  starting transfers between devices  16.7 us (48%)
  Pallas kernels  11.7 us (33%)
  waiting for transfers between devices  6.36 us (18%)
    ppermute x8, starting transfers between devices, permuted(): lax.ppermute(value, axis, [(source, target_of(source) % count) for source...  10.9 us
    ppermute x8, waiting for transfers between devices, permuted(): lax.ppermute(value, axis, [(source, target_of(source) % count) for source...  6.35 us
    ppermute x2, starting transfers between devices, on_line(): lax.ppermute(own[0], 'blk', pairs)  5.73 us
    pallas_call x1, Pallas kernels, score_own(): pl.pallas_call(own_kernel, in_specs=in_vmem(2) + [pl.BlockSpec(memory_spa...  4.53 us
    pallas_call x2, Pallas kernels, condition(): pl.pallas_call(functools.partial(condition_kernel, half * side // 2, side...  3.76 us
    pallas_call x1, Pallas kernels, score_high(): pl.pallas_call(functools.partial(high_kernel, store.shape[2] - width), in...  1.34 us
    pallas_call x1, Pallas kernels, score_low(): pl.pallas_call(low_kernel, in_specs=in_vmem(5), out_specs=in_vmem(1)[0],...  1.31 us
    pallas_call x1, Pallas kernels, finish(): pl.pallas_call(functools.partial(finish_kernel, layers), in_specs=in_vmem...  0.74 us
  transfers between devices with their start and end apart: 10, of which 4 were waited for; matrix products, arithmetic and copies ran while one was open for 0% of the time, Pallas kernels for 22%

profile of v11, /device:TPU:0, one launch (start us, length us, event | category | flops | bytes accessed | tf_op | source)
XLA Modules:
  0.0 34.9 jit_solution(4902342104918280714)
XLA Ops:
  0.0 2.0 %condition.3.low = bf16[32,2048]{1,0:T(8,128)(2,1)S(1)} custom-call(bf16[1,32,4096]{2,1,0:T(8,128)(2,1)} %queries_in.3, f32[1,64,64]{2,1,0:T(8,128)} %left_in.3, f32[1,64,64]{2,1,0:T(8,128)} %right_in.3), custom_call_target="tpu_custom_call" | custom-call | flops 536870912 | bytes 524288 | tf_op jit(solution)/shard_map/condition/pallas_call | solution.py:109
  2.0 5.1 %collective-permute-start.3 = (bf16[32,2048]{1,0:T(8,128)(2,1)S(1)}, bf16[32,2048]{1,0:T(8,128)(2,1)S(1)}, u32[]{:S(2)}, u32[]{:S(2)}) collective-permute-start(bf16[32,2048]{1,0:T(8,128)(2,1)S(1)} %condition.3.low), channel_id=1, source_target_pairs={{0,1},{1,0},{4,5},{5,4},{8,9},{9,8},{12,13},{13,12},{16,17},{17,16... | collective-permute-start | bytes 393224 | tf_op jit(solution)/shard_map/ppermute | solution.py:280
  7.0 0.1 collective-permute-start.4
  7.1 0.7 %collective-permute-start.5 = (bf16[32,2048]{1,0:T(8,128)(2,1)S(1)}, bf16[32,2048]{1,0:T(8,128)(2,1)S(1)}, u32[]{:S(2)}, u32[]{:S(2)}) collective-permute-start(bf16[32,2048]{1,0:T(8,128)(2,1)S(1)} %condition.3.low), channel_id=1, source_target_pairs={{2,3},{3,2},{6,7},{7,6},{10,11},{11,10},{14,15},{15,14},{18,19},{1... | collective-permute-start | bytes 393224 | tf_op jit(solution)/shard_map/ppermute | solution.py:280
  7.8 1.8 %condition.2.high = bf16[32,2048]{1,0:T(8,128)(2,1)S(1)} custom-call(bf16[1,32,4096]{2,1,0:T(8,128)(2,1)} %queries_in.3, f32[1,64,64]{2,1,0:T(8,128)} %left_in.3, f32[1,64,64]{2,1,0:T(8,128)} %right_in.3), custom_call_target="tpu_custom_call" | custom-call | flops 536870912 | bytes 524288 | tf_op jit(solution)/shard_map/condition/pallas_call | solution.py:109
  9.6 1.4 %collective-permute-start = (bf16[32,2048]{1,0:T(8,128)(2,1)S(1)}, bf16[32,2048]{1,0:T(8,128)(2,1)S(1)}, u32[]{:S(2)}, u32[]{:S(2)}) collective-permute-start(bf16[32,2048]{1,0:T(8,128)(2,1)S(1)} %condition.2.high), channel_id=1, source_target_pairs={{0,1},{1,0},{2,3},{3,2},{4,5},{5,4},{6,7},{7,6},{8,9},{9,8},{10,11... | collective-permute-start | bytes 393224 | tf_op jit(solution)/shard_map/ppermute | solution.py:271
  11.0 4.8 %collective-permute-start.1 = (bf16[32,2048]{1,0:T(8,128)(2,1)S(1)}, bf16[32,2048]{1,0:T(8,128)(2,1)S(1)}, u32[]{:S(2)}, u32[]{:S(2)}) collective-permute-start(bf16[32,2048]{1,0:T(8,128)(2,1)S(1)} %condition.2.high), channel_id=1, source_target_pairs={{0,2},{1,3},{2,0},{3,1},{4,6},{5,7},{6,4},{7,5},{8,10},{9,11},{10,... | collective-permute-start | bytes 393224 | tf_op jit(solution)/shard_map/ppermute | solution.py:271
  15.8 4.5 %score_own.1.own = f32[32,1024]{1,0:T(8,128)S(1)} custom-call(bf16[32,2048]{1,0:T(8,128)(2,1)S(1)} %condition.3.low, bf16[32,2048]{1,0:T(8,128)(2,1)S(1)} %condition.2.high, bf16[1,1024,4096]{2,1,0:T(8,128)(2,1)} %store.3), custom_call_target="tpu_custom_call" | custom-call | flops 268435456 | bytes 8388608 | tf_op jit(solution)/shard_map/score_own/pallas_call | solution.py:170
  20.4 0.0 copy-start.1
  20.4 0.0 collective-permute-done.3.near_first
  20.4 0.0 collective-permute-done.4.far
  20.4 0.1 collective-permute-start.6
  20.6 2.6 %collective-permute-start.2 = (bf16[32,2048]{1,0:T(8,128)(2,1)S(1)}, bf16[32,2048]{1,0:T(8,128)(2,1)S(1)}, u32[]{:S(2)}, u32[]{:S(2)}) collective-permute-start(bf16[32,2048]{1,0:T(8,128)(2,1)S(1)} %collective-permute-done.1.far), channel_id=1, source_target_pairs={{0,1},{1,0},{2,3},{3,2},{4,5},{5,4},{6,7},{7,6},{8,9},{9,8},{10,11... | collective-permute-start | bytes 393224 | tf_op jit(solution)/shard_map/ppermute | solution.py:271
  23.1 2.6 %collective-permute-done.6.last = bf16[32,2048]{1,0:T(8,128)(2,1)S(1)} collective-permute-done((bf16[32,2048]{1,0:T(8,128)(2,1)S(1)}, bf16[32,2048]{1,0:T(8,128)(2,1)S(1)}, u32[]{:S(2)}, u32[]{:S(2)}) %collective-permute-start.6) | collective-permute-done | bytes 131104 | tf_op jit(solution)/shard_map/ppermute | solution.py:271
  25.7 1.3 %score_low.1.low = f32[96,1024]{1,0:T(8,128)S(1)} custom-call(bf16[32,2048]{1,0:T(8,128)(2,1)S(1)} %collective-permute-done.3.near_first, bf16[32,2048]{1,0:T(8,128)(2,1)S(1)} %collective-permute-done.5.near_second, bf16[32,2048]{1,0:T(8,128)(2,1)S(1)} %collective-permute-done.4.far, bf16[32,2048]{1,0:T(8,128)(2,1)S(1)} %collective-permute-done.6.last, ...), custom_call_target="tpu_custom_call" | custom-call | flops 402653184 | bytes 4194304 | tf_op jit(solution)/shard_map/score_low/pallas_call | solution.py:197
  27.0 0.1 collective-permute-done.2.last
  27.1 1.3 %score_high.1 = (f32[32,1024]{1,0:T(8,128)S(1)}, bf16[32,1024]{1,0:T(8,128)(2,1)S(1)}, bf16[32,1024]{1,0:T(8,128)(2,1)S(1)}, bf16[32,1024]{1,0:T(8,128)(2,1)S(1)}) custom-call(bf16[32,2048]{1,0:T(8,128)(2,1)S(1)} %collective-permute-done.near, bf16[32,2048]{1,0:T(8,128)(2,1)S(1)} %collective-permute-done.1.far, ...), custom_call_target="tpu_custom_call" | custom-call | flops 402653184 | bytes 4194304 | tf_op jit(solution)/shard_map/score_high/pallas_call | solution.py:226
  28.5 0.1 collective-permute-start.7
  28.5 1.6 %collective-permute-start.8 = (bf16[32,1024]{1,0:T(8,128)(2,1)S(1)}, bf16[32,1024]{1,0:T(8,128)(2,1)S(1)}, u32[]{:S(2)}, u32[]{:S(2)}) collective-permute-start(bf16[32,1024]{1,0:T(8,128)(2,1)S(1)} %get-tuple-element.23), channel_id=1, source_target_pairs={{0,8},{4,12},{8,0},{12,4},{1,9},{5,13},{9,1},{13,5},{2,10},{6,14},... | collective-permute-start | bytes 196616 | tf_op jit(solution)/shard_map/ppermute | solution.py:271
  30.1 0.3 collective-permute-start.9
  30.4 0.1 copy.6.candidates
  30.5 2.6 %collective-permute-done.8.refs_2_ = bf16[32,1024]{1,0:T(8,128)(2,1)S(1)} collective-permute-done((bf16[32,1024]{1,0:T(8,128)(2,1)S(1)}, bf16[32,1024]{1,0:T(8,128)(2,1)S(1)}, u32[]{:S(2)}, u32[]{:S(2)}) %collective-permute-start.8) | collective-permute-done | bytes 65568 | tf_op jit(solution)/shard_map/ppermute | solution.py:271
  33.1 1.1 %collective-permute-done.9.refs_3_ = bf16[32,1024]{1,0:T(8,128)(2,1)S(1)} collective-permute-done((bf16[32,1024]{1,0:T(8,128)(2,1)S(1)}, bf16[32,1024]{1,0:T(8,128)(2,1)S(1)}, u32[]{:S(2)}, u32[]{:S(2)}) %collective-permute-start.9) | collective-permute-done | bytes 65568 | tf_op jit(solution)/shard_map/ppermute | solution.py:271
  34.2 0.7 %finish.1 = bf16[32,1024]{1,0:T(8,128)(2,1)} custom-call(s32[32,16]{1,0:T(8,128)S(1)} %copy.6.candidates, f32[32,1024]{1,0:T(8,128)S(1)} %get-tuple-element.21.refs_0_, bf16[32,1024]{1,0:T(8,128)(2,1)S(1)} %collective-permute-done.7.refs_1_, bf16[32,1024]{1,0:T(8,128)(2,1)S(1)} %collective-permute-done.8.refs_2_, ...), custom_call_target="tpu_custom_call" | custom-call | tf_op jit(solution)/shard_map/finish/pallas_call | solution.py:259
  (7 shorter events, 0.0 us)
Async XLA Ops:
  0.0 25.7 %copy-start = (bf16[1,1024,4096]{2,1,0:T(8,128)(2,1)S(1)}, bf16[1,1024,4096]{2,1,0:T(8,128)(2,1)}, u32[]{:S(2)}) copy-start(bf16[1,1024,4096]{2,1,0:T(8,128)(2,1)} %store.3) | copy-start | bytes 25165828
  2.0 18.4 %collective-permute-start.3 = (bf16[32,2048]{1,0:T(8,128)(2,1)S(1)}, bf16[32,2048]{1,0:T(8,128)(2,1)S(1)}, u32[]{:S(2)}, u32[]{:S(2)}) collective-permute-start(bf16[32,2048]{1,0:T(8,128)(2,1)S(1)} %condition.3.low), channel_id=1, source_target_pairs={{0,1},{1,0},{4,5},{5,4},{8,9},{9,8},{12,13},{13,12},{16,17},{17,16... | collective-permute-start | bytes 393224 | tf_op jit(solution)/shard_map/ppermute | solution.py:280
  7.0 13.4 %collective-permute-start.4 = (bf16[32,2048]{1,0:T(8,128)(2,1)S(1)}, bf16[32,2048]{1,0:T(8,128)(2,1)S(1)}, u32[]{:S(2)}, u32[]{:S(2)}) collective-permute-start(bf16[32,2048]{1,0:T(8,128)(2,1)S(1)} %condition.3.low), channel_id=1, source_target_pairs={{0,2},{1,3},{2,0},{3,1},{4,6},{5,7},{6,4},{7,5},{8,10},{9,11},{10,... | collective-permute-start | bytes 393224 | tf_op jit(solution)/shard_map/ppermute | solution.py:271
  7.1 13.3 %collective-permute-start.5 = (bf16[32,2048]{1,0:T(8,128)(2,1)S(1)}, bf16[32,2048]{1,0:T(8,128)(2,1)S(1)}, u32[]{:S(2)}, u32[]{:S(2)}) collective-permute-start(bf16[32,2048]{1,0:T(8,128)(2,1)S(1)} %condition.3.low), channel_id=1, source_target_pairs={{2,3},{3,2},{6,7},{7,6},{10,11},{11,10},{14,15},{15,14},{18,19},{1... | collective-permute-start | bytes 393224 | tf_op jit(solution)/shard_map/ppermute | solution.py:280
  9.6 11.0 %collective-permute-start = (bf16[32,2048]{1,0:T(8,128)(2,1)S(1)}, bf16[32,2048]{1,0:T(8,128)(2,1)S(1)}, u32[]{:S(2)}, u32[]{:S(2)}) collective-permute-start(bf16[32,2048]{1,0:T(8,128)(2,1)S(1)} %condition.2.high), channel_id=1, source_target_pairs={{0,1},{1,0},{2,3},{3,2},{4,5},{5,4},{6,7},{7,6},{8,9},{9,8},{10,11... | collective-permute-start | bytes 393224 | tf_op jit(solution)/shard_map/ppermute | solution.py:271
  11.0 9.6 %collective-permute-start.1 = (bf16[32,2048]{1,0:T(8,128)(2,1)S(1)}, bf16[32,2048]{1,0:T(8,128)(2,1)S(1)}, u32[]{:S(2)}, u32[]{:S(2)}) collective-permute-start(bf16[32,2048]{1,0:T(8,128)(2,1)S(1)} %condition.2.high), channel_id=1, source_target_pairs={{0,2},{1,3},{2,0},{3,1},{4,6},{5,7},{6,4},{7,5},{8,10},{9,11},{10,... | collective-permute-start | bytes 393224 | tf_op jit(solution)/shard_map/ppermute | solution.py:271
  20.4 10.0 %copy-start.1 = (s32[32,16]{0,1:T(8,128)S(1)}, s32[32,16]{0,1:T(8,128)}, u32[]{:S(2)}) copy-start(s32[32,16]{0,1:T(8,128)} %param.9) | copy-start | bytes 6148
  20.4 5.3 %collective-permute-start.6 = (bf16[32,2048]{1,0:T(8,128)(2,1)S(1)}, bf16[32,2048]{1,0:T(8,128)(2,1)S(1)}, u32[]{:S(2)}, u32[]{:S(2)}) collective-permute-start(bf16[32,2048]{1,0:T(8,128)(2,1)S(1)} %collective-permute-done.4.far), channel_id=1, source_target_pairs={{0,1},{1,0},{2,3},{3,2},{4,5},{5,4},{6,7},{7,6},{8,9},{9,8},{10,11... | collective-permute-start | bytes 393224 | tf_op jit(solution)/shard_map/ppermute | solution.py:271
  20.6 6.5 %collective-permute-start.2 = (bf16[32,2048]{1,0:T(8,128)(2,1)S(1)}, bf16[32,2048]{1,0:T(8,128)(2,1)S(1)}, u32[]{:S(2)}, u32[]{:S(2)}) collective-permute-start(bf16[32,2048]{1,0:T(8,128)(2,1)S(1)} %collective-permute-done.1.far), channel_id=1, source_target_pairs={{0,1},{1,0},{2,3},{3,2},{4,5},{5,4},{6,7},{7,6},{8,9},{9,8},{10,11... | collective-permute-start | bytes 393224 | tf_op jit(solution)/shard_map/ppermute | solution.py:271
  28.5 2.0 %collective-permute-start.7 = (bf16[32,1024]{1,0:T(8,128)(2,1)S(1)}, bf16[32,1024]{1,0:T(8,128)(2,1)S(1)}, u32[]{:S(2)}, u32[]{:S(2)}) collective-permute-start(bf16[32,1024]{1,0:T(8,128)(2,1)S(1)} %get-tuple-element.22), channel_id=1, source_target_pairs={{0,4},{4,0},{8,12},{12,8},{1,5},{5,1},{9,13},{13,9},{2,6},{6,2},{1... | collective-permute-start | bytes 196616 | tf_op jit(solution)/shard_map/ppermute | solution.py:271
  28.5 4.5 %collective-permute-start.8 = (bf16[32,1024]{1,0:T(8,128)(2,1)S(1)}, bf16[32,1024]{1,0:T(8,128)(2,1)S(1)}, u32[]{:S(2)}, u32[]{:S(2)}) collective-permute-start(bf16[32,1024]{1,0:T(8,128)(2,1)S(1)} %get-tuple-element.23), channel_id=1, source_target_pairs={{0,8},{4,12},{8,0},{12,4},{1,9},{5,13},{9,1},{13,5},{2,10},{6,14},... | collective-permute-start | bytes 196616 | tf_op jit(solution)/shard_map/ppermute | solution.py:271
  30.1 4.0 %collective-permute-start.9 = (bf16[32,1024]{1,0:T(8,128)(2,1)S(1)}, bf16[32,1024]{1,0:T(8,128)(2,1)S(1)}, u32[]{:S(2)}, u32[]{:S(2)}) collective-permute-start(bf16[32,1024]{1,0:T(8,128)(2,1)S(1)} %get-tuple-element.24), channel_id=1, source_target_pairs={{0,12},{4,8},{8,4},{12,0},{1,13},{5,9},{9,5},{13,1},{2,14},{6,10},... | collective-permute-start | bytes 196616 | tf_op jit(solution)/shard_map/ppermute | solution.py:271

commit v12 on v11

--- a/solution.py
+++ b/solution.py
@@ -187,7 +187,9 @@
     def write(place, value):
         out[:, place] = value
 
-    near = (near_first[...].astype(jnp.float32) + near_second[...].astype(jnp.float32)).astype(jnp.bfloat16)
+    in_first = lax.axis_index("blk") < 2
+    near = jnp.where(in_first, near_first[...].astype(jnp.float32), near_second[...].astype(jnp.float32))
+    near = near.astype(jnp.bfloat16)
     score_block(stacked(near, far, last), store, 0, write, step_rows=store.shape[1])
 
 
@@ -277,7 +279,7 @@
 
 def on_line(own, store, candidates, layers):
     far = [swapped(half, "blk", 2) for half in own]
-    near_first, near_second = [lax.ppermute(own[0], "blk", pairs) for pairs in ([(0, 1), (1, 0)], [(2, 3), (3, 2)])]
+    near_first, near_second = [lax.ppermute(own[0], "blk", pairs) for pairs in ([(0, 1), (1, 0), (2, 2), (3, 3)], [(0, 0), (1, 1), (2, 3), (3, 2)])]
     near_high = swapped(own[1], "blk", 1)
     own_scores = score_own(own, store)
     near_first, far[0], near_second, own_scores = lax.optimization_barrier(

time: 35.1 us -> 35.1 us (level)
  no operation moved by 1% of the time
where the time goes in v12:
time: 35.1 us; the launch traced here: 34.9 us
  starting transfers between devices  16.7 us (48%)
  Pallas kernels  11.7 us (33%)
  waiting for transfers between devices  6.36 us (18%)
    ppermute x8, starting transfers between devices, permuted(): lax.ppermute(value, axis, [(source, target_of(source) % count) for source...  10.9 us
    ppermute x8, waiting for transfers between devices, permuted(): lax.ppermute(value, axis, [(source, target_of(source) % count) for source...  6.36 us
    ppermute x2, starting transfers between devices, on_line(): lax.ppermute(own[0], 'blk', pairs)  5.73 us
    pallas_call x1, Pallas kernels, score_own(): pl.pallas_call(own_kernel, in_specs=in_vmem(2) + [pl.BlockSpec(memory_spa...  4.53 us
    pallas_call x2, Pallas kernels, condition(): pl.pallas_call(functools.partial(condition_kernel, half * side // 2, side...  3.76 us
    pallas_call x1, Pallas kernels, score_high(): pl.pallas_call(functools.partial(high_kernel, store.shape[2] - width), in...  1.34 us
    pallas_call x1, Pallas kernels, score_low(): pl.pallas_call(low_kernel, in_specs=in_vmem(5), out_specs=in_vmem(1)[0],...  1.31 us
    pallas_call x1, Pallas kernels, finish(): pl.pallas_call(functools.partial(finish_kernel, layers), in_specs=in_vmem...  0.74 us
  transfers between devices with their start and end apart: 10, of which 4 were waited for; matrix products, arithmetic and copies ran while one was open for 0% of the time, Pallas kernels for 22%

profile of v12, /device:TPU:0, one launch (start us, length us, event | category | flops | bytes accessed | tf_op | source)
XLA Modules:
  0.0 34.9 jit_solution(720881515828731441)
XLA Ops:
  0.0 2.0 %condition.3.low = bf16[32,2048]{1,0:T(8,128)(2,1)S(1)} custom-call(bf16[1,32,4096]{2,1,0:T(8,128)(2,1)} %queries_in.3, f32[1,64,64]{2,1,0:T(8,128)} %left_in.3, f32[1,64,64]{2,1,0:T(8,128)} %right_in.3), custom_call_target="tpu_custom_call" | custom-call | flops 536870912 | bytes 524288 | tf_op jit(solution)/shard_map/condition/pallas_call | solution.py:109
  2.0 5.1 %collective-permute-start.3 = (bf16[32,2048]{1,0:T(8,128)(2,1)S(1)}, bf16[32,2048]{1,0:T(8,128)(2,1)S(1)}, u32[]{:S(2)}, u32[]{:S(2)}) collective-permute-start(bf16[32,2048]{1,0:T(8,128)(2,1)S(1)} %condition.3.low), channel_id=1, source_target_pairs={{0,1},{1,0},{2,2},{3,3},{4,5},{5,4},{6,6},{7,7},{8,9},{9,8},{10,10... | collective-permute-start | bytes 393224 | tf_op jit(solution)/shard_map/ppermute | solution.py:282
  7.0 0.1 collective-permute-start.4
  7.1 0.7 %collective-permute-start.5 = (bf16[32,2048]{1,0:T(8,128)(2,1)S(1)}, bf16[32,2048]{1,0:T(8,128)(2,1)S(1)}, u32[]{:S(2)}, u32[]{:S(2)}) collective-permute-start(bf16[32,2048]{1,0:T(8,128)(2,1)S(1)} %condition.3.low), channel_id=1, source_target_pairs={{0,0},{1,1},{2,3},{3,2},{4,4},{5,5},{6,7},{7,6},{8,8},{9,9},{10,11... | collective-permute-start | bytes 393224 | tf_op jit(solution)/shard_map/ppermute | solution.py:282
  7.8 1.8 %condition.2.high = bf16[32,2048]{1,0:T(8,128)(2,1)S(1)} custom-call(bf16[1,32,4096]{2,1,0:T(8,128)(2,1)} %queries_in.3, f32[1,64,64]{2,1,0:T(8,128)} %left_in.3, f32[1,64,64]{2,1,0:T(8,128)} %right_in.3), custom_call_target="tpu_custom_call" | custom-call | flops 536870912 | bytes 524288 | tf_op jit(solution)/shard_map/condition/pallas_call | solution.py:109
  9.6 1.4 %collective-permute-start = (bf16[32,2048]{1,0:T(8,128)(2,1)S(1)}, bf16[32,2048]{1,0:T(8,128)(2,1)S(1)}, u32[]{:S(2)}, u32[]{:S(2)}) collective-permute-start(bf16[32,2048]{1,0:T(8,128)(2,1)S(1)} %condition.2.high), channel_id=1, source_target_pairs={{0,1},{1,0},{2,3},{3,2},{4,5},{5,4},{6,7},{7,6},{8,9},{9,8},{10,11... | collective-permute-start | bytes 393224 | tf_op jit(solution)/shard_map/ppermute | solution.py:273
  11.0 4.8 %collective-permute-start.1 = (bf16[32,2048]{1,0:T(8,128)(2,1)S(1)}, bf16[32,2048]{1,0:T(8,128)(2,1)S(1)}, u32[]{:S(2)}, u32[]{:S(2)}) collective-permute-start(bf16[32,2048]{1,0:T(8,128)(2,1)S(1)} %condition.2.high), channel_id=1, source_target_pairs={{0,2},{1,3},{2,0},{3,1},{4,6},{5,7},{6,4},{7,5},{8,10},{9,11},{10,... | collective-permute-start | bytes 393224 | tf_op jit(solution)/shard_map/ppermute | solution.py:273
  15.8 4.5 %score_own.1.own = f32[32,1024]{1,0:T(8,128)S(1)} custom-call(bf16[32,2048]{1,0:T(8,128)(2,1)S(1)} %condition.3.low, bf16[32,2048]{1,0:T(8,128)(2,1)S(1)} %condition.2.high, bf16[1,1024,4096]{2,1,0:T(8,128)(2,1)} %store.3), custom_call_target="tpu_custom_call" | custom-call | flops 268435456 | bytes 8388608 | tf_op jit(solution)/shard_map/score_own/pallas_call | solution.py:170
  20.4 0.0 copy-start.1
  20.4 0.0 collective-permute-done.3.near_first
  20.4 0.0 collective-permute-done.4.far
  20.4 0.1 collective-permute-start.6
  20.6 2.6 %collective-permute-start.2 = (bf16[32,2048]{1,0:T(8,128)(2,1)S(1)}, bf16[32,2048]{1,0:T(8,128)(2,1)S(1)}, u32[]{:S(2)}, u32[]{:S(2)}) collective-permute-start(bf16[32,2048]{1,0:T(8,128)(2,1)S(1)} %collective-permute-done.1.far), channel_id=1, source_target_pairs={{0,1},{1,0},{2,3},{3,2},{4,5},{5,4},{6,7},{7,6},{8,9},{9,8},{10,11... | collective-permute-start | bytes 393224 | tf_op jit(solution)/shard_map/ppermute | solution.py:273
  23.1 2.6 %collective-permute-done.6.last = bf16[32,2048]{1,0:T(8,128)(2,1)S(1)} collective-permute-done((bf16[32,2048]{1,0:T(8,128)(2,1)S(1)}, bf16[32,2048]{1,0:T(8,128)(2,1)S(1)}, u32[]{:S(2)}, u32[]{:S(2)}) %collective-permute-start.6) | collective-permute-done | bytes 131104 | tf_op jit(solution)/shard_map/ppermute | solution.py:273
  25.7 1.3 %score_low.1.low = f32[96,1024]{1,0:T(8,128)S(1)} custom-call(bf16[32,2048]{1,0:T(8,128)(2,1)S(1)} %collective-permute-done.3.near_first, bf16[32,2048]{1,0:T(8,128)(2,1)S(1)} %collective-permute-done.5.near_second, bf16[32,2048]{1,0:T(8,128)(2,1)S(1)} %collective-permute-done.4.far, bf16[32,2048]{1,0:T(8,128)(2,1)S(1)} %collective-permute-done.6.last, ...), custom_call_target="tpu_custom_call" | custom-call | flops 402653184 | bytes 4194304 | tf_op jit(solution)/shard_map/score_low/pallas_call | solution.py:199
  27.0 0.1 collective-permute-done.2.last
  27.1 1.3 %score_high.1 = (f32[32,1024]{1,0:T(8,128)S(1)}, bf16[32,1024]{1,0:T(8,128)(2,1)S(1)}, bf16[32,1024]{1,0:T(8,128)(2,1)S(1)}, bf16[32,1024]{1,0:T(8,128)(2,1)S(1)}) custom-call(bf16[32,2048]{1,0:T(8,128)(2,1)S(1)} %collective-permute-done.near, bf16[32,2048]{1,0:T(8,128)(2,1)S(1)} %collective-permute-done.1.far, ...), custom_call_target="tpu_custom_call" | custom-call | flops 402653184 | bytes 4194304 | tf_op jit(solution)/shard_map/score_high/pallas_call | solution.py:228
  28.5 0.1 collective-permute-start.7
  28.5 1.6 %collective-permute-start.8 = (bf16[32,1024]{1,0:T(8,128)(2,1)S(1)}, bf16[32,1024]{1,0:T(8,128)(2,1)S(1)}, u32[]{:S(2)}, u32[]{:S(2)}) collective-permute-start(bf16[32,1024]{1,0:T(8,128)(2,1)S(1)} %get-tuple-element.23), channel_id=1, source_target_pairs={{0,8},{4,12},{8,0},{12,4},{1,9},{5,13},{9,1},{13,5},{2,10},{6,14},... | collective-permute-start | bytes 196616 | tf_op jit(solution)/shard_map/ppermute | solution.py:273
  30.1 0.3 collective-permute-start.9
  30.4 0.1 copy.6.candidates
  30.5 2.6 %collective-permute-done.8.refs_2_ = bf16[32,1024]{1,0:T(8,128)(2,1)S(1)} collective-permute-done((bf16[32,1024]{1,0:T(8,128)(2,1)S(1)}, bf16[32,1024]{1,0:T(8,128)(2,1)S(1)}, u32[]{:S(2)}, u32[]{:S(2)}) %collective-permute-start.8) | collective-permute-done | bytes 65568 | tf_op jit(solution)/shard_map/ppermute | solution.py:273
  33.1 1.1 %collective-permute-done.9.refs_3_ = bf16[32,1024]{1,0:T(8,128)(2,1)S(1)} collective-permute-done((bf16[32,1024]{1,0:T(8,128)(2,1)S(1)}, bf16[32,1024]{1,0:T(8,128)(2,1)S(1)}, u32[]{:S(2)}, u32[]{:S(2)}) %collective-permute-start.9) | collective-permute-done | bytes 65568 | tf_op jit(solution)/shard_map/ppermute | solution.py:273
  34.2 0.7 %finish.1 = bf16[32,1024]{1,0:T(8,128)(2,1)} custom-call(s32[32,16]{1,0:T(8,128)S(1)} %copy.6.candidates, f32[32,1024]{1,0:T(8,128)S(1)} %get-tuple-element.21.refs_0_, bf16[32,1024]{1,0:T(8,128)(2,1)S(1)} %collective-permute-done.7.refs_1_, bf16[32,1024]{1,0:T(8,128)(2,1)S(1)} %collective-permute-done.8.refs_2_, ...), custom_call_target="tpu_custom_call" | custom-call | tf_op jit(solution)/shard_map/finish/pallas_call | solution.py:261
  (7 shorter events, 0.0 us)
Async XLA Ops:
  0.0 25.7 %copy-start = (bf16[1,1024,4096]{2,1,0:T(8,128)(2,1)S(1)}, bf16[1,1024,4096]{2,1,0:T(8,128)(2,1)}, u32[]{:S(2)}) copy-start(bf16[1,1024,4096]{2,1,0:T(8,128)(2,1)} %store.3) | copy-start | bytes 25165828
  2.0 18.4 %collective-permute-start.3 = (bf16[32,2048]{1,0:T(8,128)(2,1)S(1)}, bf16[32,2048]{1,0:T(8,128)(2,1)S(1)}, u32[]{:S(2)}, u32[]{:S(2)}) collective-permute-start(bf16[32,2048]{1,0:T(8,128)(2,1)S(1)} %condition.3.low), channel_id=1, source_target_pairs={{0,1},{1,0},{2,2},{3,3},{4,5},{5,4},{6,6},{7,7},{8,9},{9,8},{10,10... | collective-permute-start | bytes 393224 | tf_op jit(solution)/shard_map/ppermute | solution.py:282
  7.0 13.4 %collective-permute-start.4 = (bf16[32,2048]{1,0:T(8,128)(2,1)S(1)}, bf16[32,2048]{1,0:T(8,128)(2,1)S(1)}, u32[]{:S(2)}, u32[]{:S(2)}) collective-permute-start(bf16[32,2048]{1,0:T(8,128)(2,1)S(1)} %condition.3.low), channel_id=1, source_target_pairs={{0,2},{1,3},{2,0},{3,1},{4,6},{5,7},{6,4},{7,5},{8,10},{9,11},{10,... | collective-permute-start | bytes 393224 | tf_op jit(solution)/shard_map/ppermute | solution.py:273
  7.1 13.3 %collective-permute-start.5 = (bf16[32,2048]{1,0:T(8,128)(2,1)S(1)}, bf16[32,2048]{1,0:T(8,128)(2,1)S(1)}, u32[]{:S(2)}, u32[]{:S(2)}) collective-permute-start(bf16[32,2048]{1,0:T(8,128)(2,1)S(1)} %condition.3.low), channel_id=1, source_target_pairs={{0,0},{1,1},{2,3},{3,2},{4,4},{5,5},{6,7},{7,6},{8,8},{9,9},{10,11... | collective-permute-start | bytes 393224 | tf_op jit(solution)/shard_map/ppermute | solution.py:282
  9.6 11.0 %collective-permute-start = (bf16[32,2048]{1,0:T(8,128)(2,1)S(1)}, bf16[32,2048]{1,0:T(8,128)(2,1)S(1)}, u32[]{:S(2)}, u32[]{:S(2)}) collective-permute-start(bf16[32,2048]{1,0:T(8,128)(2,1)S(1)} %condition.2.high), channel_id=1, source_target_pairs={{0,1},{1,0},{2,3},{3,2},{4,5},{5,4},{6,7},{7,6},{8,9},{9,8},{10,11... | collective-permute-start | bytes 393224 | tf_op jit(solution)/shard_map/ppermute | solution.py:273
  11.0 9.6 %collective-permute-start.1 = (bf16[32,2048]{1,0:T(8,128)(2,1)S(1)}, bf16[32,2048]{1,0:T(8,128)(2,1)S(1)}, u32[]{:S(2)}, u32[]{:S(2)}) collective-permute-start(bf16[32,2048]{1,0:T(8,128)(2,1)S(1)} %condition.2.high), channel_id=1, source_target_pairs={{0,2},{1,3},{2,0},{3,1},{4,6},{5,7},{6,4},{7,5},{8,10},{9,11},{10,... | collective-permute-start | bytes 393224 | tf_op jit(solution)/shard_map/ppermute | solution.py:273
  20.4 10.0 %copy-start.1 = (s32[32,16]{0,1:T(8,128)S(1)}, s32[32,16]{0,1:T(8,128)}, u32[]{:S(2)}) copy-start(s32[32,16]{0,1:T(8,128)} %param.9) | copy-start | bytes 6148
  20.4 5.3 %collective-permute-start.6 = (bf16[32,2048]{1,0:T(8,128)(2,1)S(1)}, bf16[32,2048]{1,0:T(8,128)(2,1)S(1)}, u32[]{:S(2)}, u32[]{:S(2)}) collective-permute-start(bf16[32,2048]{1,0:T(8,128)(2,1)S(1)} %collective-permute-done.4.far), channel_id=1, source_target_pairs={{0,1},{1,0},{2,3},{3,2},{4,5},{5,4},{6,7},{7,6},{8,9},{9,8},{10,11... | collective-permute-start | bytes 393224 | tf_op jit(solution)/shard_map/ppermute | solution.py:273
  20.6 6.5 %collective-permute-start.2 = (bf16[32,2048]{1,0:T(8,128)(2,1)S(1)}, bf16[32,2048]{1,0:T(8,128)(2,1)S(1)}, u32[]{:S(2)}, u32[]{:S(2)}) collective-permute-start(bf16[32,2048]{1,0:T(8,128)(2,1)S(1)} %collective-permute-done.1.far), channel_id=1, source_target_pairs={{0,1},{1,0},{2,3},{3,2},{4,5},{5,4},{6,7},{7,6},{8,9},{9,8},{10,11... | collective-permute-start | bytes 393224 | tf_op jit(solution)/shard_map/ppermute | solution.py:273
  28.5 2.0 %collective-permute-start.7 = (bf16[32,1024]{1,0:T(8,128)(2,1)S(1)}, bf16[32,1024]{1,0:T(8,128)(2,1)S(1)}, u32[]{:S(2)}, u32[]{:S(2)}) collective-permute-start(bf16[32,1024]{1,0:T(8,128)(2,1)S(1)} %get-tuple-element.22), channel_id=1, source_target_pairs={{0,4},{4,0},{8,12},{12,8},{1,5},{5,1},{9,13},{13,9},{2,6},{6,2},{1... | collective-permute-start | bytes 196616 | tf_op jit(solution)/shard_map/ppermute | solution.py:273
  28.5 4.5 %collective-permute-start.8 = (bf16[32,1024]{1,0:T(8,128)(2,1)S(1)}, bf16[32,1024]{1,0:T(8,128)(2,1)S(1)}, u32[]{:S(2)}, u32[]{:S(2)}) collective-permute-start(bf16[32,1024]{1,0:T(8,128)(2,1)S(1)} %get-tuple-element.23), channel_id=1, source_target_pairs={{0,8},{4,12},{8,0},{12,4},{1,9},{5,13},{9,1},{13,5},{2,10},{6,14},... | collective-permute-start | bytes 196616 | tf_op jit(solution)/shard_map/ppermute | solution.py:273
  30.1 4.0 %collective-permute-start.9 = (bf16[32,1024]{1,0:T(8,128)(2,1)S(1)}, bf16[32,1024]{1,0:T(8,128)(2,1)S(1)}, u32[]{:S(2)}, u32[]{:S(2)}) collective-permute-start(bf16[32,1024]{1,0:T(8,128)(2,1)S(1)} %get-tuple-element.24), channel_id=1, source_target_pairs={{0,12},{4,8},{8,4},{12,0},{1,13},{5,9},{9,5},{13,1},{2,14},{6,10},... | collective-permute-start | bytes 196616 | tf_op jit(solution)/shard_map/ppermute | solution.py:273

commit v13 on v10

--- a/solution.py
+++ b/solution.py
@@ -126,6 +126,7 @@
 
 
 STEP = 256
+MASKS = (0, 2, 3, 1)
 
 
 def score_block(queries, store, first, write, arrived=None, step_rows=STEP):
@@ -143,10 +144,11 @@
     lax.fori_loop(0, store.shape[1] // step_rows, one, 0)
 
 
-def own_kernel(low, high, far_store, out, store, semaphores):
+def own_kernel(queries, far_store, out, store, semaphores):
     def copy_of(step):
         place = pl.ds(pl.multiple_of(step * STEP, STEP), STEP)
-        return pltpu.make_async_copy(far_store.at[0, place], store.at[0, place], semaphores.at[step])
+        source = far_store.at[0, place, pl.ds(0, store.shape[2])]
+        return pltpu.make_async_copy(source, store.at[0, place], semaphores.at[step])
 
     for step in range(store.shape[1] // STEP):
         copy_of(step).start()
@@ -154,8 +156,7 @@
     def write(place, value):
         out[:, place] = value
 
-    queries = jnp.concatenate([low[...], high[...]], axis=1)
-    score_block(queries, store, 0, write, lambda step: copy_of(step).wait())
+    score_block(queries[...], store, 0, write, lambda step: copy_of(step).wait())
 
 
 def score_cost(count, width, examples):
@@ -164,19 +165,22 @@
     )
 
 
-def score_own(halves, store):
-    rows, entries = halves[0].shape[0], store.shape[2]
+def score_own(queries, store):
+    rows, entries = queries.shape
     examples = store.shape[1]
     return pl.pallas_call(
         own_kernel,
-        in_specs=in_vmem(2) + [pl.BlockSpec(memory_space=pltpu.HBM)],
+        in_specs=in_vmem(1) + [pl.BlockSpec(memory_space=pltpu.HBM)],
         out_specs=in_vmem(1)[0],
         out_shape=jax.ShapeDtypeStruct((rows, examples), jnp.float32),
-        scratch_shapes=[pltpu.VMEM(store.shape, store.dtype), pltpu.SemaphoreType.DMA((examples // STEP,))],
+        scratch_shapes=[
+            pltpu.VMEM((1, examples, entries), store.dtype),
+            pltpu.SemaphoreType.DMA((examples // STEP,)),
+        ],
         compiler_params=pltpu.CompilerParams(vmem_limit_bytes=VMEM),
         cost_estimate=score_cost(rows, entries, examples),
         name="score_own",
-    )(*halves, pltpu.with_memory_space_constraint(store, pltpu.HBM))
+    )(queries, pltpu.with_memory_space_constraint(store, pltpu.HBM))
 
 
 def stacked(*blocks):
@@ -204,36 +208,36 @@
     )(near, far, last, store)
 
 
-def high_kernel(first, near, far, last, store, own, low, *refs):
+def high_kernel(first, own, near, far, last, store, own_low, low, *refs):
     outs, total = refs[:-1], refs[-1]
     rows = own.shape[0]
-    total[pl.ds(0, rows), :] = own[...]
 
     def write(place, value):
-        total[pl.ds(rows, 3 * rows), place] = value + low[:, place]
-
-    score_block(stacked(near, far, last), store, first, write, step_rows=store.shape[1])
+        total[pl.ds(0, rows), place] = value[:rows] + own_low[:, place]
+        total[pl.ds(rows, 3 * rows), place] = value[rows:] + low[:, place]
+
+    score_block(stacked(own, near, far, last), store, first, write, step_rows=store.shape[1])
     home = lax.bitwise_xor(lax.axis_index("blk"), lax.axis_index("layer"))
-    for mask, out in enumerate(outs):
+    for mask, out in zip(MASKS, outs):
         slot = lax.bitwise_xor(home, mask)
         out[...] = total[pl.ds(pl.multiple_of(slot * rows, rows), rows), :].astype(out.dtype)
 
 
-def score_high(near, far, last, store, own, low):
+def score_high(own, near, far, last, store, own_low, low):
     rows, width = far.shape
     examples = store.shape[1]
     return pl.pallas_call(
         functools.partial(high_kernel, store.shape[2] - width),
-        in_specs=in_vmem(6),
+        in_specs=in_vmem(7),
         out_specs=in_vmem(4),
         out_shape=[
-            jax.ShapeDtypeStruct((rows, examples), jnp.bfloat16 if mask else jnp.float32) for mask in range(4)
+            jax.ShapeDtypeStruct((rows, examples), jnp.bfloat16 if mask else jnp.float32) for mask in MASKS
         ],
         scratch_shapes=[pltpu.VMEM((4 * rows, examples), jnp.float32)],
         compiler_params=pltpu.CompilerParams(vmem_limit_bytes=VMEM),
-        cost_estimate=score_cost(3 * rows, width, examples),
+        cost_estimate=score_cost(4 * rows, width, examples),
         name="score_high",
-    )(near, far, last, store, own, low)
+    )(own, near, far, last, store, own_low, low)
 
 
 def write_rows(total, layers, listed, out):
@@ -277,23 +281,28 @@
 def on_line(own, store, candidates, layers):
     far = [swapped(half, "blk", 2) for half in own]
     near = [swapped(half, "blk", 1) for half in own]
-    own_scores = score_own(own, store)
-    far[0], near[0], own_scores = lax.optimization_barrier((far[0], near[0], own_scores))
+    own_low = score_own(own[0], store)
+    far[0], near[0], own_low = lax.optimization_barrier((far[0], near[0], own_low))
     far[1], near[1] = lax.optimization_barrier((far[1], near[1]))
     last = [swapped(half, "blk", 1) for half in far]
     low_scores = score_low(near[0], far[0], last[0], store)
-    parts = score_high(near[1], far[1], last[1], store, own_scores, low_scores)
-    received = [swapped(parts[mask], "layer", mask) for mask in (1, 2, 3)]
+    parts = score_high(own[1], near[1], far[1], last[1], store, own_low, low_scores)
+    received = [swapped(part, "layer", mask) for mask, part in zip(MASKS[1:], parts[1:])]
     return finish([parts[0]] + received, candidates, layers)
 
 
 def on_ring(own, store, candidates, layers):
     count = lax.axis_size("blk")
     rows = own[0].shape[0]
-    slots = [score_own(own, store)]
+    moving = jnp.concatenate(own, axis=1)
+
+    def scores():
+        return lax.dot_general(moving, store[0], (((1,), (1,)), ((), ())), preferred_element_type=jnp.float32)
+
+    slots = [scores()]
     for _ in range(count - 1):
-        own = [permuted(half, "blk", lambda source: source + 1) for half in own]
-        slots.append(score_own(own, store))
+        moving = permuted(moving, "blk", lambda source: source + 1)
+        slots.append(scores())
     turns = lax.rem(lax.axis_index("blk") - jnp.arange(count) + count, count)
     total = jnp.stack(slots)[turns].reshape(layers, count * rows // layers, store.shape[1])
     parts = lax.all_to_all(total.astype(jnp.bfloat16), "layer", 0, 0)

time: 31.9 us -> 31.9 us (level)
  waiting for transfers between devices: 7.62 us -> 9.23 us
  Pallas kernels: 11.7 us -> 10.2 us
    ppermute x9, waiting for transfers between devices: 7.62 us -> 9.23 us  [permuted(): lax.ppermute(value, axis, [(source, target_of(source) % count) for source...]
    pallas_call x1, Pallas kernels: 4.52 us -> 3.08 us  [score_own(): pl.pallas_call(own_kernel, in_specs=in_vmem(1) + [pl.BlockSpec(memory_spa...]
  transfers between devices with their start and end apart: 9 -> 9, of which waited for: 6 -> 7; matrix products, arithmetic and copies ran while one was open for 0% -> 0% of each run, Pallas kernels for 24% -> 19%
where the time goes in v13:
time: 31.9 us; the launch traced here: 31.7 us
  starting transfers between devices  12.1 us (38%)
  Pallas kernels  10.2 us (32%)
  waiting for transfers between devices  9.23 us (29%)
    ppermute x9, starting transfers between devices, permuted(): lax.ppermute(value, axis, [(source, target_of(source) % count) for source...  12.1 us
    ppermute x9, waiting for transfers between devices, permuted(): lax.ppermute(value, axis, [(source, target_of(source) % count) for source...  9.23 us
    pallas_call x2, Pallas kernels, condition(): pl.pallas_call(functools.partial(condition_kernel, half * side // 2, side...  3.76 us
    pallas_call x1, Pallas kernels, score_own(): pl.pallas_call(own_kernel, in_specs=in_vmem(1) + [pl.BlockSpec(memory_spa...  3.08 us
    pallas_call x1, Pallas kernels, score_high(): pl.pallas_call(functools.partial(high_kernel, store.shape[2] - width), in...  1.35 us
    pallas_call x1, Pallas kernels, score_low(): pl.pallas_call(low_kernel, in_specs=in_vmem(4), out_specs=in_vmem(1)[0],...  1.29 us
    pallas_call x1, Pallas kernels, finish(): pl.pallas_call(functools.partial(finish_kernel, layers), in_specs=in_vmem...  0.74 us
  transfers between devices with their start and end apart: 9, of which 7 were waited for; matrix products, arithmetic and copies ran while one was open for 0% of the time, Pallas kernels for 19%

profile of v13, /device:TPU:0, one launch (start us, length us, event | category | flops | bytes accessed | tf_op | source)
XLA Modules:
  0.0 31.7 jit_solution(15685034117338224364)
XLA Ops:
  0.0 2.0 %condition.3.queries = bf16[32,2048]{1,0:T(8,128)(2,1)S(1)} custom-call(bf16[1,32,4096]{2,1,0:T(8,128)(2,1)} %queries_in.3, f32[1,64,64]{2,1,0:T(8,128)} %left_in.3, f32[1,64,64]{2,1,0:T(8,128)} %right_in.3), custom_call_target="tpu_custom_call" | custom-call | flops 536870912 | bytes 524288 | tf_op jit(solution)/shard_map/condition/pallas_call | solution.py:109
  2.0 4.1 %collective-permute-start.3 = (bf16[32,2048]{1,0:T(8,128)(2,1)S(1)}, bf16[32,2048]{1,0:T(8,128)(2,1)S(1)}, u32[]{:S(2)}, u32[]{:S(2)}) collective-permute-start(bf16[32,2048]{1,0:T(8,128)(2,1)S(1)} %condition.3.queries), channel_id=1, source_target_pairs={{0,2},{1,3},{2,0},{3,1},{4,6},{5,7},{6,4},{7,5},{8,10},{9,11},{10,... | collective-permute-start | bytes 393224 | tf_op jit(solution)/shard_map/ppermute | solution.py:274
  6.1 1.6 %collective-permute-start.4 = (bf16[32,2048]{1,0:T(8,128)(2,1)S(1)}, bf16[32,2048]{1,0:T(8,128)(2,1)S(1)}, u32[]{:S(2)}, u32[]{:S(2)}) collective-permute-start(bf16[32,2048]{1,0:T(8,128)(2,1)S(1)} %condition.3.queries), channel_id=1, source_target_pairs={{0,1},{1,0},{2,3},{3,2},{4,5},{5,4},{6,7},{7,6},{8,9},{9,8},{10,11... | collective-permute-start | bytes 393224 | tf_op jit(solution)/shard_map/ppermute | solution.py:274
  7.6 1.8 %condition.2.own = bf16[32,2048]{1,0:T(8,128)(2,1)S(1)} custom-call(bf16[1,32,4096]{2,1,0:T(8,128)(2,1)} %queries_in.3, f32[1,64,64]{2,1,0:T(8,128)} %left_in.3, f32[1,64,64]{2,1,0:T(8,128)} %right_in.3), custom_call_target="tpu_custom_call" | custom-call | flops 536870912 | bytes 524288 | tf_op jit(solution)/shard_map/condition/pallas_call | solution.py:109
  9.5 0.4 %collective-permute-start = (bf16[32,2048]{1,0:T(8,128)(2,1)S(1)}, bf16[32,2048]{1,0:T(8,128)(2,1)S(1)}, u32[]{:S(2)}, u32[]{:S(2)}) collective-permute-start(bf16[32,2048]{1,0:T(8,128)(2,1)S(1)} %condition.2.own), channel_id=1, source_target_pairs={{0,2},{1,3},{2,0},{3,1},{4,6},{5,7},{6,4},{7,5},{8,10},{9,11},{10,... | collective-permute-start | bytes 393224 | tf_op jit(solution)/shard_map/ppermute | solution.py:274
  9.9 0.2 collective-permute-start.1
  10.1 3.1 %score_own.1.own_low = f32[32,1024]{1,0:T(8,128)S(1)} custom-call(bf16[32,2048]{1,0:T(8,128)(2,1)S(1)} %condition.3.queries, bf16[1,1024,4096]{2,1,0:T(8,128)(2,1)} %store.3), custom_call_target="tpu_custom_call" | custom-call | flops 134217728 | bytes 4194304 | tf_op jit(solution)/shard_map/score_own/pallas_call | solution.py:171
  13.1 0.0 copy-start.1
  13.1 0.0 collective-permute-done.3.far
  13.2 0.6 %collective-permute-done.4.near = bf16[32,2048]{1,0:T(8,128)(2,1)S(1)} collective-permute-done((bf16[32,2048]{1,0:T(8,128)(2,1)S(1)}, bf16[32,2048]{1,0:T(8,128)(2,1)S(1)}, u32[]{:S(2)}, u32[]{:S(2)}) %collective-permute-start.4) | collective-permute-done | bytes 131104 | tf_op jit(solution)/shard_map/ppermute | solution.py:274
  13.8 1.5 %collective-permute-start.5 = (bf16[32,2048]{1,0:T(8,128)(2,1)S(1)}, bf16[32,2048]{1,0:T(8,128)(2,1)S(1)}, u32[]{:S(2)}, u32[]{:S(2)}) collective-permute-start(bf16[32,2048]{1,0:T(8,128)(2,1)S(1)} %collective-permute-done.3.far), channel_id=1, source_target_pairs={{0,1},{1,0},{2,3},{3,2},{4,5},{5,4},{6,7},{7,6},{8,9},{9,8},{10,11... | collective-permute-start | bytes 393224 | tf_op jit(solution)/shard_map/ppermute | solution.py:274
  15.3 2.8 %collective-permute-done.far = bf16[32,2048]{1,0:T(8,128)(2,1)S(1)} collective-permute-done((bf16[32,2048]{1,0:T(8,128)(2,1)S(1)}, bf16[32,2048]{1,0:T(8,128)(2,1)S(1)}, u32[]{:S(2)}, u32[]{:S(2)}) %collective-permute-start) | collective-permute-done | bytes 131104 | tf_op jit(solution)/shard_map/ppermute | solution.py:274
  18.1 0.6 %collective-permute-done.1.near = bf16[32,2048]{1,0:T(8,128)(2,1)S(1)} collective-permute-done((bf16[32,2048]{1,0:T(8,128)(2,1)S(1)}, bf16[32,2048]{1,0:T(8,128)(2,1)S(1)}, u32[]{:S(2)}, u32[]{:S(2)}) %collective-permute-start.1) | collective-permute-done | bytes 131104 | tf_op jit(solution)/shard_map/ppermute | solution.py:274
  18.7 2.2 %collective-permute-start.2 = (bf16[32,2048]{1,0:T(8,128)(2,1)S(1)}, bf16[32,2048]{1,0:T(8,128)(2,1)S(1)}, u32[]{:S(2)}, u32[]{:S(2)}) collective-permute-start(bf16[32,2048]{1,0:T(8,128)(2,1)S(1)} %collective-permute-done.far), channel_id=1, source_target_pairs={{0,1},{1,0},{2,3},{3,2},{4,5},{5,4},{6,7},{7,6},{8,9},{9,8},{10,11... | collective-permute-start | bytes 393224 | tf_op jit(solution)/shard_map/ppermute | solution.py:274
  20.9 0.6 %collective-permute-done.5.last = bf16[32,2048]{1,0:T(8,128)(2,1)S(1)} collective-permute-done((bf16[32,2048]{1,0:T(8,128)(2,1)S(1)}, bf16[32,2048]{1,0:T(8,128)(2,1)S(1)}, u32[]{:S(2)}, u32[]{:S(2)}) %collective-permute-start.5) | collective-permute-done | bytes 131104 | tf_op jit(solution)/shard_map/ppermute | solution.py:274
  21.5 1.3 %score_low.1.low = f32[96,1024]{1,0:T(8,128)S(1)} custom-call(bf16[32,2048]{1,0:T(8,128)(2,1)S(1)} %collective-permute-done.4.near, bf16[32,2048]{1,0:T(8,128)(2,1)S(1)} %collective-permute-done.3.far, bf16[32,2048]{1,0:T(8,128)(2,1)S(1)} %collective-permute-done.5.last, bf16[1,1024,4096]{2,1,0:T(8,128)(2,1)S(1)} %copy-done), custom_call_target="tpu_custom_call" | custom-call | flops 402653184 | bytes 4194304 | tf_op jit(solution)/shard_map/score_low/pallas_call | solution.py:200
  22.8 1.1 %collective-permute-done.2.last = bf16[32,2048]{1,0:T(8,128)(2,1)S(1)} collective-permute-done((bf16[32,2048]{1,0:T(8,128)(2,1)S(1)}, bf16[32,2048]{1,0:T(8,128)(2,1)S(1)}, u32[]{:S(2)}, u32[]{:S(2)}) %collective-permute-start.2) | collective-permute-done | bytes 131104 | tf_op jit(solution)/shard_map/ppermute | solution.py:274
  23.9 1.3 %score_high.1 = (f32[32,1024]{1,0:T(8,128)S(1)}, bf16[32,1024]{1,0:T(8,128)(2,1)S(1)}, bf16[32,1024]{1,0:T(8,128)(2,1)S(1)}, bf16[32,1024]{1,0:T(8,128)(2,1)S(1)}) custom-call(bf16[32,2048]{1,0:T(8,128)(2,1)S(1)} %condition.2.own, bf16[32,2048]{1,0:T(8,128)(2,1)S(1)} %collective-permute-done.1.near, bf16[32,2048]{1,0:T(8,128)(2,1)S(1)} %collective-permute-done.far, ...), custom_call_target="tpu_custom_call" | custom-call | flops 536870912 | bytes 4194304 | tf_op jit(solution)/shard_map/score_high/pallas_call | solution.py:229
  25.3 1.6 %collective-permute-start.6 = (bf16[32,1024]{1,0:T(8,128)(2,1)S(1)}, bf16[32,1024]{1,0:T(8,128)(2,1)S(1)}, u32[]{:S(2)}, u32[]{:S(2)}) collective-permute-start(bf16[32,1024]{1,0:T(8,128)(2,1)S(1)} %get-tuple-element.20), channel_id=1, source_target_pairs={{0,8},{4,12},{8,0},{12,4},{1,9},{5,13},{9,1},{13,5},{2,10},{6,14},... | collective-permute-start | bytes 196616 | tf_op jit(solution)/shard_map/ppermute | solution.py:274
  26.9 0.6 %collective-permute-start.8 = (bf16[32,1024]{1,0:T(8,128)(2,1)S(1)}, bf16[32,1024]{1,0:T(8,128)(2,1)S(1)}, u32[]{:S(2)}, u32[]{:S(2)}) collective-permute-start(bf16[32,1024]{1,0:T(8,128)(2,1)S(1)} %get-tuple-element.22), channel_id=1, source_target_pairs={{0,4},{4,0},{8,12},{12,8},{1,5},{5,1},{9,13},{13,9},{2,6},{6,2},{1... | collective-permute-start | bytes 196616 | tf_op jit(solution)/shard_map/ppermute | solution.py:274
  27.5 0.1 copy.6.candidates
  27.6 2.0 %collective-permute-done.6.refs_1_ = bf16[32,1024]{1,0:T(8,128)(2,1)S(1)} collective-permute-done((bf16[32,1024]{1,0:T(8,128)(2,1)S(1)}, bf16[32,1024]{1,0:T(8,128)(2,1)S(1)}, u32[]{:S(2)}, u32[]{:S(2)}) %collective-permute-start.6) | collective-permute-done | bytes 65568 | tf_op jit(solution)/shard_map/ppermute | solution.py:274
  29.6 1.4 %collective-permute-done.7.refs_2_ = bf16[32,1024]{1,0:T(8,128)(2,1)S(1)} collective-permute-done((bf16[32,1024]{1,0:T(8,128)(2,1)S(1)}, bf16[32,1024]{1,0:T(8,128)(2,1)S(1)}, u32[]{:S(2)}, u32[]{:S(2)}) %collective-permute-start.7) | collective-permute-done | bytes 65568 | tf_op jit(solution)/shard_map/ppermute | solution.py:274
  31.0 0.7 %finish.1 = bf16[32,1024]{1,0:T(8,128)(2,1)} custom-call(s32[32,16]{1,0:T(8,128)S(1)} %copy.6.candidates, f32[32,1024]{1,0:T(8,128)S(1)} %get-tuple-element.19.refs_0_, bf16[32,1024]{1,0:T(8,128)(2,1)S(1)} %collective-permute-done.6.refs_1_, bf16[32,1024]{1,0:T(8,128)(2,1)S(1)} %collective-permute-done.7.refs_2_, ...), custom_call_target="tpu_custom_call" | custom-call | tf_op jit(solution)/shard_map/finish/pallas_call | solution.py:262
  (5 shorter events, 0.0 us)
Async XLA Ops:
  0.0 21.5 %copy-start = (bf16[1,1024,4096]{2,1,0:T(8,128)(2,1)S(1)}, bf16[1,1024,4096]{2,1,0:T(8,128)(2,1)}, u32[]{:S(2)}) copy-start(bf16[1,1024,4096]{2,1,0:T(8,128)(2,1)} %store.3) | copy-start | bytes 25165828
  2.0 11.2 %collective-permute-start.3 = (bf16[32,2048]{1,0:T(8,128)(2,1)S(1)}, bf16[32,2048]{1,0:T(8,128)(2,1)S(1)}, u32[]{:S(2)}, u32[]{:S(2)}) collective-permute-start(bf16[32,2048]{1,0:T(8,128)(2,1)S(1)} %condition.3.queries), channel_id=1, source_target_pairs={{0,2},{1,3},{2,0},{3,1},{4,6},{5,7},{6,4},{7,5},{8,10},{9,11},{10,... | collective-permute-start | bytes 393224 | tf_op jit(solution)/shard_map/ppermute | solution.py:274
  6.1 7.7 %collective-permute-start.4 = (bf16[32,2048]{1,0:T(8,128)(2,1)S(1)}, bf16[32,2048]{1,0:T(8,128)(2,1)S(1)}, u32[]{:S(2)}, u32[]{:S(2)}) collective-permute-start(bf16[32,2048]{1,0:T(8,128)(2,1)S(1)} %condition.3.queries), channel_id=1, source_target_pairs={{0,1},{1,0},{2,3},{3,2},{4,5},{5,4},{6,7},{7,6},{8,9},{9,8},{10,11... | collective-permute-start | bytes 393224 | tf_op jit(solution)/shard_map/ppermute | solution.py:274
  9.5 8.6 %collective-permute-start = (bf16[32,2048]{1,0:T(8,128)(2,1)S(1)}, bf16[32,2048]{1,0:T(8,128)(2,1)S(1)}, u32[]{:S(2)}, u32[]{:S(2)}) collective-permute-start(bf16[32,2048]{1,0:T(8,128)(2,1)S(1)} %condition.2.own), channel_id=1, source_target_pairs={{0,2},{1,3},{2,0},{3,1},{4,6},{5,7},{6,4},{7,5},{8,10},{9,11},{10,... | collective-permute-start | bytes 393224 | tf_op jit(solution)/shard_map/ppermute | solution.py:274
  9.9 8.8 %collective-permute-start.1 = (bf16[32,2048]{1,0:T(8,128)(2,1)S(1)}, bf16[32,2048]{1,0:T(8,128)(2,1)S(1)}, u32[]{:S(2)}, u32[]{:S(2)}) collective-permute-start(bf16[32,2048]{1,0:T(8,128)(2,1)S(1)} %condition.2.own), channel_id=1, source_target_pairs={{0,1},{1,0},{2,3},{3,2},{4,5},{5,4},{6,7},{7,6},{8,9},{9,8},{10,11... | collective-permute-start | bytes 393224 | tf_op jit(solution)/shard_map/ppermute | solution.py:274
  13.1 14.3 %copy-start.1 = (s32[32,16]{0,1:T(8,128)S(1)}, s32[32,16]{0,1:T(8,128)}, u32[]{:S(2)}) copy-start(s32[32,16]{0,1:T(8,128)} %param.9) | copy-start | bytes 6148
  13.8 7.7 %collective-permute-start.5 = (bf16[32,2048]{1,0:T(8,128)(2,1)S(1)}, bf16[32,2048]{1,0:T(8,128)(2,1)S(1)}, u32[]{:S(2)}, u32[]{:S(2)}) collective-permute-start(bf16[32,2048]{1,0:T(8,128)(2,1)S(1)} %collective-permute-done.3.far), channel_id=1, source_target_pairs={{0,1},{1,0},{2,3},{3,2},{4,5},{5,4},{6,7},{7,6},{8,9},{9,8},{10,11... | collective-permute-start | bytes 393224 | tf_op jit(solution)/shard_map/ppermute | solution.py:274
  18.7 5.2 %collective-permute-start.2 = (bf16[32,2048]{1,0:T(8,128)(2,1)S(1)}, bf16[32,2048]{1,0:T(8,128)(2,1)S(1)}, u32[]{:S(2)}, u32[]{:S(2)}) collective-permute-start(bf16[32,2048]{1,0:T(8,128)(2,1)S(1)} %collective-permute-done.far), channel_id=1, source_target_pairs={{0,1},{1,0},{2,3},{3,2},{4,5},{5,4},{6,7},{7,6},{8,9},{9,8},{10,11... | collective-permute-start | bytes 393224 | tf_op jit(solution)/shard_map/ppermute | solution.py:274
  25.3 4.3 %collective-permute-start.6 = (bf16[32,1024]{1,0:T(8,128)(2,1)S(1)}, bf16[32,1024]{1,0:T(8,128)(2,1)S(1)}, u32[]{:S(2)}, u32[]{:S(2)}) collective-permute-start(bf16[32,1024]{1,0:T(8,128)(2,1)S(1)} %get-tuple-element.20), channel_id=1, source_target_pairs={{0,8},{4,12},{8,0},{12,4},{1,9},{5,13},{9,1},{13,5},{2,10},{6,14},... | collective-permute-start | bytes 196616 | tf_op jit(solution)/shard_map/ppermute | solution.py:274
  26.9 4.1 %collective-permute-start.7 = (bf16[32,1024]{1,0:T(8,128)(2,1)S(1)}, bf16[32,1024]{1,0:T(8,128)(2,1)S(1)}, u32[]{:S(2)}, u32[]{:S(2)}) collective-permute-start(bf16[32,1024]{1,0:T(8,128)(2,1)S(1)} %get-tuple-element.21), channel_id=1, source_target_pairs={{0,12},{4,8},{8,4},{12,0},{1,13},{5,9},{9,5},{13,1},{2,14},{6,10},... | collective-permute-start | bytes 196616 | tf_op jit(solution)/shard_map/ppermute | solution.py:274
  26.9 4.1 %collective-permute-start.8 = (bf16[32,1024]{1,0:T(8,128)(2,1)S(1)}, bf16[32,1024]{1,0:T(8,128)(2,1)S(1)}, u32[]{:S(2)}, u32[]{:S(2)}) collective-permute-start(bf16[32,1024]{1,0:T(8,128)(2,1)S(1)} %get-tuple-element.22), channel_id=1, source_target_pairs={{0,4},{4,0},{8,12},{12,8},{1,5},{5,1},{9,13},{13,9},{2,6},{6,2},{1... | collective-permute-start | bytes 196616 | tf_op jit(solution)/shard_map/ppermute | solution.py:274

commit v14 on v13

--- a/solution.py
+++ b/solution.py
@@ -64,12 +64,11 @@
         copy.start()
     side = left_factor.shape[0]
     pairs = side // 2
-    copies[0].wait()
-    copies[1].wait()
+    for copy in copies:
+        copy.wait()
     left = spread_left(left_factor[...], first, count)
     right = spread_right(right_factor[...])
     low_half = iota((1, 1, LANES), 2) < side
-    copies[2].wait()
     for block in range(queries.shape[0] // GROUP):
         rows = pl.ds(block * GROUP, GROUP)
         straight = jnp.stack(
@@ -129,19 +128,8 @@
 MASKS = (0, 2, 3, 1)
 
 
-def score_block(queries, store, first, write, arrived=None, step_rows=STEP):
-    turned = queries.T
-    width = queries.shape[1]
-
-    def one(step, carry):
-        place = pl.ds(pl.multiple_of(step * step_rows, step_rows), step_rows)
-        if arrived is not None:
-            arrived(step)
-        value = dot(store[0, place, pl.ds(first, width)], turned)
-        write(place, value.T)
-        return carry
-
-    lax.fori_loop(0, store.shape[1] // step_rows, one, 0)
+def score_rows(queries, store, place, first):
+    return dot(store[0, place, pl.ds(first, queries.shape[1])], queries.T)
 
 
 def own_kernel(queries, far_store, out, store, semaphores):
@@ -150,13 +138,18 @@
         source = far_store.at[0, place, pl.ds(0, store.shape[2])]
         return pltpu.make_async_copy(source, store.at[0, place], semaphores.at[step])
 
-    for step in range(store.shape[1] // STEP):
+    steps = store.shape[1] // STEP
+    for step in range(steps):
         copy_of(step).start()
-
-    def write(place, value):
-        out[:, place] = value
-
-    score_block(queries[...], store, 0, write, lambda step: copy_of(step).wait())
+    padded = jnp.concatenate([jnp.zeros_like(queries)] * 3 + [queries[...]], axis=0)
+
+    def one(step, carry):
+        copy_of(step).wait()
+        place = pl.ds(pl.multiple_of(step * STEP, STEP), STEP)
+        out[place, :] = score_rows(padded, store, place, 0)
+        return carry
+
+    lax.fori_loop(0, steps, one, 0)
 
 
 def score_cost(count, width, examples):
@@ -172,7 +165,7 @@
         own_kernel,
         in_specs=in_vmem(1) + [pl.BlockSpec(memory_space=pltpu.HBM)],
         out_specs=in_vmem(1)[0],
-        out_shape=jax.ShapeDtypeStruct((rows, examples), jnp.float32),
+        out_shape=jax.ShapeDtypeStruct((examples, 4 * rows), jnp.float32),
         scratch_shapes=[
             pltpu.VMEM((1, examples, entries), store.dtype),
             pltpu.SemaphoreType.DMA((examples // STEP,)),
@@ -187,57 +180,50 @@
     return jnp.concatenate([block[...] for block in blocks], axis=0)
 
 
-def low_kernel(near, far, last, store, out):
-    def write(place, value):
-        out[:, place] = value
-
-    score_block(stacked(near, far, last), store, 0, write, step_rows=store.shape[1])
-
-
-def score_low(near, far, last, store):
+def low_kernel(near, far, last, store, own_low, out):
+    queries = stacked(near, far, last)
+    queries = jnp.concatenate([queries, jnp.zeros_like(near)], axis=0)
+    out[...] = score_rows(queries, store, slice(None), 0) + own_low[...]
+
+
+def score_low(near, far, last, store, own_low):
     rows, width = far.shape
     examples = store.shape[1]
     return pl.pallas_call(
         low_kernel,
-        in_specs=in_vmem(4),
+        in_specs=in_vmem(5),
         out_specs=in_vmem(1)[0],
-        out_shape=jax.ShapeDtypeStruct((3 * rows, examples), jnp.float32),
+        out_shape=jax.ShapeDtypeStruct((examples, 4 * rows), jnp.float32),
         compiler_params=pltpu.CompilerParams(vmem_limit_bytes=VMEM),
         cost_estimate=score_cost(3 * rows, width, examples),
         name="score_low",
-    )(near, far, last, store)
-
-
-def high_kernel(first, own, near, far, last, store, own_low, low, *refs):
+    )(near, far, last, store, own_low)
+
+
+def high_kernel(first, near, far, last, own, store, low, *refs):
     outs, total = refs[:-1], refs[-1]
     rows = own.shape[0]
-
-    def write(place, value):
-        total[pl.ds(0, rows), place] = value[:rows] + own_low[:, place]
-        total[pl.ds(rows, 3 * rows), place] = value[rows:] + low[:, place]
-
-    score_block(stacked(own, near, far, last), store, first, write, step_rows=store.shape[1])
+    value = score_rows(stacked(near, far, last, own), store, slice(None), first) + low[...]
+    total[...] = value.astype(total.dtype).T
     home = lax.bitwise_xor(lax.axis_index("blk"), lax.axis_index("layer"))
     for mask, out in zip(MASKS, outs):
-        slot = lax.bitwise_xor(home, mask)
-        out[...] = total[pl.ds(pl.multiple_of(slot * rows, rows), rows), :].astype(out.dtype)
-
-
-def score_high(own, near, far, last, store, own_low, low):
+        place = lax.bitwise_and(lax.bitwise_xor(home, mask) + 3, 3)
+        out[...] = total[pl.ds(pl.multiple_of(place * rows, rows), rows), :]
+
+
+def score_high(near, far, last, own, store, low):
     rows, width = far.shape
     examples = store.shape[1]
     return pl.pallas_call(
         functools.partial(high_kernel, store.shape[2] - width),
-        in_specs=in_vmem(7),
+        in_specs=in_vmem(6),
         out_specs=in_vmem(4),
-        out_shape=[
-            jax.ShapeDtypeStruct((rows, examples), jnp.bfloat16 if mask else jnp.float32) for mask in MASKS
-        ],
-        scratch_shapes=[pltpu.VMEM((4 * rows, examples), jnp.float32)],
+        out_shape=[jax.ShapeDtypeStruct((rows, examples), jnp.bfloat16)] * 4,
+        scratch_shapes=[pltpu.VMEM((4 * rows, examples), jnp.bfloat16)],
         compiler_params=pltpu.CompilerParams(vmem_limit_bytes=VMEM),
         cost_estimate=score_cost(4 * rows, width, examples),
         name="score_high",
-    )(own, near, far, last, store, own_low, low)
+    )(near, far, last, own, store, low)
 
 
 def write_rows(total, layers, listed, out):
@@ -285,8 +271,8 @@
     far[0], near[0], own_low = lax.optimization_barrier((far[0], near[0], own_low))
     far[1], near[1] = lax.optimization_barrier((far[1], near[1]))
     last = [swapped(half, "blk", 1) for half in far]
-    low_scores = score_low(near[0], far[0], last[0], store)
-    parts = score_high(own[1], near[1], far[1], last[1], store, own_low, low_scores)
+    low_scores = score_low(near[0], far[0], last[0], store, own_low)
+    parts = score_high(near[1], far[1], last[1], own[1], store, low_scores)
     received = [swapped(part, "layer", mask) for mask, part in zip(MASKS[1:], parts[1:])]
     return finish([parts[0]] + received, candidates, layers)
 

time: 31.9 us -> 31.9 us (level)
  no operation moved by 1% of the time
where the time goes in v14:
time: 31.9 us; the launch traced here: 31.8 us
  starting transfers between devices  12.2 us (38%)
  Pallas kernels  10.2 us (32%)
  waiting for transfers between devices  9.21 us (29%)
    ppermute x9, starting transfers between devices, permuted(): lax.ppermute(value, axis, [(source, target_of(source) % count) for source...  12.2 us
    ppermute x9, waiting for transfers between devices, permuted(): lax.ppermute(value, axis, [(source, target_of(source) % count) for source...  9.21 us
    pallas_call x2, Pallas kernels, condition(): pl.pallas_call(functools.partial(condition_kernel, half * side // 2, side...  3.87 us
    pallas_call x1, Pallas kernels, score_own(): pl.pallas_call(own_kernel, in_specs=in_vmem(1) + [pl.BlockSpec(memory_spa...  3.01 us
    pallas_call x1, Pallas kernels, score_high(): pl.pallas_call(functools.partial(high_kernel, store.shape[2] - width), in...  1.31 us
    pallas_call x1, Pallas kernels, score_low(): pl.pallas_call(low_kernel, in_specs=in_vmem(5), out_specs=in_vmem(1)[0],...  1.25 us
    pallas_call x1, Pallas kernels, finish(): pl.pallas_call(functools.partial(finish_kernel, layers), in_specs=in_vmem...  0.74 us
  transfers between devices with their start and end apart: 9, of which 7 were waited for; matrix products, arithmetic and copies ran while one was open for 0% of the time, Pallas kernels for 19%

profile of v14, /device:TPU:0, one launch (start us, length us, event | category | flops | bytes accessed | tf_op | source)
XLA Modules:
  0.0 31.8 jit_solution(12138065793673609904)
XLA Ops:
  0.0 2.0 %condition.3.queries = bf16[32,2048]{1,0:T(8,128)(2,1)S(1)} custom-call(bf16[1,32,4096]{2,1,0:T(8,128)(2,1)} %queries_in.3, f32[1,64,64]{2,1,0:T(8,128)} %left_in.3, f32[1,64,64]{2,1,0:T(8,128)} %right_in.3), custom_call_target="tpu_custom_call" | custom-call | flops 536870912 | bytes 524288 | tf_op jit(solution)/shard_map/condition/pallas_call | solution.py:108
  2.0 4.1 %collective-permute-start.3 = (bf16[32,2048]{1,0:T(8,128)(2,1)S(1)}, bf16[32,2048]{1,0:T(8,128)(2,1)S(1)}, u32[]{:S(2)}, u32[]{:S(2)}) collective-permute-start(bf16[32,2048]{1,0:T(8,128)(2,1)S(1)} %condition.3.queries), channel_id=1, source_target_pairs={{0,2},{1,3},{2,0},{3,1},{4,6},{5,7},{6,4},{7,5},{8,10},{9,11},{10,... | collective-permute-start | bytes 393224 | tf_op jit(solution)/shard_map/ppermute | solution.py:260
  6.1 1.6 %collective-permute-start.4 = (bf16[32,2048]{1,0:T(8,128)(2,1)S(1)}, bf16[32,2048]{1,0:T(8,128)(2,1)S(1)}, u32[]{:S(2)}, u32[]{:S(2)}) collective-permute-start(bf16[32,2048]{1,0:T(8,128)(2,1)S(1)} %condition.3.queries), channel_id=1, source_target_pairs={{0,1},{1,0},{2,3},{3,2},{4,5},{5,4},{6,7},{7,6},{8,9},{9,8},{10,11... | collective-permute-start | bytes 393224 | tf_op jit(solution)/shard_map/ppermute | solution.py:260
  7.7 1.9 %condition.2.own = bf16[32,2048]{1,0:T(8,128)(2,1)S(1)} custom-call(bf16[1,32,4096]{2,1,0:T(8,128)(2,1)} %queries_in.3, f32[1,64,64]{2,1,0:T(8,128)} %left_in.3, f32[1,64,64]{2,1,0:T(8,128)} %right_in.3), custom_call_target="tpu_custom_call" | custom-call | flops 536870912 | bytes 524288 | tf_op jit(solution)/shard_map/condition/pallas_call | solution.py:108
  9.6 0.4 %collective-permute-start = (bf16[32,2048]{1,0:T(8,128)(2,1)S(1)}, bf16[32,2048]{1,0:T(8,128)(2,1)S(1)}, u32[]{:S(2)}, u32[]{:S(2)}) collective-permute-start(bf16[32,2048]{1,0:T(8,128)(2,1)S(1)} %condition.2.own), channel_id=1, source_target_pairs={{0,2},{1,3},{2,0},{3,1},{4,6},{5,7},{6,4},{7,5},{8,10},{9,11},{10,... | collective-permute-start | bytes 393224 | tf_op jit(solution)/shard_map/ppermute | solution.py:260
  10.0 0.2 collective-permute-start.1
  10.2 3.0 %score_own.1.own_low = f32[1024,128]{1,0:T(8,128)S(1)} custom-call(bf16[32,2048]{1,0:T(8,128)(2,1)S(1)} %condition.3.queries, bf16[1,1024,4096]{2,1,0:T(8,128)(2,1)} %store.3), custom_call_target="tpu_custom_call" | custom-call | flops 134217728 | bytes 4194304 | tf_op jit(solution)/shard_map/score_own/pallas_call | solution.py:164
  13.2 0.0 copy-start.1
  13.2 0.6 %collective-permute-done.4.near = bf16[32,2048]{1,0:T(8,128)(2,1)S(1)} collective-permute-done((bf16[32,2048]{1,0:T(8,128)(2,1)S(1)}, bf16[32,2048]{1,0:T(8,128)(2,1)S(1)}, u32[]{:S(2)}, u32[]{:S(2)}) %collective-permute-start.4) | collective-permute-done | bytes 131104 | tf_op jit(solution)/shard_map/ppermute | solution.py:260
  13.8 1.5 %collective-permute-start.5 = (bf16[32,2048]{1,0:T(8,128)(2,1)S(1)}, bf16[32,2048]{1,0:T(8,128)(2,1)S(1)}, u32[]{:S(2)}, u32[]{:S(2)}) collective-permute-start(bf16[32,2048]{1,0:T(8,128)(2,1)S(1)} %collective-permute-done.3.far), channel_id=1, source_target_pairs={{0,1},{1,0},{2,3},{3,2},{4,5},{5,4},{6,7},{7,6},{8,9},{9,8},{10,11... | collective-permute-start | bytes 393224 | tf_op jit(solution)/shard_map/ppermute | solution.py:260
  15.3 2.8 %collective-permute-done.far = bf16[32,2048]{1,0:T(8,128)(2,1)S(1)} collective-permute-done((bf16[32,2048]{1,0:T(8,128)(2,1)S(1)}, bf16[32,2048]{1,0:T(8,128)(2,1)S(1)}, u32[]{:S(2)}, u32[]{:S(2)}) %collective-permute-start) | collective-permute-done | bytes 131104 | tf_op jit(solution)/shard_map/ppermute | solution.py:260
  18.1 0.6 %collective-permute-done.1.near = bf16[32,2048]{1,0:T(8,128)(2,1)S(1)} collective-permute-done((bf16[32,2048]{1,0:T(8,128)(2,1)S(1)}, bf16[32,2048]{1,0:T(8,128)(2,1)S(1)}, u32[]{:S(2)}, u32[]{:S(2)}) %collective-permute-start.1) | collective-permute-done | bytes 131104 | tf_op jit(solution)/shard_map/ppermute | solution.py:260
  18.7 2.2 %collective-permute-start.2 = (bf16[32,2048]{1,0:T(8,128)(2,1)S(1)}, bf16[32,2048]{1,0:T(8,128)(2,1)S(1)}, u32[]{:S(2)}, u32[]{:S(2)}) collective-permute-start(bf16[32,2048]{1,0:T(8,128)(2,1)S(1)} %collective-permute-done.far), channel_id=1, source_target_pairs={{0,1},{1,0},{2,3},{3,2},{4,5},{5,4},{6,7},{7,6},{8,9},{9,8},{10,11... | collective-permute-start | bytes 393224 | tf_op jit(solution)/shard_map/ppermute | solution.py:260
  20.9 0.6 %collective-permute-done.5.last = bf16[32,2048]{1,0:T(8,128)(2,1)S(1)} collective-permute-done((bf16[32,2048]{1,0:T(8,128)(2,1)S(1)}, bf16[32,2048]{1,0:T(8,128)(2,1)S(1)}, u32[]{:S(2)}, u32[]{:S(2)}) %collective-permute-start.5) | collective-permute-done | bytes 131104 | tf_op jit(solution)/shard_map/ppermute | solution.py:260
  21.5 1.2 %score_low.1.low = f32[1024,128]{1,0:T(8,128)S(1)} custom-call(bf16[32,2048]{1,0:T(8,128)(2,1)S(1)} %collective-permute-done.4.near, bf16[32,2048]{1,0:T(8,128)(2,1)S(1)} %collective-permute-done.3.far, bf16[32,2048]{1,0:T(8,128)(2,1)S(1)} %collective-permute-done.5.last, bf16[1,1024,4096]{2,1,0:T(8,128)(2,1)S(1)} %copy-done, f32[1024,128]{1,0:T(8,128)S(1)} %score_own.1.own_low), custom_call_target="tpu_custom_call" | custom-call | flops 402653184 | bytes 4194304 | tf_op jit(solution)/shard_map/score_low/pallas_call | solution.py:192
  22.8 1.2 %collective-permute-done.2.last = bf16[32,2048]{1,0:T(8,128)(2,1)S(1)} collective-permute-done((bf16[32,2048]{1,0:T(8,128)(2,1)S(1)}, bf16[32,2048]{1,0:T(8,128)(2,1)S(1)}, u32[]{:S(2)}, u32[]{:S(2)}) %collective-permute-start.2) | collective-permute-done | bytes 131104 | tf_op jit(solution)/shard_map/ppermute | solution.py:260
  24.0 1.3 %score_high.1 = (bf16[32,1024]{1,0:T(8,128)(2,1)S(1)}, bf16[32,1024]{1,0:T(8,128)(2,1)S(1)}, bf16[32,1024]{1,0:T(8,128)(2,1)S(1)}, bf16[32,1024]{1,0:T(8,128)(2,1)S(1)}) custom-call(bf16[32,2048]{1,0:T(8,128)(2,1)S(1)} %collective-permute-done.1.near, bf16[32,2048]{1,0:T(8,128)(2,1)S(1)} %collective-permute-done.far, ...), custom_call_target="tpu_custom_call" | custom-call | flops 536870912 | bytes 4194304 | tf_op jit(solution)/shard_map/score_high/pallas_call | solution.py:217
  25.3 1.6 %collective-permute-start.6 = (bf16[32,1024]{1,0:T(8,128)(2,1)S(1)}, bf16[32,1024]{1,0:T(8,128)(2,1)S(1)}, u32[]{:S(2)}, u32[]{:S(2)}) collective-permute-start(bf16[32,1024]{1,0:T(8,128)(2,1)S(1)} %get-tuple-element.20), channel_id=1, source_target_pairs={{0,8},{4,12},{8,0},{12,4},{1,9},{5,13},{9,1},{13,5},{2,10},{6,14},... | collective-permute-start | bytes 196616 | tf_op jit(solution)/shard_map/ppermute | solution.py:260
  26.9 0.0 collective-permute-start.7
  26.9 0.6 %collective-permute-start.8 = (bf16[32,1024]{1,0:T(8,128)(2,1)S(1)}, bf16[32,1024]{1,0:T(8,128)(2,1)S(1)}, u32[]{:S(2)}, u32[]{:S(2)}) collective-permute-start(bf16[32,1024]{1,0:T(8,128)(2,1)S(1)} %get-tuple-element.22), channel_id=1, source_target_pairs={{0,4},{4,0},{8,12},{12,8},{1,5},{5,1},{9,13},{13,9},{2,6},{6,2},{1... | collective-permute-start | bytes 196616 | tf_op jit(solution)/shard_map/ppermute | solution.py:260
  27.5 0.1 copy.6.candidates
  27.6 2.0 %collective-permute-done.6.refs_1_ = bf16[32,1024]{1,0:T(8,128)(2,1)S(1)} collective-permute-done((bf16[32,1024]{1,0:T(8,128)(2,1)S(1)}, bf16[32,1024]{1,0:T(8,128)(2,1)S(1)}, u32[]{:S(2)}, u32[]{:S(2)}) %collective-permute-start.6) | collective-permute-done | bytes 65568 | tf_op jit(solution)/shard_map/ppermute | solution.py:260
  29.6 1.4 %collective-permute-done.7.refs_2_ = bf16[32,1024]{1,0:T(8,128)(2,1)S(1)} collective-permute-done((bf16[32,1024]{1,0:T(8,128)(2,1)S(1)}, bf16[32,1024]{1,0:T(8,128)(2,1)S(1)}, u32[]{:S(2)}, u32[]{:S(2)}) %collective-permute-start.7) | collective-permute-done | bytes 65568 | tf_op jit(solution)/shard_map/ppermute | solution.py:260
  31.0 0.7 %finish.1 = bf16[32,1024]{1,0:T(8,128)(2,1)} custom-call(s32[32,16]{1,0:T(8,128)S(1)} %copy.6.candidates, bf16[32,1024]{1,0:T(8,128)(2,1)S(1)} %get-tuple-element.19.refs_0_, bf16[32,1024]{1,0:T(8,128)(2,1)S(1)} %collective-permute-done.6.refs_1_, bf16[32,1024]{1,0:T(8,128)(2,1)S(1)} %collective-permute-done.7.refs_2_, ...), custom_call_target="tpu_custom_call" | custom-call | tf_op jit(solution)/shard_map/finish/pallas_call | solution.py:248
  (5 shorter events, 0.0 us)
Async XLA Ops:
  0.0 21.5 %copy-start = (bf16[1,1024,4096]{2,1,0:T(8,128)(2,1)S(1)}, bf16[1,1024,4096]{2,1,0:T(8,128)(2,1)}, u32[]{:S(2)}) copy-start(bf16[1,1024,4096]{2,1,0:T(8,128)(2,1)} %store.3) | copy-start | bytes 25165828
  2.0 11.2 %collective-permute-start.3 = (bf16[32,2048]{1,0:T(8,128)(2,1)S(1)}, bf16[32,2048]{1,0:T(8,128)(2,1)S(1)}, u32[]{:S(2)}, u32[]{:S(2)}) collective-permute-start(bf16[32,2048]{1,0:T(8,128)(2,1)S(1)} %condition.3.queries), channel_id=1, source_target_pairs={{0,2},{1,3},{2,0},{3,1},{4,6},{5,7},{6,4},{7,5},{8,10},{9,11},{10,... | collective-permute-start | bytes 393224 | tf_op jit(solution)/shard_map/ppermute | solution.py:260
  6.1 7.7 %collective-permute-start.4 = (bf16[32,2048]{1,0:T(8,128)(2,1)S(1)}, bf16[32,2048]{1,0:T(8,128)(2,1)S(1)}, u32[]{:S(2)}, u32[]{:S(2)}) collective-permute-start(bf16[32,2048]{1,0:T(8,128)(2,1)S(1)} %condition.3.queries), channel_id=1, source_target_pairs={{0,1},{1,0},{2,3},{3,2},{4,5},{5,4},{6,7},{7,6},{8,9},{9,8},{10,11... | collective-permute-start | bytes 393224 | tf_op jit(solution)/shard_map/ppermute | solution.py:260
  9.6 8.6 %collective-permute-start = (bf16[32,2048]{1,0:T(8,128)(2,1)S(1)}, bf16[32,2048]{1,0:T(8,128)(2,1)S(1)}, u32[]{:S(2)}, u32[]{:S(2)}) collective-permute-start(bf16[32,2048]{1,0:T(8,128)(2,1)S(1)} %condition.2.own), channel_id=1, source_target_pairs={{0,2},{1,3},{2,0},{3,1},{4,6},{5,7},{6,4},{7,5},{8,10},{9,11},{10,... | collective-permute-start | bytes 393224 | tf_op jit(solution)/shard_map/ppermute | solution.py:260
  10.0 8.8 %collective-permute-start.1 = (bf16[32,2048]{1,0:T(8,128)(2,1)S(1)}, bf16[32,2048]{1,0:T(8,128)(2,1)S(1)}, u32[]{:S(2)}, u32[]{:S(2)}) collective-permute-start(bf16[32,2048]{1,0:T(8,128)(2,1)S(1)} %condition.2.own), channel_id=1, source_target_pairs={{0,1},{1,0},{2,3},{3,2},{4,5},{5,4},{6,7},{7,6},{8,9},{9,8},{10,11... | collective-permute-start | bytes 393224 | tf_op jit(solution)/shard_map/ppermute | solution.py:260
  13.2 14.3 %copy-start.1 = (s32[32,16]{0,1:T(8,128)S(1)}, s32[32,16]{0,1:T(8,128)}, u32[]{:S(2)}) copy-start(s32[32,16]{0,1:T(8,128)} %param.9) | copy-start | bytes 6148
  13.8 7.8 %collective-permute-start.5 = (bf16[32,2048]{1,0:T(8,128)(2,1)S(1)}, bf16[32,2048]{1,0:T(8,128)(2,1)S(1)}, u32[]{:S(2)}, u32[]{:S(2)}) collective-permute-start(bf16[32,2048]{1,0:T(8,128)(2,1)S(1)} %collective-permute-done.3.far), channel_id=1, source_target_pairs={{0,1},{1,0},{2,3},{3,2},{4,5},{5,4},{6,7},{7,6},{8,9},{9,8},{10,11... | collective-permute-start | bytes 393224 | tf_op jit(solution)/shard_map/ppermute | solution.py:260
  18.7 5.2 %collective-permute-start.2 = (bf16[32,2048]{1,0:T(8,128)(2,1)S(1)}, bf16[32,2048]{1,0:T(8,128)(2,1)S(1)}, u32[]{:S(2)}, u32[]{:S(2)}) collective-permute-start(bf16[32,2048]{1,0:T(8,128)(2,1)S(1)} %collective-permute-done.far), channel_id=1, source_target_pairs={{0,1},{1,0},{2,3},{3,2},{4,5},{5,4},{6,7},{7,6},{8,9},{9,8},{10,11... | collective-permute-start | bytes 393224 | tf_op jit(solution)/shard_map/ppermute | solution.py:260
  25.3 4.3 %collective-permute-start.6 = (bf16[32,1024]{1,0:T(8,128)(2,1)S(1)}, bf16[32,1024]{1,0:T(8,128)(2,1)S(1)}, u32[]{:S(2)}, u32[]{:S(2)}) collective-permute-start(bf16[32,1024]{1,0:T(8,128)(2,1)S(1)} %get-tuple-element.20), channel_id=1, source_target_pairs={{0,8},{4,12},{8,0},{12,4},{1,9},{5,13},{9,1},{13,5},{2,10},{6,14},... | collective-permute-start | bytes 196616 | tf_op jit(solution)/shard_map/ppermute | solution.py:260
  26.9 4.1 %collective-permute-start.7 = (bf16[32,1024]{1,0:T(8,128)(2,1)S(1)}, bf16[32,1024]{1,0:T(8,128)(2,1)S(1)}, u32[]{:S(2)}, u32[]{:S(2)}) collective-permute-start(bf16[32,1024]{1,0:T(8,128)(2,1)S(1)} %get-tuple-element.21), channel_id=1, source_target_pairs={{0,12},{4,8},{8,4},{12,0},{1,13},{5,9},{9,5},{13,1},{2,14},{6,10},... | collective-permute-start | bytes 196616 | tf_op jit(solution)/shard_map/ppermute | solution.py:260
  26.9 4.1 %collective-permute-start.8 = (bf16[32,1024]{1,0:T(8,128)(2,1)S(1)}, bf16[32,1024]{1,0:T(8,128)(2,1)S(1)}, u32[]{:S(2)}, u32[]{:S(2)}) collective-permute-start(bf16[32,1024]{1,0:T(8,128)(2,1)S(1)} %get-tuple-element.22), channel_id=1, source_target_pairs={{0,4},{4,0},{8,12},{12,8},{1,5},{5,1},{9,13},{13,9},{2,6},{6,2},{1... | collective-permute-start | bytes 196616 | tf_op jit(solution)/shard_map/ppermute | solution.py:260

commit v15 on v14

--- a/solution.py
+++ b/solution.py
@@ -64,11 +64,12 @@
         copy.start()
     side = left_factor.shape[0]
     pairs = side // 2
-    for copy in copies:
-        copy.wait()
+    copies[0].wait()
+    copies[1].wait()
     left = spread_left(left_factor[...], first, count)
     right = spread_right(right_factor[...])
     low_half = iota((1, 1, LANES), 2) < side
+    copies[2].wait()
     for block in range(queries.shape[0] // GROUP):
         rows = pl.ds(block * GROUP, GROUP)
         straight = jnp.stack(
@@ -125,7 +126,7 @@
 
 
 STEP = 256
-MASKS = (0, 2, 3, 1)
+MASKS = (3, 1, 2, 0)
 
 
 def score_rows(queries, store, place, first):
@@ -203,27 +204,42 @@
 def high_kernel(first, near, far, last, own, store, low, *refs):
     outs, total = refs[:-1], refs[-1]
     rows = own.shape[0]
-    value = score_rows(stacked(near, far, last, own), store, slice(None), first) + low[...]
-    total[...] = value.astype(total.dtype).T
+    total[...] = (score_rows(stacked(near, far, last, own), store, slice(None), first) + low[...]).T
     home = lax.bitwise_xor(lax.axis_index("blk"), lax.axis_index("layer"))
     for mask, out in zip(MASKS, outs):
         place = lax.bitwise_and(lax.bitwise_xor(home, mask) + 3, 3)
-        out[...] = total[pl.ds(pl.multiple_of(place * rows, rows), rows), :]
+        out[...] = total[pl.ds(pl.multiple_of(place * rows, rows), rows), :].astype(out.dtype)
 
 
 def score_high(near, far, last, own, store, low):
     rows, width = far.shape
     examples = store.shape[1]
+    kinds = {0: jnp.float32, 1: jnp.bfloat16, 2: jnp.float32, 3: jnp.bfloat16}
     return pl.pallas_call(
         functools.partial(high_kernel, store.shape[2] - width),
         in_specs=in_vmem(6),
         out_specs=in_vmem(4),
-        out_shape=[jax.ShapeDtypeStruct((rows, examples), jnp.bfloat16)] * 4,
-        scratch_shapes=[pltpu.VMEM((4 * rows, examples), jnp.bfloat16)],
+        out_shape=[jax.ShapeDtypeStruct((rows, examples), kinds[mask]) for mask in MASKS],
+        scratch_shapes=[pltpu.VMEM((4 * rows, examples), jnp.float32)],
         compiler_params=pltpu.CompilerParams(vmem_limit_bytes=VMEM),
         cost_estimate=score_cost(4 * rows, width, examples),
         name="score_high",
     )(near, far, last, own, store, low)
+
+
+def add_kernel(kept, received, out):
+    out[...] = (kept[...] + received[...].astype(jnp.float32)).astype(out.dtype)
+
+
+def add(kept, received):
+    return pl.pallas_call(
+        add_kernel,
+        in_specs=in_vmem(2),
+        out_specs=in_vmem(1)[0],
+        out_shape=jax.ShapeDtypeStruct(received.shape, received.dtype),
+        compiler_params=pltpu.CompilerParams(vmem_limit_bytes=VMEM),
+        name="add",
+    )(kept, received)
 
 
 def write_rows(total, layers, listed, out):
@@ -272,9 +288,9 @@
     far[1], near[1] = lax.optimization_barrier((far[1], near[1]))
     last = [swapped(half, "blk", 1) for half in far]
     low_scores = score_low(near[0], far[0], last[0], store, own_low)
-    parts = score_high(near[1], far[1], last[1], own[1], store, low_scores)
-    received = [swapped(part, "layer", mask) for mask, part in zip(MASKS[1:], parts[1:])]
-    return finish([parts[0]] + received, candidates, layers)
+    across, beside, kept, home = score_high(near[1], far[1], last[1], own[1], store, low_scores)
+    across = swapped(add(kept, swapped(across, "layer", 1)), "layer", 2)
+    return finish([home, swapped(beside, "layer", 1), across], candidates, layers)
 
 
 def on_ring(own, store, candidates, layers):

time: 31.9 us -> 31.8 us (level)
  no operation moved by 1% of the time
where the time goes in v15:
time: 31.8 us; the launch traced here: 31.7 us
  starting transfers between devices  12.1 us (38%)
  Pallas kernels  10.1 us (32%)
  waiting for transfers between devices  9.28 us (29%)
    ppermute x9, starting transfers between devices, permuted(): lax.ppermute(value, axis, [(source, target_of(source) % count) for source...  12.1 us
    ppermute x9, waiting for transfers between devices, permuted(): lax.ppermute(value, axis, [(source, target_of(source) % count) for source...  9.28 us
    pallas_call x2, Pallas kernels, condition(): pl.pallas_call(functools.partial(condition_kernel, half * side // 2, side...  3.76 us
    pallas_call x1, Pallas kernels, score_own(): pl.pallas_call(own_kernel, in_specs=in_vmem(1) + [pl.BlockSpec(memory_spa...  3.02 us
    pallas_call x1, Pallas kernels, score_high(): pl.pallas_call(functools.partial(high_kernel, store.shape[2] - width), in...  1.34 us
    pallas_call x1, Pallas kernels, score_low(): pl.pallas_call(low_kernel, in_specs=in_vmem(5), out_specs=in_vmem(1)[0],...  1.24 us
    pallas_call x1, Pallas kernels, finish(): pl.pallas_call(functools.partial(finish_kernel, layers), in_specs=in_vmem...  0.74 us
  transfers between devices with their start and end apart: 9, of which 7 were waited for; matrix products, arithmetic and copies ran while one was open for 0% of the time, Pallas kernels for 19%

profile of v15, /device:TPU:0, one launch (start us, length us, event | category | flops | bytes accessed | tf_op | source)
XLA Modules:
  0.0 31.7 jit_solution(3611901766721986583)
XLA Ops:
  0.0 2.0 %condition.3.queries = bf16[32,2048]{1,0:T(8,128)(2,1)S(1)} custom-call(bf16[1,32,4096]{2,1,0:T(8,128)(2,1)} %queries_in.3, f32[1,64,64]{2,1,0:T(8,128)} %left_in.3, f32[1,64,64]{2,1,0:T(8,128)} %right_in.3), custom_call_target="tpu_custom_call" | custom-call | flops 536870912 | bytes 524288 | tf_op jit(solution)/shard_map/condition/pallas_call | solution.py:109
  2.0 4.1 %collective-permute-start.3 = (bf16[32,2048]{1,0:T(8,128)(2,1)S(1)}, bf16[32,2048]{1,0:T(8,128)(2,1)S(1)}, u32[]{:S(2)}, u32[]{:S(2)}) collective-permute-start(bf16[32,2048]{1,0:T(8,128)(2,1)S(1)} %condition.3.queries), channel_id=1, source_target_pairs={{0,2},{1,3},{2,0},{3,1},{4,6},{5,7},{6,4},{7,5},{8,10},{9,11},{10,... | collective-permute-start | bytes 393224 | tf_op jit(solution)/shard_map/ppermute | solution.py:276
  6.1 1.6 %collective-permute-start.4 = (bf16[32,2048]{1,0:T(8,128)(2,1)S(1)}, bf16[32,2048]{1,0:T(8,128)(2,1)S(1)}, u32[]{:S(2)}, u32[]{:S(2)}) collective-permute-start(bf16[32,2048]{1,0:T(8,128)(2,1)S(1)} %condition.3.queries), channel_id=1, source_target_pairs={{0,1},{1,0},{2,3},{3,2},{4,5},{5,4},{6,7},{7,6},{8,9},{9,8},{10,11... | collective-permute-start | bytes 393224 | tf_op jit(solution)/shard_map/ppermute | solution.py:276
  7.6 1.8 %condition.2.own = bf16[32,2048]{1,0:T(8,128)(2,1)S(1)} custom-call(bf16[1,32,4096]{2,1,0:T(8,128)(2,1)} %queries_in.3, f32[1,64,64]{2,1,0:T(8,128)} %left_in.3, f32[1,64,64]{2,1,0:T(8,128)} %right_in.3), custom_call_target="tpu_custom_call" | custom-call | flops 536870912 | bytes 524288 | tf_op jit(solution)/shard_map/condition/pallas_call | solution.py:109
  9.5 0.4 %collective-permute-start = (bf16[32,2048]{1,0:T(8,128)(2,1)S(1)}, bf16[32,2048]{1,0:T(8,128)(2,1)S(1)}, u32[]{:S(2)}, u32[]{:S(2)}) collective-permute-start(bf16[32,2048]{1,0:T(8,128)(2,1)S(1)} %condition.2.own), channel_id=1, source_target_pairs={{0,2},{1,3},{2,0},{3,1},{4,6},{5,7},{6,4},{7,5},{8,10},{9,11},{10,... | collective-permute-start | bytes 393224 | tf_op jit(solution)/shard_map/ppermute | solution.py:276
  9.9 0.2 collective-permute-start.1
  10.1 3.0 %score_own.1.own_low = f32[1024,128]{1,0:T(8,128)S(1)} custom-call(bf16[32,2048]{1,0:T(8,128)(2,1)S(1)} %condition.3.queries, bf16[1,1024,4096]{2,1,0:T(8,128)(2,1)} %store.3), custom_call_target="tpu_custom_call" | custom-call | flops 134217728 | bytes 4194304 | tf_op jit(solution)/shard_map/score_own/pallas_call | solution.py:165
  13.1 0.0 copy-start.1
  13.1 0.7 %collective-permute-done.4.near = bf16[32,2048]{1,0:T(8,128)(2,1)S(1)} collective-permute-done((bf16[32,2048]{1,0:T(8,128)(2,1)S(1)}, bf16[32,2048]{1,0:T(8,128)(2,1)S(1)}, u32[]{:S(2)}, u32[]{:S(2)}) %collective-permute-start.4) | collective-permute-done | bytes 131104 | tf_op jit(solution)/shard_map/ppermute | solution.py:276
  13.8 1.5 %collective-permute-start.5 = (bf16[32,2048]{1,0:T(8,128)(2,1)S(1)}, bf16[32,2048]{1,0:T(8,128)(2,1)S(1)}, u32[]{:S(2)}, u32[]{:S(2)}) collective-permute-start(bf16[32,2048]{1,0:T(8,128)(2,1)S(1)} %collective-permute-done.3.far), channel_id=1, source_target_pairs={{0,1},{1,0},{2,3},{3,2},{4,5},{5,4},{6,7},{7,6},{8,9},{9,8},{10,11... | collective-permute-start | bytes 393224 | tf_op jit(solution)/shard_map/ppermute | solution.py:276
  15.3 2.8 %collective-permute-done.far = bf16[32,2048]{1,0:T(8,128)(2,1)S(1)} collective-permute-done((bf16[32,2048]{1,0:T(8,128)(2,1)S(1)}, bf16[32,2048]{1,0:T(8,128)(2,1)S(1)}, u32[]{:S(2)}, u32[]{:S(2)}) %collective-permute-start) | collective-permute-done | bytes 131104 | tf_op jit(solution)/shard_map/ppermute | solution.py:276
  18.1 0.6 %collective-permute-done.1.near = bf16[32,2048]{1,0:T(8,128)(2,1)S(1)} collective-permute-done((bf16[32,2048]{1,0:T(8,128)(2,1)S(1)}, bf16[32,2048]{1,0:T(8,128)(2,1)S(1)}, u32[]{:S(2)}, u32[]{:S(2)}) %collective-permute-start.1) | collective-permute-done | bytes 131104 | tf_op jit(solution)/shard_map/ppermute | solution.py:276
  18.7 2.2 %collective-permute-start.2 = (bf16[32,2048]{1,0:T(8,128)(2,1)S(1)}, bf16[32,2048]{1,0:T(8,128)(2,1)S(1)}, u32[]{:S(2)}, u32[]{:S(2)}) collective-permute-start(bf16[32,2048]{1,0:T(8,128)(2,1)S(1)} %collective-permute-done.far), channel_id=1, source_target_pairs={{0,1},{1,0},{2,3},{3,2},{4,5},{5,4},{6,7},{7,6},{8,9},{9,8},{10,11... | collective-permute-start | bytes 393224 | tf_op jit(solution)/shard_map/ppermute | solution.py:276
  20.9 0.6 %collective-permute-done.5.last = bf16[32,2048]{1,0:T(8,128)(2,1)S(1)} collective-permute-done((bf16[32,2048]{1,0:T(8,128)(2,1)S(1)}, bf16[32,2048]{1,0:T(8,128)(2,1)S(1)}, u32[]{:S(2)}, u32[]{:S(2)}) %collective-permute-start.5) | collective-permute-done | bytes 131104 | tf_op jit(solution)/shard_map/ppermute | solution.py:276
  21.5 1.2 %score_low.1.low = f32[1024,128]{1,0:T(8,128)S(1)} custom-call(bf16[32,2048]{1,0:T(8,128)(2,1)S(1)} %collective-permute-done.4.near, bf16[32,2048]{1,0:T(8,128)(2,1)S(1)} %collective-permute-done.3.far, bf16[32,2048]{1,0:T(8,128)(2,1)S(1)} %collective-permute-done.5.last, bf16[1,1024,4096]{2,1,0:T(8,128)(2,1)S(1)} %copy-done, f32[1024,128]{1,0:T(8,128)S(1)} %score_own.1.own_low), custom_call_target="tpu_custom_call" | custom-call | flops 402653184 | bytes 4194304 | tf_op jit(solution)/shard_map/score_low/pallas_call | solution.py:193
  22.7 1.2 %collective-permute-done.2.last = bf16[32,2048]{1,0:T(8,128)(2,1)S(1)} collective-permute-done((bf16[32,2048]{1,0:T(8,128)(2,1)S(1)}, bf16[32,2048]{1,0:T(8,128)(2,1)S(1)}, u32[]{:S(2)}, u32[]{:S(2)}) %collective-permute-start.2) | collective-permute-done | bytes 131104 | tf_op jit(solution)/shard_map/ppermute | solution.py:276
  23.9 1.3 %score_high.1 = (bf16[32,1024]{1,0:T(8,128)(2,1)S(1)}, bf16[32,1024]{1,0:T(8,128)(2,1)S(1)}, f32[32,1024]{1,0:T(8,128)S(1)}, f32[32,1024]{1,0:T(8,128)S(1)}) custom-call(bf16[32,2048]{1,0:T(8,128)(2,1)S(1)} %collective-permute-done.1.near, bf16[32,2048]{1,0:T(8,128)(2,1)S(1)} %collective-permute-done.far, bf16[32,2048]{1,0:T(8,128)(2,1)S(1)} %collective-permute-done.2.last, ...), custom_call_target="tpu_custom_call" | custom-call | flops 536870912 | bytes 4194304 | tf_op jit(solution)/shard_map/score_high/pallas_call | solution.py:218
  25.3 0.1 collective-permute-start.7
  25.3 0.5 %collective-permute-start.6 = (bf16[32,1024]{1,0:T(8,128)(2,1)S(1)}, bf16[32,1024]{1,0:T(8,128)(2,1)S(1)}, u32[]{:S(2)}, u32[]{:S(2)}) collective-permute-start(bf16[32,1024]{1,0:T(8,128)(2,1)S(1)} %get-tuple-element.20), channel_id=1, source_target_pairs={{0,4},{4,0},{8,12},{12,8},{1,5},{5,1},{9,13},{13,9},{2,6},{6,2},{1... | collective-permute-start | bytes 196616 | tf_op jit(solution)/shard_map/ppermute | solution.py:276
  25.8 0.7 %collective-permute-done.7.received = bf16[32,1024]{1,0:T(8,128)(2,1)S(1)} collective-permute-done((bf16[32,1024]{1,0:T(8,128)(2,1)S(1)}, bf16[32,1024]{1,0:T(8,128)(2,1)S(1)}, u32[]{:S(2)}, u32[]{:S(2)}) %collective-permute-start.7) | collective-permute-done | bytes 65568 | tf_op jit(solution)/shard_map/ppermute | solution.py:276
  26.6 1.6 %collective-permute-start.8 = (bf16[32,1024]{1,0:T(8,128)(2,1)S(1)}, bf16[32,1024]{1,0:T(8,128)(2,1)S(1)}, u32[]{:S(2)}, u32[]{:S(2)}) collective-permute-start(bf16[32,1024]{1,0:T(8,128)(2,1)S(1)} %add.1), channel_id=1, source_target_pairs={{0,8},{4,12},{8,0},{12,4},{1,9},{5,13},{9,1},{13,5},{2,10},{6,14},... | collective-permute-start | bytes 196616 | tf_op jit(solution)/shard_map/ppermute | solution.py:276
  28.2 0.1 copy.6.candidates
  28.3 2.6 %collective-permute-done.8.refs_2_ = bf16[32,1024]{1,0:T(8,128)(2,1)S(1)} collective-permute-done((bf16[32,1024]{1,0:T(8,128)(2,1)S(1)}, bf16[32,1024]{1,0:T(8,128)(2,1)S(1)}, u32[]{:S(2)}, u32[]{:S(2)}) %collective-permute-start.8) | collective-permute-done | bytes 65568 | tf_op jit(solution)/shard_map/ppermute | solution.py:276
  30.9 0.7 %finish.1 = bf16[32,1024]{1,0:T(8,128)(2,1)} custom-call(s32[32,16]{1,0:T(8,128)S(1)} %copy.6.candidates, f32[32,1024]{1,0:T(8,128)S(1)} %get-tuple-element.19.refs_0_, bf16[32,1024]{1,0:T(8,128)(2,1)S(1)} %collective-permute-done.6.refs_1_, bf16[32,1024]{1,0:T(8,128)(2,1)S(1)} %collective-permute-done.8.refs_2_), custom_call_target="tpu_custom_call" | custom-call | tf_op jit(solution)/shard_map/finish/pallas_call | solution.py:264
  (6 shorter events, 0.0 us)
Async XLA Ops:
  0.0 21.5 %copy-start = (bf16[1,1024,4096]{2,1,0:T(8,128)(2,1)S(1)}, bf16[1,1024,4096]{2,1,0:T(8,128)(2,1)}, u32[]{:S(2)}) copy-start(bf16[1,1024,4096]{2,1,0:T(8,128)(2,1)} %store.3) | copy-start | bytes 25165828
  2.0 11.1 %collective-permute-start.3 = (bf16[32,2048]{1,0:T(8,128)(2,1)S(1)}, bf16[32,2048]{1,0:T(8,128)(2,1)S(1)}, u32[]{:S(2)}, u32[]{:S(2)}) collective-permute-start(bf16[32,2048]{1,0:T(8,128)(2,1)S(1)} %condition.3.queries), channel_id=1, source_target_pairs={{0,2},{1,3},{2,0},{3,1},{4,6},{5,7},{6,4},{7,5},{8,10},{9,11},{10,... | collective-permute-start | bytes 393224 | tf_op jit(solution)/shard_map/ppermute | solution.py:276
  6.1 7.7 %collective-permute-start.4 = (bf16[32,2048]{1,0:T(8,128)(2,1)S(1)}, bf16[32,2048]{1,0:T(8,128)(2,1)S(1)}, u32[]{:S(2)}, u32[]{:S(2)}) collective-permute-start(bf16[32,2048]{1,0:T(8,128)(2,1)S(1)} %condition.3.queries), channel_id=1, source_target_pairs={{0,1},{1,0},{2,3},{3,2},{4,5},{5,4},{6,7},{7,6},{8,9},{9,8},{10,11... | collective-permute-start | bytes 393224 | tf_op jit(solution)/shard_map/ppermute | solution.py:276
  9.5 8.6 %collective-permute-start = (bf16[32,2048]{1,0:T(8,128)(2,1)S(1)}, bf16[32,2048]{1,0:T(8,128)(2,1)S(1)}, u32[]{:S(2)}, u32[]{:S(2)}) collective-permute-start(bf16[32,2048]{1,0:T(8,128)(2,1)S(1)} %condition.2.own), channel_id=1, source_target_pairs={{0,2},{1,3},{2,0},{3,1},{4,6},{5,7},{6,4},{7,5},{8,10},{9,11},{10,... | collective-permute-start | bytes 393224 | tf_op jit(solution)/shard_map/ppermute | solution.py:276
  9.9 8.8 %collective-permute-start.1 = (bf16[32,2048]{1,0:T(8,128)(2,1)S(1)}, bf16[32,2048]{1,0:T(8,128)(2,1)S(1)}, u32[]{:S(2)}, u32[]{:S(2)}) collective-permute-start(bf16[32,2048]{1,0:T(8,128)(2,1)S(1)} %condition.2.own), channel_id=1, source_target_pairs={{0,1},{1,0},{2,3},{3,2},{4,5},{5,4},{6,7},{7,6},{8,9},{9,8},{10,11... | collective-permute-start | bytes 393224 | tf_op jit(solution)/shard_map/ppermute | solution.py:276
  13.1 15.1 %copy-start.1 = (s32[32,16]{0,1:T(8,128)S(1)}, s32[32,16]{0,1:T(8,128)}, u32[]{:S(2)}) copy-start(s32[32,16]{0,1:T(8,128)} %param.9) | copy-start | bytes 6148
  13.8 7.7 %collective-permute-start.5 = (bf16[32,2048]{1,0:T(8,128)(2,1)S(1)}, bf16[32,2048]{1,0:T(8,128)(2,1)S(1)}, u32[]{:S(2)}, u32[]{:S(2)}) collective-permute-start(bf16[32,2048]{1,0:T(8,128)(2,1)S(1)} %collective-permute-done.3.far), channel_id=1, source_target_pairs={{0,1},{1,0},{2,3},{3,2},{4,5},{5,4},{6,7},{7,6},{8,9},{9,8},{10,11... | collective-permute-start | bytes 393224 | tf_op jit(solution)/shard_map/ppermute | solution.py:276
  18.7 5.2 %collective-permute-start.2 = (bf16[32,2048]{1,0:T(8,128)(2,1)S(1)}, bf16[32,2048]{1,0:T(8,128)(2,1)S(1)}, u32[]{:S(2)}, u32[]{:S(2)}) collective-permute-start(bf16[32,2048]{1,0:T(8,128)(2,1)S(1)} %collective-permute-done.far), channel_id=1, source_target_pairs={{0,1},{1,0},{2,3},{3,2},{4,5},{5,4},{6,7},{7,6},{8,9},{9,8},{10,11... | collective-permute-start | bytes 393224 | tf_op jit(solution)/shard_map/ppermute | solution.py:276
  25.3 1.3 %collective-permute-start.7 = (bf16[32,1024]{1,0:T(8,128)(2,1)S(1)}, bf16[32,1024]{1,0:T(8,128)(2,1)S(1)}, u32[]{:S(2)}, u32[]{:S(2)}) collective-permute-start(bf16[32,1024]{1,0:T(8,128)(2,1)S(1)} %get-tuple-element.22), channel_id=1, source_target_pairs={{0,4},{4,0},{8,12},{12,8},{1,5},{5,1},{9,13},{13,9},{2,6},{6,2},{1... | collective-permute-start | bytes 196616 | tf_op jit(solution)/shard_map/ppermute | solution.py:276
  25.3 2.9 %collective-permute-start.6 = (bf16[32,1024]{1,0:T(8,128)(2,1)S(1)}, bf16[32,1024]{1,0:T(8,128)(2,1)S(1)}, u32[]{:S(2)}, u32[]{:S(2)}) collective-permute-start(bf16[32,1024]{1,0:T(8,128)(2,1)S(1)} %get-tuple-element.20), channel_id=1, source_target_pairs={{0,4},{4,0},{8,12},{12,8},{1,5},{5,1},{9,13},{13,9},{2,6},{6,2},{1... | collective-permute-start | bytes 196616 | tf_op jit(solution)/shard_map/ppermute | solution.py:276
  26.6 4.3 %collective-permute-start.8 = (bf16[32,1024]{1,0:T(8,128)(2,1)S(1)}, bf16[32,1024]{1,0:T(8,128)(2,1)S(1)}, u32[]{:S(2)}, u32[]{:S(2)}) collective-permute-start(bf16[32,1024]{1,0:T(8,128)(2,1)S(1)} %add.1), channel_id=1, source_target_pairs={{0,8},{4,12},{8,0},{12,4},{1,9},{5,13},{9,1},{13,5},{2,10},{6,14},... | collective-permute-start | bytes 196616 | tf_op jit(solution)/shard_map/ppermute | solution.py:276

commit v16 on v15

--- a/solution.py
+++ b/solution.py
@@ -284,8 +284,8 @@
     far = [swapped(half, "blk", 2) for half in own]
     near = [swapped(half, "blk", 1) for half in own]
     own_low = score_own(own[0], store)
-    far[0], near[0], own_low = lax.optimization_barrier((far[0], near[0], own_low))
-    far[1], near[1] = lax.optimization_barrier((far[1], near[1]))
+    near[0], far[0], own_low = lax.optimization_barrier((near[0], far[0], own_low))
+    near[1], far[1] = lax.optimization_barrier((near[1], far[1]))
     last = [swapped(half, "blk", 1) for half in far]
     low_scores = score_low(near[0], far[0], last[0], store, own_low)
     across, beside, kept, home = score_high(near[1], far[1], last[1], own[1], store, low_scores)

time: 31.8 us -> 31.7 us (level)
  waiting for transfers between devices: 9.28 us -> 8.31 us
  starting transfers between devices: 12.1 us -> 13 us
    ppermute x9, waiting for transfers between devices: 9.28 us -> 8.31 us  [permuted(): lax.ppermute(value, axis, [(source, target_of(source) % count) for source...]
    ppermute x9, starting transfers between devices: 12.1 us -> 13 us  [permuted(): lax.ppermute(value, axis, [(source, target_of(source) % count) for source...]
  transfers between devices with their start and end apart: 9 -> 9, of which waited for: 7 -> 6; matrix products, arithmetic and copies ran while one was open for 0% -> 0% of each run, Pallas kernels for 19% -> 19%
where the time goes in v16:
time: 31.7 us; the launch traced here: 31.6 us
  starting transfers between devices  13 us (41%)
  Pallas kernels  10.1 us (32%)
  waiting for transfers between devices  8.31 us (26%)
    ppermute x9, starting transfers between devices, permuted(): lax.ppermute(value, axis, [(source, target_of(source) % count) for source...  13 us
    ppermute x9, waiting for transfers between devices, permuted(): lax.ppermute(value, axis, [(source, target_of(source) % count) for source...  8.31 us
    pallas_call x2, Pallas kernels, condition(): pl.pallas_call(functools.partial(condition_kernel, half * side // 2, side...  3.76 us
    pallas_call x1, Pallas kernels, score_own(): pl.pallas_call(own_kernel, in_specs=in_vmem(1) + [pl.BlockSpec(memory_spa...  3.02 us
    pallas_call x1, Pallas kernels, score_high(): pl.pallas_call(functools.partial(high_kernel, store.shape[2] - width), in...  1.34 us
    pallas_call x1, Pallas kernels, score_low(): pl.pallas_call(low_kernel, in_specs=in_vmem(5), out_specs=in_vmem(1)[0],...  1.24 us
    pallas_call x1, Pallas kernels, finish(): pl.pallas_call(functools.partial(finish_kernel, layers), in_specs=in_vmem...  0.74 us
  transfers between devices with their start and end apart: 9, of which 6 were waited for; matrix products, arithmetic and copies ran while one was open for 0% of the time, Pallas kernels for 19%

profile of v16, /device:TPU:0, one launch (start us, length us, event | category | flops | bytes accessed | tf_op | source)
XLA Modules:
  0.0 31.6 jit_solution(9840007532881309925)
XLA Ops:
  0.0 2.0 %condition.3.queries = bf16[32,2048]{1,0:T(8,128)(2,1)S(1)} custom-call(bf16[1,32,4096]{2,1,0:T(8,128)(2,1)} %queries_in.3, f32[1,64,64]{2,1,0:T(8,128)} %left_in.3, f32[1,64,64]{2,1,0:T(8,128)} %right_in.3), custom_call_target="tpu_custom_call" | custom-call | flops 536870912 | bytes 524288 | tf_op jit(solution)/shard_map/condition/pallas_call | solution.py:109
  2.0 3.1 %collective-permute-start.3 = (bf16[32,2048]{1,0:T(8,128)(2,1)S(1)}, bf16[32,2048]{1,0:T(8,128)(2,1)S(1)}, u32[]{:S(2)}, u32[]{:S(2)}) collective-permute-start(bf16[32,2048]{1,0:T(8,128)(2,1)S(1)} %condition.3.queries), channel_id=1, source_target_pairs={{0,1},{1,0},{2,3},{3,2},{4,5},{5,4},{6,7},{7,6},{8,9},{9,8},{10,11... | collective-permute-start | bytes 393224 | tf_op jit(solution)/shard_map/ppermute | solution.py:276
  5.1 2.6 %collective-permute-start.4 = (bf16[32,2048]{1,0:T(8,128)(2,1)S(1)}, bf16[32,2048]{1,0:T(8,128)(2,1)S(1)}, u32[]{:S(2)}, u32[]{:S(2)}) collective-permute-start(bf16[32,2048]{1,0:T(8,128)(2,1)S(1)} %condition.3.queries), channel_id=1, source_target_pairs={{0,2},{1,3},{2,0},{3,1},{4,6},{5,7},{6,4},{7,5},{8,10},{9,11},{10,... | collective-permute-start | bytes 393224 | tf_op jit(solution)/shard_map/ppermute | solution.py:276
  7.6 1.8 %condition.2.own = bf16[32,2048]{1,0:T(8,128)(2,1)S(1)} custom-call(bf16[1,32,4096]{2,1,0:T(8,128)(2,1)} %queries_in.3, f32[1,64,64]{2,1,0:T(8,128)} %left_in.3, f32[1,64,64]{2,1,0:T(8,128)} %right_in.3), custom_call_target="tpu_custom_call" | custom-call | flops 536870912 | bytes 524288 | tf_op jit(solution)/shard_map/condition/pallas_call | solution.py:109
  9.5 0.5 %collective-permute-start = (bf16[32,2048]{1,0:T(8,128)(2,1)S(1)}, bf16[32,2048]{1,0:T(8,128)(2,1)S(1)}, u32[]{:S(2)}, u32[]{:S(2)}) collective-permute-start(bf16[32,2048]{1,0:T(8,128)(2,1)S(1)} %condition.2.own), channel_id=1, source_target_pairs={{0,1},{1,0},{2,3},{3,2},{4,5},{5,4},{6,7},{7,6},{8,9},{9,8},{10,11... | collective-permute-start | bytes 393224 | tf_op jit(solution)/shard_map/ppermute | solution.py:276
  10.0 0.0 collective-permute-start.1
  10.0 3.0 %score_own.1.own_low = f32[1024,128]{1,0:T(8,128)S(1)} custom-call(bf16[32,2048]{1,0:T(8,128)(2,1)S(1)} %condition.3.queries, bf16[1,1024,4096]{2,1,0:T(8,128)(2,1)} %store.3), custom_call_target="tpu_custom_call" | custom-call | flops 134217728 | bytes 4194304 | tf_op jit(solution)/shard_map/score_own/pallas_call | solution.py:165
  13.0 0.0 copy-start.1
  13.0 0.0 collective-permute-done.3.near
  13.1 2.2 %collective-permute-start.5 = (bf16[32,2048]{1,0:T(8,128)(2,1)S(1)}, bf16[32,2048]{1,0:T(8,128)(2,1)S(1)}, u32[]{:S(2)}, u32[]{:S(2)}) collective-permute-start(bf16[32,2048]{1,0:T(8,128)(2,1)S(1)} %collective-permute-done.4.far), channel_id=1, source_target_pairs={{0,1},{1,0},{2,3},{3,2},{4,5},{5,4},{6,7},{7,6},{8,9},{9,8},{10,11... | collective-permute-start | bytes 393224 | tf_op jit(solution)/shard_map/ppermute | solution.py:276
  15.3 2.8 %collective-permute-done.near = bf16[32,2048]{1,0:T(8,128)(2,1)S(1)} collective-permute-done((bf16[32,2048]{1,0:T(8,128)(2,1)S(1)}, bf16[32,2048]{1,0:T(8,128)(2,1)S(1)}, u32[]{:S(2)}, u32[]{:S(2)}) %collective-permute-start) | collective-permute-done | bytes 131104 | tf_op jit(solution)/shard_map/ppermute | solution.py:276
  18.1 0.4 %collective-permute-done.1.far = bf16[32,2048]{1,0:T(8,128)(2,1)S(1)} collective-permute-done((bf16[32,2048]{1,0:T(8,128)(2,1)S(1)}, bf16[32,2048]{1,0:T(8,128)(2,1)S(1)}, u32[]{:S(2)}, u32[]{:S(2)}) %collective-permute-start.1) | collective-permute-done | bytes 131104 | tf_op jit(solution)/shard_map/ppermute | solution.py:276
  18.4 2.4 %collective-permute-start.2 = (bf16[32,2048]{1,0:T(8,128)(2,1)S(1)}, bf16[32,2048]{1,0:T(8,128)(2,1)S(1)}, u32[]{:S(2)}, u32[]{:S(2)}) collective-permute-start(bf16[32,2048]{1,0:T(8,128)(2,1)S(1)} %collective-permute-done.1.far), channel_id=1, source_target_pairs={{0,1},{1,0},{2,3},{3,2},{4,5},{5,4},{6,7},{7,6},{8,9},{9,8},{10,11... | collective-permute-start | bytes 393224 | tf_op jit(solution)/shard_map/ppermute | solution.py:276
  20.9 0.1 collective-permute-done.5.last
  21.0 1.2 %score_low.1.low = f32[1024,128]{1,0:T(8,128)S(1)} custom-call(bf16[32,2048]{1,0:T(8,128)(2,1)S(1)} %collective-permute-done.3.near, bf16[32,2048]{1,0:T(8,128)(2,1)S(1)} %collective-permute-done.4.far, bf16[32,2048]{1,0:T(8,128)(2,1)S(1)} %collective-permute-done.5.last, bf16[1,1024,4096]{2,1,0:T(8,128)(2,1)S(1)} %copy-done, f32[1024,128]{1,0:T(8,128)S(1)} %score_own.1.own_low), custom_call_target="tpu_custom_call" | custom-call | flops 402653184 | bytes 4194304 | tf_op jit(solution)/shard_map/score_low/pallas_call | solution.py:193
  22.2 1.6 %collective-permute-done.2.last = bf16[32,2048]{1,0:T(8,128)(2,1)S(1)} collective-permute-done((bf16[32,2048]{1,0:T(8,128)(2,1)S(1)}, bf16[32,2048]{1,0:T(8,128)(2,1)S(1)}, u32[]{:S(2)}, u32[]{:S(2)}) %collective-permute-start.2) | collective-permute-done | bytes 131104 | tf_op jit(solution)/shard_map/ppermute | solution.py:276
  23.8 1.3 %score_high.1 = (bf16[32,1024]{1,0:T(8,128)(2,1)S(1)}, bf16[32,1024]{1,0:T(8,128)(2,1)S(1)}, f32[32,1024]{1,0:T(8,128)S(1)}, f32[32,1024]{1,0:T(8,128)S(1)}) custom-call(bf16[32,2048]{1,0:T(8,128)(2,1)S(1)} %collective-permute-done.near, bf16[32,2048]{1,0:T(8,128)(2,1)S(1)} %collective-permute-done.1.far, bf16[32,2048]{1,0:T(8,128)(2,1)S(1)} %collective-permute-done.2.last, ...), custom_call_target="tpu_custom_call" | custom-call | flops 536870912 | bytes 4194304 | tf_op jit(solution)/shard_map/score_high/pallas_call | solution.py:218
  25.2 0.1 collective-permute-start.7
  25.2 0.5 %collective-permute-start.6 = (bf16[32,1024]{1,0:T(8,128)(2,1)S(1)}, bf16[32,1024]{1,0:T(8,128)(2,1)S(1)}, u32[]{:S(2)}, u32[]{:S(2)}) collective-permute-start(bf16[32,1024]{1,0:T(8,128)(2,1)S(1)} %get-tuple-element.20), channel_id=1, source_target_pairs={{0,4},{4,0},{8,12},{12,8},{1,5},{5,1},{9,13},{13,9},{2,6},{6,2},{1... | collective-permute-start | bytes 196616 | tf_op jit(solution)/shard_map/ppermute | solution.py:276
  25.7 0.7 %collective-permute-done.7.received = bf16[32,1024]{1,0:T(8,128)(2,1)S(1)} collective-permute-done((bf16[32,1024]{1,0:T(8,128)(2,1)S(1)}, bf16[32,1024]{1,0:T(8,128)(2,1)S(1)}, u32[]{:S(2)}, u32[]{:S(2)}) %collective-permute-start.7) | collective-permute-done | bytes 65568 | tf_op jit(solution)/shard_map/ppermute | solution.py:276
  26.5 1.6 %collective-permute-start.8 = (bf16[32,1024]{1,0:T(8,128)(2,1)S(1)}, bf16[32,1024]{1,0:T(8,128)(2,1)S(1)}, u32[]{:S(2)}, u32[]{:S(2)}) collective-permute-start(bf16[32,1024]{1,0:T(8,128)(2,1)S(1)} %add.1), channel_id=1, source_target_pairs={{0,8},{4,12},{8,0},{12,4},{1,9},{5,13},{9,1},{13,5},{2,10},{6,14},... | collective-permute-start | bytes 196616 | tf_op jit(solution)/shard_map/ppermute | solution.py:276
  28.1 0.1 copy.6.candidates
  28.2 2.7 %collective-permute-done.8.refs_2_ = bf16[32,1024]{1,0:T(8,128)(2,1)S(1)} collective-permute-done((bf16[32,1024]{1,0:T(8,128)(2,1)S(1)}, bf16[32,1024]{1,0:T(8,128)(2,1)S(1)}, u32[]{:S(2)}, u32[]{:S(2)}) %collective-permute-start.8) | collective-permute-done | bytes 65568 | tf_op jit(solution)/shard_map/ppermute | solution.py:276
  30.8 0.7 %finish.1 = bf16[32,1024]{1,0:T(8,128)(2,1)} custom-call(s32[32,16]{1,0:T(8,128)S(1)} %copy.6.candidates, f32[32,1024]{1,0:T(8,128)S(1)} %get-tuple-element.19.refs_0_, bf16[32,1024]{1,0:T(8,128)(2,1)S(1)} %collective-permute-done.6.refs_1_, bf16[32,1024]{1,0:T(8,128)(2,1)S(1)} %collective-permute-done.8.refs_2_), custom_call_target="tpu_custom_call" | custom-call | tf_op jit(solution)/shard_map/finish/pallas_call | solution.py:264
  (6 shorter events, 0.0 us)
Async XLA Ops:
  0.0 21.0 %copy-start = (bf16[1,1024,4096]{2,1,0:T(8,128)(2,1)S(1)}, bf16[1,1024,4096]{2,1,0:T(8,128)(2,1)}, u32[]{:S(2)}) copy-start(bf16[1,1024,4096]{2,1,0:T(8,128)(2,1)} %store.3) | copy-start | bytes 25165828
  2.0 11.1 %collective-permute-start.3 = (bf16[32,2048]{1,0:T(8,128)(2,1)S(1)}, bf16[32,2048]{1,0:T(8,128)(2,1)S(1)}, u32[]{:S(2)}, u32[]{:S(2)}) collective-permute-start(bf16[32,2048]{1,0:T(8,128)(2,1)S(1)} %condition.3.queries), channel_id=1, source_target_pairs={{0,1},{1,0},{2,3},{3,2},{4,5},{5,4},{6,7},{7,6},{8,9},{9,8},{10,11... | collective-permute-start | bytes 393224 | tf_op jit(solution)/shard_map/ppermute | solution.py:276
  5.1 8.0 %collective-permute-start.4 = (bf16[32,2048]{1,0:T(8,128)(2,1)S(1)}, bf16[32,2048]{1,0:T(8,128)(2,1)S(1)}, u32[]{:S(2)}, u32[]{:S(2)}) collective-permute-start(bf16[32,2048]{1,0:T(8,128)(2,1)S(1)} %condition.3.queries), channel_id=1, source_target_pairs={{0,2},{1,3},{2,0},{3,1},{4,6},{5,7},{6,4},{7,5},{8,10},{9,11},{10,... | collective-permute-start | bytes 393224 | tf_op jit(solution)/shard_map/ppermute | solution.py:276
  9.5 8.6 %collective-permute-start = (bf16[32,2048]{1,0:T(8,128)(2,1)S(1)}, bf16[32,2048]{1,0:T(8,128)(2,1)S(1)}, u32[]{:S(2)}, u32[]{:S(2)}) collective-permute-start(bf16[32,2048]{1,0:T(8,128)(2,1)S(1)} %condition.2.own), channel_id=1, source_target_pairs={{0,1},{1,0},{2,3},{3,2},{4,5},{5,4},{6,7},{7,6},{8,9},{9,8},{10,11... | collective-permute-start | bytes 393224 | tf_op jit(solution)/shard_map/ppermute | solution.py:276
  10.0 8.5 %collective-permute-start.1 = (bf16[32,2048]{1,0:T(8,128)(2,1)S(1)}, bf16[32,2048]{1,0:T(8,128)(2,1)S(1)}, u32[]{:S(2)}, u32[]{:S(2)}) collective-permute-start(bf16[32,2048]{1,0:T(8,128)(2,1)S(1)} %condition.2.own), channel_id=1, source_target_pairs={{0,2},{1,3},{2,0},{3,1},{4,6},{5,7},{6,4},{7,5},{8,10},{9,11},{10,... | collective-permute-start | bytes 393224 | tf_op jit(solution)/shard_map/ppermute | solution.py:276
  13.0 15.1 %copy-start.1 = (s32[32,16]{0,1:T(8,128)S(1)}, s32[32,16]{0,1:T(8,128)}, u32[]{:S(2)}) copy-start(s32[32,16]{0,1:T(8,128)} %param.9) | copy-start | bytes 6148
  13.1 7.9 %collective-permute-start.5 = (bf16[32,2048]{1,0:T(8,128)(2,1)S(1)}, bf16[32,2048]{1,0:T(8,128)(2,1)S(1)}, u32[]{:S(2)}, u32[]{:S(2)}) collective-permute-start(bf16[32,2048]{1,0:T(8,128)(2,1)S(1)} %collective-permute-done.4.far), channel_id=1, source_target_pairs={{0,1},{1,0},{2,3},{3,2},{4,5},{5,4},{6,7},{7,6},{8,9},{9,8},{10,11... | collective-permute-start | bytes 393224 | tf_op jit(solution)/shard_map/ppermute | solution.py:276
  18.4 5.4 %collective-permute-start.2 = (bf16[32,2048]{1,0:T(8,128)(2,1)S(1)}, bf16[32,2048]{1,0:T(8,128)(2,1)S(1)}, u32[]{:S(2)}, u32[]{:S(2)}) collective-permute-start(bf16[32,2048]{1,0:T(8,128)(2,1)S(1)} %collective-permute-done.1.far), channel_id=1, source_target_pairs={{0,1},{1,0},{2,3},{3,2},{4,5},{5,4},{6,7},{7,6},{8,9},{9,8},{10,11... | collective-permute-start | bytes 393224 | tf_op jit(solution)/shard_map/ppermute | solution.py:276
  25.2 1.3 %collective-permute-start.7 = (bf16[32,1024]{1,0:T(8,128)(2,1)S(1)}, bf16[32,1024]{1,0:T(8,128)(2,1)S(1)}, u32[]{:S(2)}, u32[]{:S(2)}) collective-permute-start(bf16[32,1024]{1,0:T(8,128)(2,1)S(1)} %get-tuple-element.22), channel_id=1, source_target_pairs={{0,4},{4,0},{8,12},{12,8},{1,5},{5,1},{9,13},{13,9},{2,6},{6,2},{1... | collective-permute-start | bytes 196616 | tf_op jit(solution)/shard_map/ppermute | solution.py:276
  25.2 2.9 %collective-permute-start.6 = (bf16[32,1024]{1,0:T(8,128)(2,1)S(1)}, bf16[32,1024]{1,0:T(8,128)(2,1)S(1)}, u32[]{:S(2)}, u32[]{:S(2)}) collective-permute-start(bf16[32,1024]{1,0:T(8,128)(2,1)S(1)} %get-tuple-element.20), channel_id=1, source_target_pairs={{0,4},{4,0},{8,12},{12,8},{1,5},{5,1},{9,13},{13,9},{2,6},{6,2},{1... | collective-permute-start | bytes 196616 | tf_op jit(solution)/shard_map/ppermute | solution.py:276
  26.5 4.3 %collective-permute-start.8 = (bf16[32,1024]{1,0:T(8,128)(2,1)S(1)}, bf16[32,1024]{1,0:T(8,128)(2,1)S(1)}, u32[]{:S(2)}, u32[]{:S(2)}) collective-permute-start(bf16[32,1024]{1,0:T(8,128)(2,1)S(1)} %add.1), channel_id=1, source_target_pairs={{0,8},{4,12},{8,0},{12,4},{1,9},{5,13},{9,1},{13,5},{2,10},{6,14},... | collective-permute-start | bytes 196616 | tf_op jit(solution)/shard_map/ppermute | solution.py:276

commit v17 on v16

--- a/solution.py
+++ b/solution.py
@@ -102,15 +102,15 @@
     return [pl.BlockSpec(memory_space=pltpu.VMEM)] * count
 
 
-def condition(queries, left_factor, right_factor, half):
+def condition(queries, left_factor, right_factor, first, count):
     unused, block_rows, entries = queries.shape
     side = left_factor.shape[1]
     operands = [pltpu.with_memory_space_constraint(value, pltpu.HBM) for value in (queries, left_factor, right_factor)]
     return pl.pallas_call(
-        functools.partial(condition_kernel, half * side // 2, side // 2),
+        functools.partial(condition_kernel, first, count),
         in_specs=[pl.BlockSpec(memory_space=pltpu.HBM)] * 3,
         out_specs=in_vmem(1)[0],
-        out_shape=jax.ShapeDtypeStruct((block_rows, entries // 2), jnp.bfloat16),
+        out_shape=jax.ShapeDtypeStruct((block_rows, count * side), jnp.bfloat16),
         scratch_shapes=[
             pltpu.VMEM((block_rows, entries), jnp.bfloat16),
             pltpu.VMEM((side, side), jnp.float32),
@@ -126,6 +126,7 @@
 
 
 STEP = 256
+LOW_PART = 17
 MASKS = (3, 1, 2, 0)
 
 
@@ -313,7 +314,9 @@
 
 def per_device(queries, store, left_factor, right_factor, candidates):
     layers, count = lax.axis_size("layer"), lax.axis_size("blk")
-    own = [condition(queries, left_factor, right_factor, half) for half in range(2)]
+    side = left_factor.shape[1]
+    low = side * LOW_PART // 32
+    own = [condition(queries, left_factor, right_factor, *part) for part in ((0, low), (low, side - low))]
     way = on_line if layers == 4 and count == 4 else on_ring
     return way(own, store, candidates, layers)
 

time: 31.7 us -> 31.6 us (level)
  transfers between devices with their start and end apart: 9 -> 9, of which waited for: 6 -> 6; matrix products, arithmetic and copies ran while one was open for 0% -> 0% of each run, Pallas kernels for 19% -> 20%
where the time goes in v17:
time: 31.6 us; the launch traced here: 31.5 us
  starting transfers between devices  13.1 us (41%)
  Pallas kernels  10.2 us (32%)
  waiting for transfers between devices  8.02 us (25%)
    ppermute x9, starting transfers between devices, permuted(): lax.ppermute(value, axis, [(source, target_of(source) % count) for source...  13.1 us
    ppermute x9, waiting for transfers between devices, permuted(): lax.ppermute(value, axis, [(source, target_of(source) % count) for source...  8.02 us
    pallas_call x2, Pallas kernels, condition(): pl.pallas_call(functools.partial(condition_kernel, first, count), in_spec...  3.75 us
    pallas_call x1, Pallas kernels, score_own(): pl.pallas_call(own_kernel, in_specs=in_vmem(1) + [pl.BlockSpec(memory_spa...  3.09 us
    pallas_call x1, Pallas kernels, score_high(): pl.pallas_call(functools.partial(high_kernel, store.shape[2] - width), in...  1.32 us
    pallas_call x1, Pallas kernels, score_low(): pl.pallas_call(low_kernel, in_specs=in_vmem(5), out_specs=in_vmem(1)[0],...  1.31 us
    pallas_call x1, Pallas kernels, finish(): pl.pallas_call(functools.partial(finish_kernel, layers), in_specs=in_vmem...  0.74 us
  transfers between devices with their start and end apart: 9, of which 6 were waited for; matrix products, arithmetic and copies ran while one was open for 0% of the time, Pallas kernels for 20%

profile of v17, /device:TPU:0, one launch (start us, length us, event | category | flops | bytes accessed | tf_op | source)
XLA Modules:
  0.0 31.5 jit_solution(7883048682950363769)
XLA Ops:
  0.0 2.0 %condition.3.queries = bf16[32,2176]{1,0:T(8,128)(2,1)S(1)} custom-call(bf16[1,32,4096]{2,1,0:T(8,128)(2,1)} %queries_in.3, f32[1,64,64]{2,1,0:T(8,128)} %left_in.3, f32[1,64,64]{2,1,0:T(8,128)} %right_in.3), custom_call_target="tpu_custom_call" | custom-call | flops 536870912 | bytes 524288 | tf_op jit(solution)/shard_map/condition/pallas_call | solution.py:109
  2.0 3.1 %collective-permute-start.3 = (bf16[32,2176]{1,0:T(8,128)(2,1)S(1)}, bf16[32,2176]{1,0:T(8,128)(2,1)S(1)}, u32[]{:S(2)}, u32[]{:S(2)}) collective-permute-start(bf16[32,2176]{1,0:T(8,128)(2,1)S(1)} %condition.3.queries), channel_id=1, source_target_pairs={{0,1},{1,0},{2,3},{3,2},{4,5},{5,4},{6,7},{7,6},{8,9},{9,8},{10,11... | collective-permute-start | bytes 417800 | tf_op jit(solution)/shard_map/ppermute | solution.py:277
  5.1 2.6 %collective-permute-start.4 = (bf16[32,2176]{1,0:T(8,128)(2,1)S(1)}, bf16[32,2176]{1,0:T(8,128)(2,1)S(1)}, u32[]{:S(2)}, u32[]{:S(2)}) collective-permute-start(bf16[32,2176]{1,0:T(8,128)(2,1)S(1)} %condition.3.queries), channel_id=1, source_target_pairs={{0,2},{1,3},{2,0},{3,1},{4,6},{5,7},{6,4},{7,5},{8,10},{9,11},{10,... | collective-permute-start | bytes 417800 | tf_op jit(solution)/shard_map/ppermute | solution.py:277
  7.7 1.8 %condition.2.own = bf16[32,1920]{1,0:T(8,128)(2,1)S(1)} custom-call(bf16[1,32,4096]{2,1,0:T(8,128)(2,1)} %queries_in.3, f32[1,64,64]{2,1,0:T(8,128)} %left_in.3, f32[1,64,64]{2,1,0:T(8,128)} %right_in.3), custom_call_target="tpu_custom_call" | custom-call | flops 536870912 | bytes 524288 | tf_op jit(solution)/shard_map/condition/pallas_call | solution.py:109
  9.5 0.5 %collective-permute-start = (bf16[32,1920]{1,0:T(8,128)(2,1)S(1)}, bf16[32,1920]{1,0:T(8,128)(2,1)S(1)}, u32[]{:S(2)}, u32[]{:S(2)}) collective-permute-start(bf16[32,1920]{1,0:T(8,128)(2,1)S(1)} %condition.2.own), channel_id=1, source_target_pairs={{0,1},{1,0},{2,3},{3,2},{4,5},{5,4},{6,7},{7,6},{8,9},{9,8},{10,11... | collective-permute-start | bytes 368648 | tf_op jit(solution)/shard_map/ppermute | solution.py:277
  10.0 0.0 collective-permute-start.1
  10.0 3.1 %score_own.1.own_low = f32[1024,128]{1,0:T(8,128)S(1)} custom-call(bf16[32,2176]{1,0:T(8,128)(2,1)S(1)} %condition.3.queries, bf16[1,1024,4096]{2,1,0:T(8,128)(2,1)} %store.3), custom_call_target="tpu_custom_call" | custom-call | flops 142606336 | bytes 4456448 | tf_op jit(solution)/shard_map/score_own/pallas_call | solution.py:166
  13.1 0.0 copy-start.1
  13.1 0.0 collective-permute-done.3.near
  13.1 0.2 collective-permute-done.4.far
  13.3 2.3 %collective-permute-start.5 = (bf16[32,2176]{1,0:T(8,128)(2,1)S(1)}, bf16[32,2176]{1,0:T(8,128)(2,1)S(1)}, u32[]{:S(2)}, u32[]{:S(2)}) collective-permute-start(bf16[32,2176]{1,0:T(8,128)(2,1)S(1)} %collective-permute-done.4.far), channel_id=1, source_target_pairs={{0,1},{1,0},{2,3},{3,2},{4,5},{5,4},{6,7},{7,6},{8,9},{9,8},{10,11... | collective-permute-start | bytes 417800 | tf_op jit(solution)/shard_map/ppermute | solution.py:277
  15.6 1.5 %collective-permute-done.near = bf16[32,1920]{1,0:T(8,128)(2,1)S(1)} collective-permute-done((bf16[32,1920]{1,0:T(8,128)(2,1)S(1)}, bf16[32,1920]{1,0:T(8,128)(2,1)S(1)}, u32[]{:S(2)}, u32[]{:S(2)}) %collective-permute-start) | collective-permute-done | bytes 122912 | tf_op jit(solution)/shard_map/ppermute | solution.py:277
  17.1 1.4 %collective-permute-done.1.far = bf16[32,1920]{1,0:T(8,128)(2,1)S(1)} collective-permute-done((bf16[32,1920]{1,0:T(8,128)(2,1)S(1)}, bf16[32,1920]{1,0:T(8,128)(2,1)S(1)}, u32[]{:S(2)}, u32[]{:S(2)}) %collective-permute-start.1) | collective-permute-done | bytes 122912 | tf_op jit(solution)/shard_map/ppermute | solution.py:277
  18.5 2.4 %collective-permute-start.2 = (bf16[32,1920]{1,0:T(8,128)(2,1)S(1)}, bf16[32,1920]{1,0:T(8,128)(2,1)S(1)}, u32[]{:S(2)}, u32[]{:S(2)}) collective-permute-start(bf16[32,1920]{1,0:T(8,128)(2,1)S(1)} %collective-permute-done.1.far), channel_id=1, source_target_pairs={{0,1},{1,0},{2,3},{3,2},{4,5},{5,4},{6,7},{7,6},{8,9},{9,8},{10,11... | collective-permute-start | bytes 368648 | tf_op jit(solution)/shard_map/ppermute | solution.py:277
  20.9 1.3 %score_low.1.low = f32[1024,128]{1,0:T(8,128)S(1)} custom-call(bf16[32,2176]{1,0:T(8,128)(2,1)S(1)} %collective-permute-done.3.near, bf16[32,2176]{1,0:T(8,128)(2,1)S(1)} %collective-permute-done.4.far, bf16[32,2176]{1,0:T(8,128)(2,1)S(1)} %collective-permute-done.5.last, bf16[1,1024,4096]{2,1,0:T(8,128)(2,1)S(1)} %copy-done, f32[1024,128]{1,0:T(8,128)S(1)} %score_own.1.own_low), custom_call_target="tpu_custom_call" | custom-call | flops 427819008 | bytes 4456448 | tf_op jit(solution)/shard_map/score_low/pallas_call | solution.py:194
  22.2 1.5 %collective-permute-done.2.last = bf16[32,1920]{1,0:T(8,128)(2,1)S(1)} collective-permute-done((bf16[32,1920]{1,0:T(8,128)(2,1)S(1)}, bf16[32,1920]{1,0:T(8,128)(2,1)S(1)}, u32[]{:S(2)}, u32[]{:S(2)}) %collective-permute-start.2) | collective-permute-done | bytes 122912 | tf_op jit(solution)/shard_map/ppermute | solution.py:277
  23.7 1.3 %score_high.1 = (bf16[32,1024]{1,0:T(8,128)(2,1)S(1)}, bf16[32,1024]{1,0:T(8,128)(2,1)S(1)}, f32[32,1024]{1,0:T(8,128)S(1)}, f32[32,1024]{1,0:T(8,128)S(1)}) custom-call(bf16[32,1920]{1,0:T(8,128)(2,1)S(1)} %collective-permute-done.near, bf16[32,1920]{1,0:T(8,128)(2,1)S(1)} %collective-permute-done.1.far, bf16[32,1920]{1,0:T(8,128)(2,1)S(1)} %collective-permute-done.2.last, ...), custom_call_target="tpu_custom_call" | custom-call | flops 503316480 | bytes 3932160 | tf_op jit(solution)/shard_map/score_high/pallas_call | solution.py:219
  25.1 0.1 collective-permute-start.7
  25.2 0.5 %collective-permute-start.6 = (bf16[32,1024]{1,0:T(8,128)(2,1)S(1)}, bf16[32,1024]{1,0:T(8,128)(2,1)S(1)}, u32[]{:S(2)}, u32[]{:S(2)}) collective-permute-start(bf16[32,1024]{1,0:T(8,128)(2,1)S(1)} %get-tuple-element.20), channel_id=1, source_target_pairs={{0,4},{4,0},{8,12},{12,8},{1,5},{5,1},{9,13},{13,9},{2,6},{6,2},{1... | collective-permute-start | bytes 196616 | tf_op jit(solution)/shard_map/ppermute | solution.py:277
  25.6 0.7 %collective-permute-done.7.received = bf16[32,1024]{1,0:T(8,128)(2,1)S(1)} collective-permute-done((bf16[32,1024]{1,0:T(8,128)(2,1)S(1)}, bf16[32,1024]{1,0:T(8,128)(2,1)S(1)}, u32[]{:S(2)}, u32[]{:S(2)}) %collective-permute-start.7) | collective-permute-done | bytes 65568 | tf_op jit(solution)/shard_map/ppermute | solution.py:277
  26.4 1.6 %collective-permute-start.8 = (bf16[32,1024]{1,0:T(8,128)(2,1)S(1)}, bf16[32,1024]{1,0:T(8,128)(2,1)S(1)}, u32[]{:S(2)}, u32[]{:S(2)}) collective-permute-start(bf16[32,1024]{1,0:T(8,128)(2,1)S(1)} %add.1), channel_id=1, source_target_pairs={{0,8},{4,12},{8,0},{12,4},{1,9},{5,13},{9,1},{13,5},{2,10},{6,14},... | collective-permute-start | bytes 196616 | tf_op jit(solution)/shard_map/ppermute | solution.py:277
  28.0 0.1 copy.6.candidates
  28.1 2.7 %collective-permute-done.8.refs_2_ = bf16[32,1024]{1,0:T(8,128)(2,1)S(1)} collective-permute-done((bf16[32,1024]{1,0:T(8,128)(2,1)S(1)}, bf16[32,1024]{1,0:T(8,128)(2,1)S(1)}, u32[]{:S(2)}, u32[]{:S(2)}) %collective-permute-start.8) | collective-permute-done | bytes 65568 | tf_op jit(solution)/shard_map/ppermute | solution.py:277
  30.7 0.7 %finish.1 = bf16[32,1024]{1,0:T(8,128)(2,1)} custom-call(s32[32,16]{1,0:T(8,128)S(1)} %copy.6.candidates, f32[32,1024]{1,0:T(8,128)S(1)} %get-tuple-element.19.refs_0_, bf16[32,1024]{1,0:T(8,128)(2,1)S(1)} %collective-permute-done.6.refs_1_, bf16[32,1024]{1,0:T(8,128)(2,1)S(1)} %collective-permute-done.8.refs_2_), custom_call_target="tpu_custom_call" | custom-call | tf_op jit(solution)/shard_map/finish/pallas_call | solution.py:265
  (6 shorter events, 0.0 us)
Async XLA Ops:
  0.0 20.9 %copy-start = (bf16[1,1024,4096]{2,1,0:T(8,128)(2,1)S(1)}, bf16[1,1024,4096]{2,1,0:T(8,128)(2,1)}, u32[]{:S(2)}) copy-start(bf16[1,1024,4096]{2,1,0:T(8,128)(2,1)} %store.3) | copy-start | bytes 25165828
  2.0 11.1 %collective-permute-start.3 = (bf16[32,2176]{1,0:T(8,128)(2,1)S(1)}, bf16[32,2176]{1,0:T(8,128)(2,1)S(1)}, u32[]{:S(2)}, u32[]{:S(2)}) collective-permute-start(bf16[32,2176]{1,0:T(8,128)(2,1)S(1)} %condition.3.queries), channel_id=1, source_target_pairs={{0,1},{1,0},{2,3},{3,2},{4,5},{5,4},{6,7},{7,6},{8,9},{9,8},{10,11... | collective-permute-start | bytes 417800 | tf_op jit(solution)/shard_map/ppermute | solution.py:277
  5.1 8.2 %collective-permute-start.4 = (bf16[32,2176]{1,0:T(8,128)(2,1)S(1)}, bf16[32,2176]{1,0:T(8,128)(2,1)S(1)}, u32[]{:S(2)}, u32[]{:S(2)}) collective-permute-start(bf16[32,2176]{1,0:T(8,128)(2,1)S(1)} %condition.3.queries), channel_id=1, source_target_pairs={{0,2},{1,3},{2,0},{3,1},{4,6},{5,7},{6,4},{7,5},{8,10},{9,11},{10,... | collective-permute-start | bytes 417800 | tf_op jit(solution)/shard_map/ppermute | solution.py:277
  9.5 7.6 %collective-permute-start = (bf16[32,1920]{1,0:T(8,128)(2,1)S(1)}, bf16[32,1920]{1,0:T(8,128)(2,1)S(1)}, u32[]{:S(2)}, u32[]{:S(2)}) collective-permute-start(bf16[32,1920]{1,0:T(8,128)(2,1)S(1)} %condition.2.own), channel_id=1, source_target_pairs={{0,1},{1,0},{2,3},{3,2},{4,5},{5,4},{6,7},{7,6},{8,9},{9,8},{10,11... | collective-permute-start | bytes 368648 | tf_op jit(solution)/shard_map/ppermute | solution.py:277
  10.0 8.5 %collective-permute-start.1 = (bf16[32,1920]{1,0:T(8,128)(2,1)S(1)}, bf16[32,1920]{1,0:T(8,128)(2,1)S(1)}, u32[]{:S(2)}, u32[]{:S(2)}) collective-permute-start(bf16[32,1920]{1,0:T(8,128)(2,1)S(1)} %condition.2.own), channel_id=1, source_target_pairs={{0,2},{1,3},{2,0},{3,1},{4,6},{5,7},{6,4},{7,5},{8,10},{9,11},{10,... | collective-permute-start | bytes 368648 | tf_op jit(solution)/shard_map/ppermute | solution.py:277
  13.1 14.9 %copy-start.1 = (s32[32,16]{0,1:T(8,128)S(1)}, s32[32,16]{0,1:T(8,128)}, u32[]{:S(2)}) copy-start(s32[32,16]{0,1:T(8,128)} %param.9) | copy-start | bytes 6148
  13.3 7.6 %collective-permute-start.5 = (bf16[32,2176]{1,0:T(8,128)(2,1)S(1)}, bf16[32,2176]{1,0:T(8,128)(2,1)S(1)}, u32[]{:S(2)}, u32[]{:S(2)}) collective-permute-start(bf16[32,2176]{1,0:T(8,128)(2,1)S(1)} %collective-permute-done.4.far), channel_id=1, source_target_pairs={{0,1},{1,0},{2,3},{3,2},{4,5},{5,4},{6,7},{7,6},{8,9},{9,8},{10,11... | collective-permute-start | bytes 417800 | tf_op jit(solution)/shard_map/ppermute | solution.py:277
  18.5 5.3 %collective-permute-start.2 = (bf16[32,1920]{1,0:T(8,128)(2,1)S(1)}, bf16[32,1920]{1,0:T(8,128)(2,1)S(1)}, u32[]{:S(2)}, u32[]{:S(2)}) collective-permute-start(bf16[32,1920]{1,0:T(8,128)(2,1)S(1)} %collective-permute-done.1.far), channel_id=1, source_target_pairs={{0,1},{1,0},{2,3},{3,2},{4,5},{5,4},{6,7},{7,6},{8,9},{9,8},{10,11... | collective-permute-start | bytes 368648 | tf_op jit(solution)/shard_map/ppermute | solution.py:277
  25.1 1.3 %collective-permute-start.7 = (bf16[32,1024]{1,0:T(8,128)(2,1)S(1)}, bf16[32,1024]{1,0:T(8,128)(2,1)S(1)}, u32[]{:S(2)}, u32[]{:S(2)}) collective-permute-start(bf16[32,1024]{1,0:T(8,128)(2,1)S(1)} %get-tuple-element.22), channel_id=1, source_target_pairs={{0,4},{4,0},{8,12},{12,8},{1,5},{5,1},{9,13},{13,9},{2,6},{6,2},{1... | collective-permute-start | bytes 196616 | tf_op jit(solution)/shard_map/ppermute | solution.py:277
  25.2 2.9 %collective-permute-start.6 = (bf16[32,1024]{1,0:T(8,128)(2,1)S(1)}, bf16[32,1024]{1,0:T(8,128)(2,1)S(1)}, u32[]{:S(2)}, u32[]{:S(2)}) collective-permute-start(bf16[32,1024]{1,0:T(8,128)(2,1)S(1)} %get-tuple-element.20), channel_id=1, source_target_pairs={{0,4},{4,0},{8,12},{12,8},{1,5},{5,1},{9,13},{13,9},{2,6},{6,2},{1... | collective-permute-start | bytes 196616 | tf_op jit(solution)/shard_map/ppermute | solution.py:277
  26.4 4.3 %collective-permute-start.8 = (bf16[32,1024]{1,0:T(8,128)(2,1)S(1)}, bf16[32,1024]{1,0:T(8,128)(2,1)S(1)}, u32[]{:S(2)}, u32[]{:S(2)}) collective-permute-start(bf16[32,1024]{1,0:T(8,128)(2,1)S(1)} %add.1), channel_id=1, source_target_pairs={{0,8},{4,12},{8,0},{12,4},{1,9},{5,13},{9,1},{13,5},{2,10},{6,14},... | collective-permute-start | bytes 196616 | tf_op jit(solution)/shard_map/ppermute | solution.py:277

commit v18 on v17

--- a/solution.py
+++ b/solution.py
@@ -126,7 +126,7 @@
 
 
 STEP = 256
-LOW_PART = 17
+LOW_PART = 18
 MASKS = (3, 1, 2, 0)
 
 

time: 31.6 us -> 31.5 us (level)
  transfers between devices with their start and end apart: 9 -> 9, of which waited for: 6 -> 5; matrix products, arithmetic and copies ran while one was open for 0% -> 0% of each run, Pallas kernels for 20% -> 20%
where the time goes in v18:
time: 31.5 us; the launch traced here: 31.3 us
  starting transfers between devices  13.1 us (42%)
  Pallas kernels  10.3 us (33%)
  waiting for transfers between devices  7.75 us (25%)
    ppermute x9, starting transfers between devices, permuted(): lax.ppermute(value, axis, [(source, target_of(source) % count) for source...  13.1 us
    ppermute x9, waiting for transfers between devices, permuted(): lax.ppermute(value, axis, [(source, target_of(source) % count) for source...  7.75 us
    pallas_call x2, Pallas kernels, condition(): pl.pallas_call(functools.partial(condition_kernel, first, count), in_spec...  3.76 us
    pallas_call x1, Pallas kernels, score_own(): pl.pallas_call(own_kernel, in_specs=in_vmem(1) + [pl.BlockSpec(memory_spa...  3.21 us
    pallas_call x1, Pallas kernels, score_low(): pl.pallas_call(low_kernel, in_specs=in_vmem(5), out_specs=in_vmem(1)[0],...  1.37 us
    pallas_call x1, Pallas kernels, score_high(): pl.pallas_call(functools.partial(high_kernel, store.shape[2] - width), in...  1.21 us
    pallas_call x1, Pallas kernels, finish(): pl.pallas_call(functools.partial(finish_kernel, layers), in_specs=in_vmem...  0.74 us
  transfers between devices with their start and end apart: 9, of which 5 were waited for; matrix products, arithmetic and copies ran while one was open for 0% of the time, Pallas kernels for 20%

profile of v18, /device:TPU:0, one launch (start us, length us, event | category | flops | bytes accessed | tf_op | source)
XLA Modules:
  0.0 31.3 jit_solution(12108152887334290502)
XLA Ops:
  0.0 2.0 %condition.3.queries = bf16[32,2304]{1,0:T(8,128)(2,1)S(1)} custom-call(bf16[1,32,4096]{2,1,0:T(8,128)(2,1)} %queries_in.3, f32[1,64,64]{2,1,0:T(8,128)} %left_in.3, f32[1,64,64]{2,1,0:T(8,128)} %right_in.3), custom_call_target="tpu_custom_call" | custom-call | flops 536870912 | bytes 524288 | tf_op jit(solution)/shard_map/condition/pallas_call | solution.py:109
  2.0 3.1 %collective-permute-start.3 = (bf16[32,2304]{1,0:T(8,128)(2,1)S(1)}, bf16[32,2304]{1,0:T(8,128)(2,1)S(1)}, u32[]{:S(2)}, u32[]{:S(2)}) collective-permute-start(bf16[32,2304]{1,0:T(8,128)(2,1)S(1)} %condition.3.queries), channel_id=1, source_target_pairs={{0,1},{1,0},{2,3},{3,2},{4,5},{5,4},{6,7},{7,6},{8,9},{9,8},{10,11... | collective-permute-start | bytes 442376 | tf_op jit(solution)/shard_map/ppermute | solution.py:277
  5.1 2.6 %collective-permute-start.4 = (bf16[32,2304]{1,0:T(8,128)(2,1)S(1)}, bf16[32,2304]{1,0:T(8,128)(2,1)S(1)}, u32[]{:S(2)}, u32[]{:S(2)}) collective-permute-start(bf16[32,2304]{1,0:T(8,128)(2,1)S(1)} %condition.3.queries), channel_id=1, source_target_pairs={{0,2},{1,3},{2,0},{3,1},{4,6},{5,7},{6,4},{7,5},{8,10},{9,11},{10,... | collective-permute-start | bytes 442376 | tf_op jit(solution)/shard_map/ppermute | solution.py:277
  7.7 1.8 %condition.2.own = bf16[32,1792]{1,0:T(8,128)(2,1)S(1)} custom-call(bf16[1,32,4096]{2,1,0:T(8,128)(2,1)} %queries_in.3, f32[1,64,64]{2,1,0:T(8,128)} %left_in.3, f32[1,64,64]{2,1,0:T(8,128)} %right_in.3), custom_call_target="tpu_custom_call" | custom-call | flops 536870912 | bytes 524288 | tf_op jit(solution)/shard_map/condition/pallas_call | solution.py:109
  9.5 0.5 %collective-permute-start = (bf16[32,1792]{1,0:T(8,128)(2,1)S(1)}, bf16[32,1792]{1,0:T(8,128)(2,1)S(1)}, u32[]{:S(2)}, u32[]{:S(2)}) collective-permute-start(bf16[32,1792]{1,0:T(8,128)(2,1)S(1)} %condition.2.own), channel_id=1, source_target_pairs={{0,1},{1,0},{2,3},{3,2},{4,5},{5,4},{6,7},{7,6},{8,9},{9,8},{10,11... | collective-permute-start | bytes 344072 | tf_op jit(solution)/shard_map/ppermute | solution.py:277
  10.0 0.0 collective-permute-start.1
  10.0 3.2 %score_own.1.own_low = f32[1024,128]{1,0:T(8,128)S(1)} custom-call(bf16[32,2304]{1,0:T(8,128)(2,1)S(1)} %condition.3.queries, bf16[1,1024,4096]{2,1,0:T(8,128)(2,1)} %store.3), custom_call_target="tpu_custom_call" | custom-call | flops 150994944 | bytes 4718592 | tf_op jit(solution)/shard_map/score_own/pallas_call | solution.py:166
  13.2 0.0 copy-start.1
  13.2 0.5 %collective-permute-done.4.far = bf16[32,2304]{1,0:T(8,128)(2,1)S(1)} collective-permute-done((bf16[32,2304]{1,0:T(8,128)(2,1)S(1)}, bf16[32,2304]{1,0:T(8,128)(2,1)S(1)}, u32[]{:S(2)}, u32[]{:S(2)}) %collective-permute-start.4) | collective-permute-done | bytes 147488 | tf_op jit(solution)/shard_map/ppermute | solution.py:277
  13.7 2.3 %collective-permute-start.5 = (bf16[32,2304]{1,0:T(8,128)(2,1)S(1)}, bf16[32,2304]{1,0:T(8,128)(2,1)S(1)}, u32[]{:S(2)}, u32[]{:S(2)}) collective-permute-start(bf16[32,2304]{1,0:T(8,128)(2,1)S(1)} %collective-permute-done.4.far), channel_id=1, source_target_pairs={{0,1},{1,0},{2,3},{3,2},{4,5},{5,4},{6,7},{7,6},{8,9},{9,8},{10,11... | collective-permute-start | bytes 442376 | tf_op jit(solution)/shard_map/ppermute | solution.py:277
  16.0 0.0 collective-permute-done.near
  16.0 2.5 %collective-permute-done.1.far = bf16[32,1792]{1,0:T(8,128)(2,1)S(1)} collective-permute-done((bf16[32,1792]{1,0:T(8,128)(2,1)S(1)}, bf16[32,1792]{1,0:T(8,128)(2,1)S(1)}, u32[]{:S(2)}, u32[]{:S(2)}) %collective-permute-start.1) | collective-permute-done | bytes 114720 | tf_op jit(solution)/shard_map/ppermute | solution.py:277
  18.5 2.4 %collective-permute-start.2 = (bf16[32,1792]{1,0:T(8,128)(2,1)S(1)}, bf16[32,1792]{1,0:T(8,128)(2,1)S(1)}, u32[]{:S(2)}, u32[]{:S(2)}) collective-permute-start(bf16[32,1792]{1,0:T(8,128)(2,1)S(1)} %collective-permute-done.1.far), channel_id=1, source_target_pairs={{0,1},{1,0},{2,3},{3,2},{4,5},{5,4},{6,7},{7,6},{8,9},{9,8},{10,11... | collective-permute-start | bytes 344072 | tf_op jit(solution)/shard_map/ppermute | solution.py:277
  20.9 1.4 %score_low.1.low = f32[1024,128]{1,0:T(8,128)S(1)} custom-call(bf16[32,2304]{1,0:T(8,128)(2,1)S(1)} %collective-permute-done.3.near, bf16[32,2304]{1,0:T(8,128)(2,1)S(1)} %collective-permute-done.4.far, bf16[32,2304]{1,0:T(8,128)(2,1)S(1)} %collective-permute-done.5.last, bf16[1,1024,4096]{2,1,0:T(8,128)(2,1)S(1)} %copy-done, f32[1024,128]{1,0:T(8,128)S(1)} %score_own.1.own_low), custom_call_target="tpu_custom_call" | custom-call | flops 452984832 | bytes 4718592 | tf_op jit(solution)/shard_map/score_low/pallas_call | solution.py:194
  22.3 1.4 %collective-permute-done.2.last = bf16[32,1792]{1,0:T(8,128)(2,1)S(1)} collective-permute-done((bf16[32,1792]{1,0:T(8,128)(2,1)S(1)}, bf16[32,1792]{1,0:T(8,128)(2,1)S(1)}, u32[]{:S(2)}, u32[]{:S(2)}) %collective-permute-start.2) | collective-permute-done | bytes 114720 | tf_op jit(solution)/shard_map/ppermute | solution.py:277
  23.7 1.2 %score_high.1 = (bf16[32,1024]{1,0:T(8,128)(2,1)S(1)}, bf16[32,1024]{1,0:T(8,128)(2,1)S(1)}, f32[32,1024]{1,0:T(8,128)S(1)}, f32[32,1024]{1,0:T(8,128)S(1)}) custom-call(bf16[32,1792]{1,0:T(8,128)(2,1)S(1)} %collective-permute-done.near, bf16[32,1792]{1,0:T(8,128)(2,1)S(1)} %collective-permute-done.1.far, bf16[32,1792]{1,0:T(8,128)(2,1)S(1)} %collective-permute-done.2.last, ...), custom_call_target="tpu_custom_call" | custom-call | flops 469762048 | bytes 3670016 | tf_op jit(solution)/shard_map/score_high/pallas_call | solution.py:219
  24.9 0.1 collective-permute-start.7
  25.0 0.5 %collective-permute-start.6 = (bf16[32,1024]{1,0:T(8,128)(2,1)S(1)}, bf16[32,1024]{1,0:T(8,128)(2,1)S(1)}, u32[]{:S(2)}, u32[]{:S(2)}) collective-permute-start(bf16[32,1024]{1,0:T(8,128)(2,1)S(1)} %get-tuple-element.20), channel_id=1, source_target_pairs={{0,4},{4,0},{8,12},{12,8},{1,5},{5,1},{9,13},{13,9},{2,6},{6,2},{1... | collective-permute-start | bytes 196616 | tf_op jit(solution)/shard_map/ppermute | solution.py:277
  25.5 0.7 %collective-permute-done.7.received = bf16[32,1024]{1,0:T(8,128)(2,1)S(1)} collective-permute-done((bf16[32,1024]{1,0:T(8,128)(2,1)S(1)}, bf16[32,1024]{1,0:T(8,128)(2,1)S(1)}, u32[]{:S(2)}, u32[]{:S(2)}) %collective-permute-start.7) | collective-permute-done | bytes 65568 | tf_op jit(solution)/shard_map/ppermute | solution.py:277
  26.2 1.6 %collective-permute-start.8 = (bf16[32,1024]{1,0:T(8,128)(2,1)S(1)}, bf16[32,1024]{1,0:T(8,128)(2,1)S(1)}, u32[]{:S(2)}, u32[]{:S(2)}) collective-permute-start(bf16[32,1024]{1,0:T(8,128)(2,1)S(1)} %add.1), channel_id=1, source_target_pairs={{0,8},{4,12},{8,0},{12,4},{1,9},{5,13},{9,1},{13,5},{2,10},{6,14},... | collective-permute-start | bytes 196616 | tf_op jit(solution)/shard_map/ppermute | solution.py:277
  27.8 0.1 copy.6.candidates
  27.9 0.0 collective-permute-done.6.refs_1_
  27.9 2.7 %collective-permute-done.8.refs_2_ = bf16[32,1024]{1,0:T(8,128)(2,1)S(1)} collective-permute-done((bf16[32,1024]{1,0:T(8,128)(2,1)S(1)}, bf16[32,1024]{1,0:T(8,128)(2,1)S(1)}, u32[]{:S(2)}, u32[]{:S(2)}) %collective-permute-start.8) | collective-permute-done | bytes 65568 | tf_op jit(solution)/shard_map/ppermute | solution.py:277
  30.6 0.7 %finish.1 = bf16[32,1024]{1,0:T(8,128)(2,1)} custom-call(s32[32,16]{1,0:T(8,128)S(1)} %copy.6.candidates, f32[32,1024]{1,0:T(8,128)S(1)} %get-tuple-element.19.refs_0_, bf16[32,1024]{1,0:T(8,128)(2,1)S(1)} %collective-permute-done.6.refs_1_, bf16[32,1024]{1,0:T(8,128)(2,1)S(1)} %collective-permute-done.8.refs_2_), custom_call_target="tpu_custom_call" | custom-call | tf_op jit(solution)/shard_map/finish/pallas_call | solution.py:265
  (6 shorter events, 0.0 us)
Async XLA Ops:
  0.0 20.9 %copy-start = (bf16[1,1024,4096]{2,1,0:T(8,128)(2,1)S(1)}, bf16[1,1024,4096]{2,1,0:T(8,128)(2,1)}, u32[]{:S(2)}) copy-start(bf16[1,1024,4096]{2,1,0:T(8,128)(2,1)} %store.3) | copy-start | bytes 25165828
  2.0 11.2 %collective-permute-start.3 = (bf16[32,2304]{1,0:T(8,128)(2,1)S(1)}, bf16[32,2304]{1,0:T(8,128)(2,1)S(1)}, u32[]{:S(2)}, u32[]{:S(2)}) collective-permute-start(bf16[32,2304]{1,0:T(8,128)(2,1)S(1)} %condition.3.queries), channel_id=1, source_target_pairs={{0,1},{1,0},{2,3},{3,2},{4,5},{5,4},{6,7},{7,6},{8,9},{9,8},{10,11... | collective-permute-start | bytes 442376 | tf_op jit(solution)/shard_map/ppermute | solution.py:277
  5.1 8.6 %collective-permute-start.4 = (bf16[32,2304]{1,0:T(8,128)(2,1)S(1)}, bf16[32,2304]{1,0:T(8,128)(2,1)S(1)}, u32[]{:S(2)}, u32[]{:S(2)}) collective-permute-start(bf16[32,2304]{1,0:T(8,128)(2,1)S(1)} %condition.3.queries), channel_id=1, source_target_pairs={{0,2},{1,3},{2,0},{3,1},{4,6},{5,7},{6,4},{7,5},{8,10},{9,11},{10,... | collective-permute-start | bytes 442376 | tf_op jit(solution)/shard_map/ppermute | solution.py:277
  9.5 6.6 %collective-permute-start = (bf16[32,1792]{1,0:T(8,128)(2,1)S(1)}, bf16[32,1792]{1,0:T(8,128)(2,1)S(1)}, u32[]{:S(2)}, u32[]{:S(2)}) collective-permute-start(bf16[32,1792]{1,0:T(8,128)(2,1)S(1)} %condition.2.own), channel_id=1, source_target_pairs={{0,1},{1,0},{2,3},{3,2},{4,5},{5,4},{6,7},{7,6},{8,9},{9,8},{10,11... | collective-permute-start | bytes 344072 | tf_op jit(solution)/shard_map/ppermute | solution.py:277
  10.0 8.5 %collective-permute-start.1 = (bf16[32,1792]{1,0:T(8,128)(2,1)S(1)}, bf16[32,1792]{1,0:T(8,128)(2,1)S(1)}, u32[]{:S(2)}, u32[]{:S(2)}) collective-permute-start(bf16[32,1792]{1,0:T(8,128)(2,1)S(1)} %condition.2.own), channel_id=1, source_target_pairs={{0,2},{1,3},{2,0},{3,1},{4,6},{5,7},{6,4},{7,5},{8,10},{9,11},{10,... | collective-permute-start | bytes 344072 | tf_op jit(solution)/shard_map/ppermute | solution.py:277
  13.2 14.6 %copy-start.1 = (s32[32,16]{0,1:T(8,128)S(1)}, s32[32,16]{0,1:T(8,128)}, u32[]{:S(2)}) copy-start(s32[32,16]{0,1:T(8,128)} %param.9) | copy-start | bytes 6148
  13.7 7.3 %collective-permute-start.5 = (bf16[32,2304]{1,0:T(8,128)(2,1)S(1)}, bf16[32,2304]{1,0:T(8,128)(2,1)S(1)}, u32[]{:S(2)}, u32[]{:S(2)}) collective-permute-start(bf16[32,2304]{1,0:T(8,128)(2,1)S(1)} %collective-permute-done.4.far), channel_id=1, source_target_pairs={{0,1},{1,0},{2,3},{3,2},{4,5},{5,4},{6,7},{7,6},{8,9},{9,8},{10,11... | collective-permute-start | bytes 442376 | tf_op jit(solution)/shard_map/ppermute | solution.py:277
  18.5 5.2 %collective-permute-start.2 = (bf16[32,1792]{1,0:T(8,128)(2,1)S(1)}, bf16[32,1792]{1,0:T(8,128)(2,1)S(1)}, u32[]{:S(2)}, u32[]{:S(2)}) collective-permute-start(bf16[32,1792]{1,0:T(8,128)(2,1)S(1)} %collective-permute-done.1.far), channel_id=1, source_target_pairs={{0,1},{1,0},{2,3},{3,2},{4,5},{5,4},{6,7},{7,6},{8,9},{9,8},{10,11... | collective-permute-start | bytes 344072 | tf_op jit(solution)/shard_map/ppermute | solution.py:277
  24.9 1.3 %collective-permute-start.7 = (bf16[32,1024]{1,0:T(8,128)(2,1)S(1)}, bf16[32,1024]{1,0:T(8,128)(2,1)S(1)}, u32[]{:S(2)}, u32[]{:S(2)}) collective-permute-start(bf16[32,1024]{1,0:T(8,128)(2,1)S(1)} %get-tuple-element.22), channel_id=1, source_target_pairs={{0,4},{4,0},{8,12},{12,8},{1,5},{5,1},{9,13},{13,9},{2,6},{6,2},{1... | collective-permute-start | bytes 196616 | tf_op jit(solution)/shard_map/ppermute | solution.py:277
  25.0 2.9 %collective-permute-start.6 = (bf16[32,1024]{1,0:T(8,128)(2,1)S(1)}, bf16[32,1024]{1,0:T(8,128)(2,1)S(1)}, u32[]{:S(2)}, u32[]{:S(2)}) collective-permute-start(bf16[32,1024]{1,0:T(8,128)(2,1)S(1)} %get-tuple-element.20), channel_id=1, source_target_pairs={{0,4},{4,0},{8,12},{12,8},{1,5},{5,1},{9,13},{13,9},{2,6},{6,2},{1... | collective-permute-start | bytes 196616 | tf_op jit(solution)/shard_map/ppermute | solution.py:277
  26.2 4.3 %collective-permute-start.8 = (bf16[32,1024]{1,0:T(8,128)(2,1)S(1)}, bf16[32,1024]{1,0:T(8,128)(2,1)S(1)}, u32[]{:S(2)}, u32[]{:S(2)}) collective-permute-start(bf16[32,1024]{1,0:T(8,128)(2,1)S(1)} %add.1), channel_id=1, source_target_pairs={{0,8},{4,12},{8,0},{12,4},{1,9},{5,13},{9,1},{13,5},{2,10},{6,14},... | collective-permute-start | bytes 196616 | tf_op jit(solution)/shard_map/ppermute | solution.py:277

commit v19 on v18

--- a/solution.py
+++ b/solution.py
@@ -126,7 +126,7 @@
 
 
 STEP = 256
-LOW_PART = 18
+LOW_PART = 20
 MASKS = (3, 1, 2, 0)
 
 

time: 31.5 us -> 38 us (1.21)
  waiting for transfers between devices: 7.75 us -> 16 us
  starting transfers between devices: 13.1 us -> 11.2 us
    ppermute x9, waiting for transfers between devices: 7.75 us -> 16 us  [permuted(): lax.ppermute(value, axis, [(source, target_of(source) % count) for source...]
    ppermute x9, starting transfers between devices: 13.1 us -> 11.2 us  [permuted(): lax.ppermute(value, axis, [(source, target_of(source) % count) for source...]
  transfers between devices with their start and end apart: 9 -> 9, of which waited for: 5 -> 7; matrix products, arithmetic and copies ran while one was open for 0% -> 0% of each run, Pallas kernels for 20% -> 17%
where the time goes in v19:
time: 38 us; the launch traced here: 37.9 us
  waiting for transfers between devices  16 us (42%)
  starting transfers between devices  11.2 us (29%)
  Pallas kernels  10.5 us (28%)
    ppermute x9, waiting for transfers between devices, permuted(): lax.ppermute(value, axis, [(source, target_of(source) % count) for source...  16 us
    ppermute x9, starting transfers between devices, permuted(): lax.ppermute(value, axis, [(source, target_of(source) % count) for source...  11.2 us
    pallas_call x2, Pallas kernels, condition(): pl.pallas_call(functools.partial(condition_kernel, first, count), in_spec...  3.77 us
    pallas_call x1, Pallas kernels, score_own(): pl.pallas_call(own_kernel, in_specs=in_vmem(1) + [pl.BlockSpec(memory_spa...  3.36 us
    pallas_call x1, Pallas kernels, score_low(): pl.pallas_call(low_kernel, in_specs=in_vmem(5), out_specs=in_vmem(1)[0],...  1.5 us
    pallas_call x1, Pallas kernels, score_high(): pl.pallas_call(functools.partial(high_kernel, store.shape[2] - width), in...  1.08 us
  transfers between devices with their start and end apart: 9, of which 7 were waited for; matrix products, arithmetic and copies ran while one was open for 0% of the time, Pallas kernels for 17%

profile of v19, /device:TPU:0, one launch (start us, length us, event | category | flops | bytes accessed | tf_op | source)
XLA Modules:
  0.0 37.9 jit_solution(15829257846659020970)
XLA Ops:
  0.0 2.0 %condition.3.queries = bf16[32,2560]{1,0:T(8,128)(2,1)S(1)} custom-call(bf16[1,32,4096]{2,1,0:T(8,128)(2,1)} %queries_in.3, f32[1,64,64]{2,1,0:T(8,128)} %left_in.3, f32[1,64,64]{2,1,0:T(8,128)} %right_in.3), custom_call_target="tpu_custom_call" | custom-call | flops 536870912 | bytes 524288 | tf_op jit(solution)/shard_map/condition/pallas_call | solution.py:109
  2.1 3.1 %collective-permute-start.3 = (bf16[32,2560]{1,0:T(8,128)(2,1)S(1)}, bf16[32,2560]{1,0:T(8,128)(2,1)S(1)}, u32[]{:S(2)}, u32[]{:S(2)}) collective-permute-start(bf16[32,2560]{1,0:T(8,128)(2,1)S(1)} %condition.3.queries), channel_id=1, source_target_pairs={{0,1},{1,0},{2,3},{3,2},{4,5},{5,4},{6,7},{7,6},{8,9},{9,8},{10,11... | collective-permute-start | bytes 491528 | tf_op jit(solution)/shard_map/ppermute | solution.py:277
  5.1 2.6 %collective-permute-start.4 = (bf16[32,2560]{1,0:T(8,128)(2,1)S(1)}, bf16[32,2560]{1,0:T(8,128)(2,1)S(1)}, u32[]{:S(2)}, u32[]{:S(2)}) collective-permute-start(bf16[32,2560]{1,0:T(8,128)(2,1)S(1)} %condition.3.queries), channel_id=1, source_target_pairs={{0,2},{1,3},{2,0},{3,1},{4,6},{5,7},{6,4},{7,5},{8,10},{9,11},{10,... | collective-permute-start | bytes 491528 | tf_op jit(solution)/shard_map/ppermute | solution.py:277
  7.7 3.4 %score_own.1.own_low = f32[1024,128]{1,0:T(8,128)S(1)} custom-call(bf16[32,2560]{1,0:T(8,128)(2,1)S(1)} %condition.3.queries, bf16[1,1024,4096]{2,1,0:T(8,128)(2,1)} %store.3), custom_call_target="tpu_custom_call" | custom-call | flops 167772160 | bytes 5242880 | tf_op jit(solution)/shard_map/score_own/pallas_call | solution.py:166
  11.1 1.5 %collective-permute-done.3.near = bf16[32,2560]{1,0:T(8,128)(2,1)S(1)} collective-permute-done((bf16[32,2560]{1,0:T(8,128)(2,1)S(1)}, bf16[32,2560]{1,0:T(8,128)(2,1)S(1)}, u32[]{:S(2)}, u32[]{:S(2)}) %collective-permute-start.3) | collective-permute-done | bytes 163872 | tf_op jit(solution)/shard_map/ppermute | solution.py:277
  12.6 2.7 %collective-permute-done.4.far = bf16[32,2560]{1,0:T(8,128)(2,1)S(1)} collective-permute-done((bf16[32,2560]{1,0:T(8,128)(2,1)S(1)}, bf16[32,2560]{1,0:T(8,128)(2,1)S(1)}, u32[]{:S(2)}, u32[]{:S(2)}) %collective-permute-start.4) | collective-permute-done | bytes 163872 | tf_op jit(solution)/shard_map/ppermute | solution.py:277
  15.3 0.4 %collective-permute-start.5 = (bf16[32,2560]{1,0:T(8,128)(2,1)S(1)}, bf16[32,2560]{1,0:T(8,128)(2,1)S(1)}, u32[]{:S(2)}, u32[]{:S(2)}) collective-permute-start(bf16[32,2560]{1,0:T(8,128)(2,1)S(1)} %collective-permute-done.4.far), channel_id=1, source_target_pairs={{0,1},{1,0},{2,3},{3,2},{4,5},{5,4},{6,7},{7,6},{8,9},{9,8},{10,11... | collective-permute-start | bytes 491528 | tf_op jit(solution)/shard_map/ppermute | solution.py:277
  15.7 1.7 %condition.2.own = bf16[32,1536]{1,0:T(8,128)(2,1)S(1)} custom-call(bf16[1,32,4096]{2,1,0:T(8,128)(2,1)} %queries_in.3, f32[1,64,64]{2,1,0:T(8,128)} %left_in.3, f32[1,64,64]{2,1,0:T(8,128)} %right_in.3), custom_call_target="tpu_custom_call" | custom-call | flops 536870912 | bytes 524288 | tf_op jit(solution)/shard_map/condition/pallas_call | solution.py:109
  17.4 0.0 copy-start.1
  17.5 1.6 %collective-permute-start = (bf16[32,1536]{1,0:T(8,128)(2,1)S(1)}, bf16[32,1536]{1,0:T(8,128)(2,1)S(1)}, u32[]{:S(2)}, u32[]{:S(2)}) collective-permute-start(bf16[32,1536]{1,0:T(8,128)(2,1)S(1)} %condition.2.own), channel_id=1, source_target_pairs={{0,1},{1,0},{2,3},{3,2},{4,5},{5,4},{6,7},{7,6},{8,9},{9,8},{10,11... | collective-permute-start | bytes 294920 | tf_op jit(solution)/shard_map/ppermute | solution.py:277
  19.1 1.2 %collective-permute-start.1 = (bf16[32,1536]{1,0:T(8,128)(2,1)S(1)}, bf16[32,1536]{1,0:T(8,128)(2,1)S(1)}, u32[]{:S(2)}, u32[]{:S(2)}) collective-permute-start(bf16[32,1536]{1,0:T(8,128)(2,1)S(1)} %condition.2.own), channel_id=1, source_target_pairs={{0,2},{1,3},{2,0},{3,1},{4,6},{5,7},{6,4},{7,5},{8,10},{9,11},{10,... | collective-permute-start | bytes 294920 | tf_op jit(solution)/shard_map/ppermute | solution.py:277
  20.3 3.4 %collective-permute-done.near = bf16[32,1536]{1,0:T(8,128)(2,1)S(1)} collective-permute-done((bf16[32,1536]{1,0:T(8,128)(2,1)S(1)}, bf16[32,1536]{1,0:T(8,128)(2,1)S(1)}, u32[]{:S(2)}, u32[]{:S(2)}) %collective-permute-start) | collective-permute-done | bytes 98336 | tf_op jit(solution)/shard_map/ppermute | solution.py:277
  23.7 2.1 %collective-permute-done.1.far = bf16[32,1536]{1,0:T(8,128)(2,1)S(1)} collective-permute-done((bf16[32,1536]{1,0:T(8,128)(2,1)S(1)}, bf16[32,1536]{1,0:T(8,128)(2,1)S(1)}, u32[]{:S(2)}, u32[]{:S(2)}) %collective-permute-start.1) | collective-permute-done | bytes 98336 | tf_op jit(solution)/shard_map/ppermute | solution.py:277
  25.8 0.2 collective-permute-start.2
  26.0 1.5 %score_low.1.low = f32[1024,128]{1,0:T(8,128)S(1)} custom-call(bf16[32,2560]{1,0:T(8,128)(2,1)S(1)} %collective-permute-done.3.near, bf16[32,2560]{1,0:T(8,128)(2,1)S(1)} %collective-permute-done.4.far, bf16[32,2560]{1,0:T(8,128)(2,1)S(1)} %collective-permute-done.5.last, bf16[1,1024,4096]{2,1,0:T(8,128)(2,1)S(1)} %copy-done, f32[1024,128]{1,0:T(8,128)S(1)} %score_own.1.own_low), custom_call_target="tpu_custom_call" | custom-call | flops 503316480 | bytes 5242880 | tf_op jit(solution)/shard_map/score_low/pallas_call | solution.py:194
  27.5 2.9 %collective-permute-done.2.last = bf16[32,1536]{1,0:T(8,128)(2,1)S(1)} collective-permute-done((bf16[32,1536]{1,0:T(8,128)(2,1)S(1)}, bf16[32,1536]{1,0:T(8,128)(2,1)S(1)}, u32[]{:S(2)}, u32[]{:S(2)}) %collective-permute-start.2) | collective-permute-done | bytes 98336 | tf_op jit(solution)/shard_map/ppermute | solution.py:277
  30.4 1.1 %score_high.1 = (bf16[32,1024]{1,0:T(8,128)(2,1)S(1)}, bf16[32,1024]{1,0:T(8,128)(2,1)S(1)}, f32[32,1024]{1,0:T(8,128)S(1)}, f32[32,1024]{1,0:T(8,128)S(1)}) custom-call(bf16[32,1536]{1,0:T(8,128)(2,1)S(1)} %collective-permute-done.near, bf16[32,1536]{1,0:T(8,128)(2,1)S(1)} %collective-permute-done.1.far, bf16[32,1536]{1,0:T(8,128)(2,1)S(1)} %collective-permute-done.2.last, ...), custom_call_target="tpu_custom_call" | custom-call | flops 402653184 | bytes 3145728 | tf_op jit(solution)/shard_map/score_high/pallas_call | solution.py:219
  31.5 0.1 collective-permute-start.7
  31.6 0.5 %collective-permute-start.6 = (bf16[32,1024]{1,0:T(8,128)(2,1)S(1)}, bf16[32,1024]{1,0:T(8,128)(2,1)S(1)}, u32[]{:S(2)}, u32[]{:S(2)}) collective-permute-start(bf16[32,1024]{1,0:T(8,128)(2,1)S(1)} %get-tuple-element.20), channel_id=1, source_target_pairs={{0,4},{4,0},{8,12},{12,8},{1,5},{5,1},{9,13},{13,9},{2,6},{6,2},{1... | collective-permute-start | bytes 196616 | tf_op jit(solution)/shard_map/ppermute | solution.py:277
  32.0 0.7 %collective-permute-done.7.received = bf16[32,1024]{1,0:T(8,128)(2,1)S(1)} collective-permute-done((bf16[32,1024]{1,0:T(8,128)(2,1)S(1)}, bf16[32,1024]{1,0:T(8,128)(2,1)S(1)}, u32[]{:S(2)}, u32[]{:S(2)}) %collective-permute-start.7) | collective-permute-done | bytes 65568 | tf_op jit(solution)/shard_map/ppermute | solution.py:277
  32.8 1.6 %collective-permute-start.8 = (bf16[32,1024]{1,0:T(8,128)(2,1)S(1)}, bf16[32,1024]{1,0:T(8,128)(2,1)S(1)}, u32[]{:S(2)}, u32[]{:S(2)}) collective-permute-start(bf16[32,1024]{1,0:T(8,128)(2,1)S(1)} %add.1), channel_id=1, source_target_pairs={{0,8},{4,12},{8,0},{12,4},{1,9},{5,13},{9,1},{13,5},{2,10},{6,14},... | collective-permute-start | bytes 196616 | tf_op jit(solution)/shard_map/ppermute | solution.py:277
  34.4 0.1 copy.6.candidates
  34.4 2.7 %collective-permute-done.8.refs_2_ = bf16[32,1024]{1,0:T(8,128)(2,1)S(1)} collective-permute-done((bf16[32,1024]{1,0:T(8,128)(2,1)S(1)}, bf16[32,1024]{1,0:T(8,128)(2,1)S(1)}, u32[]{:S(2)}, u32[]{:S(2)}) %collective-permute-start.8) | collective-permute-done | bytes 65568 | tf_op jit(solution)/shard_map/ppermute | solution.py:277
  37.1 0.7 %finish.1 = bf16[32,1024]{1,0:T(8,128)(2,1)} custom-call(s32[32,16]{1,0:T(8,128)S(1)} %copy.6.candidates, f32[32,1024]{1,0:T(8,128)S(1)} %get-tuple-element.19.refs_0_, bf16[32,1024]{1,0:T(8,128)(2,1)S(1)} %collective-permute-done.6.refs_1_, bf16[32,1024]{1,0:T(8,128)(2,1)S(1)} %collective-permute-done.8.refs_2_), custom_call_target="tpu_custom_call" | custom-call | tf_op jit(solution)/shard_map/finish/pallas_call | solution.py:265
  (6 shorter events, 0.0 us)
Async XLA Ops:
  0.0 26.0 %copy-start = (bf16[1,1024,4096]{2,1,0:T(8,128)(2,1)S(1)}, bf16[1,1024,4096]{2,1,0:T(8,128)(2,1)}, u32[]{:S(2)}) copy-start(bf16[1,1024,4096]{2,1,0:T(8,128)(2,1)} %store.3) | copy-start | bytes 25165828
  2.1 10.5 %collective-permute-start.3 = (bf16[32,2560]{1,0:T(8,128)(2,1)S(1)}, bf16[32,2560]{1,0:T(8,128)(2,1)S(1)}, u32[]{:S(2)}, u32[]{:S(2)}) collective-permute-start(bf16[32,2560]{1,0:T(8,128)(2,1)S(1)} %condition.3.queries), channel_id=1, source_target_pairs={{0,1},{1,0},{2,3},{3,2},{4,5},{5,4},{6,7},{7,6},{8,9},{9,8},{10,11... | collective-permute-start | bytes 491528 | tf_op jit(solution)/shard_map/ppermute | solution.py:277
  5.1 10.1 %collective-permute-start.4 = (bf16[32,2560]{1,0:T(8,128)(2,1)S(1)}, bf16[32,2560]{1,0:T(8,128)(2,1)S(1)}, u32[]{:S(2)}, u32[]{:S(2)}) collective-permute-start(bf16[32,2560]{1,0:T(8,128)(2,1)S(1)} %condition.3.queries), channel_id=1, source_target_pairs={{0,2},{1,3},{2,0},{3,1},{4,6},{5,7},{6,4},{7,5},{8,10},{9,11},{10,... | collective-permute-start | bytes 491528 | tf_op jit(solution)/shard_map/ppermute | solution.py:277
  15.3 10.7 %collective-permute-start.5 = (bf16[32,2560]{1,0:T(8,128)(2,1)S(1)}, bf16[32,2560]{1,0:T(8,128)(2,1)S(1)}, u32[]{:S(2)}, u32[]{:S(2)}) collective-permute-start(bf16[32,2560]{1,0:T(8,128)(2,1)S(1)} %collective-permute-done.4.far), channel_id=1, source_target_pairs={{0,1},{1,0},{2,3},{3,2},{4,5},{5,4},{6,7},{7,6},{8,9},{9,8},{10,11... | collective-permute-start | bytes 491528 | tf_op jit(solution)/shard_map/ppermute | solution.py:277
  17.4 16.9 %copy-start.1 = (s32[32,16]{0,1:T(8,128)S(1)}, s32[32,16]{0,1:T(8,128)}, u32[]{:S(2)}) copy-start(s32[32,16]{0,1:T(8,128)} %param.9) | copy-start | bytes 6148
  17.5 6.2 %collective-permute-start = (bf16[32,1536]{1,0:T(8,128)(2,1)S(1)}, bf16[32,1536]{1,0:T(8,128)(2,1)S(1)}, u32[]{:S(2)}, u32[]{:S(2)}) collective-permute-start(bf16[32,1536]{1,0:T(8,128)(2,1)S(1)} %condition.2.own), channel_id=1, source_target_pairs={{0,1},{1,0},{2,3},{3,2},{4,5},{5,4},{6,7},{7,6},{8,9},{9,8},{10,11... | collective-permute-start | bytes 294920 | tf_op jit(solution)/shard_map/ppermute | solution.py:277
  19.1 6.7 %collective-permute-start.1 = (bf16[32,1536]{1,0:T(8,128)(2,1)S(1)}, bf16[32,1536]{1,0:T(8,128)(2,1)S(1)}, u32[]{:S(2)}, u32[]{:S(2)}) collective-permute-start(bf16[32,1536]{1,0:T(8,128)(2,1)S(1)} %condition.2.own), channel_id=1, source_target_pairs={{0,2},{1,3},{2,0},{3,1},{4,6},{5,7},{6,4},{7,5},{8,10},{9,11},{10,... | collective-permute-start | bytes 294920 | tf_op jit(solution)/shard_map/ppermute | solution.py:277
  25.8 4.6 %collective-permute-start.2 = (bf16[32,1536]{1,0:T(8,128)(2,1)S(1)}, bf16[32,1536]{1,0:T(8,128)(2,1)S(1)}, u32[]{:S(2)}, u32[]{:S(2)}) collective-permute-start(bf16[32,1536]{1,0:T(8,128)(2,1)S(1)} %collective-permute-done.1.far), channel_id=1, source_target_pairs={{0,1},{1,0},{2,3},{3,2},{4,5},{5,4},{6,7},{7,6},{8,9},{9,8},{10,11... | collective-permute-start | bytes 294920 | tf_op jit(solution)/shard_map/ppermute | solution.py:277
  31.5 1.3 %collective-permute-start.7 = (bf16[32,1024]{1,0:T(8,128)(2,1)S(1)}, bf16[32,1024]{1,0:T(8,128)(2,1)S(1)}, u32[]{:S(2)}, u32[]{:S(2)}) collective-permute-start(bf16[32,1024]{1,0:T(8,128)(2,1)S(1)} %get-tuple-element.22), channel_id=1, source_target_pairs={{0,4},{4,0},{8,12},{12,8},{1,5},{5,1},{9,13},{13,9},{2,6},{6,2},{1... | collective-permute-start | bytes 196616 | tf_op jit(solution)/shard_map/ppermute | solution.py:277
  31.6 2.9 %collective-permute-start.6 = (bf16[32,1024]{1,0:T(8,128)(2,1)S(1)}, bf16[32,1024]{1,0:T(8,128)(2,1)S(1)}, u32[]{:S(2)}, u32[]{:S(2)}) collective-permute-start(bf16[32,1024]{1,0:T(8,128)(2,1)S(1)} %get-tuple-element.20), channel_id=1, source_target_pairs={{0,4},{4,0},{8,12},{12,8},{1,5},{5,1},{9,13},{13,9},{2,6},{6,2},{1... | collective-permute-start | bytes 196616 | tf_op jit(solution)/shard_map/ppermute | solution.py:277
  32.8 4.3 %collective-permute-start.8 = (bf16[32,1024]{1,0:T(8,128)(2,1)S(1)}, bf16[32,1024]{1,0:T(8,128)(2,1)S(1)}, u32[]{:S(2)}, u32[]{:S(2)}) collective-permute-start(bf16[32,1024]{1,0:T(8,128)(2,1)S(1)} %add.1), channel_id=1, source_target_pairs={{0,8},{4,12},{8,0},{12,4},{1,9},{5,13},{9,1},{13,5},{2,10},{6,14},... | collective-permute-start | bytes 196616 | tf_op jit(solution)/shard_map/ppermute | solution.py:277

commit v20 on v19

--- a/solution.py
+++ b/solution.py
@@ -284,7 +284,8 @@
 def on_line(own, store, candidates, layers):
     far = [swapped(half, "blk", 2) for half in own]
     near = [swapped(half, "blk", 1) for half in own]
-    own_low = score_own(own[0], store)
+    own_first, own[1] = lax.optimization_barrier((own[0], own[1]))
+    own_low = score_own(own_first, store)
     near[0], far[0], own_low = lax.optimization_barrier((near[0], far[0], own_low))
     near[1], far[1] = lax.optimization_barrier((near[1], far[1]))
     last = [swapped(half, "blk", 1) for half in far]

time: 38 us -> 35.5 us (0.934)
  waiting for transfers between devices: 16 us -> 12.3 us
  starting transfers between devices: 11.2 us -> 12.5 us
    ppermute x9, waiting for transfers between devices: 16 us -> 12.3 us  [permuted(): lax.ppermute(value, axis, [(source, target_of(source) % count) for source...]
    ppermute x9, starting transfers between devices: 11.2 us -> 12.5 us  [permuted(): lax.ppermute(value, axis, [(source, target_of(source) % count) for source...]
  transfers between devices with their start and end apart: 9 -> 9, of which waited for: 7 -> 5; matrix products, arithmetic and copies ran while one was open for 0% -> 0% of each run, Pallas kernels for 17% -> 19%
where the time goes in v20:
time: 35.5 us; the launch traced here: 35.4 us
  starting transfers between devices  12.5 us (35%)
  waiting for transfers between devices  12.3 us (35%)
  Pallas kernels  10.5 us (30%)
    ppermute x9, starting transfers between devices, permuted(): lax.ppermute(value, axis, [(source, target_of(source) % count) for source...  12.5 us
    ppermute x9, waiting for transfers between devices, permuted(): lax.ppermute(value, axis, [(source, target_of(source) % count) for source...  12.3 us
    pallas_call x2, Pallas kernels, condition(): pl.pallas_call(functools.partial(condition_kernel, first, count), in_spec...  3.77 us
    pallas_call x1, Pallas kernels, score_own(): pl.pallas_call(own_kernel, in_specs=in_vmem(1) + [pl.BlockSpec(memory_spa...  3.37 us
    pallas_call x1, Pallas kernels, score_low(): pl.pallas_call(low_kernel, in_specs=in_vmem(5), out_specs=in_vmem(1)[0],...  1.5 us
    pallas_call x1, Pallas kernels, score_high(): pl.pallas_call(functools.partial(high_kernel, store.shape[2] - width), in...  1.08 us
    pallas_call x1, Pallas kernels, finish(): pl.pallas_call(functools.partial(finish_kernel, layers), in_specs=in_vmem...  0.74 us
  transfers between devices with their start and end apart: 9, of which 5 were waited for; matrix products, arithmetic and copies ran while one was open for 0% of the time, Pallas kernels for 19%

profile of v20, /device:TPU:0, one launch (start us, length us, event | category | flops | bytes accessed | tf_op | source)
XLA Modules:
  0.0 35.4 jit_solution(237398274112190860)
XLA Ops:
  0.0 2.0 %condition.3.queries = bf16[32,2560]{1,0:T(8,128)(2,1)S(1)} custom-call(bf16[1,32,4096]{2,1,0:T(8,128)(2,1)} %queries_in.3, f32[1,64,64]{2,1,0:T(8,128)} %left_in.3, f32[1,64,64]{2,1,0:T(8,128)} %right_in.3), custom_call_target="tpu_custom_call" | custom-call | flops 536870912 | bytes 524288 | tf_op jit(solution)/shard_map/condition/pallas_call | solution.py:109
  2.1 3.1 %collective-permute-start.3 = (bf16[32,2560]{1,0:T(8,128)(2,1)S(1)}, bf16[32,2560]{1,0:T(8,128)(2,1)S(1)}, u32[]{:S(2)}, u32[]{:S(2)}) collective-permute-start(bf16[32,2560]{1,0:T(8,128)(2,1)S(1)} %condition.3.queries), channel_id=1, source_target_pairs={{0,1},{1,0},{2,3},{3,2},{4,5},{5,4},{6,7},{7,6},{8,9},{9,8},{10,11... | collective-permute-start | bytes 491528 | tf_op jit(solution)/shard_map/ppermute | solution.py:277
  5.1 2.6 %collective-permute-start.4 = (bf16[32,2560]{1,0:T(8,128)(2,1)S(1)}, bf16[32,2560]{1,0:T(8,128)(2,1)S(1)}, u32[]{:S(2)}, u32[]{:S(2)}) collective-permute-start(bf16[32,2560]{1,0:T(8,128)(2,1)S(1)} %condition.3.queries), channel_id=1, source_target_pairs={{0,2},{1,3},{2,0},{3,1},{4,6},{5,7},{6,4},{7,5},{8,10},{9,11},{10,... | collective-permute-start | bytes 491528 | tf_op jit(solution)/shard_map/ppermute | solution.py:277
  7.7 1.7 %condition.2.own = bf16[32,1536]{1,0:T(8,128)(2,1)S(1)} custom-call(bf16[1,32,4096]{2,1,0:T(8,128)(2,1)} %queries_in.3, f32[1,64,64]{2,1,0:T(8,128)} %left_in.3, f32[1,64,64]{2,1,0:T(8,128)} %right_in.3), custom_call_target="tpu_custom_call" | custom-call | flops 536870912 | bytes 524288 | tf_op jit(solution)/shard_map/condition/pallas_call | solution.py:109
  9.5 3.4 %score_own.1.own_low = f32[1024,128]{1,0:T(8,128)S(1)} custom-call(bf16[32,2560]{1,0:T(8,128)(2,1)S(1)} %condition.3.queries, bf16[1,1024,4096]{2,1,0:T(8,128)(2,1)} %store.3), custom_call_target="tpu_custom_call" | custom-call | flops 167772160 | bytes 5242880 | tf_op jit(solution)/shard_map/score_own/pallas_call | solution.py:166
  12.8 0.0 copy-start.1
  12.9 0.0 collective-permute-done.3.near
  12.9 2.4 %collective-permute-done.4.far = bf16[32,2560]{1,0:T(8,128)(2,1)S(1)} collective-permute-done((bf16[32,2560]{1,0:T(8,128)(2,1)S(1)}, bf16[32,2560]{1,0:T(8,128)(2,1)S(1)}, u32[]{:S(2)}, u32[]{:S(2)}) %collective-permute-start.4) | collective-permute-done | bytes 163872 | tf_op jit(solution)/shard_map/ppermute | solution.py:277
  15.3 0.4 %collective-permute-start.5 = (bf16[32,2560]{1,0:T(8,128)(2,1)S(1)}, bf16[32,2560]{1,0:T(8,128)(2,1)S(1)}, u32[]{:S(2)}, u32[]{:S(2)}) collective-permute-start(bf16[32,2560]{1,0:T(8,128)(2,1)S(1)} %collective-permute-done.4.far), channel_id=1, source_target_pairs={{0,1},{1,0},{2,3},{3,2},{4,5},{5,4},{6,7},{7,6},{8,9},{9,8},{10,11... | collective-permute-start | bytes 491528 | tf_op jit(solution)/shard_map/ppermute | solution.py:277
  15.7 1.6 %collective-permute-start = (bf16[32,1536]{1,0:T(8,128)(2,1)S(1)}, bf16[32,1536]{1,0:T(8,128)(2,1)S(1)}, u32[]{:S(2)}, u32[]{:S(2)}) collective-permute-start(bf16[32,1536]{1,0:T(8,128)(2,1)S(1)} %condition.2.own), channel_id=1, source_target_pairs={{0,1},{1,0},{2,3},{3,2},{4,5},{5,4},{6,7},{7,6},{8,9},{9,8},{10,11... | collective-permute-start | bytes 294920 | tf_op jit(solution)/shard_map/ppermute | solution.py:277
  17.3 1.1 %collective-permute-start.1 = (bf16[32,1536]{1,0:T(8,128)(2,1)S(1)}, bf16[32,1536]{1,0:T(8,128)(2,1)S(1)}, u32[]{:S(2)}, u32[]{:S(2)}) collective-permute-start(bf16[32,1536]{1,0:T(8,128)(2,1)S(1)} %condition.2.own), channel_id=1, source_target_pairs={{0,2},{1,3},{2,0},{3,1},{4,6},{5,7},{6,4},{7,5},{8,10},{9,11},{10,... | collective-permute-start | bytes 294920 | tf_op jit(solution)/shard_map/ppermute | solution.py:277
  18.4 4.9 %collective-permute-done.near = bf16[32,1536]{1,0:T(8,128)(2,1)S(1)} collective-permute-done((bf16[32,1536]{1,0:T(8,128)(2,1)S(1)}, bf16[32,1536]{1,0:T(8,128)(2,1)S(1)}, u32[]{:S(2)}, u32[]{:S(2)}) %collective-permute-start) | collective-permute-done | bytes 98336 | tf_op jit(solution)/shard_map/ppermute | solution.py:277
  23.3 1.5 %collective-permute-start.2 = (bf16[32,1536]{1,0:T(8,128)(2,1)S(1)}, bf16[32,1536]{1,0:T(8,128)(2,1)S(1)}, u32[]{:S(2)}, u32[]{:S(2)}) collective-permute-start(bf16[32,1536]{1,0:T(8,128)(2,1)S(1)} %collective-permute-done.1.far), channel_id=1, source_target_pairs={{0,1},{1,0},{2,3},{3,2},{4,5},{5,4},{6,7},{7,6},{8,9},{9,8},{10,11... | collective-permute-start | bytes 294920 | tf_op jit(solution)/shard_map/ppermute | solution.py:277
  24.8 0.0 collective-permute-done.5.last
  24.8 1.5 %score_low.1.low = f32[1024,128]{1,0:T(8,128)S(1)} custom-call(bf16[32,2560]{1,0:T(8,128)(2,1)S(1)} %collective-permute-done.3.near, bf16[32,2560]{1,0:T(8,128)(2,1)S(1)} %collective-permute-done.4.far, bf16[32,2560]{1,0:T(8,128)(2,1)S(1)} %collective-permute-done.5.last, bf16[1,1024,4096]{2,1,0:T(8,128)(2,1)S(1)} %copy-done, f32[1024,128]{1,0:T(8,128)S(1)} %score_own.1.own_low), custom_call_target="tpu_custom_call" | custom-call | flops 503316480 | bytes 5242880 | tf_op jit(solution)/shard_map/score_low/pallas_call | solution.py:194
  26.3 1.6 %collective-permute-done.2.last = bf16[32,1536]{1,0:T(8,128)(2,1)S(1)} collective-permute-done((bf16[32,1536]{1,0:T(8,128)(2,1)S(1)}, bf16[32,1536]{1,0:T(8,128)(2,1)S(1)}, u32[]{:S(2)}, u32[]{:S(2)}) %collective-permute-start.2) | collective-permute-done | bytes 98336 | tf_op jit(solution)/shard_map/ppermute | solution.py:277
  27.9 1.1 %score_high.1 = (bf16[32,1024]{1,0:T(8,128)(2,1)S(1)}, bf16[32,1024]{1,0:T(8,128)(2,1)S(1)}, f32[32,1024]{1,0:T(8,128)S(1)}, f32[32,1024]{1,0:T(8,128)S(1)}) custom-call(bf16[32,1536]{1,0:T(8,128)(2,1)S(1)} %collective-permute-done.near, bf16[32,1536]{1,0:T(8,128)(2,1)S(1)} %collective-permute-done.1.far, bf16[32,1536]{1,0:T(8,128)(2,1)S(1)} %collective-permute-done.2.last, ...), custom_call_target="tpu_custom_call" | custom-call | flops 402653184 | bytes 3145728 | tf_op jit(solution)/shard_map/score_high/pallas_call | solution.py:219
  29.0 0.1 collective-permute-start.7
  29.1 0.5 %collective-permute-start.6 = (bf16[32,1024]{1,0:T(8,128)(2,1)S(1)}, bf16[32,1024]{1,0:T(8,128)(2,1)S(1)}, u32[]{:S(2)}, u32[]{:S(2)}) collective-permute-start(bf16[32,1024]{1,0:T(8,128)(2,1)S(1)} %get-tuple-element.24), channel_id=1, source_target_pairs={{0,4},{4,0},{8,12},{12,8},{1,5},{5,1},{9,13},{13,9},{2,6},{6,2},{1... | collective-permute-start | bytes 196616 | tf_op jit(solution)/shard_map/ppermute | solution.py:277
  29.6 0.7 %collective-permute-done.7.received = bf16[32,1024]{1,0:T(8,128)(2,1)S(1)} collective-permute-done((bf16[32,1024]{1,0:T(8,128)(2,1)S(1)}, bf16[32,1024]{1,0:T(8,128)(2,1)S(1)}, u32[]{:S(2)}, u32[]{:S(2)}) %collective-permute-start.7) | collective-permute-done | bytes 65568 | tf_op jit(solution)/shard_map/ppermute | solution.py:277
  30.3 1.6 %collective-permute-start.8 = (bf16[32,1024]{1,0:T(8,128)(2,1)S(1)}, bf16[32,1024]{1,0:T(8,128)(2,1)S(1)}, u32[]{:S(2)}, u32[]{:S(2)}) collective-permute-start(bf16[32,1024]{1,0:T(8,128)(2,1)S(1)} %add.1), channel_id=1, source_target_pairs={{0,8},{4,12},{8,0},{12,4},{1,9},{5,13},{9,1},{13,5},{2,10},{6,14},... | collective-permute-start | bytes 196616 | tf_op jit(solution)/shard_map/ppermute | solution.py:277
  31.9 0.1 copy.6.candidates
  32.0 2.7 %collective-permute-done.8.refs_2_ = bf16[32,1024]{1,0:T(8,128)(2,1)S(1)} collective-permute-done((bf16[32,1024]{1,0:T(8,128)(2,1)S(1)}, bf16[32,1024]{1,0:T(8,128)(2,1)S(1)}, u32[]{:S(2)}, u32[]{:S(2)}) %collective-permute-start.8) | collective-permute-done | bytes 65568 | tf_op jit(solution)/shard_map/ppermute | solution.py:277
  34.7 0.7 %finish.1 = bf16[32,1024]{1,0:T(8,128)(2,1)} custom-call(s32[32,16]{1,0:T(8,128)S(1)} %copy.6.candidates, f32[32,1024]{1,0:T(8,128)S(1)} %get-tuple-element.23.refs_0_, bf16[32,1024]{1,0:T(8,128)(2,1)S(1)} %collective-permute-done.6.refs_1_, bf16[32,1024]{1,0:T(8,128)(2,1)S(1)} %collective-permute-done.8.refs_2_), custom_call_target="tpu_custom_call" | custom-call | tf_op jit(solution)/shard_map/finish/pallas_call | solution.py:265
  (6 shorter events, 0.0 us)
Async XLA Ops:
  0.0 24.8 %copy-start = (bf16[1,1024,4096]{2,1,0:T(8,128)(2,1)S(1)}, bf16[1,1024,4096]{2,1,0:T(8,128)(2,1)}, u32[]{:S(2)}) copy-start(bf16[1,1024,4096]{2,1,0:T(8,128)(2,1)} %store.3) | copy-start | bytes 25165828
  2.1 10.8 %collective-permute-start.3 = (bf16[32,2560]{1,0:T(8,128)(2,1)S(1)}, bf16[32,2560]{1,0:T(8,128)(2,1)S(1)}, u32[]{:S(2)}, u32[]{:S(2)}) collective-permute-start(bf16[32,2560]{1,0:T(8,128)(2,1)S(1)} %condition.3.queries), channel_id=1, source_target_pairs={{0,1},{1,0},{2,3},{3,2},{4,5},{5,4},{6,7},{7,6},{8,9},{9,8},{10,11... | collective-permute-start | bytes 491528 | tf_op jit(solution)/shard_map/ppermute | solution.py:277
  5.1 10.1 %collective-permute-start.4 = (bf16[32,2560]{1,0:T(8,128)(2,1)S(1)}, bf16[32,2560]{1,0:T(8,128)(2,1)S(1)}, u32[]{:S(2)}, u32[]{:S(2)}) collective-permute-start(bf16[32,2560]{1,0:T(8,128)(2,1)S(1)} %condition.3.queries), channel_id=1, source_target_pairs={{0,2},{1,3},{2,0},{3,1},{4,6},{5,7},{6,4},{7,5},{8,10},{9,11},{10,... | collective-permute-start | bytes 491528 | tf_op jit(solution)/shard_map/ppermute | solution.py:277
  12.8 19.0 %copy-start.1 = (s32[32,16]{0,1:T(8,128)S(1)}, s32[32,16]{0,1:T(8,128)}, u32[]{:S(2)}) copy-start(s32[32,16]{0,1:T(8,128)} %param.9) | copy-start | bytes 6148
  15.3 9.6 %collective-permute-start.5 = (bf16[32,2560]{1,0:T(8,128)(2,1)S(1)}, bf16[32,2560]{1,0:T(8,128)(2,1)S(1)}, u32[]{:S(2)}, u32[]{:S(2)}) collective-permute-start(bf16[32,2560]{1,0:T(8,128)(2,1)S(1)} %collective-permute-done.4.far), channel_id=1, source_target_pairs={{0,1},{1,0},{2,3},{3,2},{4,5},{5,4},{6,7},{7,6},{8,9},{9,8},{10,11... | collective-permute-start | bytes 491528 | tf_op jit(solution)/shard_map/ppermute | solution.py:277
  15.7 7.6 %collective-permute-start = (bf16[32,1536]{1,0:T(8,128)(2,1)S(1)}, bf16[32,1536]{1,0:T(8,128)(2,1)S(1)}, u32[]{:S(2)}, u32[]{:S(2)}) collective-permute-start(bf16[32,1536]{1,0:T(8,128)(2,1)S(1)} %condition.2.own), channel_id=1, source_target_pairs={{0,1},{1,0},{2,3},{3,2},{4,5},{5,4},{6,7},{7,6},{8,9},{9,8},{10,11... | collective-permute-start | bytes 294920 | tf_op jit(solution)/shard_map/ppermute | solution.py:277
  17.3 6.0 %collective-permute-start.1 = (bf16[32,1536]{1,0:T(8,128)(2,1)S(1)}, bf16[32,1536]{1,0:T(8,128)(2,1)S(1)}, u32[]{:S(2)}, u32[]{:S(2)}) collective-permute-start(bf16[32,1536]{1,0:T(8,128)(2,1)S(1)} %condition.2.own), channel_id=1, source_target_pairs={{0,2},{1,3},{2,0},{3,1},{4,6},{5,7},{6,4},{7,5},{8,10},{9,11},{10,... | collective-permute-start | bytes 294920 | tf_op jit(solution)/shard_map/ppermute | solution.py:277
  23.3 4.6 %collective-permute-start.2 = (bf16[32,1536]{1,0:T(8,128)(2,1)S(1)}, bf16[32,1536]{1,0:T(8,128)(2,1)S(1)}, u32[]{:S(2)}, u32[]{:S(2)}) collective-permute-start(bf16[32,1536]{1,0:T(8,128)(2,1)S(1)} %collective-permute-done.1.far), channel_id=1, source_target_pairs={{0,1},{1,0},{2,3},{3,2},{4,5},{5,4},{6,7},{7,6},{8,9},{9,8},{10,11... | collective-permute-start | bytes 294920 | tf_op jit(solution)/shard_map/ppermute | solution.py:277
  29.0 1.3 %collective-permute-start.7 = (bf16[32,1024]{1,0:T(8,128)(2,1)S(1)}, bf16[32,1024]{1,0:T(8,128)(2,1)S(1)}, u32[]{:S(2)}, u32[]{:S(2)}) collective-permute-start(bf16[32,1024]{1,0:T(8,128)(2,1)S(1)} %get-tuple-element.26), channel_id=1, source_target_pairs={{0,4},{4,0},{8,12},{12,8},{1,5},{5,1},{9,13},{13,9},{2,6},{6,2},{1... | collective-permute-start | bytes 196616 | tf_op jit(solution)/shard_map/ppermute | solution.py:277
  29.1 2.9 %collective-permute-start.6 = (bf16[32,1024]{1,0:T(8,128)(2,1)S(1)}, bf16[32,1024]{1,0:T(8,128)(2,1)S(1)}, u32[]{:S(2)}, u32[]{:S(2)}) collective-permute-start(bf16[32,1024]{1,0:T(8,128)(2,1)S(1)} %get-tuple-element.24), channel_id=1, source_target_pairs={{0,4},{4,0},{8,12},{12,8},{1,5},{5,1},{9,13},{13,9},{2,6},{6,2},{1... | collective-permute-start | bytes 196616 | tf_op jit(solution)/shard_map/ppermute | solution.py:277
  30.3 4.3 %collective-permute-start.8 = (bf16[32,1024]{1,0:T(8,128)(2,1)S(1)}, bf16[32,1024]{1,0:T(8,128)(2,1)S(1)}, u32[]{:S(2)}, u32[]{:S(2)}) collective-permute-start(bf16[32,1024]{1,0:T(8,128)(2,1)S(1)} %add.1), channel_id=1, source_target_pairs={{0,8},{4,12},{8,0},{12,4},{1,9},{5,13},{9,1},{13,5},{2,10},{6,14},... | collective-permute-start | bytes 196616 | tf_op jit(solution)/shard_map/ppermute | solution.py:277

commit v21 on v18

--- a/solution.py
+++ b/solution.py
@@ -57,19 +57,19 @@
     copies = [
         pltpu.make_async_copy(source.at[0], target, arrived.at[place])
         for place, (source, target) in enumerate(
-            [(left_in, left_factor), (right_in, right_factor), (queries_in, queries)]
+            [(queries_in, queries), (left_in, left_factor), (right_in, right_factor)]
         )
     ]
     for copy in copies:
         copy.start()
     side = left_factor.shape[0]
     pairs = side // 2
-    copies[0].wait()
     copies[1].wait()
+    copies[2].wait()
     left = spread_left(left_factor[...], first, count)
     right = spread_right(right_factor[...])
     low_half = iota((1, 1, LANES), 2) < side
-    copies[2].wait()
+    copies[0].wait()
     for block in range(queries.shape[0] // GROUP):
         rows = pl.ds(block * GROUP, GROUP)
         straight = jnp.stack(
@@ -243,30 +243,37 @@
     )(kept, received)
 
 
-def write_rows(total, layers, listed, out):
-    scaled = total / jnp.sqrt(jnp.float32(layers))
+def finish_kernel(layers, candidates, *refs):
+    parts, (out, staged, semaphores) = refs[:-3], refs[-3:]
     tiles_here = out.shape[1] // TILE
     first = lax.axis_index("blk") * tiles_here
-    for tile in range(tiles_here):
-        hit = jnp.max(jnp.where(listed == first + tile, 1.0, 0.0), axis=1, keepdims=True)
-        columns = slice(tile * TILE, (tile + 1) * TILE)
-        out[:, columns] = jnp.where(hit > 0.0, scaled[:, columns], 0.0).astype(out.dtype)
-
-
-def finish_kernel(layers, candidates, *refs):
-    parts, out = refs[:-1], refs[-1]
-    total = parts[0][...].astype(jnp.float32)
-    for part in parts[1:]:
-        total = total + part[...].astype(jnp.float32)
-    write_rows(total, layers, candidates[...], out)
+    listed = candidates[...]
+    width = out.shape[1] // semaphores.shape[0]
+    copies = []
+    for place in range(semaphores.shape[0]):
+        for tile in range(place * width // TILE, (place + 1) * width // TILE):
+            columns = slice(tile * TILE, (tile + 1) * TILE)
+            total = parts[0][:, columns].astype(jnp.float32)
+            for part in parts[1:]:
+                total = total + part[:, columns].astype(jnp.float32)
+            scaled = total / jnp.sqrt(jnp.float32(layers))
+            hit = jnp.max(jnp.where(listed == first + tile, 1.0, 0.0), axis=1, keepdims=True)
+            staged[:, columns] = jnp.where(hit > 0.0, scaled, 0.0).astype(staged.dtype)
+        here = pl.ds(place * width, width)
+        copies.append(pltpu.make_async_copy(staged.at[:, here], out.at[:, here], semaphores.at[place]))
+        copies[-1].start()
+    for copy in copies:
+        copy.wait()
 
 
 def finish(parts, candidates, layers):
+    shape = parts[0].shape
     return pl.pallas_call(
         functools.partial(finish_kernel, layers),
         in_specs=in_vmem(1 + len(parts)),
-        out_specs=in_vmem(1)[0],
-        out_shape=jax.ShapeDtypeStruct(parts[0].shape, jnp.bfloat16),
+        out_specs=pl.BlockSpec(memory_space=pltpu.HBM),
+        out_shape=jax.ShapeDtypeStruct(shape, jnp.bfloat16),
+        scratch_shapes=[pltpu.VMEM(shape, jnp.bfloat16), pltpu.SemaphoreType.DMA((4,))],
         compiler_params=pltpu.CompilerParams(vmem_limit_bytes=VMEM),
         name="finish",
     )(candidates, *parts)

time: 31.5 us -> 31.5 us (level)
  no operation moved by 1% of the time
where the time goes in v21:
time: 31.5 us; the launch traced here: 31.4 us
  starting transfers between devices  13.1 us (42%)
  Pallas kernels  10.4 us (33%)
  waiting for transfers between devices  7.7 us (24%)
    ppermute x9, starting transfers between devices, permuted(): lax.ppermute(value, axis, [(source, target_of(source) % count) for source...  13.1 us
    ppermute x9, waiting for transfers between devices, permuted(): lax.ppermute(value, axis, [(source, target_of(source) % count) for source...  7.7 us
    pallas_call x2, Pallas kernels, condition(): pl.pallas_call(functools.partial(condition_kernel, first, count), in_spec...  3.86 us
    pallas_call x1, Pallas kernels, score_own(): pl.pallas_call(own_kernel, in_specs=in_vmem(1) + [pl.BlockSpec(memory_spa...  3.22 us
    pallas_call x1, Pallas kernels, score_low(): pl.pallas_call(low_kernel, in_specs=in_vmem(5), out_specs=in_vmem(1)[0],...  1.37 us
    pallas_call x1, Pallas kernels, score_high(): pl.pallas_call(functools.partial(high_kernel, store.shape[2] - width), in...  1.21 us
    pallas_call x1, Pallas kernels, finish(): pl.pallas_call(functools.partial(finish_kernel, layers), in_specs=in_vmem...  0.75 us
  transfers between devices with their start and end apart: 9, of which 5 were waited for; matrix products, arithmetic and copies ran while one was open for 0% of the time, Pallas kernels for 20%

profile of v21, /device:TPU:0, one launch (start us, length us, event | category | flops | bytes accessed | tf_op | source)
XLA Modules:
  0.0 31.4 jit_solution(5413002322910053627)
XLA Ops:
  0.0 2.1 %condition.3.queries = bf16[32,2304]{1,0:T(8,128)(2,1)S(1)} custom-call(bf16[1,32,4096]{2,1,0:T(8,128)(2,1)} %queries_in.3, f32[1,64,64]{2,1,0:T(8,128)} %left_in.3, f32[1,64,64]{2,1,0:T(8,128)} %right_in.3), custom_call_target="tpu_custom_call" | custom-call | flops 536870912 | bytes 524288 | tf_op jit(solution)/shard_map/condition/pallas_call | solution.py:109
  2.1 3.1 %collective-permute-start.3 = (bf16[32,2304]{1,0:T(8,128)(2,1)S(1)}, bf16[32,2304]{1,0:T(8,128)(2,1)S(1)}, u32[]{:S(2)}, u32[]{:S(2)}) collective-permute-start(bf16[32,2304]{1,0:T(8,128)(2,1)S(1)} %condition.3.queries), channel_id=1, source_target_pairs={{0,1},{1,0},{2,3},{3,2},{4,5},{5,4},{6,7},{7,6},{8,9},{9,8},{10,11... | collective-permute-start | bytes 442376 | tf_op jit(solution)/shard_map/ppermute | solution.py:284
  5.2 2.6 %collective-permute-start.4 = (bf16[32,2304]{1,0:T(8,128)(2,1)S(1)}, bf16[32,2304]{1,0:T(8,128)(2,1)S(1)}, u32[]{:S(2)}, u32[]{:S(2)}) collective-permute-start(bf16[32,2304]{1,0:T(8,128)(2,1)S(1)} %condition.3.queries), channel_id=1, source_target_pairs={{0,2},{1,3},{2,0},{3,1},{4,6},{5,7},{6,4},{7,5},{8,10},{9,11},{10,... | collective-permute-start | bytes 442376 | tf_op jit(solution)/shard_map/ppermute | solution.py:284
  7.7 1.8 %condition.2.own = bf16[32,1792]{1,0:T(8,128)(2,1)S(1)} custom-call(bf16[1,32,4096]{2,1,0:T(8,128)(2,1)} %queries_in.3, f32[1,64,64]{2,1,0:T(8,128)} %left_in.3, f32[1,64,64]{2,1,0:T(8,128)} %right_in.3), custom_call_target="tpu_custom_call" | custom-call | flops 536870912 | bytes 524288 | tf_op jit(solution)/shard_map/condition/pallas_call | solution.py:109
  9.6 0.5 %collective-permute-start = (bf16[32,1792]{1,0:T(8,128)(2,1)S(1)}, bf16[32,1792]{1,0:T(8,128)(2,1)S(1)}, u32[]{:S(2)}, u32[]{:S(2)}) collective-permute-start(bf16[32,1792]{1,0:T(8,128)(2,1)S(1)} %condition.2.own), channel_id=1, source_target_pairs={{0,1},{1,0},{2,3},{3,2},{4,5},{5,4},{6,7},{7,6},{8,9},{9,8},{10,11... | collective-permute-start | bytes 344072 | tf_op jit(solution)/shard_map/ppermute | solution.py:284
  10.1 0.0 collective-permute-start.1
  10.1 3.2 %score_own.1.own_low = f32[1024,128]{1,0:T(8,128)S(1)} custom-call(bf16[32,2304]{1,0:T(8,128)(2,1)S(1)} %condition.3.queries, bf16[1,1024,4096]{2,1,0:T(8,128)(2,1)} %store.3), custom_call_target="tpu_custom_call" | custom-call | flops 150994944 | bytes 4718592 | tf_op jit(solution)/shard_map/score_own/pallas_call | solution.py:166
  13.3 0.0 copy-start.1
  13.3 0.0 collective-permute-done.3.near
  13.3 0.4 %collective-permute-done.4.far = bf16[32,2304]{1,0:T(8,128)(2,1)S(1)} collective-permute-done((bf16[32,2304]{1,0:T(8,128)(2,1)S(1)}, bf16[32,2304]{1,0:T(8,128)(2,1)S(1)}, u32[]{:S(2)}, u32[]{:S(2)}) %collective-permute-start.4) | collective-permute-done | bytes 147488 | tf_op jit(solution)/shard_map/ppermute | solution.py:284
  13.7 2.3 %collective-permute-start.5 = (bf16[32,2304]{1,0:T(8,128)(2,1)S(1)}, bf16[32,2304]{1,0:T(8,128)(2,1)S(1)}, u32[]{:S(2)}, u32[]{:S(2)}) collective-permute-start(bf16[32,2304]{1,0:T(8,128)(2,1)S(1)} %collective-permute-done.4.far), channel_id=1, source_target_pairs={{0,1},{1,0},{2,3},{3,2},{4,5},{5,4},{6,7},{7,6},{8,9},{9,8},{10,11... | collective-permute-start | bytes 442376 | tf_op jit(solution)/shard_map/ppermute | solution.py:284
  16.1 0.0 collective-permute-done.near
  16.1 2.5 %collective-permute-done.1.far = bf16[32,1792]{1,0:T(8,128)(2,1)S(1)} collective-permute-done((bf16[32,1792]{1,0:T(8,128)(2,1)S(1)}, bf16[32,1792]{1,0:T(8,128)(2,1)S(1)}, u32[]{:S(2)}, u32[]{:S(2)}) %collective-permute-start.1) | collective-permute-done | bytes 114720 | tf_op jit(solution)/shard_map/ppermute | solution.py:284
  18.6 2.4 %collective-permute-start.2 = (bf16[32,1792]{1,0:T(8,128)(2,1)S(1)}, bf16[32,1792]{1,0:T(8,128)(2,1)S(1)}, u32[]{:S(2)}, u32[]{:S(2)}) collective-permute-start(bf16[32,1792]{1,0:T(8,128)(2,1)S(1)} %collective-permute-done.1.far), channel_id=1, source_target_pairs={{0,1},{1,0},{2,3},{3,2},{4,5},{5,4},{6,7},{7,6},{8,9},{9,8},{10,11... | collective-permute-start | bytes 344072 | tf_op jit(solution)/shard_map/ppermute | solution.py:284
  21.0 1.4 %score_low.1.low = f32[1024,128]{1,0:T(8,128)S(1)} custom-call(bf16[32,2304]{1,0:T(8,128)(2,1)S(1)} %collective-permute-done.3.near, bf16[32,2304]{1,0:T(8,128)(2,1)S(1)} %collective-permute-done.4.far, bf16[32,2304]{1,0:T(8,128)(2,1)S(1)} %collective-permute-done.5.last, bf16[1,1024,4096]{2,1,0:T(8,128)(2,1)S(1)} %copy-done, f32[1024,128]{1,0:T(8,128)S(1)} %score_own.1.own_low), custom_call_target="tpu_custom_call" | custom-call | flops 452984832 | bytes 4718592 | tf_op jit(solution)/shard_map/score_low/pallas_call | solution.py:194
  22.4 1.4 %collective-permute-done.2.last = bf16[32,1792]{1,0:T(8,128)(2,1)S(1)} collective-permute-done((bf16[32,1792]{1,0:T(8,128)(2,1)S(1)}, bf16[32,1792]{1,0:T(8,128)(2,1)S(1)}, u32[]{:S(2)}, u32[]{:S(2)}) %collective-permute-start.2) | collective-permute-done | bytes 114720 | tf_op jit(solution)/shard_map/ppermute | solution.py:284
  23.8 1.2 %score_high.1 = (bf16[32,1024]{1,0:T(8,128)(2,1)S(1)}, bf16[32,1024]{1,0:T(8,128)(2,1)S(1)}, f32[32,1024]{1,0:T(8,128)S(1)}, f32[32,1024]{1,0:T(8,128)S(1)}) custom-call(bf16[32,1792]{1,0:T(8,128)(2,1)S(1)} %collective-permute-done.near, bf16[32,1792]{1,0:T(8,128)(2,1)S(1)} %collective-permute-done.1.far, bf16[32,1792]{1,0:T(8,128)(2,1)S(1)} %collective-permute-done.2.last, ...), custom_call_target="tpu_custom_call" | custom-call | flops 469762048 | bytes 3670016 | tf_op jit(solution)/shard_map/score_high/pallas_call | solution.py:219
  25.0 0.1 collective-permute-start.7
  25.0 0.5 %collective-permute-start.6 = (bf16[32,1024]{1,0:T(8,128)(2,1)S(1)}, bf16[32,1024]{1,0:T(8,128)(2,1)S(1)}, u32[]{:S(2)}, u32[]{:S(2)}) collective-permute-start(bf16[32,1024]{1,0:T(8,128)(2,1)S(1)} %get-tuple-element.20), channel_id=1, source_target_pairs={{0,4},{4,0},{8,12},{12,8},{1,5},{5,1},{9,13},{13,9},{2,6},{6,2},{1... | collective-permute-start | bytes 196616 | tf_op jit(solution)/shard_map/ppermute | solution.py:284
  25.5 0.7 %collective-permute-done.7.received = bf16[32,1024]{1,0:T(8,128)(2,1)S(1)} collective-permute-done((bf16[32,1024]{1,0:T(8,128)(2,1)S(1)}, bf16[32,1024]{1,0:T(8,128)(2,1)S(1)}, u32[]{:S(2)}, u32[]{:S(2)}) %collective-permute-start.7) | collective-permute-done | bytes 65568 | tf_op jit(solution)/shard_map/ppermute | solution.py:284
  26.3 1.6 %collective-permute-start.8 = (bf16[32,1024]{1,0:T(8,128)(2,1)S(1)}, bf16[32,1024]{1,0:T(8,128)(2,1)S(1)}, u32[]{:S(2)}, u32[]{:S(2)}) collective-permute-start(bf16[32,1024]{1,0:T(8,128)(2,1)S(1)} %add.1), channel_id=1, source_target_pairs={{0,8},{4,12},{8,0},{12,4},{1,9},{5,13},{9,1},{13,5},{2,10},{6,14},... | collective-permute-start | bytes 196616 | tf_op jit(solution)/shard_map/ppermute | solution.py:284
  27.9 0.1 copy.6.candidates
  27.9 2.7 %collective-permute-done.8.refs_2_ = bf16[32,1024]{1,0:T(8,128)(2,1)S(1)} collective-permute-done((bf16[32,1024]{1,0:T(8,128)(2,1)S(1)}, bf16[32,1024]{1,0:T(8,128)(2,1)S(1)}, u32[]{:S(2)}, u32[]{:S(2)}) %collective-permute-start.8) | collective-permute-done | bytes 65568 | tf_op jit(solution)/shard_map/ppermute | solution.py:284
  30.6 0.8 %finish.1 = bf16[32,1024]{1,0:T(8,128)(2,1)} custom-call(s32[32,16]{1,0:T(8,128)S(1)} %copy.6.candidates, f32[32,1024]{1,0:T(8,128)S(1)} %get-tuple-element.19.refs_0_, bf16[32,1024]{1,0:T(8,128)(2,1)S(1)} %collective-permute-done.6.refs_1_, bf16[32,1024]{1,0:T(8,128)(2,1)S(1)} %collective-permute-done.8.refs_2_), custom_call_target="tpu_custom_call" | custom-call | tf_op jit(solution)/shard_map/finish/pallas_call | solution.py:271
  (6 shorter events, 0.0 us)
Async XLA Ops:
  0.0 21.0 %copy-start = (bf16[1,1024,4096]{2,1,0:T(8,128)(2,1)S(1)}, bf16[1,1024,4096]{2,1,0:T(8,128)(2,1)}, u32[]{:S(2)}) copy-start(bf16[1,1024,4096]{2,1,0:T(8,128)(2,1)} %store.3) | copy-start | bytes 25165828
  2.1 11.3 %collective-permute-start.3 = (bf16[32,2304]{1,0:T(8,128)(2,1)S(1)}, bf16[32,2304]{1,0:T(8,128)(2,1)S(1)}, u32[]{:S(2)}, u32[]{:S(2)}) collective-permute-start(bf16[32,2304]{1,0:T(8,128)(2,1)S(1)} %condition.3.queries), channel_id=1, source_target_pairs={{0,1},{1,0},{2,3},{3,2},{4,5},{5,4},{6,7},{7,6},{8,9},{9,8},{10,11... | collective-permute-start | bytes 442376 | tf_op jit(solution)/shard_map/ppermute | solution.py:284
  5.2 8.6 %collective-permute-start.4 = (bf16[32,2304]{1,0:T(8,128)(2,1)S(1)}, bf16[32,2304]{1,0:T(8,128)(2,1)S(1)}, u32[]{:S(2)}, u32[]{:S(2)}) collective-permute-start(bf16[32,2304]{1,0:T(8,128)(2,1)S(1)} %condition.3.queries), channel_id=1, source_target_pairs={{0,2},{1,3},{2,0},{3,1},{4,6},{5,7},{6,4},{7,5},{8,10},{9,11},{10,... | collective-permute-start | bytes 442376 | tf_op jit(solution)/shard_map/ppermute | solution.py:284
  9.6 6.5 %collective-permute-start = (bf16[32,1792]{1,0:T(8,128)(2,1)S(1)}, bf16[32,1792]{1,0:T(8,128)(2,1)S(1)}, u32[]{:S(2)}, u32[]{:S(2)}) collective-permute-start(bf16[32,1792]{1,0:T(8,128)(2,1)S(1)} %condition.2.own), channel_id=1, source_target_pairs={{0,1},{1,0},{2,3},{3,2},{4,5},{5,4},{6,7},{7,6},{8,9},{9,8},{10,11... | collective-permute-start | bytes 344072 | tf_op jit(solution)/shard_map/ppermute | solution.py:284
  10.1 8.5 %collective-permute-start.1 = (bf16[32,1792]{1,0:T(8,128)(2,1)S(1)}, bf16[32,1792]{1,0:T(8,128)(2,1)S(1)}, u32[]{:S(2)}, u32[]{:S(2)}) collective-permute-start(bf16[32,1792]{1,0:T(8,128)(2,1)S(1)} %condition.2.own), channel_id=1, source_target_pairs={{0,2},{1,3},{2,0},{3,1},{4,6},{5,7},{6,4},{7,5},{8,10},{9,11},{10,... | collective-permute-start | bytes 344072 | tf_op jit(solution)/shard_map/ppermute | solution.py:284
  13.3 14.5 %copy-start.1 = (s32[32,16]{0,1:T(8,128)S(1)}, s32[32,16]{0,1:T(8,128)}, u32[]{:S(2)}) copy-start(s32[32,16]{0,1:T(8,128)} %param.9) | copy-start | bytes 6148
  13.7 7.2 %collective-permute-start.5 = (bf16[32,2304]{1,0:T(8,128)(2,1)S(1)}, bf16[32,2304]{1,0:T(8,128)(2,1)S(1)}, u32[]{:S(2)}, u32[]{:S(2)}) collective-permute-start(bf16[32,2304]{1,0:T(8,128)(2,1)S(1)} %collective-permute-done.4.far), channel_id=1, source_target_pairs={{0,1},{1,0},{2,3},{3,2},{4,5},{5,4},{6,7},{7,6},{8,9},{9,8},{10,11... | collective-permute-start | bytes 442376 | tf_op jit(solution)/shard_map/ppermute | solution.py:284
  18.6 5.2 %collective-permute-start.2 = (bf16[32,1792]{1,0:T(8,128)(2,1)S(1)}, bf16[32,1792]{1,0:T(8,128)(2,1)S(1)}, u32[]{:S(2)}, u32[]{:S(2)}) collective-permute-start(bf16[32,1792]{1,0:T(8,128)(2,1)S(1)} %collective-permute-done.1.far), channel_id=1, source_target_pairs={{0,1},{1,0},{2,3},{3,2},{4,5},{5,4},{6,7},{7,6},{8,9},{9,8},{10,11... | collective-permute-start | bytes 344072 | tf_op jit(solution)/shard_map/ppermute | solution.py:284
  25.0 1.3 %collective-permute-start.7 = (bf16[32,1024]{1,0:T(8,128)(2,1)S(1)}, bf16[32,1024]{1,0:T(8,128)(2,1)S(1)}, u32[]{:S(2)}, u32[]{:S(2)}) collective-permute-start(bf16[32,1024]{1,0:T(8,128)(2,1)S(1)} %get-tuple-element.22), channel_id=1, source_target_pairs={{0,4},{4,0},{8,12},{12,8},{1,5},{5,1},{9,13},{13,9},{2,6},{6,2},{1... | collective-permute-start | bytes 196616 | tf_op jit(solution)/shard_map/ppermute | solution.py:284
  25.0 2.9 %collective-permute-start.6 = (bf16[32,1024]{1,0:T(8,128)(2,1)S(1)}, bf16[32,1024]{1,0:T(8,128)(2,1)S(1)}, u32[]{:S(2)}, u32[]{:S(2)}) collective-permute-start(bf16[32,1024]{1,0:T(8,128)(2,1)S(1)} %get-tuple-element.20), channel_id=1, source_target_pairs={{0,4},{4,0},{8,12},{12,8},{1,5},{5,1},{9,13},{13,9},{2,6},{6,2},{1... | collective-permute-start | bytes 196616 | tf_op jit(solution)/shard_map/ppermute | solution.py:284
  26.3 4.3 %collective-permute-start.8 = (bf16[32,1024]{1,0:T(8,128)(2,1)S(1)}, bf16[32,1024]{1,0:T(8,128)(2,1)S(1)}, u32[]{:S(2)}, u32[]{:S(2)}) collective-permute-start(bf16[32,1024]{1,0:T(8,128)(2,1)S(1)} %add.1), channel_id=1, source_target_pairs={{0,8},{4,12},{8,0},{12,4},{1,9},{5,13},{9,1},{13,5},{2,10},{6,14},... | collective-permute-start | bytes 196616 | tf_op jit(solution)/shard_map/ppermute | solution.py:284

commit v22 on v18

--- a/solution.py
+++ b/solution.py
@@ -32,14 +32,16 @@
     return jnp.where(condition, 1.0, 0.0).astype(jnp.bfloat16)
 
 
-def spread_left(left_factor, first, count):
-    side = left_factor.shape[0]
+def spread_left(factor_rows):
+    count, side = factor_rows.shape
     wide = ones_where(iota((side, side * ROWS), 1) // ROWS == iota((side, side * ROWS), 0))
-    parts = [part[first : first + count] for part in two_parts(left_factor)]
-    columns = dot(jnp.concatenate(parts, axis=0), wide).reshape(2, count, 1, side * ROWS)
     same = iota((1, ROWS, side * ROWS), 1) == iota((1, ROWS, side * ROWS), 2) % ROWS
-    parts = [jnp.where(same, columns[part], 0.0).reshape(count * ROWS, side * ROWS) for part in range(2)]
-    return jnp.concatenate([part.astype(jnp.bfloat16) for part in parts], axis=1)
+
+    def one(part):
+        columns = dot(part, wide).reshape(count, 1, side * ROWS)
+        return jnp.where(same, columns, 0.0).reshape(count * ROWS, side * ROWS).astype(jnp.bfloat16)
+
+    return jnp.concatenate([one(part) for part in two_parts(factor_rows)], axis=1)
 
 
 def spread_right(right_factor):
@@ -66,7 +68,7 @@
     pairs = side // 2
     copies[0].wait()
     copies[1].wait()
-    left = spread_left(left_factor[...], first, count)
+    left = spread_left(left_factor[pl.ds(first, count), :])
     right = spread_right(right_factor[...])
     low_half = iota((1, 1, LANES), 2) < side
     copies[2].wait()

time: 31.5 us -> 31.5 us (level)
  no operation moved by 1% of the time
where the time goes in v22:
time: 31.5 us; the launch traced here: 31.3 us
  starting transfers between devices  13.1 us (42%)
  Pallas kernels  10.3 us (33%)
  waiting for transfers between devices  7.75 us (25%)
    ppermute x9, starting transfers between devices, permuted(): lax.ppermute(value, axis, [(source, target_of(source) % count) for source...  13.1 us
    ppermute x9, waiting for transfers between devices, permuted(): lax.ppermute(value, axis, [(source, target_of(source) % count) for source...  7.75 us
    pallas_call x2, Pallas kernels, condition(): pl.pallas_call(functools.partial(condition_kernel, first, count), in_spec...  3.76 us
    pallas_call x1, Pallas kernels, score_own(): pl.pallas_call(own_kernel, in_specs=in_vmem(1) + [pl.BlockSpec(memory_spa...  3.21 us
    pallas_call x1, Pallas kernels, score_low(): pl.pallas_call(low_kernel, in_specs=in_vmem(5), out_specs=in_vmem(1)[0],...  1.37 us
    pallas_call x1, Pallas kernels, score_high(): pl.pallas_call(functools.partial(high_kernel, store.shape[2] - width), in...  1.21 us
    pallas_call x1, Pallas kernels, finish(): pl.pallas_call(functools.partial(finish_kernel, layers), in_specs=in_vmem...  0.74 us
  transfers between devices with their start and end apart: 9, of which 5 were waited for; matrix products, arithmetic and copies ran while one was open for 0% of the time, Pallas kernels for 20%

profile of v22, /device:TPU:0, one launch (start us, length us, event | category | flops | bytes accessed | tf_op | source)
XLA Modules:
  0.0 31.3 jit_solution(5837546554847640573)
XLA Ops:
  0.0 2.0 %condition.3.queries = bf16[32,2304]{1,0:T(8,128)(2,1)S(1)} custom-call(bf16[1,32,4096]{2,1,0:T(8,128)(2,1)} %queries_in.3, f32[1,64,64]{2,1,0:T(8,128)} %left_in.3, f32[1,64,64]{2,1,0:T(8,128)} %right_in.3), custom_call_target="tpu_custom_call" | custom-call | flops 536870912 | bytes 524288 | tf_op jit(solution)/shard_map/condition/pallas_call | solution.py:111
  2.0 3.1 %collective-permute-start.3 = (bf16[32,2304]{1,0:T(8,128)(2,1)S(1)}, bf16[32,2304]{1,0:T(8,128)(2,1)S(1)}, u32[]{:S(2)}, u32[]{:S(2)}) collective-permute-start(bf16[32,2304]{1,0:T(8,128)(2,1)S(1)} %condition.3.queries), channel_id=1, source_target_pairs={{0,1},{1,0},{2,3},{3,2},{4,5},{5,4},{6,7},{7,6},{8,9},{9,8},{10,11... | collective-permute-start | bytes 442376 | tf_op jit(solution)/shard_map/ppermute | solution.py:279
  5.1 2.6 %collective-permute-start.4 = (bf16[32,2304]{1,0:T(8,128)(2,1)S(1)}, bf16[32,2304]{1,0:T(8,128)(2,1)S(1)}, u32[]{:S(2)}, u32[]{:S(2)}) collective-permute-start(bf16[32,2304]{1,0:T(8,128)(2,1)S(1)} %condition.3.queries), channel_id=1, source_target_pairs={{0,2},{1,3},{2,0},{3,1},{4,6},{5,7},{6,4},{7,5},{8,10},{9,11},{10,... | collective-permute-start | bytes 442376 | tf_op jit(solution)/shard_map/ppermute | solution.py:279
  7.7 1.8 %condition.2.own = bf16[32,1792]{1,0:T(8,128)(2,1)S(1)} custom-call(bf16[1,32,4096]{2,1,0:T(8,128)(2,1)} %queries_in.3, f32[1,64,64]{2,1,0:T(8,128)} %left_in.3, f32[1,64,64]{2,1,0:T(8,128)} %right_in.3), custom_call_target="tpu_custom_call" | custom-call | flops 536870912 | bytes 524288 | tf_op jit(solution)/shard_map/condition/pallas_call | solution.py:111
  9.5 0.5 %collective-permute-start = (bf16[32,1792]{1,0:T(8,128)(2,1)S(1)}, bf16[32,1792]{1,0:T(8,128)(2,1)S(1)}, u32[]{:S(2)}, u32[]{:S(2)}) collective-permute-start(bf16[32,1792]{1,0:T(8,128)(2,1)S(1)} %condition.2.own), channel_id=1, source_target_pairs={{0,1},{1,0},{2,3},{3,2},{4,5},{5,4},{6,7},{7,6},{8,9},{9,8},{10,11... | collective-permute-start | bytes 344072 | tf_op jit(solution)/shard_map/ppermute | solution.py:279
  10.0 0.0 collective-permute-start.1
  10.0 3.2 %score_own.1.own_low = f32[1024,128]{1,0:T(8,128)S(1)} custom-call(bf16[32,2304]{1,0:T(8,128)(2,1)S(1)} %condition.3.queries, bf16[1,1024,4096]{2,1,0:T(8,128)(2,1)} %store.3), custom_call_target="tpu_custom_call" | custom-call | flops 150994944 | bytes 4718592 | tf_op jit(solution)/shard_map/score_own/pallas_call | solution.py:168
  13.2 0.0 copy-start.1
  13.2 0.5 %collective-permute-done.4.far = bf16[32,2304]{1,0:T(8,128)(2,1)S(1)} collective-permute-done((bf16[32,2304]{1,0:T(8,128)(2,1)S(1)}, bf16[32,2304]{1,0:T(8,128)(2,1)S(1)}, u32[]{:S(2)}, u32[]{:S(2)}) %collective-permute-start.4) | collective-permute-done | bytes 147488 | tf_op jit(solution)/shard_map/ppermute | solution.py:279
  13.7 2.3 %collective-permute-start.5 = (bf16[32,2304]{1,0:T(8,128)(2,1)S(1)}, bf16[32,2304]{1,0:T(8,128)(2,1)S(1)}, u32[]{:S(2)}, u32[]{:S(2)}) collective-permute-start(bf16[32,2304]{1,0:T(8,128)(2,1)S(1)} %collective-permute-done.4.far), channel_id=1, source_target_pairs={{0,1},{1,0},{2,3},{3,2},{4,5},{5,4},{6,7},{7,6},{8,9},{9,8},{10,11... | collective-permute-start | bytes 442376 | tf_op jit(solution)/shard_map/ppermute | solution.py:279
  16.0 0.0 collective-permute-done.near
  16.0 2.5 %collective-permute-done.1.far = bf16[32,1792]{1,0:T(8,128)(2,1)S(1)} collective-permute-done((bf16[32,1792]{1,0:T(8,128)(2,1)S(1)}, bf16[32,1792]{1,0:T(8,128)(2,1)S(1)}, u32[]{:S(2)}, u32[]{:S(2)}) %collective-permute-start.1) | collective-permute-done | bytes 114720 | tf_op jit(solution)/shard_map/ppermute | solution.py:279
  18.5 2.4 %collective-permute-start.2 = (bf16[32,1792]{1,0:T(8,128)(2,1)S(1)}, bf16[32,1792]{1,0:T(8,128)(2,1)S(1)}, u32[]{:S(2)}, u32[]{:S(2)}) collective-permute-start(bf16[32,1792]{1,0:T(8,128)(2,1)S(1)} %collective-permute-done.1.far), channel_id=1, source_target_pairs={{0,1},{1,0},{2,3},{3,2},{4,5},{5,4},{6,7},{7,6},{8,9},{9,8},{10,11... | collective-permute-start | bytes 344072 | tf_op jit(solution)/shard_map/ppermute | solution.py:279
  20.9 1.4 %score_low.1.low = f32[1024,128]{1,0:T(8,128)S(1)} custom-call(bf16[32,2304]{1,0:T(8,128)(2,1)S(1)} %collective-permute-done.3.near, bf16[32,2304]{1,0:T(8,128)(2,1)S(1)} %collective-permute-done.4.far, bf16[32,2304]{1,0:T(8,128)(2,1)S(1)} %collective-permute-done.5.last, bf16[1,1024,4096]{2,1,0:T(8,128)(2,1)S(1)} %copy-done, f32[1024,128]{1,0:T(8,128)S(1)} %score_own.1.own_low), custom_call_target="tpu_custom_call" | custom-call | flops 452984832 | bytes 4718592 | tf_op jit(solution)/shard_map/score_low/pallas_call | solution.py:196
  22.3 1.4 %collective-permute-done.2.last = bf16[32,1792]{1,0:T(8,128)(2,1)S(1)} collective-permute-done((bf16[32,1792]{1,0:T(8,128)(2,1)S(1)}, bf16[32,1792]{1,0:T(8,128)(2,1)S(1)}, u32[]{:S(2)}, u32[]{:S(2)}) %collective-permute-start.2) | collective-permute-done | bytes 114720 | tf_op jit(solution)/shard_map/ppermute | solution.py:279
  23.7 1.2 %score_high.1 = (bf16[32,1024]{1,0:T(8,128)(2,1)S(1)}, bf16[32,1024]{1,0:T(8,128)(2,1)S(1)}, f32[32,1024]{1,0:T(8,128)S(1)}, f32[32,1024]{1,0:T(8,128)S(1)}) custom-call(bf16[32,1792]{1,0:T(8,128)(2,1)S(1)} %collective-permute-done.near, bf16[32,1792]{1,0:T(8,128)(2,1)S(1)} %collective-permute-done.1.far, bf16[32,1792]{1,0:T(8,128)(2,1)S(1)} %collective-permute-done.2.last, ...), custom_call_target="tpu_custom_call" | custom-call | flops 469762048 | bytes 3670016 | tf_op jit(solution)/shard_map/score_high/pallas_call | solution.py:221
  24.9 0.1 collective-permute-start.7
  25.0 0.5 %collective-permute-start.6 = (bf16[32,1024]{1,0:T(8,128)(2,1)S(1)}, bf16[32,1024]{1,0:T(8,128)(2,1)S(1)}, u32[]{:S(2)}, u32[]{:S(2)}) collective-permute-start(bf16[32,1024]{1,0:T(8,128)(2,1)S(1)} %get-tuple-element.20), channel_id=1, source_target_pairs={{0,4},{4,0},{8,12},{12,8},{1,5},{5,1},{9,13},{13,9},{2,6},{6,2},{1... | collective-permute-start | bytes 196616 | tf_op jit(solution)/shard_map/ppermute | solution.py:279
  25.5 0.7 %collective-permute-done.7.received = bf16[32,1024]{1,0:T(8,128)(2,1)S(1)} collective-permute-done((bf16[32,1024]{1,0:T(8,128)(2,1)S(1)}, bf16[32,1024]{1,0:T(8,128)(2,1)S(1)}, u32[]{:S(2)}, u32[]{:S(2)}) %collective-permute-start.7) | collective-permute-done | bytes 65568 | tf_op jit(solution)/shard_map/ppermute | solution.py:279
  26.2 1.6 %collective-permute-start.8 = (bf16[32,1024]{1,0:T(8,128)(2,1)S(1)}, bf16[32,1024]{1,0:T(8,128)(2,1)S(1)}, u32[]{:S(2)}, u32[]{:S(2)}) collective-permute-start(bf16[32,1024]{1,0:T(8,128)(2,1)S(1)} %add.1), channel_id=1, source_target_pairs={{0,8},{4,12},{8,0},{12,4},{1,9},{5,13},{9,1},{13,5},{2,10},{6,14},... | collective-permute-start | bytes 196616 | tf_op jit(solution)/shard_map/ppermute | solution.py:279
  27.8 0.1 copy.6.candidates
  27.9 0.0 collective-permute-done.6.refs_1_
  27.9 2.7 %collective-permute-done.8.refs_2_ = bf16[32,1024]{1,0:T(8,128)(2,1)S(1)} collective-permute-done((bf16[32,1024]{1,0:T(8,128)(2,1)S(1)}, bf16[32,1024]{1,0:T(8,128)(2,1)S(1)}, u32[]{:S(2)}, u32[]{:S(2)}) %collective-permute-start.8) | collective-permute-done | bytes 65568 | tf_op jit(solution)/shard_map/ppermute | solution.py:279
  30.6 0.7 %finish.1 = bf16[32,1024]{1,0:T(8,128)(2,1)} custom-call(s32[32,16]{1,0:T(8,128)S(1)} %copy.6.candidates, f32[32,1024]{1,0:T(8,128)S(1)} %get-tuple-element.19.refs_0_, bf16[32,1024]{1,0:T(8,128)(2,1)S(1)} %collective-permute-done.6.refs_1_, bf16[32,1024]{1,0:T(8,128)(2,1)S(1)} %collective-permute-done.8.refs_2_), custom_call_target="tpu_custom_call" | custom-call | tf_op jit(solution)/shard_map/finish/pallas_call | solution.py:267
  (6 shorter events, 0.0 us)
Async XLA Ops:
  0.0 20.9 %copy-start = (bf16[1,1024,4096]{2,1,0:T(8,128)(2,1)S(1)}, bf16[1,1024,4096]{2,1,0:T(8,128)(2,1)}, u32[]{:S(2)}) copy-start(bf16[1,1024,4096]{2,1,0:T(8,128)(2,1)} %store.3) | copy-start | bytes 25165828
  2.0 11.2 %collective-permute-start.3 = (bf16[32,2304]{1,0:T(8,128)(2,1)S(1)}, bf16[32,2304]{1,0:T(8,128)(2,1)S(1)}, u32[]{:S(2)}, u32[]{:S(2)}) collective-permute-start(bf16[32,2304]{1,0:T(8,128)(2,1)S(1)} %condition.3.queries), channel_id=1, source_target_pairs={{0,1},{1,0},{2,3},{3,2},{4,5},{5,4},{6,7},{7,6},{8,9},{9,8},{10,11... | collective-permute-start | bytes 442376 | tf_op jit(solution)/shard_map/ppermute | solution.py:279
  5.1 8.6 %collective-permute-start.4 = (bf16[32,2304]{1,0:T(8,128)(2,1)S(1)}, bf16[32,2304]{1,0:T(8,128)(2,1)S(1)}, u32[]{:S(2)}, u32[]{:S(2)}) collective-permute-start(bf16[32,2304]{1,0:T(8,128)(2,1)S(1)} %condition.3.queries), channel_id=1, source_target_pairs={{0,2},{1,3},{2,0},{3,1},{4,6},{5,7},{6,4},{7,5},{8,10},{9,11},{10,... | collective-permute-start | bytes 442376 | tf_op jit(solution)/shard_map/ppermute | solution.py:279
  9.5 6.6 %collective-permute-start = (bf16[32,1792]{1,0:T(8,128)(2,1)S(1)}, bf16[32,1792]{1,0:T(8,128)(2,1)S(1)}, u32[]{:S(2)}, u32[]{:S(2)}) collective-permute-start(bf16[32,1792]{1,0:T(8,128)(2,1)S(1)} %condition.2.own), channel_id=1, source_target_pairs={{0,1},{1,0},{2,3},{3,2},{4,5},{5,4},{6,7},{7,6},{8,9},{9,8},{10,11... | collective-permute-start | bytes 344072 | tf_op jit(solution)/shard_map/ppermute | solution.py:279
  10.0 8.5 %collective-permute-start.1 = (bf16[32,1792]{1,0:T(8,128)(2,1)S(1)}, bf16[32,1792]{1,0:T(8,128)(2,1)S(1)}, u32[]{:S(2)}, u32[]{:S(2)}) collective-permute-start(bf16[32,1792]{1,0:T(8,128)(2,1)S(1)} %condition.2.own), channel_id=1, source_target_pairs={{0,2},{1,3},{2,0},{3,1},{4,6},{5,7},{6,4},{7,5},{8,10},{9,11},{10,... | collective-permute-start | bytes 344072 | tf_op jit(solution)/shard_map/ppermute | solution.py:279
  13.2 14.6 %copy-start.1 = (s32[32,16]{0,1:T(8,128)S(1)}, s32[32,16]{0,1:T(8,128)}, u32[]{:S(2)}) copy-start(s32[32,16]{0,1:T(8,128)} %param.9) | copy-start | bytes 6148
  13.7 7.3 %collective-permute-start.5 = (bf16[32,2304]{1,0:T(8,128)(2,1)S(1)}, bf16[32,2304]{1,0:T(8,128)(2,1)S(1)}, u32[]{:S(2)}, u32[]{:S(2)}) collective-permute-start(bf16[32,2304]{1,0:T(8,128)(2,1)S(1)} %collective-permute-done.4.far), channel_id=1, source_target_pairs={{0,1},{1,0},{2,3},{3,2},{4,5},{5,4},{6,7},{7,6},{8,9},{9,8},{10,11... | collective-permute-start | bytes 442376 | tf_op jit(solution)/shard_map/ppermute | solution.py:279
  18.5 5.2 %collective-permute-start.2 = (bf16[32,1792]{1,0:T(8,128)(2,1)S(1)}, bf16[32,1792]{1,0:T(8,128)(2,1)S(1)}, u32[]{:S(2)}, u32[]{:S(2)}) collective-permute-start(bf16[32,1792]{1,0:T(8,128)(2,1)S(1)} %collective-permute-done.1.far), channel_id=1, source_target_pairs={{0,1},{1,0},{2,3},{3,2},{4,5},{5,4},{6,7},{7,6},{8,9},{9,8},{10,11... | collective-permute-start | bytes 344072 | tf_op jit(solution)/shard_map/ppermute | solution.py:279
  24.9 1.3 %collective-permute-start.7 = (bf16[32,1024]{1,0:T(8,128)(2,1)S(1)}, bf16[32,1024]{1,0:T(8,128)(2,1)S(1)}, u32[]{:S(2)}, u32[]{:S(2)}) collective-permute-start(bf16[32,1024]{1,0:T(8,128)(2,1)S(1)} %get-tuple-element.22), channel_id=1, source_target_pairs={{0,4},{4,0},{8,12},{12,8},{1,5},{5,1},{9,13},{13,9},{2,6},{6,2},{1... | collective-permute-start | bytes 196616 | tf_op jit(solution)/shard_map/ppermute | solution.py:279
  25.0 2.9 %collective-permute-start.6 = (bf16[32,1024]{1,0:T(8,128)(2,1)S(1)}, bf16[32,1024]{1,0:T(8,128)(2,1)S(1)}, u32[]{:S(2)}, u32[]{:S(2)}) collective-permute-start(bf16[32,1024]{1,0:T(8,128)(2,1)S(1)} %get-tuple-element.20), channel_id=1, source_target_pairs={{0,4},{4,0},{8,12},{12,8},{1,5},{5,1},{9,13},{13,9},{2,6},{6,2},{1... | collective-permute-start | bytes 196616 | tf_op jit(solution)/shard_map/ppermute | solution.py:279
  26.2 4.3 %collective-permute-start.8 = (bf16[32,1024]{1,0:T(8,128)(2,1)S(1)}, bf16[32,1024]{1,0:T(8,128)(2,1)S(1)}, u32[]{:S(2)}, u32[]{:S(2)}) collective-permute-start(bf16[32,1024]{1,0:T(8,128)(2,1)S(1)} %add.1), channel_id=1, source_target_pairs={{0,8},{4,12},{8,0},{12,4},{1,9},{5,13},{9,1},{13,5},{2,10},{6,14},... | collective-permute-start | bytes 196616 | tf_op jit(solution)/shard_map/ppermute | solution.py:279

commit v23 on v22

--- a/solution.py
+++ b/solution.py
@@ -128,7 +128,7 @@
 
 
 STEP = 256
-LOW_PART = 18
+LOW_PART = 19
 MASKS = (3, 1, 2, 0)
 
 

time: 31.5 us -> 31.4 us (level)
  transfers between devices with their start and end apart: 9 -> 9, of which waited for: 5 -> 5; matrix products, arithmetic and copies ran while one was open for 0% -> 0% of each run, Pallas kernels for 20% -> 21%
where the time goes in v23:
time: 31.4 us; the launch traced here: 31.3 us
  starting transfers between devices  13.1 us (42%)
  Pallas kernels  10.5 us (33%)
  waiting for transfers between devices  7.57 us (24%)
    ppermute x9, starting transfers between devices, permuted(): lax.ppermute(value, axis, [(source, target_of(source) % count) for source...  13.1 us
    ppermute x9, waiting for transfers between devices, permuted(): lax.ppermute(value, axis, [(source, target_of(source) % count) for source...  7.57 us
    pallas_call x2, Pallas kernels, condition(): pl.pallas_call(functools.partial(condition_kernel, first, count), in_spec...  3.76 us
    pallas_call x1, Pallas kernels, score_own(): pl.pallas_call(own_kernel, in_specs=in_vmem(1) + [pl.BlockSpec(memory_spa...  3.35 us
    pallas_call x1, Pallas kernels, score_low(): pl.pallas_call(low_kernel, in_specs=in_vmem(5), out_specs=in_vmem(1)[0],...  1.45 us
    pallas_call x1, Pallas kernels, score_high(): pl.pallas_call(functools.partial(high_kernel, store.shape[2] - width), in...  1.19 us
    pallas_call x1, Pallas kernels, finish(): pl.pallas_call(functools.partial(finish_kernel, layers), in_specs=in_vmem...  0.74 us
  transfers between devices with their start and end apart: 9, of which 5 were waited for; matrix products, arithmetic and copies ran while one was open for 0% of the time, Pallas kernels for 21%

profile of v23, /device:TPU:0, one launch (start us, length us, event | category | flops | bytes accessed | tf_op | source)
XLA Modules:
  0.0 31.3 jit_solution(12460936491599798069)
XLA Ops:
  0.0 2.0 %condition.3.queries = bf16[32,2432]{1,0:T(8,128)(2,1)S(1)} custom-call(bf16[1,32,4096]{2,1,0:T(8,128)(2,1)} %queries_in.3, f32[1,64,64]{2,1,0:T(8,128)} %left_in.3, f32[1,64,64]{2,1,0:T(8,128)} %right_in.3), custom_call_target="tpu_custom_call" | custom-call | flops 536870912 | bytes 524288 | tf_op jit(solution)/shard_map/condition/pallas_call | solution.py:111
  2.0 3.1 %collective-permute-start.3 = (bf16[32,2432]{1,0:T(8,128)(2,1)S(1)}, bf16[32,2432]{1,0:T(8,128)(2,1)S(1)}, u32[]{:S(2)}, u32[]{:S(2)}) collective-permute-start(bf16[32,2432]{1,0:T(8,128)(2,1)S(1)} %condition.3.queries), channel_id=1, source_target_pairs={{0,1},{1,0},{2,3},{3,2},{4,5},{5,4},{6,7},{7,6},{8,9},{9,8},{10,11... | collective-permute-start | bytes 466952 | tf_op jit(solution)/shard_map/ppermute | solution.py:279
  5.1 2.6 %collective-permute-start.4 = (bf16[32,2432]{1,0:T(8,128)(2,1)S(1)}, bf16[32,2432]{1,0:T(8,128)(2,1)S(1)}, u32[]{:S(2)}, u32[]{:S(2)}) collective-permute-start(bf16[32,2432]{1,0:T(8,128)(2,1)S(1)} %condition.3.queries), channel_id=1, source_target_pairs={{0,2},{1,3},{2,0},{3,1},{4,6},{5,7},{6,4},{7,5},{8,10},{9,11},{10,... | collective-permute-start | bytes 466952 | tf_op jit(solution)/shard_map/ppermute | solution.py:279
  7.7 1.7 %condition.2.own = bf16[32,1664]{1,0:T(8,128)(2,1)S(1)} custom-call(bf16[1,32,4096]{2,1,0:T(8,128)(2,1)} %queries_in.3, f32[1,64,64]{2,1,0:T(8,128)} %left_in.3, f32[1,64,64]{2,1,0:T(8,128)} %right_in.3), custom_call_target="tpu_custom_call" | custom-call | flops 536870912 | bytes 524288 | tf_op jit(solution)/shard_map/condition/pallas_call | solution.py:111
  9.5 0.5 %collective-permute-start = (bf16[32,1664]{1,0:T(8,128)(2,1)S(1)}, bf16[32,1664]{1,0:T(8,128)(2,1)S(1)}, u32[]{:S(2)}, u32[]{:S(2)}) collective-permute-start(bf16[32,1664]{1,0:T(8,128)(2,1)S(1)} %condition.2.own), channel_id=1, source_target_pairs={{0,1},{1,0},{2,3},{3,2},{4,5},{5,4},{6,7},{7,6},{8,9},{9,8},{10,11... | collective-permute-start | bytes 319496 | tf_op jit(solution)/shard_map/ppermute | solution.py:279
  10.0 0.0 collective-permute-start.1
  10.0 3.3 %score_own.1.own_low = f32[1024,128]{1,0:T(8,128)S(1)} custom-call(bf16[32,2432]{1,0:T(8,128)(2,1)S(1)} %condition.3.queries, bf16[1,1024,4096]{2,1,0:T(8,128)(2,1)} %store.3), custom_call_target="tpu_custom_call" | custom-call | flops 159383552 | bytes 4980736 | tf_op jit(solution)/shard_map/score_own/pallas_call | solution.py:168
  13.3 0.0 copy-start.1
  13.4 0.9 %collective-permute-done.4.far = bf16[32,2432]{1,0:T(8,128)(2,1)S(1)} collective-permute-done((bf16[32,2432]{1,0:T(8,128)(2,1)S(1)}, bf16[32,2432]{1,0:T(8,128)(2,1)S(1)}, u32[]{:S(2)}, u32[]{:S(2)}) %collective-permute-start.4) | collective-permute-done | bytes 155680 | tf_op jit(solution)/shard_map/ppermute | solution.py:279
  14.2 2.2 %collective-permute-start.5 = (bf16[32,2432]{1,0:T(8,128)(2,1)S(1)}, bf16[32,2432]{1,0:T(8,128)(2,1)S(1)}, u32[]{:S(2)}, u32[]{:S(2)}) collective-permute-start(bf16[32,2432]{1,0:T(8,128)(2,1)S(1)} %collective-permute-done.4.far), channel_id=1, source_target_pairs={{0,1},{1,0},{2,3},{3,2},{4,5},{5,4},{6,7},{7,6},{8,9},{9,8},{10,11... | collective-permute-start | bytes 466952 | tf_op jit(solution)/shard_map/ppermute | solution.py:279
  16.4 2.0 %collective-permute-done.1.far = bf16[32,1664]{1,0:T(8,128)(2,1)S(1)} collective-permute-done((bf16[32,1664]{1,0:T(8,128)(2,1)S(1)}, bf16[32,1664]{1,0:T(8,128)(2,1)S(1)}, u32[]{:S(2)}, u32[]{:S(2)}) %collective-permute-start.1) | collective-permute-done | bytes 106528 | tf_op jit(solution)/shard_map/ppermute | solution.py:279
  18.5 2.5 %collective-permute-start.2 = (bf16[32,1664]{1,0:T(8,128)(2,1)S(1)}, bf16[32,1664]{1,0:T(8,128)(2,1)S(1)}, u32[]{:S(2)}, u32[]{:S(2)}) collective-permute-start(bf16[32,1664]{1,0:T(8,128)(2,1)S(1)} %collective-permute-done.1.far), channel_id=1, source_target_pairs={{0,1},{1,0},{2,3},{3,2},{4,5},{5,4},{6,7},{7,6},{8,9},{9,8},{10,11... | collective-permute-start | bytes 319496 | tf_op jit(solution)/shard_map/ppermute | solution.py:279
  21.0 0.0 collective-permute-done.5.last
  21.0 1.4 %score_low.1.low = f32[1024,128]{1,0:T(8,128)S(1)} custom-call(bf16[32,2432]{1,0:T(8,128)(2,1)S(1)} %collective-permute-done.3.near, bf16[32,2432]{1,0:T(8,128)(2,1)S(1)} %collective-permute-done.4.far, bf16[32,2432]{1,0:T(8,128)(2,1)S(1)} %collective-permute-done.5.last, bf16[1,1024,4096]{2,1,0:T(8,128)(2,1)S(1)} %copy-done, f32[1024,128]{1,0:T(8,128)S(1)} %score_own.1.own_low), custom_call_target="tpu_custom_call" | custom-call | flops 478150656 | bytes 4980736 | tf_op jit(solution)/shard_map/score_low/pallas_call | solution.py:196
  22.5 1.2 %collective-permute-done.2.last = bf16[32,1664]{1,0:T(8,128)(2,1)S(1)} collective-permute-done((bf16[32,1664]{1,0:T(8,128)(2,1)S(1)}, bf16[32,1664]{1,0:T(8,128)(2,1)S(1)}, u32[]{:S(2)}, u32[]{:S(2)}) %collective-permute-start.2) | collective-permute-done | bytes 106528 | tf_op jit(solution)/shard_map/ppermute | solution.py:279
  23.7 1.2 %score_high.1 = (bf16[32,1024]{1,0:T(8,128)(2,1)S(1)}, bf16[32,1024]{1,0:T(8,128)(2,1)S(1)}, f32[32,1024]{1,0:T(8,128)S(1)}, f32[32,1024]{1,0:T(8,128)S(1)}) custom-call(bf16[32,1664]{1,0:T(8,128)(2,1)S(1)} %collective-permute-done.near, bf16[32,1664]{1,0:T(8,128)(2,1)S(1)} %collective-permute-done.1.far, bf16[32,1664]{1,0:T(8,128)(2,1)S(1)} %collective-permute-done.2.last, ...), custom_call_target="tpu_custom_call" | custom-call | flops 436207616 | bytes 3407872 | tf_op jit(solution)/shard_map/score_high/pallas_call | solution.py:221
  24.9 0.1 collective-permute-start.7
  25.0 0.5 %collective-permute-start.6 = (bf16[32,1024]{1,0:T(8,128)(2,1)S(1)}, bf16[32,1024]{1,0:T(8,128)(2,1)S(1)}, u32[]{:S(2)}, u32[]{:S(2)}) collective-permute-start(bf16[32,1024]{1,0:T(8,128)(2,1)S(1)} %get-tuple-element.20), channel_id=1, source_target_pairs={{0,4},{4,0},{8,12},{12,8},{1,5},{5,1},{9,13},{13,9},{2,6},{6,2},{1... | collective-permute-start | bytes 196616 | tf_op jit(solution)/shard_map/ppermute | solution.py:279
  25.4 0.7 %collective-permute-done.7.received = bf16[32,1024]{1,0:T(8,128)(2,1)S(1)} collective-permute-done((bf16[32,1024]{1,0:T(8,128)(2,1)S(1)}, bf16[32,1024]{1,0:T(8,128)(2,1)S(1)}, u32[]{:S(2)}, u32[]{:S(2)}) %collective-permute-start.7) | collective-permute-done | bytes 65568 | tf_op jit(solution)/shard_map/ppermute | solution.py:279
  26.2 1.6 %collective-permute-start.8 = (bf16[32,1024]{1,0:T(8,128)(2,1)S(1)}, bf16[32,1024]{1,0:T(8,128)(2,1)S(1)}, u32[]{:S(2)}, u32[]{:S(2)}) collective-permute-start(bf16[32,1024]{1,0:T(8,128)(2,1)S(1)} %add.1), channel_id=1, source_target_pairs={{0,8},{4,12},{8,0},{12,4},{1,9},{5,13},{9,1},{13,5},{2,10},{6,14},... | collective-permute-start | bytes 196616 | tf_op jit(solution)/shard_map/ppermute | solution.py:279
  27.8 0.1 copy.6.candidates
  27.9 0.0 collective-permute-done.6.refs_1_
  27.9 2.7 %collective-permute-done.8.refs_2_ = bf16[32,1024]{1,0:T(8,128)(2,1)S(1)} collective-permute-done((bf16[32,1024]{1,0:T(8,128)(2,1)S(1)}, bf16[32,1024]{1,0:T(8,128)(2,1)S(1)}, u32[]{:S(2)}, u32[]{:S(2)}) %collective-permute-start.8) | collective-permute-done | bytes 65568 | tf_op jit(solution)/shard_map/ppermute | solution.py:279
  30.5 0.7 %finish.1 = bf16[32,1024]{1,0:T(8,128)(2,1)} custom-call(s32[32,16]{1,0:T(8,128)S(1)} %copy.6.candidates, f32[32,1024]{1,0:T(8,128)S(1)} %get-tuple-element.19.refs_0_, bf16[32,1024]{1,0:T(8,128)(2,1)S(1)} %collective-permute-done.6.refs_1_, bf16[32,1024]{1,0:T(8,128)(2,1)S(1)} %collective-permute-done.8.refs_2_), custom_call_target="tpu_custom_call" | custom-call | tf_op jit(solution)/shard_map/finish/pallas_call | solution.py:267
  (6 shorter events, 0.0 us)
Async XLA Ops:
  0.0 21.0 %copy-start = (bf16[1,1024,4096]{2,1,0:T(8,128)(2,1)S(1)}, bf16[1,1024,4096]{2,1,0:T(8,128)(2,1)}, u32[]{:S(2)}) copy-start(bf16[1,1024,4096]{2,1,0:T(8,128)(2,1)} %store.3) | copy-start | bytes 25165828
  2.0 11.3 %collective-permute-start.3 = (bf16[32,2432]{1,0:T(8,128)(2,1)S(1)}, bf16[32,2432]{1,0:T(8,128)(2,1)S(1)}, u32[]{:S(2)}, u32[]{:S(2)}) collective-permute-start(bf16[32,2432]{1,0:T(8,128)(2,1)S(1)} %condition.3.queries), channel_id=1, source_target_pairs={{0,1},{1,0},{2,3},{3,2},{4,5},{5,4},{6,7},{7,6},{8,9},{9,8},{10,11... | collective-permute-start | bytes 466952 | tf_op jit(solution)/shard_map/ppermute | solution.py:279
  5.1 9.1 %collective-permute-start.4 = (bf16[32,2432]{1,0:T(8,128)(2,1)S(1)}, bf16[32,2432]{1,0:T(8,128)(2,1)S(1)}, u32[]{:S(2)}, u32[]{:S(2)}) collective-permute-start(bf16[32,2432]{1,0:T(8,128)(2,1)S(1)} %condition.3.queries), channel_id=1, source_target_pairs={{0,2},{1,3},{2,0},{3,1},{4,6},{5,7},{6,4},{7,5},{8,10},{9,11},{10,... | collective-permute-start | bytes 466952 | tf_op jit(solution)/shard_map/ppermute | solution.py:279
  9.5 7.0 %collective-permute-start = (bf16[32,1664]{1,0:T(8,128)(2,1)S(1)}, bf16[32,1664]{1,0:T(8,128)(2,1)S(1)}, u32[]{:S(2)}, u32[]{:S(2)}) collective-permute-start(bf16[32,1664]{1,0:T(8,128)(2,1)S(1)} %condition.2.own), channel_id=1, source_target_pairs={{0,1},{1,0},{2,3},{3,2},{4,5},{5,4},{6,7},{7,6},{8,9},{9,8},{10,11... | collective-permute-start | bytes 319496 | tf_op jit(solution)/shard_map/ppermute | solution.py:279
  10.0 8.5 %collective-permute-start.1 = (bf16[32,1664]{1,0:T(8,128)(2,1)S(1)}, bf16[32,1664]{1,0:T(8,128)(2,1)S(1)}, u32[]{:S(2)}, u32[]{:S(2)}) collective-permute-start(bf16[32,1664]{1,0:T(8,128)(2,1)S(1)} %condition.2.own), channel_id=1, source_target_pairs={{0,2},{1,3},{2,0},{3,1},{4,6},{5,7},{6,4},{7,5},{8,10},{9,11},{10,... | collective-permute-start | bytes 319496 | tf_op jit(solution)/shard_map/ppermute | solution.py:279
  13.3 14.4 %copy-start.1 = (s32[32,16]{0,1:T(8,128)S(1)}, s32[32,16]{0,1:T(8,128)}, u32[]{:S(2)}) copy-start(s32[32,16]{0,1:T(8,128)} %param.9) | copy-start | bytes 6148
  14.2 6.8 %collective-permute-start.5 = (bf16[32,2432]{1,0:T(8,128)(2,1)S(1)}, bf16[32,2432]{1,0:T(8,128)(2,1)S(1)}, u32[]{:S(2)}, u32[]{:S(2)}) collective-permute-start(bf16[32,2432]{1,0:T(8,128)(2,1)S(1)} %collective-permute-done.4.far), channel_id=1, source_target_pairs={{0,1},{1,0},{2,3},{3,2},{4,5},{5,4},{6,7},{7,6},{8,9},{9,8},{10,11... | collective-permute-start | bytes 466952 | tf_op jit(solution)/shard_map/ppermute | solution.py:279
  18.5 5.2 %collective-permute-start.2 = (bf16[32,1664]{1,0:T(8,128)(2,1)S(1)}, bf16[32,1664]{1,0:T(8,128)(2,1)S(1)}, u32[]{:S(2)}, u32[]{:S(2)}) collective-permute-start(bf16[32,1664]{1,0:T(8,128)(2,1)S(1)} %collective-permute-done.1.far), channel_id=1, source_target_pairs={{0,1},{1,0},{2,3},{3,2},{4,5},{5,4},{6,7},{7,6},{8,9},{9,8},{10,11... | collective-permute-start | bytes 319496 | tf_op jit(solution)/shard_map/ppermute | solution.py:279
  24.9 1.3 %collective-permute-start.7 = (bf16[32,1024]{1,0:T(8,128)(2,1)S(1)}, bf16[32,1024]{1,0:T(8,128)(2,1)S(1)}, u32[]{:S(2)}, u32[]{:S(2)}) collective-permute-start(bf16[32,1024]{1,0:T(8,128)(2,1)S(1)} %get-tuple-element.22), channel_id=1, source_target_pairs={{0,4},{4,0},{8,12},{12,8},{1,5},{5,1},{9,13},{13,9},{2,6},{6,2},{1... | collective-permute-start | bytes 196616 | tf_op jit(solution)/shard_map/ppermute | solution.py:279
  25.0 2.9 %collective-permute-start.6 = (bf16[32,1024]{1,0:T(8,128)(2,1)S(1)}, bf16[32,1024]{1,0:T(8,128)(2,1)S(1)}, u32[]{:S(2)}, u32[]{:S(2)}) collective-permute-start(bf16[32,1024]{1,0:T(8,128)(2,1)S(1)} %get-tuple-element.20), channel_id=1, source_target_pairs={{0,4},{4,0},{8,12},{12,8},{1,5},{5,1},{9,13},{13,9},{2,6},{6,2},{1... | collective-permute-start | bytes 196616 | tf_op jit(solution)/shard_map/ppermute | solution.py:279
  26.2 4.3 %collective-permute-start.8 = (bf16[32,1024]{1,0:T(8,128)(2,1)S(1)}, bf16[32,1024]{1,0:T(8,128)(2,1)S(1)}, u32[]{:S(2)}, u32[]{:S(2)}) collective-permute-start(bf16[32,1024]{1,0:T(8,128)(2,1)S(1)} %add.1), channel_id=1, source_target_pairs={{0,8},{4,12},{8,0},{12,4},{1,9},{5,13},{9,1},{13,5},{2,10},{6,14},... | collective-permute-start | bytes 196616 | tf_op jit(solution)/shard_map/ppermute | solution.py:279
